TPU v7x, 32 devices: a whole 2x2x4 slice. The times are simulated.
32 devices in a mesh: lead: 4 (over x, core), lat: 2 (over y), lon: 4 (over z).
Axes of the slice: x: 2, y: 2, z: 4, core: 2. Of those that a mesh axis runs over, the one named last changes fastest.
Arguments:
- head_grads: bfloat16 [8, 8, 8, 128, 128], P('lead', None, 'lat', 'lon'), may hold values from -6 to 6
- head_weights: bfloat16 [8, 9, 256, 128], P('lead'), may hold values from -0.0625 to 0.0625
- encoder_input: bfloat16 [8, 8, 128, 128], P('lead', 'lat', 'lon'), may hold values from -6 to 6
- pre_first: bfloat16 [8, 8, 128, 256], P('lead', 'lat', 'lon'), may hold values from -8 to 8
- pre_second: bfloat16 [8, 8, 128, 256], P('lead', 'lat', 'lon'), may hold values from -8 to 8
- w_first: bfloat16 [9, 128, 256], replicated, may hold values from -0.1875 to 0.1875
- w_second: bfloat16 [9, 256, 256], replicated, may hold values from -0.125 to 0.125
Outputs:
- input_grad: bfloat16 [8, 8, 128, 128], P('lead', 'lat', 'lon')
- weight_grad_first: float32 [294912], P(('lat', 'lon'))
- weight_grad_second: float32 [589824], P(('lat', 'lon'))
All inputs are finite; a program needn't handle non-finite values.
Results may differ from a plain program's by a relative error of at most 0.022.
Values may be sent and summed in bfloat16 or wider, within the bound.
No kernel may reach another device: no remote copies, remote signals or barrier semaphores. Data moves between devices by JAX's collectives and lax.ppermute only.
A program may use at most 64 MiB of HBM per device.

v0:
```python
import math

import jax
import jax.numpy as jnp
from jax import lax
from jax.sharding import PartitionSpec as P

OFFSETS = [(-1, -1), (-1, 0), (-1, 1), (0, -1), (0, 0), (0, 1), (1, -1), (1, 0), (1, 1)]


def with_halo(block, sides, width, periodic):
    for axis, dim in sides:
        count = lax.axis_size(axis)
        forward = [(i, i + 1) for i in range(count - 1)]
        if periodic:
            forward.append((count - 1, 0))
        backward = [(target, source) for source, target in forward]
        low = lax.ppermute(
            lax.slice_in_dim(block, block.shape[dim] - width, None, axis=dim), axis, forward
        )
        high = lax.ppermute(lax.slice_in_dim(block, 0, width, axis=dim), axis, backward)
        block = jnp.concatenate([low, block, high], axis=dim)
    return block


def gelu_value(values):
    return 0.5 * values * (1.0 + lax.erf(values * 0.7071067811865476))


def gelu_slope(values):
    return (
        0.5 * (1.0 + lax.erf(values * 0.7071067811865476))
        + values * jnp.exp(-0.5 * values * values) * 0.3989422804014327
    )


def widen(source):
    extended = with_halo(source, (("lon", 2),), 1, True)
    return with_halo(extended, (("lat", 1),), 1, False)


def window(padded, step_row, step_col):
    height = padded.shape[-3] - 2
    breadth = padded.shape[-2] - 2
    return padded[
        ..., 1 + step_row : 1 + step_row + height, 1 + step_col : 1 + step_col + breadth, :
    ]


def per_device(head_grads, head_weights, encoder_input, pre_first, pre_second, w_first, w_second):
    heads_here, batch_all, height, breadth, head_channels = head_grads.shape
    samples = encoder_input.shape[0]
    latent_width = head_weights.shape[2]
    merged = head_grads.reshape(heads_here * batch_all, height, breadth, head_channels)
    padded_heads = widen(merged).reshape(
        heads_here, batch_all, height + 2, breadth + 2, head_channels
    )
    summed = jnp.zeros(
        (samples * lax.axis_size("lead"), height, breadth, latent_width), jnp.float32
    )
    for latent_offset, (latent_step_row, latent_step_col) in enumerate(OFFSETS):
        moved = window(padded_heads, -latent_step_row, -latent_step_col)
        summed = summed + jnp.einsum(
            "hbrcj,hdj->brcd",
            moved,
            head_weights[:, latent_offset],
            preferred_element_type=jnp.float32,
        )
    latent_grad = lax.psum_scatter(
        summed.astype(jnp.bfloat16), "lead", scatter_dimension=0, tiled=True
    ).astype(jnp.float32)
    pre_two = pre_second.astype(jnp.float32)
    pre_one = pre_first.astype(jnp.float32)
    da_second = (latent_grad * gelu_slope(pre_two)).astype(jnp.bfloat16)
    act_first = gelu_value(pre_one).astype(jnp.bfloat16)
    padded_act = widen(act_first)
    padded_input = widen(encoder_input)
    padded_second = widen(da_second)
    grad_second = []
    linear_first = jnp.zeros((samples, height, breadth, latent_width), jnp.float32)
    for offset, (step_row, step_col) in enumerate(OFFSETS):
        grad_second.append(
            jnp.einsum(
                "brci,brcd->id",
                window(padded_act, step_row, step_col),
                da_second,
                preferred_element_type=jnp.float32,
            )
        )
        linear_first = linear_first + jnp.einsum(
            "brcd,id->brci",
            window(padded_second, -step_row, -step_col),
            w_second[offset],
            preferred_element_type=jnp.float32,
        )
    da_first = (linear_first * gelu_slope(pre_one)).astype(jnp.bfloat16)
    padded_first = widen(da_first)
    grad_first = []
    input_sum = jnp.zeros((samples, height, breadth, w_first.shape[1]), jnp.float32)
    for offset, (step_row, step_col) in enumerate(OFFSETS):
        grad_first.append(
            jnp.einsum(
                "brcj,brcd->jd",
                window(padded_input, step_row, step_col),
                da_first,
                preferred_element_type=jnp.float32,
            )
        )
        input_sum = input_sum + jnp.einsum(
            "brcd,jd->brcj",
            window(padded_first, -step_row, -step_col),
            w_first[offset],
            preferred_element_type=jnp.float32,
        )
    input_grad = input_sum.astype(jnp.bfloat16)
    cells_total = (
        samples
        * lax.axis_size("lead")
        * height
        * lax.axis_size("lat")
        * breadth
        * lax.axis_size("lon")
    )
    norm_factor = 1.0 / math.sqrt(cells_total)
    flat_first = (jnp.stack(grad_first) * norm_factor).reshape(-1)
    flat_second = (jnp.stack(grad_second) * norm_factor).reshape(-1)
    whole_first, whole_second = (
        lax.psum(flat_first.astype(jnp.bfloat16), "lead").astype(jnp.float32),
        lax.psum(flat_second.astype(jnp.bfloat16), "lead").astype(jnp.float32),
    )
    result_first, result_second = (
        lax.psum_scatter(whole_first, ("lat", "lon"), scatter_dimension=0, tiled=True),
        lax.psum_scatter(whole_second, ("lat", "lon"), scatter_dimension=0, tiled=True),
    )
    return (input_grad, result_first, result_second)


def solution(mesh):
    in_specs = (
        P("lead", None, "lat", "lon", None),
        P("lead", None, None, None),
        P("lead", "lat", "lon", None),
        P("lead", "lat", "lon", None),
        P("lead", "lat", "lon", None),
        P(),
        P(),
    )
    out_specs = (P("lead", "lat", "lon", None), P(("lat", "lon")), P(("lat", "lon")))
    return jax.shard_map(
        per_device, mesh=mesh, in_specs=in_specs, out_specs=out_specs, check_vma=False
    )
```

profile of v0, /device:TPU:0, one launch (start us, length us, event | category | flops | bytes accessed | tf_op | source)
XLA Modules:
  0.0 282.0 jit_solution(11314492975673343995)
XLA Ops:
  7.2 1.4 copy.154
  8.6 3.1 %collective-permute-start = (bf16[16,4,1,128]{3,0,2,1:T(8,128)(2,1)S(1)}, bf16[16,4,1,128]{3,0,2,1:T(8,128)(2,1)S(1)}, u32[]{:S(2)}, u32[]{:S(2)}) collective-permute-start(bf16[16,4,1,128]{3,0,2,1:T(8,128)(2,1)S(1)} %get-tuple-element.18), channel_id=1, source_target_pairs={{0,1},{1,2},{2,3},{3,0},{4,5},{5,6},{6,7},{7,4},{8,9},{9,10},{10,1... | collective-permute-start | bytes 49160 | tf_op jit(solution)/shard_map/ppermute | solution.py:18
  11.7 2.1 collective-permute-start.1
  13.8 1.8 collective-permute-done
  15.6 3.5 %collective-permute-start.2 = (bf16[16,1,34,128]{3,0,2,1:T(8,128)(2,1)S(1)}, bf16[16,1,34,128]{3,0,2,1:T(8,128)(2,1)S(1)}, u32[]{:S(2)}, u32[]{:S(2)}) collective-permute-start(bf16[16,1,34,128]{3,0,2,1:T(8,128)(2,1)S(1)} %get-tuple-element.16), channel_id=1, source_target_pairs={{0,4},{1,5},{2,6},{3,7},{8,12},{9,13},{10,14},{11,15},{16,20},{17,... | collective-permute-start | bytes 417800 | tf_op jit(solution)/shard_map/ppermute | solution.py:18
  19.1 1.3 collective-permute-start.3
  20.4 1.3 collective-permute-done.2
  21.7 4.4 %collective-permute-done.3 = bf16[16,1,34,128]{3,0,2,1:T(8,128)(2,1)S(1)} collective-permute-done((bf16[16,1,34,128]{3,0,2,1:T(8,128)(2,1)S(1)}, bf16[16,1,34,128]{3,0,2,1:T(8,128)(2,1)S(1)}, u32[]{:S(2)}, u32[]{:S(2)}) %collective-permute-start.3) | collective-permute-done | bytes 139296 | tf_op jit(solution)/shard_map/ppermute | solution.py:21
  26.2 0.7 fusion.175
  27.0 0.5 copy-done.2
  27.5 0.3 convolution_bitcast_fusion
  27.9 0.3 convolution_bitcast_fusion.1
  28.2 0.3 convolution_bitcast_fusion.2
  28.6 0.3 convolution_bitcast_fusion.3
  28.9 0.3 convolution_bitcast_fusion.4
  29.3 0.3 convolution_bitcast_fusion.5
  29.6 0.3 convolution_bitcast_fusion.6
  30.0 0.3 convolution_bitcast_fusion.7
  30.4 1.5 fusion.8
  31.9 1.4 collective-permute-start.12
  33.3 2.5 collective-permute-start.13
  36.0 3.8 %collective-permute-start.17 = (bf16[2,4,1,256]{3,2,1,0:T(2,128)(2,1)S(1)}, bf16[2,4,1,256]{3,2,1,0:T(2,128)(2,1)S(1)}, u32[]{:S(2)}, u32[]{:S(2)}) collective-permute-start(bf16[2,4,1,256]{3,2,1,0:T(2,128)(2,1)S(1)} %get-tuple-element.33), channel_id=1, source_target_pairs={{1,0},{2,1},{3,2},{0,3},{5,4},{6,5},{7,6},{4,7},{9,8},{10,9},{11,1... | collective-permute-start | bytes 12296 | tf_op jit(solution)/shard_map/ppermute | solution.py:21
  39.8 0.6 dynamic-slice
  41.8 1.5 collective-permute-start.14
  43.3 1.3 collective-permute-start.15
  44.6 4.5 %collective-permute-start.18 = (bf16[2,1,34,256]{3,2,1,0:T(8,128)(2,1)S(1)}, bf16[2,1,34,256]{3,2,1,0:T(8,128)(2,1)S(1)}, u32[]{:S(2)}, u32[]{:S(2)}) collective-permute-start(bf16[2,1,34,256]{3,2,1,0:T(8,128)(2,1)S(1)} %get-tuple-element.23), channel_id=1, source_target_pairs={{0,4},{1,5},{2,6},{3,7},{8,12},{9,13},{10,14},{11,15},{16,20},{17,... | collective-permute-start | bytes 104456 | tf_op jit(solution)/shard_map/ppermute | solution.py:18
  49.2 1.3 collective-permute-start.19
  50.8 4.2 %collective-permute-done.19 = bf16[2,1,34,256]{3,2,1,0:T(8,128)(2,1)S(1)} collective-permute-done((bf16[2,1,34,256]{3,2,1,0:T(8,128)(2,1)S(1)}, bf16[2,1,34,256]{3,2,1,0:T(8,128)(2,1)S(1)}, u32[]{:S(2)}, u32[]{:S(2)}) %collective-permute-start.19) | collective-permute-done | bytes 34848 | tf_op jit(solution)/shard_map/ppermute | solution.py:21
  55.2 1.0 fusion.65
  58.7 2.3 collective-permute-start.5
  61.3 2.2 copy.134
  63.5 3.0 %collective-permute-done.4 = bf16[2,4,1,256]{3,2,1,0:T(2,128)(2,1)S(1)} collective-permute-done((bf16[2,4,1,256]{3,2,1,0:T(2,128)(2,1)S(1)}, bf16[2,4,1,256]{3,2,1,0:T(2,128)(2,1)S(1)}, u32[]{:S(2)}, u32[]{:S(2)}) %collective-permute-start.4) | collective-permute-done | bytes 4128 | tf_op jit(solution)/shard_map/ppermute | solution.py:18
  66.5 1.3 collective-permute-start.6
  67.8 4.5 %collective-permute-start.7 = (bf16[2,1,34,256]{3,2,1,0:T(8,128)(2,1)S(1)}, bf16[2,1,34,256]{3,2,1,0:T(8,128)(2,1)S(1)}, u32[]{:S(2)}, u32[]{:S(2)}) collective-permute-start(bf16[2,1,34,256]{3,2,1,0:T(8,128)(2,1)S(1)} %get-tuple-element.31), channel_id=1, source_target_pairs={{0,4},{1,5},{2,6},{3,7},{8,12},{9,13},{10,14},{11,15},{16,20},{17,... | collective-permute-start | bytes 104456 | tf_op jit(solution)/shard_map/ppermute | solution.py:18
  72.6 1.4 collective-permute-done.7
  75.5 0.3 fusion.25
  77.8 0.9 collective-permute-start.9
  78.7 1.2 collective-permute-start.8
  80.0 1.3 copy.133
  81.5 2.6 collective-permute-done.8
  84.2 1.3 collective-permute-start.10
  85.5 4.5 %collective-permute-start.11 = (bf16[2,1,34,256]{3,2,1,0:T(8,128)(2,1)S(1)}, bf16[2,1,34,256]{3,2,1,0:T(8,128)(2,1)S(1)}, u32[]{:S(2)}, u32[]{:S(2)}) collective-permute-start(bf16[2,1,34,256]{3,2,1,0:T(8,128)(2,1)S(1)} %get-tuple-element.27), channel_id=1, source_target_pairs={{0,4},{1,5},{2,6},{3,7},{8,12},{9,13},{10,14},{11,15},{16,20},{17,... | collective-permute-start | bytes 104456 | tf_op jit(solution)/shard_map/ppermute | solution.py:18
  90.2 1.5 collective-permute-done.11
  92.9 0.8 fusion.41
  93.7 34.2 %all-reduce.7.cloned.1.call-done = (bf16[294912]{0:T(1024)(128)(2,1)}, bf16[589824]{0:T(1024)(128)(2,1)}) async-done(((bf16[294912]{0:T(1024)(128)(2,1)}, bf16[589824]{0:T(1024)(128)(2,1)}), (bf16[294912]{0:T(1024)(128)(2,1)}, bf16[589824]{0:T(1024)(128)(2,1)})) %all-reduce.7.cloned.1.call-update) | async-done | bytes 1769488 | tf_op jit(solution)/shard_map/psum | solution.py:128
  128.0 145.7 %all-reduce.8 = (f32[294912]{0:T(1024)S(1)}, f32[589824]{0:T(1024)S(1)}) all-reduce(bf16[294912]{0:T(1024)(128)(2,1)} %get-tuple-element.5, bf16[589824]{0:T(1024)(128)(2,1)} %get-tuple-element.6), channel_id=3, replica_groups=mesh['lead'=4,'lat'=2,'lon'=4] {'lat','lon'}, use_global_device_ids=true, to_apply=%region_2.0.clone | all-reduce | flops 884736 | bytes 5308416
  273.7 0.7 dynamic-slice.3
  274.5 0.7 dynamic-slice.1
  (84 shorter events, 8.9 us)
Async XLA Ops:
  7.2 48.0 %reduce-scatter.2.cloned.1.call-start = ((), (), s32[]{:S(2)}) async-start(), calls=%async_computation.1 | async-start | bytes 655360 | tf_op jit(solution)/shard_map/reduce_scatter | solution.py:69
  8.6 6.9 %collective-permute-start = (bf16[16,4,1,128]{3,0,2,1:T(8,128)(2,1)S(1)}, bf16[16,4,1,128]{3,0,2,1:T(8,128)(2,1)S(1)}, u32[]{:S(2)}, u32[]{:S(2)}) collective-permute-start(bf16[16,4,1,128]{3,0,2,1:T(8,128)(2,1)S(1)} %get-tuple-element.18), channel_id=1, source_target_pairs={{0,1},{1,2},{2,3},{3,0},{4,5},{5,6},{6,7},{7,4},{8,9},{9,10},{10,1... | collective-permute-start | bytes 49160 | tf_op jit(solution)/shard_map/ppermute | solution.py:18
  11.7 3.9 %collective-permute-start.1 = (bf16[16,4,1,128]{3,0,2,1:T(8,128)(2,1)S(1)}, bf16[16,4,1,128]{3,0,2,1:T(8,128)(2,1)S(1)}, u32[]{:S(2)}, u32[]{:S(2)}) collective-permute-start(bf16[16,4,1,128]{3,0,2,1:T(8,128)(2,1)S(1)} %get-tuple-element.19), channel_id=1, source_target_pairs={{1,0},{2,1},{3,2},{0,3},{5,4},{6,5},{7,6},{4,7},{9,8},{10,9},{11,1... | collective-permute-start | bytes 49160 | tf_op jit(solution)/shard_map/ppermute | solution.py:21
  15.6 6.1 %collective-permute-start.2 = (bf16[16,1,34,128]{3,0,2,1:T(8,128)(2,1)S(1)}, bf16[16,1,34,128]{3,0,2,1:T(8,128)(2,1)S(1)}, u32[]{:S(2)}, u32[]{:S(2)}) collective-permute-start(bf16[16,1,34,128]{3,0,2,1:T(8,128)(2,1)S(1)} %get-tuple-element.16), channel_id=1, source_target_pairs={{0,4},{1,5},{2,6},{3,7},{8,12},{9,13},{10,14},{11,15},{16,20},{17,... | collective-permute-start | bytes 417800 | tf_op jit(solution)/shard_map/ppermute | solution.py:18
  19.1 6.9 %collective-permute-start.3 = (bf16[16,1,34,128]{3,0,2,1:T(8,128)(2,1)S(1)}, bf16[16,1,34,128]{3,0,2,1:T(8,128)(2,1)S(1)}, u32[]{:S(2)}, u32[]{:S(2)}) collective-permute-start(bf16[16,1,34,128]{3,0,2,1:T(8,128)(2,1)S(1)} %get-tuple-element.17), channel_id=1, source_target_pairs={{4,0},{5,1},{6,2},{7,3},{12,8},{13,9},{14,10},{15,11},{20,16},{21,... | collective-permute-start | bytes 417800 | tf_op jit(solution)/shard_map/ppermute | solution.py:21
  26.2 1.3 copy-start.2
  30.3 1.6 copy-start
  30.3 5.5 %copy-start.3 = (bf16[2,4,32,256]{3,2,1,0:T(8,128)(2,1)S(1)}, bf16[2,4,32,256]{3,2,1,0:T(8,128)(2,1)}, u32[]{:S(2)}) copy-start(bf16[2,4,32,256]{3,2,1,0:T(8,128)(2,1)} %param.10) | copy-start | bytes 393220
  30.4 9.5 %copy-start.6 = (u32[32]{0:T(128)S(1)}, u32[32]{0:T(128)}, u32[]{:S(2)}) copy-start(u32[32]{0:T(128)} %constant.20) | copy-start | bytes 388
  31.8 23.4 %copy-start.5 = (bf16[2,4,32,256]{3,2,1,0:T(8,128)(2,1)S(1)}, bf16[2,4,32,256]{3,2,1,0:T(8,128)(2,1)}, u32[]{:S(2)}) copy-start(bf16[2,4,32,256]{3,2,1,0:T(8,128)(2,1)} %param.11) | copy-start | bytes 393220
  31.9 96.1 %all-reduce.7.cloned.1.call-start = ((), (), s32[]{:S(2)}) async-start(), calls=%async_computation.2 | async-start | bytes 3538944 | tf_op jit(solution)/shard_map/psum | solution.py:128
  31.9 9.8 %collective-permute-start.12 = (bf16[2,4,1,128]{3,2,1,0:T(2,128)(2,1)S(1)}, bf16[2,4,1,128]{3,2,1,0:T(2,128)(2,1)S(1)}, u32[]{:S(2)}, u32[]{:S(2)}) collective-permute-start(bf16[2,4,1,128]{3,2,1,0:T(2,128)(2,1)S(1)} %get-tuple-element.42), channel_id=1, source_target_pairs={{0,1},{1,2},{2,3},{3,0},{4,5},{5,6},{6,7},{7,4},{8,9},{9,10},{10,1... | collective-permute-start | bytes 6152 | tf_op jit(solution)/shard_map/ppermute | solution.py:18
  33.3 8.4 %collective-permute-start.13 = (bf16[2,4,1,128]{3,2,1,0:T(2,128)(2,1)S(1)}, bf16[2,4,1,128]{3,2,1,0:T(2,128)(2,1)S(1)}, u32[]{:S(2)}, u32[]{:S(2)}) collective-permute-start(bf16[2,4,1,128]{3,2,1,0:T(2,128)(2,1)S(1)} %get-tuple-element.43), channel_id=1, source_target_pairs={{1,0},{2,1},{3,2},{0,3},{5,4},{6,5},{7,6},{4,7},{9,8},{10,9},{11,1... | collective-permute-start | bytes 6152 | tf_op jit(solution)/shard_map/ppermute | solution.py:21
  36.0 8.6 %collective-permute-start.16 = (bf16[2,4,1,256]{3,2,1,0:T(2,128)(2,1)S(1)}, bf16[2,4,1,256]{3,2,1,0:T(2,128)(2,1)S(1)}, u32[]{:S(2)}, u32[]{:S(2)}) collective-permute-start(bf16[2,4,1,256]{3,2,1,0:T(2,128)(2,1)S(1)} %get-tuple-element.32), channel_id=1, source_target_pairs={{0,1},{1,2},{2,3},{3,0},{4,5},{5,6},{6,7},{7,4},{8,9},{9,10},{10,1... | collective-permute-start | bytes 12296 | tf_op jit(solution)/shard_map/ppermute | solution.py:18
  36.0 8.5 %collective-permute-start.17 = (bf16[2,4,1,256]{3,2,1,0:T(2,128)(2,1)S(1)}, bf16[2,4,1,256]{3,2,1,0:T(2,128)(2,1)S(1)}, u32[]{:S(2)}, u32[]{:S(2)}) collective-permute-start(bf16[2,4,1,256]{3,2,1,0:T(2,128)(2,1)S(1)} %get-tuple-element.33), channel_id=1, source_target_pairs={{1,0},{2,1},{3,2},{0,3},{5,4},{6,5},{7,6},{4,7},{9,8},{10,9},{11,1... | collective-permute-start | bytes 12296 | tf_op jit(solution)/shard_map/ppermute | solution.py:21
  41.8 8.7 %collective-permute-start.14 = (bf16[2,1,34,128]{3,2,1,0:T(8,128)(2,1)S(1)}, bf16[2,1,34,128]{3,2,1,0:T(8,128)(2,1)S(1)}, u32[]{:S(2)}, u32[]{:S(2)}) collective-permute-start(bf16[2,1,34,128]{3,2,1,0:T(8,128)(2,1)S(1)} %get-tuple-element.41), channel_id=1, source_target_pairs={{0,4},{1,5},{2,6},{3,7},{8,12},{9,13},{10,14},{11,15},{16,20},{17,... | collective-permute-start | bytes 52232 | tf_op jit(solution)/shard_map/ppermute | solution.py:18
  43.3 7.2 %collective-permute-start.15 = (bf16[2,1,34,128]{3,2,1,0:T(8,128)(2,1)S(1)}, bf16[2,1,34,128]{3,2,1,0:T(8,128)(2,1)S(1)}, u32[]{:S(2)}, u32[]{:S(2)}) collective-permute-start(bf16[2,1,34,128]{3,2,1,0:T(8,128)(2,1)S(1)} %get-tuple-element.40), channel_id=1, source_target_pairs={{4,0},{5,1},{6,2},{7,3},{12,8},{13,9},{14,10},{15,11},{20,16},{21,... | collective-permute-start | bytes 52232 | tf_op jit(solution)/shard_map/ppermute | solution.py:21
  44.6 6.2 %collective-permute-start.18 = (bf16[2,1,34,256]{3,2,1,0:T(8,128)(2,1)S(1)}, bf16[2,1,34,256]{3,2,1,0:T(8,128)(2,1)S(1)}, u32[]{:S(2)}, u32[]{:S(2)}) collective-permute-start(bf16[2,1,34,256]{3,2,1,0:T(8,128)(2,1)S(1)} %get-tuple-element.23), channel_id=1, source_target_pairs={{0,4},{1,5},{2,6},{3,7},{8,12},{9,13},{10,14},{11,15},{16,20},{17,... | collective-permute-start | bytes 104456 | tf_op jit(solution)/shard_map/ppermute | solution.py:18
  49.2 5.9 %collective-permute-start.19 = (bf16[2,1,34,256]{3,2,1,0:T(8,128)(2,1)S(1)}, bf16[2,1,34,256]{3,2,1,0:T(8,128)(2,1)S(1)}, u32[]{:S(2)}, u32[]{:S(2)}) collective-permute-start(bf16[2,1,34,256]{3,2,1,0:T(8,128)(2,1)S(1)} %get-tuple-element.22), channel_id=1, source_target_pairs={{4,0},{5,1},{6,2},{7,3},{12,8},{13,9},{14,10},{15,11},{20,16},{21,... | collective-permute-start | bytes 104456 | tf_op jit(solution)/shard_map/ppermute | solution.py:21
  58.4 2.6 copy-start.1
  58.7 4.8 %collective-permute-start.5 = (bf16[2,4,1,256]{3,2,1,0:T(2,128)(2,1)S(1)}, bf16[2,4,1,256]{3,2,1,0:T(2,128)(2,1)S(1)}, u32[]{:S(2)}, u32[]{:S(2)}) collective-permute-start(bf16[2,4,1,256]{3,2,1,0:T(2,128)(2,1)S(1)} %get-tuple-element.37), channel_id=1, source_target_pairs={{1,0},{2,1},{3,2},{0,3},{5,4},{6,5},{7,6},{4,7},{9,8},{10,9},{11,1... | collective-permute-start | bytes 12296 | tf_op jit(solution)/shard_map/ppermute | solution.py:21
  61.0 5.4 %collective-permute-start.4 = (bf16[2,4,1,256]{3,2,1,0:T(2,128)(2,1)S(1)}, bf16[2,4,1,256]{3,2,1,0:T(2,128)(2,1)S(1)}, u32[]{:S(2)}, u32[]{:S(2)}) collective-permute-start(bf16[2,4,1,256]{3,2,1,0:T(2,128)(2,1)S(1)} %get-tuple-element.36), channel_id=1, source_target_pairs={{0,1},{1,2},{2,3},{3,0},{4,5},{5,6},{6,7},{7,4},{8,9},{9,10},{10,1... | collective-permute-start | bytes 12296 | tf_op jit(solution)/shard_map/ppermute | solution.py:18
  66.5 6.1 %collective-permute-start.6 = (bf16[2,1,34,256]{3,2,1,0:T(8,128)(2,1)S(1)}, bf16[2,1,34,256]{3,2,1,0:T(8,128)(2,1)S(1)}, u32[]{:S(2)}, u32[]{:S(2)}) collective-permute-start(bf16[2,1,34,256]{3,2,1,0:T(8,128)(2,1)S(1)} %get-tuple-element.30), channel_id=1, source_target_pairs={{4,0},{5,1},{6,2},{7,3},{12,8},{13,9},{14,10},{15,11},{20,16},{21,... | collective-permute-start | bytes 104456 | tf_op jit(solution)/shard_map/ppermute | solution.py:21
  67.8 6.2 %collective-permute-start.7 = (bf16[2,1,34,256]{3,2,1,0:T(8,128)(2,1)S(1)}, bf16[2,1,34,256]{3,2,1,0:T(8,128)(2,1)S(1)}, u32[]{:S(2)}, u32[]{:S(2)}) collective-permute-start(bf16[2,1,34,256]{3,2,1,0:T(8,128)(2,1)S(1)} %get-tuple-element.31), channel_id=1, source_target_pairs={{0,4},{1,5},{2,6},{3,7},{8,12},{9,13},{10,14},{11,15},{16,20},{17,... | collective-permute-start | bytes 104456 | tf_op jit(solution)/shard_map/ppermute | solution.py:18
  77.2 2.6 copy-start.4
  77.8 3.7 %collective-permute-start.9 = (bf16[2,4,1,256]{3,2,1,0:T(2,128)(2,1)S(1)}, bf16[2,4,1,256]{3,2,1,0:T(2,128)(2,1)S(1)}, u32[]{:S(2)}, u32[]{:S(2)}) collective-permute-start(bf16[2,4,1,256]{3,2,1,0:T(2,128)(2,1)S(1)} %get-tuple-element.35), channel_id=1, source_target_pairs={{1,0},{2,1},{3,2},{0,3},{5,4},{6,5},{7,6},{4,7},{9,8},{10,9},{11,1... | collective-permute-start | bytes 12296 | tf_op jit(solution)/shard_map/ppermute | solution.py:21
  78.7 5.4 %collective-permute-start.8 = (bf16[2,4,1,256]{3,2,1,0:T(2,128)(2,1)S(1)}, bf16[2,4,1,256]{3,2,1,0:T(2,128)(2,1)S(1)}, u32[]{:S(2)}, u32[]{:S(2)}) collective-permute-start(bf16[2,4,1,256]{3,2,1,0:T(2,128)(2,1)S(1)} %get-tuple-element.34), channel_id=1, source_target_pairs={{0,1},{1,2},{2,3},{3,0},{4,5},{5,6},{6,7},{7,4},{8,9},{9,10},{10,1... | collective-permute-start | bytes 12296 | tf_op jit(solution)/shard_map/ppermute | solution.py:18
  84.2 6.0 %collective-permute-start.10 = (bf16[2,1,34,256]{3,2,1,0:T(8,128)(2,1)S(1)}, bf16[2,1,34,256]{3,2,1,0:T(8,128)(2,1)S(1)}, u32[]{:S(2)}, u32[]{:S(2)}) collective-permute-start(bf16[2,1,34,256]{3,2,1,0:T(8,128)(2,1)S(1)} %get-tuple-element.26), channel_id=1, source_target_pairs={{4,0},{5,1},{6,2},{7,3},{12,8},{13,9},{14,10},{15,11},{20,16},{21,... | collective-permute-start | bytes 104456 | tf_op jit(solution)/shard_map/ppermute | solution.py:21
  85.5 6.2 %collective-permute-start.11 = (bf16[2,1,34,256]{3,2,1,0:T(8,128)(2,1)S(1)}, bf16[2,1,34,256]{3,2,1,0:T(8,128)(2,1)S(1)}, u32[]{:S(2)}, u32[]{:S(2)}) collective-permute-start(bf16[2,1,34,256]{3,2,1,0:T(8,128)(2,1)S(1)} %get-tuple-element.27), channel_id=1, source_target_pairs={{0,4},{1,5},{2,6},{3,7},{8,12},{9,13},{10,14},{11,15},{16,20},{17,... | collective-permute-start | bytes 104456 | tf_op jit(solution)/shard_map/ppermute | solution.py:18
Sparse Core Ops, SparseCore 0:
  32.0 22.1 reduce-scatter.1
  81.5 46.3 all-reduce.6
where the time goes:
time: 282 us
  blocking collectives  146 us (52%)
  waiting for transfers between devices  54.9 us (19%)
  starting transfers between devices  42.5 us (15%)
  between operations  16 us (6%)
  matrix products  12.5 us (4%)
  local copies, waits for them, and re-layouts  8.32 us (3%)
    unnamed x1, blocking collectives  146 us
    psum x1, waiting for transfers between devices, per_device(): lax.psum(flat_first.astype(jnp.bfloat16), 'lead').astype(jnp.float32)  34.2 us
    ppermute x10, starting transfers between devices, with_halo(): lax.ppermute(lax.slice_in_dim(block, block.shape[dim] - width, None, axis...  24.3 us
    ppermute x10, starting transfers between devices, with_halo(): lax.ppermute(lax.slice_in_dim(block, 0, width, axis=dim), axis, backward)  18.1 us
    ppermute x10, waiting for transfers between devices, with_halo(): lax.ppermute(lax.slice_in_dim(block, block.shape[dim] - width, None, axis...  11.8 us
    ppermute x10, waiting for transfers between devices, with_halo(): lax.ppermute(lax.slice_in_dim(block, 0, width, axis=dim), axis, backward)  8.77 us
    unnamed x20, local copies, waits for them, and re-layouts  7.53 us
  transfers between devices with their start and end apart: 22, of which 12 were waited for; matrix products, arithmetic and copies ran while one was open for 3% of the time, Pallas kernels for 0%

commit v1 on v0

v1 whole, which is shorter than its diff:
```python
import functools
import math

import jax
import jax.numpy as jnp
from jax import lax
from jax.experimental import pallas as pl
from jax.experimental.pallas import tpu as pltpu
from jax.sharding import PartitionSpec as P

BF = jnp.bfloat16
F32 = jnp.float32
STEPS = (-1, 0, 1)
EDGE = 4
LANES = 128
VMEM_BYTES = 24 * 1024 * 1024


def erf_part(values):
    return 0.5 * (1.0 + lax.erf(values * 0.7071067811865476))


def gelu_slope(values):
    return erf_part(values) + values * jnp.exp(-0.5 * values * values) * 0.3989422804014327


def gelu_value(values):
    return values * erf_part(values)


def dot_last(left, right):
    return lax.dot_general(left, right, (((1,), (1,)), ((), ())), preferred_element_type=F32)


def dot_plain(left, right):
    return lax.dot_general(left, right, (((1,), (0,)), ((), ())), preferred_element_type=F32)


def run(name, kernel, out_shape, arrays, scratch=(), scalars=None, flops=0):
    specs = [pl.BlockSpec(memory_space=pltpu.VMEM)] * len(arrays)
    if scalars is not None:
        specs = [pl.BlockSpec(memory_space=pltpu.SMEM)] + specs
        arrays = [scalars] + list(arrays)
    touched = sum(a.size * a.dtype.itemsize for a in arrays)
    touched += sum(math.prod(s.shape) * s.dtype.itemsize for s in out_shape)
    return pl.pallas_call(
        kernel,
        name=name,
        out_shape=out_shape,
        in_specs=specs,
        out_specs=[pl.BlockSpec(memory_space=pltpu.VMEM)] * len(out_shape),
        scratch_shapes=list(scratch),
        compiler_params=pltpu.CompilerParams(vmem_limit_bytes=VMEM_BYTES),
        cost_estimate=pl.CostEstimate(flops=flops, bytes_accessed=touched, transcendentals=0),
    )(*arrays)


def pack_kernel(grads_ref, second_ref, first_ref, right_ref, left_ref, edges, edges_wide, packed):
    heads, batch, height, breadth, _ = grads_ref.shape
    samples = second_ref.shape[0]
    rows = 6 * height
    for side, out_ref in ((0, right_ref), (1, left_ref)):
        start = breadth - 8 if side == 0 else 0
        for h in range(heads):
            for b in range(batch):
                block = grads_ref[h, b, :, start : start + 8, :].astype(F32)
                edges[(h * batch + b) * height * 8 : (h * batch + b + 1) * height * 8, :] = block.reshape(height * 8, LANES)
        for j, ref in enumerate((second_ref, first_ref)):
            for s in range(samples):
                block = ref[s, :, start : start + 8, :].astype(F32)
                at = (j * samples + s) * height * 8
                for half in range(2):
                    lanes = slice(half * LANES, (half + 1) * LANES)
                    edges_wide[half, at : at + height * 8, :] = block[:, :, lanes].reshape(height * 8, LANES)
        for b in range(batch):
            for col in range(3):
                inner = 5 + col if side == 0 else col
                for h in range(heads):
                    at = b * rows + (col * 2 + h) * height
                    packed[at : at + height, :] = edges[pl.ds((h * batch + b) * height * 8 + inner, height, stride=8), :]
        for s in range(samples):
            for q in range(3):
                j, col, width = (0, q, 2) if q < 2 else (1, 0, 1)
                inner = 8 - width + col if side == 0 else col
                for half in range(2):
                    at = (batch + s) * rows + (q * 2 + half) * height
                    packed[at : at + height, :] = edges_wide[
                        half, pl.ds((j * samples + s) * height * 8 + inner, height, stride=8), :
                    ]
        out_ref[...] = packed[...].astype(BF).reshape(out_ref.shape)


def pack(head_grads, pre_second, pre_first):
    heads, batch, height, _, _ = head_grads.shape
    samples = pre_second.shape[0]
    shape = jax.ShapeDtypeStruct((batch + samples, 6 * height, LANES), BF)
    return run(
        "pack_columns",
        pack_kernel,
        [shape, shape],
        [head_grads, pre_second, pre_first],
        [
            pltpu.VMEM((heads * batch * height * 8, LANES), F32),
            pltpu.VMEM((2, 2 * samples * height * 8, LANES), F32),
            pltpu.VMEM(((batch + samples) * 6 * height, LANES), F32),
        ],
    )


def heads_kernel(at_ref, grads_ref, low_ref, high_ref, weights_ref, out_ref, wide, shifted, total):
    heads, batch, height, breadth, _ = grads_ref.shape
    slots, _, kept, depth = out_ref.shape
    pitch = kept + 16
    own = 8 + EDGE
    for slot in range(slots):
        group = at_ref[1] if slot < slots // 2 else 1 - at_ref[1]
        b = (2 * group + at_ref[0]) * (slots // 2) + slot % (slots // 2)
        low = low_ref[b].astype(F32)
        high = high_ref[b].astype(F32)
        for r in range(height):
            at = (slot * height + r) * pitch + own
            for h in range(heads):
                wide[h, at : at + breadth, :] = grads_ref[h, b, r].astype(F32)
        for col in range(3):
            for h in range(heads):
                here = (col * 2 + h) * height
                at = slot * height * pitch + own + col
                wide[h, pl.ds(at - 3, height, stride=pitch), :] = low[here : here + height]
                wide[h, pl.ds(at + breadth, height, stride=pitch), :] = high[here : here + height]
        for v in STEPS:
            for h in range(heads):
                starts = [(slot * height + r) * pitch + 8 - v for r in range(height)]
                moved = jnp.concatenate([wide[h, at : at + kept, :] for at in starts], axis=0).astype(BF)
                lane = ((v + 1) * heads + h) * LANES
                shifted[slot * height * kept : (slot + 1) * height * kept, lane : lane + LANES] = moved
    total[:, height:, :, :] = jnp.zeros((slots, 2, kept, depth), F32)
    for u in STEPS:
        weights = jnp.concatenate(
            [weights_ref[h, 3 * (u + 1) + (v + 1)] for v in STEPS for h in range(heads)], axis=1
        )
        part = dot_last(shifted[...], weights).reshape(slots, height, kept, depth)
        if u == -1:
            total[:, :height] = part
        else:
            total[:, 1 + u : 1 + u + height] += part
    out_ref[...] = total[...].astype(BF)


def head_conv(scalars, head_grads, low, high, head_weights, samples):
    heads, batch, height, breadth, _ = head_grads.shape
    depth = head_weights.shape[2]
    kept = breadth + 2 * EDGE
    slots = 2 * samples
    return run(
        "head_conv",
        heads_kernel,
        [jax.ShapeDtypeStruct((slots, height + 2, kept, depth), BF)],
        [head_grads, low, high, head_weights],
        [
            pltpu.VMEM((heads, slots * height * (kept + 16), LANES), F32),
            pltpu.VMEM((slots * height * kept, 3 * heads * LANES), BF),
            pltpu.VMEM((slots, height + 2, kept, depth), F32),
        ],
        scalars,
        flops=2 * slots * height * kept * 9 * heads * LANES * depth,
    )[0]


def saved_kernel(second_ref, first_ref, input_ref, low_ref, high_ref, second_out, first_out, slope_second, slope_first, act_out, input_out, wide):
    samples, height, breadth, depth = second_ref.shape
    kept = breadth + 2 * EDGE
    batch = low_ref.shape[0] - samples
    for ref, width, out_ref, slope_ref in (
        (second_ref, 2, second_out, slope_second),
        (first_ref, 1, first_out, slope_first),
    ):
        wide[...] = jnp.zeros(wide.shape, F32)
        for s in range(samples):
            for r in range(height):
                at = (s * height + r) * kept + EDGE
                for half in range(2):
                    lanes = slice(half * LANES, (half + 1) * LANES)
                    wide[half, at : at + breadth, :] = ref[s, r, :, lanes].astype(F32)
            low = low_ref[batch + s].astype(F32)
            high = high_ref[batch + s].astype(F32)
            for col in range(width):
                for half in range(2):
                    here = ((col if width == 2 else 2) * 2 + half) * height
                    at = s * height * kept + EDGE + col
                    wide[half, pl.ds(at - width, height, stride=kept), :] = low[here : here + height]
                    wide[half, pl.ds(at + breadth, height, stride=kept), :] = high[here : here + height]
        value = jnp.concatenate([wide[0], wide[1]], axis=1)
        out_ref[...] = value.astype(BF).reshape(out_ref.shape)
        slope_ref[...] = gelu_slope(value).reshape(slope_ref.shape)
    active = gelu_value(first_ref[...].astype(F32).reshape(samples * height * breadth, depth)).astype(BF).astype(F32)
    act_out[...] = active.T.astype(BF)
    cells = input_ref[...].astype(F32).reshape(samples * height * breadth, input_ref.shape[3])
    input_out[...] = cells.T.astype(BF)


def saved(pre_second, pre_first, encoder_input, low, high):
    samples, height, breadth, depth = pre_second.shape
    kept = breadth + 2 * EDGE
    cells = samples * height * breadth
    return run(
        "saved_parts",
        saved_kernel,
        [
            jax.ShapeDtypeStruct((samples, height, kept, depth), BF),
            jax.ShapeDtypeStruct((samples, height, kept, depth), BF),
            jax.ShapeDtypeStruct((samples, height, kept, depth), F32),
            jax.ShapeDtypeStruct((samples, height, kept, depth), F32),
            jax.ShapeDtypeStruct((depth, cells), BF),
            jax.ShapeDtypeStruct((encoder_input.shape[3], cells), BF),
        ],
        [pre_second, pre_first, encoder_input, low, high],
        [pltpu.VMEM((2, samples * height * kept, LANES), F32)],
    )


def spread_kernel(at_ref, mine_ref, got_ref, second_ref, first_ref, own_ref, cross_ref, *strips):
    samples = own_ref.shape[0]
    height = second_ref.shape[1]
    total = mine_ref[...].astype(F32) + got_ref[...].astype(F32)
    total = total.astype(BF)
    own_ref[...] = total[:samples]
    cross_ref[...] = total[samples:]
    for way in range(len(strips) // 2):
        line_ref, corner_ref = strips[2 * way], strips[2 * way + 1]
        down = at_ref[way]
        line_ref[:, 0:3] = own_ref[:, pl.ds((height - 1) * down, 3)]
        corner_ref[...] = cross_ref[:, pl.ds((height - 1) * down, 3)]
        line_ref[:, 3:5] = second_ref[:, pl.ds((height - 2) * down, 2)]
        line_ref[:, 5:6] = first_ref[:, pl.ds((height - 1) * down, 1)]


def spread(scalars, mine, got, second, first, ways):
    slots, rows, kept, depth = mine.shape
    samples = slots // 2
    whole = jax.ShapeDtypeStruct((samples, rows, kept, depth), BF)
    strips = [
        jax.ShapeDtypeStruct((samples, 6, kept, depth), BF),
        jax.ShapeDtypeStruct((samples, 3, kept, depth), BF),
    ] * ways
    return run("core_sum", spread_kernel, [whole, whole] + strips, [mine, got, second, first], (), scalars)


def encoder_kernel(norm_factor, ways, at_ref, own_ref, cross_ref, *refs):
    strips, refs = refs[: 2 * ways], refs[2 * ways :]
    slope_second_ref, slope_first_ref, act_ref, input_ref, w_second_ref = refs[:5]
    moved_out, first_mine, first_other, second_mine, second_other = refs[5:10]
    latent, slope_second, slope_first, wide, cat, cat_own, wide_first = refs[10:]
    samples, rows, kept, depth = own_ref.shape
    height = rows - 2
    breadth = kept - 2 * EDGE
    lat, bands, core = at_ref[0], at_ref[1], at_ref[2]
    own = 8 + EDGE
    blank = jnp.zeros((samples, kept, depth), F32)
    latent[:, 0] = blank
    latent[:, height + 3] = blank
    latent[:, 1 : height + 3] = own_ref[...].astype(F32) + cross_ref[...].astype(F32)
    slope_second[:, 2 : 2 + height] = slope_second_ref[...]
    slope_first[:, 1 : 1 + height] = slope_first_ref[...]
    for way in range(ways):
        line_ref, corner_ref = strips[2 * way], strips[2 * way + 1]
        below = at_ref[3 + way]
        at = (height + 1) * below
        latent[:, pl.ds(at, 3)] += line_ref[:, 0:3].astype(F32) + corner_ref[...].astype(F32)
        slope_second[:, pl.ds((height + 2) * below, 2)] = gelu_slope(line_ref[:, 3:5].astype(F32))
        slope_first[:, pl.ds((height + 1) * below, 1)] = gelu_slope(line_ref[:, 5:6].astype(F32))
    for i in range(height + 4):
        row = lat * height + i - 2
        valid = jnp.logical_and(row >= 0, row < bands * height)
        value = latent[:, i] * slope_second[:, i]
        if i < 2 or i >= height + 2:
            value = jnp.where(valid, value, 0.0)
        wide[:, i, 8 : 8 + kept, :] = value.astype(BF).astype(F32)
    for v in STEPS:
        lanes = slice((v + 1) * depth, (v + 2) * depth)
        cat[:, :, :, lanes] = wide[:, :, 8 - v : 8 - v + kept + 8, :].astype(BF)
        cat_own[:, :, :, lanes] = wide[:, 1 : height + 3, own - v : own - v + breadth, :].astype(BF)
    linear = None
    for u in STEPS:
        weights = jnp.concatenate([w_second_ref[3 * (u + 1) + (v + 1)] for v in STEPS], axis=1)
        left = cat[:, 1 - u : 1 - u + rows].reshape(samples * rows * (kept + 8), 3 * depth)
        part = dot_last(left, weights)
        linear = part if linear is None else linear + part
    linear = linear.reshape(samples, rows, kept + 8, depth)
    for i in range(rows):
        row = lat * height + i - 1
        valid = jnp.logical_and(row >= 0, row < bands * height)
        value = linear[:, i, :kept] * slope_first[:, i]
        if i < 1 or i >= height + 1:
            value = jnp.where(valid, value, 0.0)
        wide_first[:, i, 8 : 8 + kept, :] = value.astype(BF).astype(F32)
    for v in STEPS:
        lanes = slice((v + 1) * depth, (v + 2) * depth)
        moved_out[:, :, :, lanes] = wide_first[:, :, own - v : own - v + breadth, :].astype(BF)
    for left_ref, source, mine_ref, other_ref in (
        (input_ref, moved_out, first_mine, first_other),
        (act_ref, cat_own, second_mine, second_other),
    ):
        for u in STEPS:
            right = source[:, 1 - u : 1 - u + height].reshape(samples * height * breadth, 3 * depth)
            part = dot_plain(left_ref[...], right) * norm_factor
            for v in STEPS:
                k = 3 * (u + 1) + (v + 1)
                lower = part[:, (v + 1) * depth : (v + 1) * depth + LANES]
                upper = part[:, (v + 1) * depth + LANES : (v + 2) * depth]
                mine_ref[k] = jnp.where(core == 0, lower, upper).astype(BF)
                other_ref[k] = jnp.where(core == 0, upper, lower).astype(BF)


def encoder(scalars, ways, norm_factor, own, cross, strips, slope_second, slope_first, act, cells_in, w_second):
    samples, rows, kept, depth = own.shape
    height, breadth = rows - 2, kept - 2 * EDGE
    channels = cells_in.shape[0]
    return run(
        "encoder_grads",
        functools.partial(encoder_kernel, norm_factor, ways),
        [
            jax.ShapeDtypeStruct((samples, rows, breadth, 3 * depth), BF),
            jax.ShapeDtypeStruct((9, channels, LANES), BF),
            jax.ShapeDtypeStruct((9, channels, LANES), BF),
            jax.ShapeDtypeStruct((9, depth, LANES), BF),
            jax.ShapeDtypeStruct((9, depth, LANES), BF),
        ],
        [own, cross, *strips, slope_second, slope_first, act, cells_in, w_second],
        [
            pltpu.VMEM((samples, height + 4, kept, depth), F32),
            pltpu.VMEM((samples, height + 4, kept, depth), F32),
            pltpu.VMEM((samples, height + 2, kept, depth), F32),
            pltpu.VMEM((samples, height + 4, kept + 24, depth), F32),
            pltpu.VMEM((samples, height + 4, kept + 8, 3 * depth), BF),
            pltpu.VMEM((samples, height + 2, breadth, 3 * depth), BF),
            pltpu.VMEM((samples, height + 2, kept + 16, depth), F32),
        ],
        scalars,
        flops=2 * 9 * depth * (samples * rows * (kept + 8) * depth + samples * height * breadth * (depth + channels)),
    )


def input_kernel(moved_ref, w_first_ref, out_ref):
    samples, rows, breadth, triple = moved_ref.shape
    height = rows - 2
    total = None
    for u in STEPS:
        weights = jnp.concatenate([w_first_ref[3 * (u + 1) + (v + 1)] for v in STEPS], axis=1)
        part = dot_last(moved_ref[:, 1 - u : 1 - u + height].reshape(samples * height * breadth, triple), weights)
        total = part if total is None else total + part
    out_ref[...] = total.astype(BF).reshape(out_ref.shape)


def input_conv(moved, w_first):
    samples, rows, breadth, triple = moved.shape
    shape = (samples, rows - 2, breadth, w_first.shape[1])
    return run(
        "input_conv",
        input_kernel,
        [jax.ShapeDtypeStruct(shape, BF)],
        [moved, w_first],
        flops=2 * 3 * math.prod(shape) * triple,
    )[0]


def join_kernel(rows_first, at_ref, mine_ref, cross_ref, core_ref, both_ref, first_ref, second_ref):
    here = mine_ref[...].astype(F32) + cross_ref[...].astype(F32)
    there = core_ref[...].astype(F32) + both_ref[...].astype(F32)
    core = at_ref[2]
    lower = jnp.where(core == 0, here, there)
    upper = jnp.where(core == 0, there, here)
    rows_second = here.shape[0] - rows_first
    for half, value in ((0, lower), (1, upper)):
        first_ref[pl.ds(half, rows_first, stride=2), :] = value[:rows_first]
        second_ref[pl.ds(half, rows_second, stride=2), :] = value[rows_first:]


def swap(array, axis, flip):
    count = lax.axis_size(axis)
    return lax.ppermute(array, axis, [(i, i ^ flip) for i in range(count)])


def around(array, axis, step, periodic=True):
    count = lax.axis_size(axis)
    pairs = [(i, (i + step) % count) for i in range(count) if periodic or 0 <= i + step < count]
    return lax.ppermute(array, axis, pairs)


def corner(array, step):
    lead, lat = lax.axis_size("lead"), lax.axis_size("lat")
    pairs = []
    for a in range(lead):
        for b in range(lat):
            target = (b ^ 1) if step is None else b + step
            if 0 <= target < lat:
                pairs.append((a * lat + b, (a ^ 2) * lat + target))
    return lax.ppermute(array, ("lead", "lat"), pairs)


def per_device(head_grads, head_weights, encoder_input, pre_first, pre_second, w_first, w_second):
    samples, height, breadth, _ = encoder_input.shape
    bands, columns = lax.axis_size("lat"), lax.axis_size("lon")
    lead, lat, lon = lax.axis_index("lead"), lax.axis_index("lat"), lax.axis_index("lon")
    core, chip = lead % 2, lead // 2
    cells_total = samples * lax.axis_size("lead") * height * bands * breadth * columns
    norm_factor = 1.0 / math.sqrt(cells_total)

    to_right, to_left = pack(head_grads, pre_second, pre_first)
    low = around(to_right, "lon", 1)
    high = around(to_left, "lon", -1)

    theirs = head_conv(jnp.stack([1 - core, chip]).astype(jnp.int32), head_grads, low, high, head_weights, samples)
    got = swap(theirs, "lead", 1)
    mine = head_conv(jnp.stack([core, chip]).astype(jnp.int32), head_grads, low, high, head_weights, samples)
    second, first, slope_second, slope_first, act, cells_in = saved(pre_second, pre_first, encoder_input, low, high)

    if bands == 2:
        steps = [None]
        goes_down = jnp.stack([1 - lat])
        from_below = jnp.stack([1 - lat])
    else:
        steps = [1, -1]
        goes_down = jnp.array([1, 0])
        from_below = jnp.array([0, 1])
    spreads = spread(goes_down.astype(jnp.int32), mine, got, second, first, len(steps))
    own = spreads[0]
    cross = swap(spreads[1], "lead", 2)
    strips = []
    for way, step in enumerate(steps):
        line, angle = spreads[2 + 2 * way], spreads[3 + 2 * way]
        strips.append(swap(line, "lat", 1) if step is None else around(line, "lat", step, False))
        strips.append(corner(angle, step))

    place = jnp.concatenate([jnp.stack([lat, jnp.int32(bands), core]), from_below]).astype(jnp.int32)
    moved, first_mine, first_other, second_mine, second_other = encoder(
        place, len(steps), norm_factor, own, cross, strips, slope_second, slope_first, act, cells_in, w_second
    )
    input_grad = input_conv(moved, w_first)

    first_got = swap(first_other, "lead", 1)
    second_got = swap(second_other, "lead", 1)
    shares = bands * columns

    def in_shares(array):
        return array.reshape(bands, columns, -1, LANES)

    def add(*terms):
        total = terms[0].astype(F32)
        for term in terms[1:]:
            total = total + term.astype(F32)
        return total

    rows_first = first_mine.size // LANES // shares
    total = jnp.concatenate(
        [in_shares(add(first_mine, first_got)), in_shares(add(second_mine, second_got))], axis=2
    ).astype(BF)
    left = bands
    while left > 1:
        left //= 2
        bit = (lat // left) % 2
        halves = total.reshape((2, left) + total.shape[1:])
        away = lax.dynamic_index_in_dim(halves, 1 - bit, 0, keepdims=False)
        keep = lax.dynamic_index_in_dim(halves, bit, 0, keepdims=False)
        total = add(keep, swap(away, "lat", left)).astype(BF)
    total = total[0]
    parts = [lax.dynamic_index_in_dim(total, lon, 0, keepdims=False)]
    for step in range(1, columns):
        away = lax.dynamic_index_in_dim(total, (lon + step) % columns, 0, keepdims=False)
        parts.append(around(away, "lon", step))
    share = add(*parts).astype(BF)
    peers = [swap(share, "lead", flip) for flip in (2, 1, 3)]
    rows_second = share.shape[0] - rows_first
    result_first, result_second = run(
        "join_halves",
        functools.partial(join_kernel, rows_first),
        [
            jax.ShapeDtypeStruct((2 * rows_first, LANES), F32),
            jax.ShapeDtypeStruct((2 * rows_second, LANES), F32),
        ],
        [share, *peers],
        (),
        place,
    )
    return input_grad, result_first.reshape(-1), result_second.reshape(-1)


def solution(mesh):
    in_specs = (
        P("lead", None, "lat", "lon", None),
        P("lead", None, None, None),
        P("lead", "lat", "lon", None),
        P("lead", "lat", "lon", None),
        P("lead", "lat", "lon", None),
        P(),
        P(),
    )
    out_specs = (P("lead", "lat", "lon", None), P(("lat", "lon")), P(("lat", "lon")))
    return jax.shard_map(
        per_device, mesh=mesh, in_specs=in_specs, out_specs=out_specs, check_vma=False
    )
```

time: 282 us -> 68 us (0.24)
  blocking collectives: 146 us -> 0 us
  starting transfers between devices: 42.5 us -> 17.2 us
  waiting for transfers between devices: 54.9 us -> 34.1 us
  between operations: 16 us -> 0.8 us
  matrix products: 12.5 us -> 0 us
  Pallas kernels: 0 us -> 9.68 us
  local copies, waits for them, and re-layouts: 8.32 us -> 5.22 us
    unnamed x1 -> x0, blocking collectives: 146 us -> none
    psum x1 -> x0, waiting for transfers between devices: 34.2 us -> none  [per_device(): lax.psum(flat_first.astype(jnp.bfloat16), 'lead').astype(jnp.float32)]
    ppermute x20 -> x15, starting transfers between devices: 42.4 us -> 17.2 us  [the longest x5 9.19 us: around(): return lax.ppermute(array, axis, pairs)]
    ppermute x20 -> x15, waiting for transfers between devices: 20.6 us -> 34.1 us  [the longest x9 16.1 us: swap(): return lax.ppermute(array, axis, [(i, i ^ flip) for i in range(count)])]
    dot_general x45 -> x0, matrix products: 12.5 us -> none  [the longest x9 4.23 us: per_device(): jnp.einsum('hbrcj,hdj->brcd', moved, head_weights[:, latent_offset], pref...]
    pallas_call x0 -> x8, Pallas kernels: none -> 9.68 us  [run(): pl.pallas_call(kernel, name=name, out_shape=out_shape, in_specs=specs, ou...]
    unnamed x20 -> x24, local copies, waits for them, and re-layouts: 7.53 us -> 5.18 us
  transfers between devices with their start and end apart: 22 -> 15, of which waited for: 12 -> 9; matrix products, arithmetic and copies ran while one was open for 3% -> 0% of each run, Pallas kernels for 0% -> 5%
where the time goes in v1:
time: 68 us; the launch traced here: 67.7 us
  waiting for transfers between devices  34.1 us (50%)
  starting transfers between devices  17.2 us (25%)
  Pallas kernels  9.68 us (14%)
  local copies, waits for them, and re-layouts  5.22 us (8%)
  between operations  0.8 us (1%)
  other arithmetic  0.69 us (1%)
    ppermute x9, waiting for transfers between devices, swap(): return lax.ppermute(array, axis, [(i, i ^ flip) for i in range(count)])  16.1 us
    pallas_call x8, Pallas kernels, run(): pl.pallas_call(kernel, name=name, out_shape=out_shape, in_specs=specs, ou...  9.68 us
    ppermute x5, waiting for transfers between devices, around(): return lax.ppermute(array, axis, pairs)  9.58 us
    ppermute x5, starting transfers between devices, around(): return lax.ppermute(array, axis, pairs)  9.19 us
    ppermute x1, waiting for transfers between devices, corner(): return lax.ppermute(array, ('lead', 'lat'), pairs)  8.48 us
    ppermute x9, starting transfers between devices, swap(): return lax.ppermute(array, axis, [(i, i ^ flip) for i in range(count)])  7.51 us
    unnamed x24, local copies, waits for them, and re-layouts  5.18 us
  transfers between devices with their start and end apart: 15, of which 9 were waited for; matrix products, arithmetic and copies ran while one was open for 0% of the time, Pallas kernels for 5%

profile of v1, /device:TPU:0, one launch (start us, length us, event | category | flops | bytes accessed | tf_op | source)
XLA Modules:
  0.0 67.7 jit_solution(16981803833780224346)
XLA Ops:
  0.6 0.0 copy-start.1
  0.6 1.0 %copy-done.1 = bf16[2,8,4,32,128]{4,3,2,1,0:T(8,128)(2,1)S(1)} copy-done((bf16[2,8,4,32,128]{4,3,2,1,0:T(8,128)(2,1)S(1)}, bf16[2,8,4,32,128]{4,3,2,1,0:T(8,128)(2,1)}, u32[]{:S(2)}) %copy-start.1) | copy-done | bytes 524312
  1.7 0.9 %copy-done.4 = bf16[2,4,32,256]{3,2,1,0:T(8,128)(2,1)S(1)} copy-done((bf16[2,4,32,256]{3,2,1,0:T(8,128)(2,1)S(1)}, bf16[2,4,32,256]{3,2,1,0:T(8,128)(2,1)}, u32[]{:S(2)}) %copy-start.4) | copy-done | bytes 131096
  2.6 0.9 %copy-done.6 = bf16[2,4,32,256]{3,2,1,0:T(8,128)(2,1)S(1)} copy-done((bf16[2,4,32,256]{3,2,1,0:T(8,128)(2,1)S(1)}, bf16[2,4,32,256]{3,2,1,0:T(8,128)(2,1)}, u32[]{:S(2)}) %copy-start.6) | copy-done | bytes 131096
  3.5 0.1 pack_columns.1
  3.6 3.1 %collective-permute-start = (bf16[10,24,128]{2,1,0:T(8,128)(2,1)S(1)}, bf16[10,24,128]{2,1,0:T(8,128)(2,1)S(1)}, u32[]{:S(2)}, u32[]{:S(2)}) collective-permute-start(bf16[10,24,128]{2,1,0:T(8,128)(2,1)S(1)} %get-tuple-element.22), channel_id=1, source_target_pairs={{0,1},{1,2},{2,3},{3,0},{4,5},{5,6},{6,7},{7,4},{8,9},{9,10},{10,1... | collective-permute-start | bytes 184328 | tf_op jit(solution)/shard_map/ppermute | solution.py:386
  6.7 2.1 %collective-permute-start.1 = (bf16[10,24,128]{2,1,0:T(8,128)(2,1)S(1)}, bf16[10,24,128]{2,1,0:T(8,128)(2,1)S(1)}, u32[]{:S(2)}, u32[]{:S(2)}) collective-permute-start(bf16[10,24,128]{2,1,0:T(8,128)(2,1)S(1)} %get-tuple-element.23), channel_id=1, source_target_pairs={{0,3},{1,0},{2,1},{3,2},{4,7},{5,4},{6,5},{7,6},{8,11},{9,8},{10,9... | collective-permute-start | bytes 184328 | tf_op jit(solution)/shard_map/ppermute | solution.py:386
  8.8 0.1 pad_add_fusion.2.at_ref
  8.9 2.2 %collective-permute-done.low_ref = bf16[10,24,128]{2,1,0:T(8,128)(2,1)S(1)} collective-permute-done((bf16[10,24,128]{2,1,0:T(8,128)(2,1)S(1)}, bf16[10,24,128]{2,1,0:T(8,128)(2,1)S(1)}, u32[]{:S(2)}, u32[]{:S(2)}) %collective-permute-start) | collective-permute-done | bytes 61472 | tf_op jit(solution)/shard_map/ppermute | solution.py:386
  11.0 0.5 collective-permute-done.1.high_ref
  11.6 1.0 %copy-done.2 = bf16[2,8,4,32,128]{4,3,2,1,0:T(8,128)(2,1)S(1)} copy-done((bf16[2,8,4,32,128]{4,3,2,1,0:T(8,128)(2,1)S(1)}, bf16[2,8,4,32,128]{4,3,2,1,0:T(8,128)(2,1)}, u32[]{:S(2)}) %copy-start.2) | copy-done | bytes 524312
  12.6 1.3 %copy-done.9 = bf16[2,9,256,128]{3,2,1,0:T(8,128)(2,1)S(1)} copy-done((bf16[2,9,256,128]{3,2,1,0:T(8,128)(2,1)S(1)}, bf16[2,9,256,128]{3,2,1,0:T(8,128)(2,1)}, u32[]{:S(2)}) %copy-start.9) | copy-done | bytes 1179672
  13.9 1.5 %head_conv.3 = bf16[4,6,40,256]{3,2,1,0:T(8,128)(2,1)S(1)} custom-call(s32[2]{0:T(128)S(1)} %pad_add_fusion.2.at_ref, bf16[2,8,4,32,128]{4,3,2,1,0:T(8,128)(2,1)S(1)} %copy-done.2, bf16[10,24,128]{2,1,0:T(8,128)(2,1)S(1)} %collective-permute-done.low_ref, bf16[10,24,128]{2,1,0:T(8,128)(2,1)S(1)} %collective-permute-done.1.high_ref, ...), custom_call_target="tpu_custom_call" | custom-call | flops 754974720 | bytes 2318344 | tf_op jit(solution)/shard_map/head_conv/pallas_call | solution.py:46
  15.5 0.1 collective-permute-start.2
  15.5 0.1 pad_add_fusion.1.at_ref
  15.6 0.6 saved_parts.1
  16.2 1.6 %head_conv.2.mine_ref = bf16[4,6,40,256]{3,2,1,0:T(8,128)(2,1)S(1)} custom-call(s32[2]{0:T(128)S(1)} %pad_add_fusion.1.at_ref, bf16[2,8,4,32,128]{4,3,2,1,0:T(8,128)(2,1)S(1)} %copy-done.3, bf16[10,24,128]{2,1,0:T(8,128)(2,1)S(1)} %collective-permute-done.low_ref, bf16[10,24,128]{2,1,0:T(8,128)(2,1)S(1)} %collective-permute-done.1.high_ref, ...), custom_call_target="tpu_custom_call" | custom-call | flops 754974720 | bytes 2318344 | tf_op jit(solution)/shard_map/head_conv/pallas_call | solution.py:46
  17.8 0.0 copy-start.11
  17.8 0.0 collective-permute-done.2.got_ref
  17.8 0.3 core_sum.1
  18.1 1.6 %collective-permute-start.3 = (bf16[2,6,40,256]{3,2,1,0:T(8,128)(2,1)S(1)}, bf16[2,6,40,256]{3,2,1,0:T(8,128)(2,1)S(1)}, u32[]{:S(2)}, u32[]{:S(2)}) collective-permute-start(bf16[2,6,40,256]{3,2,1,0:T(8,128)(2,1)S(1)} %get-tuple-element.27), channel_id=1, source_target_pairs={{0,16},{8,24},{16,0},{24,8},{1,17},{9,25},{17,1},{25,9},{2,18},{10... | collective-permute-start | bytes 737288 | tf_op jit(solution)/shard_map/ppermute | solution.py:380
  19.6 1.5 %collective-permute-start.4 = (bf16[2,6,40,256]{3,2,1,0:T(8,128)(2,1)S(1)}, bf16[2,6,40,256]{3,2,1,0:T(8,128)(2,1)S(1)}, u32[]{:S(2)}, u32[]{:S(2)}) collective-permute-start(bf16[2,6,40,256]{3,2,1,0:T(8,128)(2,1)S(1)} %get-tuple-element.28), channel_id=1, source_target_pairs={{0,4},{4,0},{1,5},{5,1},{2,6},{6,2},{3,7},{7,3},{8,12},{12,8},{9,1... | collective-permute-start | bytes 737288 | tf_op jit(solution)/shard_map/ppermute | solution.py:380
  21.2 0.5 collective-permute-start.5
  21.6 0.1 pad_add_fusion.at_ref
  21.7 8.5 %collective-permute-done.5.refs_1_ = bf16[2,3,40,256]{3,2,1,0:T(8,128)(2,1)S(1)} collective-permute-done((bf16[2,3,40,256]{3,2,1,0:T(8,128)(2,1)S(1)}, bf16[2,3,40,256]{3,2,1,0:T(8,128)(2,1)S(1)}, u32[]{:S(2)}, u32[]{:S(2)}) %collective-permute-start.5) | collective-permute-done | bytes 122912 | tf_op jit(solution)/shard_map/ppermute | solution.py:397
  30.2 0.0 collective-permute-done.3.cross_ref
  30.2 0.1 collective-permute-done.4.refs_0_
  30.3 3.2 %encoder_grads.1 = (bf16[2,6,32,768]{3,2,1,0:T(8,128)(2,1)S(1)}, bf16[9,128,128]{2,1,0:T(8,128)(2,1)S(1)}, bf16[9,128,128]{2,1,0:T(8,128)(2,1)S(1)}, bf16[9,256,...) custom-call(s32[4]{0:T(128)S(1)} %pad_add_fusion.at_ref, bf16[2,6,40,256]{3,2,1,0:T(8,128)(2,1)S(1)} %get-tuple-element.26.own_ref, ...), custom_call_target="tpu_custom_call" | custom-call | flops 1132462080 | bytes 5251088 | tf_op jit(solution)/shard_map/encoder_grads/pallas_call | solution.py:46
  33.5 0.1 collective-permute-start.7
  33.6 0.5 collective-permute-start.6
  34.1 1.9 %collective-permute-done.6 = bf16[9,128,128]{2,1,0:T(8,128)(2,1)S(1)} collective-permute-done((bf16[9,128,128]{2,1,0:T(8,128)(2,1)S(1)}, bf16[9,128,128]{2,1,0:T(8,128)(2,1)S(1)}, u32[]{:S(2)}, u32[]{:S(2)}) %collective-permute-start.6) | collective-permute-done | bytes 294944 | tf_op jit(solution)/shard_map/ppermute | solution.py:380
  36.0 0.1 add_convert_fusion.2
  36.1 0.0 collective-permute-done.7
  36.1 0.2 add_convert_fusion
  36.3 1.6 %collective-permute-start.8 = (bf16[1,4,432,128]{3,2,1,0:T(8,128)(2,1)S(1)}, bf16[1,4,432,128]{3,2,1,0:T(8,128)(2,1)S(1)}, u32[]{:S(2)}, u32[]{:S(2)}) collective-permute-start(bf16[1,4,432,128]{3,2,1,0:T(8,128)(2,1)S(1)} %fusion), channel_id=1, source_target_pairs={{0,4},{4,0},{1,5},{5,1},{2,6},{6,2},{3,7},{7,3},{8,12},{12,8},{9,1... | collective-permute-start | bytes 1327112 | tf_op jit(solution)/shard_map/ppermute | solution.py:380
  37.9 10.7 %collective-permute-done.8 = bf16[1,4,432,128]{3,2,1,0:T(8,128)(2,1)S(1)} collective-permute-done((bf16[1,4,432,128]{3,2,1,0:T(8,128)(2,1)S(1)}, bf16[1,4,432,128]{3,2,1,0:T(8,128)(2,1)S(1)}, u32[]{:S(2)}, u32[]{:S(2)}) %collective-permute-start.8) | collective-permute-done | bytes 442400 | tf_op jit(solution)/shard_map/ppermute | solution.py:380
  48.6 0.1 add_convert_fusion.1
  48.8 2.0 %collective-permute-start.10 = (bf16[432,128]{1,0:T(8,128)(2,1)S(1)}, bf16[432,128]{1,0:T(8,128)(2,1)S(1)}, u32[]{:S(2)}, u32[]{:S(2)}) collective-permute-start(bf16[432,128]{1,0:T(8,128)(2,1)S(1)} %get-tuple-element.43), channel_id=1, source_target_pairs={{0,2},{1,3},{2,0},{3,1},{4,6},{5,7},{6,4},{7,5},{8,10},{9,11},{10,... | collective-permute-start | bytes 331784 | tf_op jit(solution)/shard_map/ppermute | solution.py:386
  50.8 1.5 %collective-permute-start.11 = (bf16[432,128]{1,0:T(8,128)(2,1)S(1)}, bf16[432,128]{1,0:T(8,128)(2,1)S(1)}, u32[]{:S(2)}, u32[]{:S(2)}) collective-permute-start(bf16[432,128]{1,0:T(8,128)(2,1)S(1)} %get-tuple-element.42), channel_id=1, source_target_pairs={{0,3},{1,0},{2,1},{3,2},{4,7},{5,4},{6,5},{7,6},{8,11},{9,8},{10,9... | collective-permute-start | bytes 331784 | tf_op jit(solution)/shard_map/ppermute | solution.py:386
  52.3 0.5 collective-permute-start.9
  52.8 6.9 %collective-permute-done.10 = bf16[432,128]{1,0:T(8,128)(2,1)S(1)} collective-permute-done((bf16[432,128]{1,0:T(8,128)(2,1)S(1)}, bf16[432,128]{1,0:T(8,128)(2,1)S(1)}, u32[]{:S(2)}, u32[]{:S(2)}) %collective-permute-start.10) | collective-permute-done | bytes 110624 | tf_op jit(solution)/shard_map/ppermute | solution.py:386
  59.7 0.1 fusion.4.mine_ref
  59.7 1.3 %collective-permute-start.12 = (bf16[432,128]{1,0:T(8,128)(2,1)S(1)}, bf16[432,128]{1,0:T(8,128)(2,1)S(1)}, u32[]{:S(2)}, u32[]{:S(2)}) collective-permute-start(bf16[432,128]{1,0:T(8,128)(2,1)S(1)} %fusion.4.mine_ref), channel_id=1, source_target_pairs={{0,16},{8,24},{16,0},{24,8},{1,17},{9,25},{17,1},{25,9},{2,18},{10... | collective-permute-start | bytes 331784 | tf_op jit(solution)/shard_map/ppermute | solution.py:380
  61.0 0.9 %collective-permute-start.14 = (bf16[432,128]{1,0:T(8,128)(2,1)S(1)}, bf16[432,128]{1,0:T(8,128)(2,1)S(1)}, u32[]{:S(2)}, u32[]{:S(2)}) collective-permute-start(bf16[432,128]{1,0:T(8,128)(2,1)S(1)} %fusion.4.mine_ref), channel_id=1, source_target_pairs={{0,24},{8,16},{16,8},{24,0},{1,25},{9,17},{17,9},{25,1},{2,26},{10... | collective-permute-start | bytes 331784 | tf_op jit(solution)/shard_map/ppermute | solution.py:380
  61.9 1.1 %input_conv.1 = bf16[2,4,32,128]{3,2,1,0:T(8,128)(2,1)} custom-call(bf16[2,6,32,768]{3,2,1,0:T(8,128)(2,1)S(1)} %get-tuple-element.34.moved_ref, bf16[9,128,256]{2,1,0:T(8,128)(2,1)S(1)} %copy-done), custom_call_target="tpu_custom_call" | custom-call | flops 150994944 | bytes 1245184 | tf_op jit(solution)/shard_map/input_conv/pallas_call | solution.py:46
  63.0 2.1 %collective-permute-done.12.cross_ref = bf16[432,128]{1,0:T(8,128)(2,1)S(1)} collective-permute-done((bf16[432,128]{1,0:T(8,128)(2,1)S(1)}, bf16[432,128]{1,0:T(8,128)(2,1)S(1)}, u32[]{:S(2)}, u32[]{:S(2)}) %collective-permute-start.12) | collective-permute-done | bytes 110624 | tf_op jit(solution)/shard_map/ppermute | solution.py:380
  65.1 1.3 %collective-permute-done.14.both_ref = bf16[432,128]{1,0:T(8,128)(2,1)S(1)} collective-permute-done((bf16[432,128]{1,0:T(8,128)(2,1)S(1)}, bf16[432,128]{1,0:T(8,128)(2,1)S(1)}, u32[]{:S(2)}, u32[]{:S(2)}) %collective-permute-start.14) | collective-permute-done | bytes 110624 | tf_op jit(solution)/shard_map/ppermute | solution.py:380
  66.3 1.4 %join_halves.1 = (f32[288,128]{1,0:T(8,128)}, f32[576,128]{1,0:T(8,128)}) custom-call(s32[4]{0:T(128)S(1)} %pad_add_fusion.at_ref, bf16[432,128]{1,0:T(8,128)(2,1)S(1)} %fusion.4.mine_ref, bf16[432,128]{1,0:T(8,128)(2,1)S(1)} %collective-permute-done.12.cross_ref, bf16[432,128]{1,0:T(8,128)(2,1)S(1)} %collective-permute-done.13.core_ref, ...), custom_call_target="tpu_custom_call" | custom-call | bytes 884752 | tf_op jit(solution)/shard_map/join_halves/pallas_call | solution.py:46
  (23 shorter events, 0.1 us)
Async XLA Ops:
  0.6 1.0 %copy-start.1 = (bf16[2,8,4,32,128]{4,3,2,1,0:T(8,128)(2,1)S(1)}, bf16[2,8,4,32,128]{4,3,2,1,0:T(8,128)(2,1)}, u32[]{:S(2)}) copy-start(bf16[2,8,4,32,128]{4,3,2,1,0:T(8,128)(2,1)} %grads_ref.5) | copy-start | bytes 1572868
  1.7 0.9 %copy-start.4 = (bf16[2,4,32,256]{3,2,1,0:T(8,128)(2,1)S(1)}, bf16[2,4,32,256]{3,2,1,0:T(8,128)(2,1)}, u32[]{:S(2)}) copy-start(bf16[2,4,32,256]{3,2,1,0:T(8,128)(2,1)} %second_ref.3) | copy-start | bytes 393220
  2.6 0.9 %copy-start.6 = (bf16[2,4,32,256]{3,2,1,0:T(8,128)(2,1)S(1)}, bf16[2,4,32,256]{3,2,1,0:T(8,128)(2,1)}, u32[]{:S(2)}) copy-start(bf16[2,4,32,256]{3,2,1,0:T(8,128)(2,1)} %first_ref.3) | copy-start | bytes 393220
  3.6 7.4 %collective-permute-start = (bf16[10,24,128]{2,1,0:T(8,128)(2,1)S(1)}, bf16[10,24,128]{2,1,0:T(8,128)(2,1)S(1)}, u32[]{:S(2)}, u32[]{:S(2)}) collective-permute-start(bf16[10,24,128]{2,1,0:T(8,128)(2,1)S(1)} %get-tuple-element.22), channel_id=1, source_target_pairs={{0,1},{1,2},{2,3},{3,0},{4,5},{5,6},{6,7},{7,4},{8,9},{9,10},{10,1... | collective-permute-start | bytes 184328 | tf_op jit(solution)/shard_map/ppermute | solution.py:386
  6.7 4.9 %collective-permute-start.1 = (bf16[10,24,128]{2,1,0:T(8,128)(2,1)S(1)}, bf16[10,24,128]{2,1,0:T(8,128)(2,1)S(1)}, u32[]{:S(2)}, u32[]{:S(2)}) collective-permute-start(bf16[10,24,128]{2,1,0:T(8,128)(2,1)S(1)} %get-tuple-element.23), channel_id=1, source_target_pairs={{0,3},{1,0},{2,1},{3,2},{4,7},{5,4},{6,5},{7,6},{8,11},{9,8},{10,9... | collective-permute-start | bytes 184328 | tf_op jit(solution)/shard_map/ppermute | solution.py:386
  11.6 1.0 %copy-start.2 = (bf16[2,8,4,32,128]{4,3,2,1,0:T(8,128)(2,1)S(1)}, bf16[2,8,4,32,128]{4,3,2,1,0:T(8,128)(2,1)}, u32[]{:S(2)}) copy-start(bf16[2,8,4,32,128]{4,3,2,1,0:T(8,128)(2,1)} %grads_ref.5) | copy-start | bytes 1572868
  12.6 1.3 %copy-start.9 = (bf16[2,9,256,128]{3,2,1,0:T(8,128)(2,1)S(1)}, bf16[2,9,256,128]{3,2,1,0:T(8,128)(2,1)}, u32[]{:S(2)}) copy-start(bf16[2,9,256,128]{3,2,1,0:T(8,128)(2,1)} %weights_ref.3) | copy-start | bytes 3538948
  13.9 1.7 %copy-start.5 = (bf16[2,4,32,256]{3,2,1,0:T(8,128)(2,1)S(1)}, bf16[2,4,32,256]{3,2,1,0:T(8,128)(2,1)}, u32[]{:S(2)}) copy-start(bf16[2,4,32,256]{3,2,1,0:T(8,128)(2,1)} %second_ref.3) | copy-start | bytes 393220
  13.9 1.7 %copy-start.7 = (bf16[2,4,32,256]{3,2,1,0:T(8,128)(2,1)S(1)}, bf16[2,4,32,256]{3,2,1,0:T(8,128)(2,1)}, u32[]{:S(2)}) copy-start(bf16[2,4,32,256]{3,2,1,0:T(8,128)(2,1)} %first_ref.3) | copy-start | bytes 393220
  13.9 1.7 %copy-start.8 = (bf16[2,4,32,128]{3,2,1,0:T(8,128)(2,1)S(1)}, bf16[2,4,32,128]{3,2,1,0:T(8,128)(2,1)}, u32[]{:S(2)}) copy-start(bf16[2,4,32,128]{3,2,1,0:T(8,128)(2,1)} %input_ref.1) | copy-start | bytes 196612
  13.9 2.3 %copy-start.3 = (bf16[2,8,4,32,128]{4,3,2,1,0:T(8,128)(2,1)S(1)}, bf16[2,8,4,32,128]{4,3,2,1,0:T(8,128)(2,1)}, u32[]{:S(2)}) copy-start(bf16[2,8,4,32,128]{4,3,2,1,0:T(8,128)(2,1)} %grads_ref.5) | copy-start | bytes 1572868
  13.9 2.3 %copy-start.10 = (bf16[2,9,256,128]{3,2,1,0:T(8,128)(2,1)S(1)}, bf16[2,9,256,128]{3,2,1,0:T(8,128)(2,1)}, u32[]{:S(2)}) copy-start(bf16[2,9,256,128]{3,2,1,0:T(8,128)(2,1)} %weights_ref.3) | copy-start | bytes 3538948
  15.5 2.3 %collective-permute-start.2 = (bf16[4,6,40,256]{3,2,1,0:T(8,128)(2,1)S(1)}, bf16[4,6,40,256]{3,2,1,0:T(8,128)(2,1)S(1)}, u32[]{:S(2)}, u32[]{:S(2)}) collective-permute-start(bf16[4,6,40,256]{3,2,1,0:T(8,128)(2,1)S(1)} %head_conv.3), channel_id=1, source_target_pairs={{0,8},{8,0},{16,24},{24,16},{1,9},{9,1},{17,25},{25,17},{2,10},{10... | collective-permute-start | bytes 1474568 | tf_op jit(solution)/shard_map/ppermute | solution.py:380
  17.8 12.6 %copy-start.11 = (bf16[9,256,256]{2,1,0:T(8,128)(2,1)S(1)}, bf16[9,256,256]{2,1,0:T(8,128)(2,1)}, u32[]{:S(2)}) copy-start(bf16[9,256,256]{2,1,0:T(8,128)(2,1)} %refs_6_.1) | copy-start | bytes 3538948
  18.1 12.1 %collective-permute-start.3 = (bf16[2,6,40,256]{3,2,1,0:T(8,128)(2,1)S(1)}, bf16[2,6,40,256]{3,2,1,0:T(8,128)(2,1)S(1)}, u32[]{:S(2)}, u32[]{:S(2)}) collective-permute-start(bf16[2,6,40,256]{3,2,1,0:T(8,128)(2,1)S(1)} %get-tuple-element.27), channel_id=1, source_target_pairs={{0,16},{8,24},{16,0},{24,8},{1,17},{9,25},{17,1},{25,9},{2,18},{10... | collective-permute-start | bytes 737288 | tf_op jit(solution)/shard_map/ppermute | solution.py:380
  19.6 10.7 %collective-permute-start.4 = (bf16[2,6,40,256]{3,2,1,0:T(8,128)(2,1)S(1)}, bf16[2,6,40,256]{3,2,1,0:T(8,128)(2,1)S(1)}, u32[]{:S(2)}, u32[]{:S(2)}) collective-permute-start(bf16[2,6,40,256]{3,2,1,0:T(8,128)(2,1)S(1)} %get-tuple-element.28), channel_id=1, source_target_pairs={{0,4},{4,0},{1,5},{5,1},{2,6},{6,2},{3,7},{7,3},{8,12},{12,8},{9,1... | collective-permute-start | bytes 737288 | tf_op jit(solution)/shard_map/ppermute | solution.py:380
  21.2 9.0 %collective-permute-start.5 = (bf16[2,3,40,256]{3,2,1,0:T(8,128)(2,1)S(1)}, bf16[2,3,40,256]{3,2,1,0:T(8,128)(2,1)S(1)}, u32[]{:S(2)}, u32[]{:S(2)}) collective-permute-start(bf16[2,3,40,256]{3,2,1,0:T(8,128)(2,1)S(1)} %get-tuple-element.29), channel_id=1, source_target_pairs={{0,20},{4,16},{8,28},{12,24},{16,4},{20,0},{24,12},{28,8},{1,21},{... | collective-permute-start | bytes 368648 | tf_op jit(solution)/shard_map/ppermute | solution.py:397
  33.5 2.6 %collective-permute-start.7 = (bf16[9,256,128]{2,1,0:T(8,128)(2,1)S(1)}, bf16[9,256,128]{2,1,0:T(8,128)(2,1)S(1)}, u32[]{:S(2)}, u32[]{:S(2)}) collective-permute-start(bf16[9,256,128]{2,1,0:T(8,128)(2,1)S(1)} %get-tuple-element.38), channel_id=1, source_target_pairs={{0,8},{8,0},{16,24},{24,16},{1,9},{9,1},{17,25},{25,17},{2,10},{10... | collective-permute-start | bytes 1769480 | tf_op jit(solution)/shard_map/ppermute | solution.py:380
  33.6 2.4 %collective-permute-start.6 = (bf16[9,128,128]{2,1,0:T(8,128)(2,1)S(1)}, bf16[9,128,128]{2,1,0:T(8,128)(2,1)S(1)}, u32[]{:S(2)}, u32[]{:S(2)}) collective-permute-start(bf16[9,128,128]{2,1,0:T(8,128)(2,1)S(1)} %get-tuple-element.36), channel_id=1, source_target_pairs={{0,8},{8,0},{16,24},{24,16},{1,9},{9,1},{17,25},{25,17},{2,10},{10... | collective-permute-start | bytes 884744 | tf_op jit(solution)/shard_map/ppermute | solution.py:380
  36.3 12.3 %collective-permute-start.8 = (bf16[1,4,432,128]{3,2,1,0:T(8,128)(2,1)S(1)}, bf16[1,4,432,128]{3,2,1,0:T(8,128)(2,1)S(1)}, u32[]{:S(2)}, u32[]{:S(2)}) collective-permute-start(bf16[1,4,432,128]{3,2,1,0:T(8,128)(2,1)S(1)} %fusion), channel_id=1, source_target_pairs={{0,4},{4,0},{1,5},{5,1},{2,6},{6,2},{3,7},{7,3},{8,12},{12,8},{9,1... | collective-permute-start | bytes 1327112 | tf_op jit(solution)/shard_map/ppermute | solution.py:380
  37.9 24.0 %copy-start = (bf16[9,128,256]{2,1,0:T(8,128)(2,1)S(1)}, bf16[9,128,256]{2,1,0:T(8,128)(2,1)}, u32[]{:S(2)}) copy-start(bf16[9,128,256]{2,1,0:T(8,128)(2,1)} %w_first_ref.1) | copy-start | bytes 1769476
  48.8 10.9 %collective-permute-start.10 = (bf16[432,128]{1,0:T(8,128)(2,1)S(1)}, bf16[432,128]{1,0:T(8,128)(2,1)S(1)}, u32[]{:S(2)}, u32[]{:S(2)}) collective-permute-start(bf16[432,128]{1,0:T(8,128)(2,1)S(1)} %get-tuple-element.43), channel_id=1, source_target_pairs={{0,2},{1,3},{2,0},{3,1},{4,6},{5,7},{6,4},{7,5},{8,10},{9,11},{10,... | collective-permute-start | bytes 331784 | tf_op jit(solution)/shard_map/ppermute | solution.py:386
  50.8 8.9 %collective-permute-start.11 = (bf16[432,128]{1,0:T(8,128)(2,1)S(1)}, bf16[432,128]{1,0:T(8,128)(2,1)S(1)}, u32[]{:S(2)}, u32[]{:S(2)}) collective-permute-start(bf16[432,128]{1,0:T(8,128)(2,1)S(1)} %get-tuple-element.42), channel_id=1, source_target_pairs={{0,3},{1,0},{2,1},{3,2},{4,7},{5,4},{6,5},{7,6},{8,11},{9,8},{10,9... | collective-permute-start | bytes 331784 | tf_op jit(solution)/shard_map/ppermute | solution.py:386
  52.3 7.4 %collective-permute-start.9 = (bf16[432,128]{1,0:T(8,128)(2,1)S(1)}, bf16[432,128]{1,0:T(8,128)(2,1)S(1)}, u32[]{:S(2)}, u32[]{:S(2)}) collective-permute-start(bf16[432,128]{1,0:T(8,128)(2,1)S(1)} %get-tuple-element.41), channel_id=1, source_target_pairs={{0,1},{1,2},{2,3},{3,0},{4,5},{5,6},{6,7},{7,4},{8,9},{9,10},{10,1... | collective-permute-start | bytes 331784 | tf_op jit(solution)/shard_map/ppermute | solution.py:386
  59.7 5.4 %collective-permute-start.12 = (bf16[432,128]{1,0:T(8,128)(2,1)S(1)}, bf16[432,128]{1,0:T(8,128)(2,1)S(1)}, u32[]{:S(2)}, u32[]{:S(2)}) collective-permute-start(bf16[432,128]{1,0:T(8,128)(2,1)S(1)} %fusion.4.mine_ref), channel_id=1, source_target_pairs={{0,16},{8,24},{16,0},{24,8},{1,17},{9,25},{17,1},{25,9},{2,18},{10... | collective-permute-start | bytes 331784 | tf_op jit(solution)/shard_map/ppermute | solution.py:380
  61.0 4.1 %collective-permute-start.13 = (bf16[432,128]{1,0:T(8,128)(2,1)S(1)}, bf16[432,128]{1,0:T(8,128)(2,1)S(1)}, u32[]{:S(2)}, u32[]{:S(2)}) collective-permute-start(bf16[432,128]{1,0:T(8,128)(2,1)S(1)} %fusion.4.mine_ref), channel_id=1, source_target_pairs={{0,8},{8,0},{16,24},{24,16},{1,9},{9,1},{17,25},{25,17},{2,10},{10... | collective-permute-start | bytes 331784 | tf_op jit(solution)/shard_map/ppermute | solution.py:380
  61.0 5.3 %collective-permute-start.14 = (bf16[432,128]{1,0:T(8,128)(2,1)S(1)}, bf16[432,128]{1,0:T(8,128)(2,1)S(1)}, u32[]{:S(2)}, u32[]{:S(2)}) collective-permute-start(bf16[432,128]{1,0:T(8,128)(2,1)S(1)} %fusion.4.mine_ref), channel_id=1, source_target_pairs={{0,24},{8,16},{16,8},{24,0},{1,25},{9,17},{17,9},{25,1},{2,26},{10... | collective-permute-start | bytes 331784 | tf_op jit(solution)/shard_map/ppermute | solution.py:380

commit v2 on v1

--- a/solution.py
+++ b/solution.py
@@ -36,11 +36,15 @@
     return lax.dot_general(left, right, (((1,), (0,)), ((), ())), preferred_element_type=F32)
 
 
-def run(name, kernel, out_shape, arrays, scratch=(), scalars=None, flops=0):
-    specs = [pl.BlockSpec(memory_space=pltpu.VMEM)] * len(arrays)
-    if scalars is not None:
-        specs = [pl.BlockSpec(memory_space=pltpu.SMEM)] + specs
-        arrays = [scalars] + list(arrays)
+def core_and_chip():
+    lead = lax.axis_index("lead")
+    return lax.rem(lead, 2), lax.div(lead, 2)
+
+
+def run(name, kernel, out_shape, arrays, scratch=(), flops=0, far=False):
+    specs = [pl.BlockSpec(memory_space=pltpu.HBM if far else pltpu.VMEM)] * len(arrays)
+    if far:
+        arrays = [pltpu.with_memory_space_constraint(a, pltpu.HBM) for a in arrays]
     touched = sum(a.size * a.dtype.itemsize for a in arrays)
     touched += sum(math.prod(s.shape) * s.dtype.itemsize for s in out_shape)
     return pl.pallas_call(
@@ -55,12 +59,22 @@
     )(*arrays)
 
 
-def pack_kernel(grads_ref, second_ref, first_ref, right_ref, left_ref, edges, edges_wide, packed):
-    heads, batch, height, breadth, _ = grads_ref.shape
-    samples = second_ref.shape[0]
+def pack_kernel(grads_far, second_far, first_far, right_ref, left_ref, grads_near, second_near, first_near, edges, edges_wide, packed, sems):
+    heads, batch, height, breadth, _ = grads_far.shape
+    samples = second_far.shape[0]
     rows = 6 * height
+    copies = []
+    for side in range(2):
+        columns = pl.ds(breadth - 16 if side == 0 else 0, 16)
+        for j, (far, near) in enumerate(((grads_far, grads_near), (second_far, second_near), (first_far, first_near))):
+            source = far.at[:, :, :, columns, :] if j == 0 else far.at[:, :, columns, :]
+            copies.append(pltpu.make_async_copy(source, near.at[side], sems.at[side, j]))
+            copies[-1].start()
+    for copy in copies:
+        copy.wait()
     for side, out_ref in ((0, right_ref), (1, left_ref)):
-        start = breadth - 8 if side == 0 else 0
+        start = 8 if side == 0 else 0
+        grads_ref, second_ref, first_ref = grads_near.at[side], second_near.at[side], first_near.at[side]
         for h in range(heads):
             for b in range(batch):
                 block = grads_ref[h, b, :, start : start + 8, :].astype(F32)
@@ -100,21 +114,43 @@
         [shape, shape],
         [head_grads, pre_second, pre_first],
         [
+            pltpu.VMEM((2, heads, batch, height, 16, LANES), BF),
+            pltpu.VMEM((2, samples, height, 16, 2 * LANES), BF),
+            pltpu.VMEM((2, samples, height, 16, 2 * LANES), BF),
             pltpu.VMEM((heads * batch * height * 8, LANES), F32),
             pltpu.VMEM((2, 2 * samples * height * 8, LANES), F32),
             pltpu.VMEM(((batch + samples) * 6 * height, LANES), F32),
+            pltpu.SemaphoreType.DMA((2, 3)),
         ],
-    )
-
-
-def heads_kernel(at_ref, grads_ref, low_ref, high_ref, weights_ref, out_ref, wide, shifted, total):
+        far=True,
+    )
+
+
+def stage_kernel(*refs):
+    count = len(refs) // 2
+    sems = refs[-1]
+    copies = [pltpu.make_async_copy(refs[i], refs[count + i], sems.at[i]) for i in range(count)]
+    for copy in copies:
+        copy.start()
+    for copy in copies:
+        copy.wait()
+
+
+def stage(*arrays):
+    shapes = [pltpu.VMEM(a.shape, a.dtype) for a in arrays]
+    return run("stage", stage_kernel, shapes, list(arrays), [pltpu.SemaphoreType.DMA((len(arrays),))], far=True, flops=1 << 30)
+
+
+def heads_kernel(other_core, grads_ref, low_ref, high_ref, weights_ref, out_ref, wide, shifted, total):
     heads, batch, height, breadth, _ = grads_ref.shape
     slots, _, kept, depth = out_ref.shape
     pitch = kept + 16
     own = 8 + EDGE
+    core, chip = core_and_chip()
+    core = 1 - core if other_core else core
     for slot in range(slots):
-        group = at_ref[1] if slot < slots // 2 else 1 - at_ref[1]
-        b = (2 * group + at_ref[0]) * (slots // 2) + slot % (slots // 2)
+        group = chip if slot < slots // 2 else 1 - chip
+        b = (2 * group + core) * (slots // 2) + slot % (slots // 2)
         low = low_ref[b].astype(F32)
         high = high_ref[b].astype(F32)
         for r in range(height):
@@ -146,14 +182,14 @@
     out_ref[...] = total[...].astype(BF)
 
 
-def head_conv(scalars, head_grads, low, high, head_weights, samples):
+def head_conv(other_core, head_grads, low, high, head_weights, samples):
     heads, batch, height, breadth, _ = head_grads.shape
     depth = head_weights.shape[2]
     kept = breadth + 2 * EDGE
     slots = 2 * samples
     return run(
         "head_conv",
-        heads_kernel,
+        functools.partial(heads_kernel, other_core),
         [jax.ShapeDtypeStruct((slots, height + 2, kept, depth), BF)],
         [head_grads, low, high, head_weights],
         [
@@ -161,7 +197,6 @@
             pltpu.VMEM((slots * height * kept, 3 * heads * LANES), BF),
             pltpu.VMEM((slots, height + 2, kept, depth), F32),
         ],
-        scalars,
         flops=2 * slots * height * kept * 9 * heads * LANES * depth,
     )[0]
 
@@ -218,7 +253,7 @@
     )
 
 
-def spread_kernel(at_ref, mine_ref, got_ref, second_ref, first_ref, own_ref, cross_ref, *strips):
+def spread_kernel(mine_ref, got_ref, second_ref, first_ref, own_ref, cross_ref, *strips):
     samples = own_ref.shape[0]
     height = second_ref.shape[1]
     total = mine_ref[...].astype(F32) + got_ref[...].astype(F32)
@@ -227,14 +262,14 @@
     cross_ref[...] = total[samples:]
     for way in range(len(strips) // 2):
         line_ref, corner_ref = strips[2 * way], strips[2 * way + 1]
-        down = at_ref[way]
+        down = 1 - lax.axis_index("lat") if len(strips) == 2 else 1 - way
         line_ref[:, 0:3] = own_ref[:, pl.ds((height - 1) * down, 3)]
         corner_ref[...] = cross_ref[:, pl.ds((height - 1) * down, 3)]
         line_ref[:, 3:5] = second_ref[:, pl.ds((height - 2) * down, 2)]
         line_ref[:, 5:6] = first_ref[:, pl.ds((height - 1) * down, 1)]
 
 
-def spread(scalars, mine, got, second, first, ways):
+def spread(mine, got, second, first, ways):
     slots, rows, kept, depth = mine.shape
     samples = slots // 2
     whole = jax.ShapeDtypeStruct((samples, rows, kept, depth), BF)
@@ -242,46 +277,73 @@
         jax.ShapeDtypeStruct((samples, 6, kept, depth), BF),
         jax.ShapeDtypeStruct((samples, 3, kept, depth), BF),
     ] * ways
-    return run("core_sum", spread_kernel, [whole, whole] + strips, [mine, got, second, first], (), scalars)
-
-
-def encoder_kernel(norm_factor, ways, at_ref, own_ref, cross_ref, *refs):
+    return run("core_sum", spread_kernel, [whole, whole] + strips, [mine, got, second, first])
+
+
+def latent_kernel(ways, bands, own_ref, cross_ref, *refs):
     strips, refs = refs[: 2 * ways], refs[2 * ways :]
-    slope_second_ref, slope_first_ref, act_ref, input_ref, w_second_ref = refs[:5]
-    moved_out, first_mine, first_other, second_mine, second_other = refs[5:10]
-    latent, slope_second, slope_first, wide, cat, cat_own, wide_first = refs[10:]
+    slope_second_ref, slope_first_ref, grad_ref, away_ref, slope_out, latent, slope_second = refs
     samples, rows, kept, depth = own_ref.shape
     height = rows - 2
-    breadth = kept - 2 * EDGE
-    lat, bands, core = at_ref[0], at_ref[1], at_ref[2]
-    own = 8 + EDGE
+    lat = lax.axis_index("lat")
+    _, chip = core_and_chip()
     blank = jnp.zeros((samples, kept, depth), F32)
     latent[:, 0] = blank
     latent[:, height + 3] = blank
     latent[:, 1 : height + 3] = own_ref[...].astype(F32) + cross_ref[...].astype(F32)
     slope_second[:, 2 : 2 + height] = slope_second_ref[...]
-    slope_first[:, 1 : 1 + height] = slope_first_ref[...]
+    slope_out[:, 1 : 1 + height] = slope_first_ref[...]
     for way in range(ways):
         line_ref, corner_ref = strips[2 * way], strips[2 * way + 1]
-        below = at_ref[3 + way]
+        below = 1 - lat if ways == 1 else way
         at = (height + 1) * below
         latent[:, pl.ds(at, 3)] += line_ref[:, 0:3].astype(F32) + corner_ref[...].astype(F32)
         slope_second[:, pl.ds((height + 2) * below, 2)] = gelu_slope(line_ref[:, 3:5].astype(F32))
-        slope_first[:, pl.ds((height + 1) * below, 1)] = gelu_slope(line_ref[:, 5:6].astype(F32))
+        slope_out[:, pl.ds((height + 1) * below, 1)] = gelu_slope(line_ref[:, 5:6].astype(F32))
     for i in range(height + 4):
         row = lat * height + i - 2
         valid = jnp.logical_and(row >= 0, row < bands * height)
         value = latent[:, i] * slope_second[:, i]
         if i < 2 or i >= height + 2:
             value = jnp.where(valid, value, 0.0)
-        wide[:, i, 8 : 8 + kept, :] = value.astype(BF).astype(F32)
+        grad_ref[:, i] = value.astype(BF)
+        if 0 < i < height + 3:
+            away_ref[:, i - 1] = jnp.where(chip == 0, value[:, :, LANES:], value[:, :, :LANES]).astype(BF)
+
+
+def latent_grads(ways, bands, own, cross, strips, slope_second, slope_first):
+    samples, rows, kept, depth = own.shape
+    return run(
+        "latent_grads",
+        functools.partial(latent_kernel, ways, bands),
+        [
+            jax.ShapeDtypeStruct((samples, rows + 2, kept, depth), BF),
+            jax.ShapeDtypeStruct((samples, rows, kept, LANES), BF),
+            jax.ShapeDtypeStruct((samples, rows, kept, depth), F32),
+        ],
+        [own, cross, *strips, slope_second, slope_first],
+        [
+            pltpu.VMEM((samples, rows + 2, kept, depth), F32),
+            pltpu.VMEM((samples, rows + 2, kept, depth), F32),
+        ],
+    )
+
+
+def encoder_kernel(norm_factor, bands, grad_ref, slope_ref, input_ref, weights_ref, moved_out, mine_ref, other_ref, wide, cat, wide_first):
+    samples, tall, kept, depth = grad_ref.shape
+    rows = tall - 2
+    height = rows - 2
+    breadth = kept - 2 * EDGE
+    lat = lax.axis_index("lat")
+    core, _ = core_and_chip()
+    own = 8 + EDGE
+    wide[:, :, 8 : 8 + kept, :] = grad_ref[...].astype(F32)
     for v in STEPS:
         lanes = slice((v + 1) * depth, (v + 2) * depth)
         cat[:, :, :, lanes] = wide[:, :, 8 - v : 8 - v + kept + 8, :].astype(BF)
-        cat_own[:, :, :, lanes] = wide[:, 1 : height + 3, own - v : own - v + breadth, :].astype(BF)
     linear = None
     for u in STEPS:
-        weights = jnp.concatenate([w_second_ref[3 * (u + 1) + (v + 1)] for v in STEPS], axis=1)
+        weights = jnp.concatenate([weights_ref[3 * (u + 1) + (v + 1)] for v in STEPS], axis=1)
         left = cat[:, 1 - u : 1 - u + rows].reshape(samples * rows * (kept + 8), 3 * depth)
         part = dot_last(left, weights)
         linear = part if linear is None else linear + part
@@ -289,55 +351,131 @@
     for i in range(rows):
         row = lat * height + i - 1
         valid = jnp.logical_and(row >= 0, row < bands * height)
-        value = linear[:, i, :kept] * slope_first[:, i]
+        value = linear[:, i, :kept] * slope_ref[:, i]
         if i < 1 or i >= height + 1:
             value = jnp.where(valid, value, 0.0)
         wide_first[:, i, 8 : 8 + kept, :] = value.astype(BF).astype(F32)
     for v in STEPS:
         lanes = slice((v + 1) * depth, (v + 2) * depth)
         moved_out[:, :, :, lanes] = wide_first[:, :, own - v : own - v + breadth, :].astype(BF)
-    for left_ref, source, mine_ref, other_ref in (
-        (input_ref, moved_out, first_mine, first_other),
-        (act_ref, cat_own, second_mine, second_other),
-    ):
-        for u in STEPS:
-            right = source[:, 1 - u : 1 - u + height].reshape(samples * height * breadth, 3 * depth)
-            part = dot_plain(left_ref[...], right) * norm_factor
-            for v in STEPS:
-                k = 3 * (u + 1) + (v + 1)
-                lower = part[:, (v + 1) * depth : (v + 1) * depth + LANES]
-                upper = part[:, (v + 1) * depth + LANES : (v + 2) * depth]
-                mine_ref[k] = jnp.where(core == 0, lower, upper).astype(BF)
-                other_ref[k] = jnp.where(core == 0, upper, lower).astype(BF)
-
-
-def encoder(scalars, ways, norm_factor, own, cross, strips, slope_second, slope_first, act, cells_in, w_second):
-    samples, rows, kept, depth = own.shape
-    height, breadth = rows - 2, kept - 2 * EDGE
+    for u in STEPS:
+        right = moved_out[:, 1 - u : 1 - u + height].reshape(samples * height * breadth, 3 * depth)
+        part = dot_plain(input_ref[...], right) * norm_factor
+        for v in STEPS:
+            k = 3 * (u + 1) + (v + 1)
+            lower = part[:, (v + 1) * depth : (v + 1) * depth + LANES]
+            upper = part[:, (v + 1) * depth + LANES : (v + 2) * depth]
+            mine_ref[k] = jnp.where(core == 0, lower, upper).astype(BF)
+            other_ref[k] = jnp.where(core == 0, upper, lower).astype(BF)
+
+
+def encoder(norm_factor, bands, grad, slope, cells_in, w_second):
+    samples, tall, kept, depth = grad.shape
+    rows, height, breadth = tall - 2, tall - 4, kept - 2 * EDGE
     channels = cells_in.shape[0]
+    half = jax.ShapeDtypeStruct((9, channels, LANES), BF)
     return run(
         "encoder_grads",
-        functools.partial(encoder_kernel, norm_factor, ways),
+        functools.partial(encoder_kernel, norm_factor, bands),
+        [jax.ShapeDtypeStruct((samples, rows, breadth, 3 * depth), BF), half, half],
+        [grad, slope, cells_in, w_second],
         [
-            jax.ShapeDtypeStruct((samples, rows, breadth, 3 * depth), BF),
-            jax.ShapeDtypeStruct((9, channels, LANES), BF),
-            jax.ShapeDtypeStruct((9, channels, LANES), BF),
-            jax.ShapeDtypeStruct((9, depth, LANES), BF),
-            jax.ShapeDtypeStruct((9, depth, LANES), BF),
+            pltpu.VMEM((samples, tall, kept + 24, depth), F32),
+            pltpu.VMEM((samples, tall, kept + 8, 3 * depth), BF),
+            pltpu.VMEM((samples, rows, kept + 16, depth), F32),
         ],
-        [own, cross, *strips, slope_second, slope_first, act, cells_in, w_second],
-        [
-            pltpu.VMEM((samples, height + 4, kept, depth), F32),
-            pltpu.VMEM((samples, height + 4, kept, depth), F32),
-            pltpu.VMEM((samples, height + 2, kept, depth), F32),
-            pltpu.VMEM((samples, height + 4, kept + 24, depth), F32),
-            pltpu.VMEM((samples, height + 4, kept + 8, 3 * depth), BF),
-            pltpu.VMEM((samples, height + 2, breadth, 3 * depth), BF),
-            pltpu.VMEM((samples, height + 2, kept + 16, depth), F32),
-        ],
-        scalars,
-        flops=2 * 9 * depth * (samples * rows * (kept + 8) * depth + samples * height * breadth * (depth + channels)),
-    )
+        flops=2 * 9 * depth * (samples * rows * (kept + 8) * depth + samples * height * breadth * channels),
+    )
+
+
+def second_kernel(norm_factor, shares, grad_ref, got_ref, act_ref, act_got_ref, *refs):
+    full_ref, wide, cat = refs[-3:]
+    samples, tall, kept, depth = grad_ref.shape
+    rows, height, breadth = tall - 2, tall - 4, kept - 2 * EDGE
+    core, chip = core_and_chip()
+    own = 8 + EDGE
+    lower = grad_ref[:, 1 : 1 + rows, :, :LANES].astype(F32)
+    upper = grad_ref[:, 1 : 1 + rows, :, LANES:].astype(F32)
+    wide[:samples, :, 8 : 8 + kept, :] = jnp.where(chip == 0, lower, upper)
+    wide[samples:, :, 8 : 8 + kept, :] = got_ref[...].astype(F32)
+    for v in STEPS:
+        lanes = slice((v + 1) * LANES, (v + 2) * LANES)
+        cat[:, :, :, lanes] = wide[:, :, own - v : own - v + breadth, :].astype(BF)
+    cells = samples * height * breadth
+    for u in STEPS:
+        right = cat[:, 1 - u : 1 - u + height].reshape(2 * cells, 3 * LANES)
+        part = dot_plain(act_ref[...], right[:cells]) + dot_plain(act_got_ref[...], right[cells:])
+        part = part * norm_factor
+        for v in STEPS:
+            k = 3 * (u + 1) + (v + 1)
+            full_ref[k * depth : (k + 1) * depth, :] = part[:, (v + 1) * LANES : (v + 2) * LANES].astype(BF)
+    if len(refs) == 5:
+        size = 9 * depth // shares // 2
+        for i in range(shares):
+            for out_ref, half in ((refs[0], core), (refs[1], 1 - core)):
+                out_ref[i] = full_ref[pl.ds(pl.multiple_of((2 * i + half) * size, 16), size), :]
+
+
+def second_grads(norm_factor, shares, grad, got, act, act_got):
+    samples, tall, kept, depth = grad.shape
+    rows, height, breadth = tall - 2, tall - 4, kept - 2 * EDGE
+    size = 9 * depth // shares // 2
+    inside = size % 16 == 0
+    half = jax.ShapeDtypeStruct((shares, size, LANES), BF)
+    scratch = [
+        pltpu.VMEM((2 * samples, rows, kept + 16, LANES), F32),
+        pltpu.VMEM((2 * samples, rows, breadth, 3 * LANES), BF),
+    ]
+    results = run(
+        "second_weight_grads",
+        functools.partial(second_kernel, norm_factor, shares),
+        [half, half] if inside else [jax.ShapeDtypeStruct((9 * depth, LANES), BF)],
+        [grad, got, act, act_got],
+        [pltpu.VMEM((9 * depth, LANES), BF)] + scratch if inside else scratch,
+        flops=2 * 9 * depth * LANES * 2 * samples * height * breadth,
+    )
+    if inside:
+        return results
+    halves = results[0].reshape(shares, 2, size, LANES)
+    core, _ = core_and_chip()
+    return [lax.dynamic_index_in_dim(halves, part, 1, keepdims=False) for part in (core, 1 - core)]
+
+
+def act_kernel(source_ref, out_ref):
+    samples, height, breadth, depth = source_ref.shape
+    active = gelu_value(source_ref[...].astype(F32).reshape(samples * height * breadth, depth)).astype(BF).astype(F32)
+    out_ref[...] = active.T.astype(BF)
+
+
+def activated(source):
+    samples, height, breadth, depth = source.shape
+    return run("activated", act_kernel, [jax.ShapeDtypeStruct((depth, samples * height * breadth), BF)], [source])[0]
+
+
+def other_band_kernel(*refs):
+    terms, out_ref = refs[:-1], refs[-1]
+    band = 1 - lax.rem(lax.axis_index("lat"), 2)
+    for layer in range(2):
+        parts = [t[band].astype(F32) for t in terms[layer * len(terms) // 2 : (layer + 1) * len(terms) // 2]]
+        out_ref[layer] = sum(parts[1:], parts[0]).astype(BF)
+
+
+def own_band_kernel(*refs):
+    columns = refs[0].shape[1]
+    terms, came, outs = refs[: -columns - 1], refs[-columns - 1], refs[-columns:]
+    band, lon = lax.rem(lax.axis_index("lat"), 2), lax.axis_index("lon")
+    for step in range(columns):
+        block = lax.rem(lon + step, columns)
+        for layer in range(2):
+            parts = [t[band, block].astype(F32) for t in terms[layer * len(terms) // 2 : (layer + 1) * len(terms) // 2]]
+            outs[step][layer] = sum(parts, came[layer, block].astype(F32)).astype(BF)
+
+
+def sum_kernel(*refs):
+    total = refs[0][...].astype(F32)
+    for ref in refs[1:-1]:
+        total = total + ref[...].astype(F32)
+    refs[-1][...] = total.astype(BF)
 
 
 def input_kernel(moved_ref, w_first_ref, out_ref):
@@ -363,16 +501,18 @@
     )[0]
 
 
-def join_kernel(rows_first, at_ref, mine_ref, cross_ref, core_ref, both_ref, first_ref, second_ref):
-    here = mine_ref[...].astype(F32) + cross_ref[...].astype(F32)
-    there = core_ref[...].astype(F32) + both_ref[...].astype(F32)
-    core = at_ref[2]
-    lower = jnp.where(core == 0, here, there)
-    upper = jnp.where(core == 0, there, here)
-    rows_second = here.shape[0] - rows_first
-    for half, value in ((0, lower), (1, upper)):
-        first_ref[pl.ds(half, rows_first, stride=2), :] = value[:rows_first]
-        second_ref[pl.ds(half, rows_second, stride=2), :] = value[rows_first:]
+def join_kernel(mine_ref, cross_ref, core_ref, both_ref, first_ref, second_ref):
+    core, chip = core_and_chip()
+    rows = mine_ref.shape[1]
+    here = mine_ref[0].astype(F32) + cross_ref[0].astype(F32)
+    there = core_ref[0].astype(F32) + both_ref[0].astype(F32)
+    first_ref[pl.ds(0, rows, stride=2), :] = jnp.where(core == 0, here, there)
+    first_ref[pl.ds(1, rows, stride=2), :] = jnp.where(core == 0, there, here)
+    mine, cross, other, both = (ref[1].astype(F32) for ref in (mine_ref, cross_ref, core_ref, both_ref))
+    for part in range(2):
+        near, far = jnp.where(core == part, mine, other), jnp.where(core == part, cross, both)
+        second_ref[pl.ds(2 * rows * part, rows, stride=2), :] = jnp.where(chip == 0, near, far)
+        second_ref[pl.ds(2 * rows * part + 1, rows, stride=2), :] = jnp.where(chip == 0, far, near)
 
 
 def swap(array, axis, flip):
@@ -400,29 +540,26 @@
 def per_device(head_grads, head_weights, encoder_input, pre_first, pre_second, w_first, w_second):
     samples, height, breadth, _ = encoder_input.shape
     bands, columns = lax.axis_size("lat"), lax.axis_size("lon")
-    lead, lat, lon = lax.axis_index("lead"), lax.axis_index("lat"), lax.axis_index("lon")
-    core, chip = lead % 2, lead // 2
     cells_total = samples * lax.axis_size("lead") * height * bands * breadth * columns
     norm_factor = 1.0 / math.sqrt(cells_total)
 
     to_right, to_left = pack(head_grads, pre_second, pre_first)
+    to_right, to_left, to_cross = lax.optimization_barrier((to_right, to_left, pre_first))
     low = around(to_right, "lon", 1)
     high = around(to_left, "lon", -1)
-
-    theirs = head_conv(jnp.stack([1 - core, chip]).astype(jnp.int32), head_grads, low, high, head_weights, samples)
+    act_got = activated(swap(to_cross, "lead", 2))
+    head_grads, head_weights, w_second, pre_second, pre_first, encoder_input = stage(
+        head_grads, head_weights, w_second, pre_second, pre_first, encoder_input
+    )
+    low, high, act_got = lax.optimization_barrier((low, high, act_got))
+
+    theirs = head_conv(True, head_grads, low, high, head_weights, samples)
     got = swap(theirs, "lead", 1)
-    mine = head_conv(jnp.stack([core, chip]).astype(jnp.int32), head_grads, low, high, head_weights, samples)
+    mine = head_conv(False, head_grads, low, high, head_weights, samples)
     second, first, slope_second, slope_first, act, cells_in = saved(pre_second, pre_first, encoder_input, low, high)
 
-    if bands == 2:
-        steps = [None]
-        goes_down = jnp.stack([1 - lat])
-        from_below = jnp.stack([1 - lat])
-    else:
-        steps = [1, -1]
-        goes_down = jnp.array([1, 0])
-        from_below = jnp.array([0, 1])
-    spreads = spread(goes_down.astype(jnp.int32), mine, got, second, first, len(steps))
+    steps = [None] if bands == 2 else [1, -1]
+    spreads = spread(mine, got, second, first, len(steps))
     own = spreads[0]
     cross = swap(spreads[1], "lead", 2)
     strips = []
@@ -431,55 +568,43 @@
         strips.append(swap(line, "lat", 1) if step is None else around(line, "lat", step, False))
         strips.append(corner(angle, step))
 
-    place = jnp.concatenate([jnp.stack([lat, jnp.int32(bands), core]), from_below]).astype(jnp.int32)
-    moved, first_mine, first_other, second_mine, second_other = encoder(
-        place, len(steps), norm_factor, own, cross, strips, slope_second, slope_first, act, cells_in, w_second
-    )
+    grad, away, slope = latent_grads(len(steps), bands, own, cross, strips, slope_second, slope_first)
+    grad_got = swap(away, "lead", 2)
+    moved, first_mine, first_other = encoder(norm_factor, bands, grad, slope, cells_in, w_second)
     input_grad = input_conv(moved, w_first)
-
     first_got = swap(first_other, "lead", 1)
+    second_mine, second_other = second_grads(norm_factor, bands * columns, grad, grad_got, act, act_got)
     second_got = swap(second_other, "lead", 1)
-    shares = bands * columns
-
-    def in_shares(array):
-        return array.reshape(bands, columns, -1, LANES)
-
-    def add(*terms):
-        total = terms[0].astype(F32)
-        for term in terms[1:]:
-            total = total + term.astype(F32)
-        return total
-
-    rows_first = first_mine.size // LANES // shares
-    total = jnp.concatenate(
-        [in_shares(add(first_mine, first_got)), in_shares(add(second_mine, second_got))], axis=2
-    ).astype(BF)
+
+    terms = [[first_mine, first_got], [second_mine, second_got]]
     left = bands
-    while left > 1:
-        left //= 2
-        bit = (lat // left) % 2
-        halves = total.reshape((2, left) + total.shape[1:])
-        away = lax.dynamic_index_in_dim(halves, 1 - bit, 0, keepdims=False)
-        keep = lax.dynamic_index_in_dim(halves, bit, 0, keepdims=False)
-        total = add(keep, swap(away, "lat", left)).astype(BF)
-    total = total[0]
-    parts = [lax.dynamic_index_in_dim(total, lon, 0, keepdims=False)]
-    for step in range(1, columns):
-        away = lax.dynamic_index_in_dim(total, (lon + step) % columns, 0, keepdims=False)
-        parts.append(around(away, "lon", step))
-    share = add(*parts).astype(BF)
+    if left > 2:
+        lat = lax.axis_index("lat")
+        summed = jnp.stack([a.reshape(-1, LANES).astype(F32) + b.reshape(-1, LANES).astype(F32) for a, b in terms])
+        summed = summed.astype(BF)
+        while left > 2:
+            left //= 2
+            bit = (lat // left) % 2
+            parts = summed.reshape(2, 2, -1, LANES)
+            send = lax.dynamic_index_in_dim(parts, 1 - bit, 1, keepdims=False)
+            keep = lax.dynamic_index_in_dim(parts, bit, 1, keepdims=False)
+            summed = (keep.astype(F32) + swap(send, "lat", left).astype(F32)).astype(BF)
+        terms = [[summed[0]], [summed[1]]]
+    blocks = [t.reshape(2, columns, -1, LANES) for ts in terms for t in ts]
+    shape = blocks[0].shape
+    rows = shape[2]
+    sent = run("other_band", other_band_kernel, [jax.ShapeDtypeStruct(shape, BF)], blocks)[0]
+    came = swap(sent, "lat", 1)
+    share_shape = jax.ShapeDtypeStruct((2, rows, LANES), BF)
+    shares = run("own_band", own_band_kernel, [share_shape] * columns, blocks + [came])
+    parts = [around(shares[step], "lon", step) for step in range(1, columns)]
+    share = run("share", sum_kernel, [share_shape], [shares[0], *parts])[0]
     peers = [swap(share, "lead", flip) for flip in (2, 1, 3)]
-    rows_second = share.shape[0] - rows_first
     result_first, result_second = run(
         "join_halves",
-        functools.partial(join_kernel, rows_first),
-        [
-            jax.ShapeDtypeStruct((2 * rows_first, LANES), F32),
-            jax.ShapeDtypeStruct((2 * rows_second, LANES), F32),
-        ],
+        join_kernel,
+        [jax.ShapeDtypeStruct((2 * rows, LANES), F32), jax.ShapeDtypeStruct((4 * rows, LANES), F32)],
         [share, *peers],
-        (),
-        place,
     )
     return input_grad, result_first.reshape(-1), result_second.reshape(-1)
 

time: 68 us -> 59.3 us (0.87)
  waiting for transfers between devices: 34.1 us -> 28.2 us
  local copies, waits for them, and re-layouts: 5.22 us -> 0.01 us
  starting transfers between devices: 17.2 us -> 19.3 us
  Pallas kernels: 9.68 us -> 10.8 us
  other arithmetic: 0.69 us -> 0 us
    unnamed x24 -> x2, local copies, waits for them, and re-layouts: 5.18 us -> 0.01 us
    ppermute x5, waiting for transfers between devices: 9.58 us -> 5.01 us  [around(): return lax.ppermute(array, axis, pairs)]
    ppermute x9 -> x11, starting transfers between devices: 7.51 us -> 9.26 us  [swap(): return lax.ppermute(array, axis, [(i, i ^ flip) for i in range(count)])]
    pallas_call x8 -> x15, Pallas kernels: 9.68 us -> 10.8 us  [run(): pl.pallas_call(kernel, name=name, out_shape=out_shape, in_specs=specs, ou...]
    ppermute x9 -> x11, waiting for transfers between devices: 16.1 us -> 15 us  [swap(): return lax.ppermute(array, axis, [(i, i ^ flip) for i in range(count)])]
    ppermute x1, starting transfers between devices: 0.48 us -> 1.44 us  [corner(): return lax.ppermute(array, ('lead', 'lat'), pairs)]
  transfers between devices with their start and end apart: 15 -> 17, of which waited for: 9 -> 11; matrix products, arithmetic and copies ran while one was open for 0% -> 0% of each run, Pallas kernels for 5% -> 12%
where the time goes in v2:
time: 59.3 us; the launch traced here: 59.1 us
  waiting for transfers between devices  28.2 us (48%)
  starting transfers between devices  19.3 us (33%)
  Pallas kernels  10.8 us (18%)
  between operations  0.77 us (1%)
    ppermute x11, waiting for transfers between devices, swap(): return lax.ppermute(array, axis, [(i, i ^ flip) for i in range(count)])  15 us
    pallas_call x15, Pallas kernels, run(): pl.pallas_call(kernel, name=name, out_shape=out_shape, in_specs=specs, ou...  10.8 us
    ppermute x11, starting transfers between devices, swap(): return lax.ppermute(array, axis, [(i, i ^ flip) for i in range(count)])  9.26 us
    ppermute x5, starting transfers between devices, around(): return lax.ppermute(array, axis, pairs)  8.61 us
    ppermute x1, waiting for transfers between devices, corner(): return lax.ppermute(array, ('lead', 'lat'), pairs)  8.19 us
    ppermute x5, waiting for transfers between devices, around(): return lax.ppermute(array, axis, pairs)  5.01 us
    ppermute x1, starting transfers between devices, corner(): return lax.ppermute(array, ('lead', 'lat'), pairs)  1.44 us
  transfers between devices with their start and end apart: 17, of which 11 were waited for; matrix products, arithmetic and copies ran while one was open for 0% of the time, Pallas kernels for 12%

profile of v2, /device:TPU:0, one launch (start us, length us, event | category | flops | bytes accessed | tf_op | source)
XLA Modules:
  0.0 59.1 jit_solution(7275424040030167316)
XLA Ops:
  0.6 1.3 %pack_columns.1 = (bf16[10,24,128]{2,1,0:T(8,128)(2,1)S(1)}, bf16[10,24,128]{2,1,0:T(8,128)(2,1)S(1)}) custom-call(bf16[2,8,4,32,128]{4,3,2,1,0:T(8,128)(2,1)} %grads_far.1, bf16[2,4,32,256]{3,2,1,0:T(8,128)(2,1)} %second_far.1, bf16[2,4,32,256]{3,2,1,0:T(8,128)(2,1)} %first_far.1), custom_call_target="tpu_custom_call" | custom-call | bytes 909312 | tf_op jit(solution)/shard_map/pack_columns/pallas_call | solution.py:50
  1.9 3.0 %collective-permute-start.2 = (bf16[2,4,32,256]{3,2,1,0:T(8,128)(2,1)}, bf16[2,4,32,256]{3,2,1,0:T(8,128)(2,1)S(1)}, u32[]{:S(2)}, u32[]{:S(2)}) collective-permute-start(bf16[2,4,32,256]{3,2,1,0:T(8,128)(2,1)} %first_far.1), channel_id=1, source_target_pairs={{0,16},{8,24},{16,0},{24,8},{1,17},{9,25},{17,1},{25,9},{2,18},{10... | collective-permute-start | bytes 393224 | tf_op jit(solution)/shard_map/ppermute | solution.py:520
  4.9 1.6 %collective-permute-start = (bf16[10,24,128]{2,1,0:T(8,128)(2,1)S(1)}, bf16[10,24,128]{2,1,0:T(8,128)(2,1)S(1)}, u32[]{:S(2)}, u32[]{:S(2)}) collective-permute-start(bf16[10,24,128]{2,1,0:T(8,128)(2,1)S(1)} %get-tuple-element.44), channel_id=1, source_target_pairs={{0,1},{1,2},{2,3},{3,0},{4,5},{5,6},{6,7},{7,4},{8,9},{9,10},{10,1... | collective-permute-start | bytes 184328 | tf_op jit(solution)/shard_map/ppermute | solution.py:526
  6.5 2.2 %collective-permute-start.1 = (bf16[10,24,128]{2,1,0:T(8,128)(2,1)S(1)}, bf16[10,24,128]{2,1,0:T(8,128)(2,1)S(1)}, u32[]{:S(2)}, u32[]{:S(2)}) collective-permute-start(bf16[10,24,128]{2,1,0:T(8,128)(2,1)S(1)} %get-tuple-element.45), channel_id=1, source_target_pairs={{0,3},{1,0},{2,1},{3,2},{4,7},{5,4},{6,5},{7,6},{8,11},{9,8},{10,9... | collective-permute-start | bytes 184328 | tf_op jit(solution)/shard_map/ppermute | solution.py:526
  8.7 1.9 %stage.1 = (bf16[2,8,4,32,128]{4,3,2,1,0:T(8,128)(2,1)S(1)}, bf16[2,9,256,128]{3,2,1,0:T(8,128)(2,1)S(1)}, bf16[9,256,256]{2,1,0:T(8,128)(2,1)S(1)}, bf16[2,4,32...) custom-call(bf16[2,8,4,32,128]{4,3,2,1,0:T(8,128)(2,1)} %grads_far.1, ...), custom_call_target="tpu_custom_call" | custom-call | flops 1073741824 | bytes 6422528 | tf_op jit(solution)/shard_map/stage/pallas_call | solution.py:50
  10.6 0.0 collective-permute-done.2.source_ref
  10.6 0.1 activated.1.act_got_ref
  10.8 0.7 %collective-permute-done.low_ref = bf16[10,24,128]{2,1,0:T(8,128)(2,1)S(1)} collective-permute-done((bf16[10,24,128]{2,1,0:T(8,128)(2,1)S(1)}, bf16[10,24,128]{2,1,0:T(8,128)(2,1)S(1)}, u32[]{:S(2)}, u32[]{:S(2)}) %collective-permute-start) | collective-permute-done | bytes 61472 | tf_op jit(solution)/shard_map/ppermute | solution.py:526
  11.5 0.0 collective-permute-done.1.high_ref
  11.5 1.0 %head_conv.3 = bf16[4,6,40,256]{3,2,1,0:T(8,128)(2,1)S(1)} custom-call(bf16[2,8,4,32,128]{4,3,2,1,0:T(8,128)(2,1)S(1)} %get-tuple-element.41.grads_ref, bf16[10,24,128]{2,1,0:T(8,128)(2,1)S(1)} %collective-permute-done.low_ref, bf16[10,24,128]{2,1,0:T(8,128)(2,1)S(1)} %collective-permute-done.1.high_ref, ...), custom_call_target="tpu_custom_call" | custom-call | flops 754974720 | bytes 2318336 | tf_op jit(solution)/shard_map/head_conv/pallas_call | solution.py:50
  12.5 0.1 collective-permute-start.3
  12.6 0.6 saved_parts.1
  13.1 1.0 %head_conv.2.mine_ref = bf16[4,6,40,256]{3,2,1,0:T(8,128)(2,1)S(1)} custom-call(bf16[2,8,4,32,128]{4,3,2,1,0:T(8,128)(2,1)S(1)} %get-tuple-element.41.grads_ref, bf16[10,24,128]{2,1,0:T(8,128)(2,1)S(1)} %collective-permute-done.low_ref, bf16[10,24,128]{2,1,0:T(8,128)(2,1)S(1)} %collective-permute-done.1.high_ref, ...), custom_call_target="tpu_custom_call" | custom-call | flops 754974720 | bytes 2318336 | tf_op jit(solution)/shard_map/head_conv/pallas_call | solution.py:50
  14.1 0.3 collective-permute-done.3.got_ref
  14.4 0.3 core_sum.1
  14.7 0.5 collective-permute-start.4
  15.2 1.6 %collective-permute-start.5 = (bf16[2,6,40,256]{3,2,1,0:T(8,128)(2,1)S(1)}, bf16[2,6,40,256]{3,2,1,0:T(8,128)(2,1)S(1)}, u32[]{:S(2)}, u32[]{:S(2)}) collective-permute-start(bf16[2,6,40,256]{3,2,1,0:T(8,128)(2,1)S(1)} %get-tuple-element.57), channel_id=1, source_target_pairs={{0,4},{4,0},{1,5},{5,1},{2,6},{6,2},{3,7},{7,3},{8,12},{12,8},{9,1... | collective-permute-start | bytes 737288 | tf_op jit(solution)/shard_map/ppermute | solution.py:520
  16.8 1.4 %collective-permute-start.6 = (bf16[2,3,40,256]{3,2,1,0:T(8,128)(2,1)S(1)}, bf16[2,3,40,256]{3,2,1,0:T(8,128)(2,1)S(1)}, u32[]{:S(2)}, u32[]{:S(2)}) collective-permute-start(bf16[2,3,40,256]{3,2,1,0:T(8,128)(2,1)S(1)} %get-tuple-element.58), channel_id=1, source_target_pairs={{0,20},{4,16},{8,28},{12,24},{16,4},{20,0},{24,12},{28,8},{1,21},{... | collective-permute-start | bytes 368648 | tf_op jit(solution)/shard_map/ppermute | solution.py:537
  18.3 8.2 %collective-permute-done.6.refs_1_ = bf16[2,3,40,256]{3,2,1,0:T(8,128)(2,1)S(1)} collective-permute-done((bf16[2,3,40,256]{3,2,1,0:T(8,128)(2,1)S(1)}, bf16[2,3,40,256]{3,2,1,0:T(8,128)(2,1)S(1)}, u32[]{:S(2)}, u32[]{:S(2)}) %collective-permute-start.6) | collective-permute-done | bytes 122912 | tf_op jit(solution)/shard_map/ppermute | solution.py:537
  26.4 0.0 collective-permute-done.4.cross_ref
  26.4 0.0 collective-permute-done.5.refs_0_
  26.4 0.3 latent_grads.1
  26.8 0.8 %collective-permute-start.8 = (bf16[2,6,40,128]{3,2,1,0:T(8,128)(2,1)S(1)}, bf16[2,6,40,128]{3,2,1,0:T(8,128)(2,1)S(1)}, u32[]{:S(2)}, u32[]{:S(2)}) collective-permute-start(bf16[2,6,40,128]{3,2,1,0:T(8,128)(2,1)S(1)} %get-tuple-element.68), channel_id=1, source_target_pairs={{0,16},{8,24},{16,0},{24,8},{1,17},{9,25},{17,1},{25,9},{2,18},{10... | collective-permute-start | bytes 368648 | tf_op jit(solution)/shard_map/ppermute | solution.py:520
  27.6 1.6 %encoder_grads.1 = (bf16[2,6,32,768]{3,2,1,0:T(8,128)(2,1)S(1)}, bf16[9,128,128]{2,1,0:T(8,128)(2,1)S(1)}, bf16[9,128,128]{2,1,0:T(8,128)(2,1)S(1)}) custom-call(bf16[2,8,40,256]{3,2,1,0:T(8,128)(2,1)S(1)} %get-tuple-element.61.grad_ref, f32[2,6,40,256]{3,2,1,0:T(8,128)S(1)} %get-tuple-element.62.slope_ref, ...), custom_call_target="tpu_custom_call" | custom-call | flops 830472192 | bytes 3244032 | tf_op jit(solution)/shard_map/encoder_grads/pallas_call | solution.py:50
  29.2 0.1 collective-permute-start.7
  29.3 2.4 %collective-permute-done.8.got_ref = bf16[2,6,40,128]{3,2,1,0:T(8,128)(2,1)S(1)} collective-permute-done((bf16[2,6,40,128]{3,2,1,0:T(8,128)(2,1)S(1)}, bf16[2,6,40,128]{3,2,1,0:T(8,128)(2,1)S(1)}, u32[]{:S(2)}, u32[]{:S(2)}) %collective-permute-start.8) | collective-permute-done | bytes 122912 | tf_op jit(solution)/shard_map/ppermute | solution.py:520
  31.7 0.7 %second_weight_grads.1 = (bf16[8,144,128]{2,1,0:T(8,128)(2,1)S(1)}, bf16[8,144,128]{2,1,0:T(8,128)(2,1)S(1)}) custom-call(bf16[2,8,40,256]{3,2,1,0:T(8,128)(2,1)S(1)} %get-tuple-element.61.grad_ref, bf16[2,6,40,128]{3,2,1,0:T(8,128)(2,1)S(1)} %collective-permute-done.8.got_ref, bf16[256,256]{1,0:T(8,128)(2,1)S(1)} %get-tuple-element.69.act_ref, ...), custom_call_target="tpu_custom_call" | custom-call | flops 301989888 | bytes 1302528 | tf_op jit(solution)/shard_map/second_weight_grads/pallas_call | solution.py:50
  32.4 0.1 collective-permute-start.9
  32.5 1.6 %collective-permute-done.9 = bf16[8,144,128]{2,1,0:T(8,128)(2,1)S(1)} collective-permute-done((bf16[8,144,128]{2,1,0:T(8,128)(2,1)S(1)}, bf16[8,144,128]{2,1,0:T(8,128)(2,1)S(1)}, u32[]{:S(2)}, u32[]{:S(2)}) %collective-permute-start.9) | collective-permute-done | bytes 294944 | tf_op jit(solution)/shard_map/ppermute | solution.py:520
  34.1 0.1 other_band.1
  34.1 0.0 copy-start
  34.2 0.9 %collective-permute-start.10 = (bf16[2,4,144,128]{3,2,1,0:T(8,128)(2,1)S(1)}, bf16[2,4,144,128]{3,2,1,0:T(8,128)(2,1)S(1)}, u32[]{:S(2)}, u32[]{:S(2)}) collective-permute-start(bf16[2,4,144,128]{3,2,1,0:T(8,128)(2,1)S(1)} %other_band.1), channel_id=1, source_target_pairs={{0,4},{4,0},{1,5},{5,1},{2,6},{6,2},{3,7},{7,3},{8,12},{12,8},{9,1... | collective-permute-start | bytes 884744 | tf_op jit(solution)/shard_map/ppermute | solution.py:520
  35.0 8.2 %collective-permute-done.10.refs_4_ = bf16[2,4,144,128]{3,2,1,0:T(8,128)(2,1)S(1)} collective-permute-done((bf16[2,4,144,128]{3,2,1,0:T(8,128)(2,1)S(1)}, bf16[2,4,144,128]{3,2,1,0:T(8,128)(2,1)S(1)}, u32[]{:S(2)}, u32[]{:S(2)}) %collective-permute-start.10) | collective-permute-done | bytes 294944 | tf_op jit(solution)/shard_map/ppermute | solution.py:520
  43.3 0.1 own_band.1
  43.4 1.1 %collective-permute-start.11 = (bf16[2,144,128]{2,1,0:T(8,128)(2,1)S(1)}, bf16[2,144,128]{2,1,0:T(8,128)(2,1)S(1)}, u32[]{:S(2)}, u32[]{:S(2)}) collective-permute-start(bf16[2,144,128]{2,1,0:T(8,128)(2,1)S(1)} %get-tuple-element.74), channel_id=1, source_target_pairs={{0,1},{1,2},{2,3},{3,0},{4,5},{5,6},{6,7},{7,4},{8,9},{9,10},{10,1... | collective-permute-start | bytes 221192 | tf_op jit(solution)/shard_map/ppermute | solution.py:526
  44.4 2.8 %collective-permute-start.12 = (bf16[2,144,128]{2,1,0:T(8,128)(2,1)S(1)}, bf16[2,144,128]{2,1,0:T(8,128)(2,1)S(1)}, u32[]{:S(2)}, u32[]{:S(2)}) collective-permute-start(bf16[2,144,128]{2,1,0:T(8,128)(2,1)S(1)} %get-tuple-element.75), channel_id=1, source_target_pairs={{0,2},{1,3},{2,0},{3,1},{4,6},{5,7},{6,4},{7,5},{8,10},{9,11},{10,... | collective-permute-start | bytes 221192 | tf_op jit(solution)/shard_map/ppermute | solution.py:526
  47.3 0.9 %collective-permute-start.13 = (bf16[2,144,128]{2,1,0:T(8,128)(2,1)S(1)}, bf16[2,144,128]{2,1,0:T(8,128)(2,1)S(1)}, u32[]{:S(2)}, u32[]{:S(2)}) collective-permute-start(bf16[2,144,128]{2,1,0:T(8,128)(2,1)S(1)} %get-tuple-element.76), channel_id=1, source_target_pairs={{0,3},{1,0},{2,1},{3,2},{4,7},{5,4},{6,5},{7,6},{8,11},{9,8},{10,9... | collective-permute-start | bytes 221192 | tf_op jit(solution)/shard_map/ppermute | solution.py:526
  48.2 2.2 %collective-permute-done.11.refs_1_ = bf16[2,144,128]{2,1,0:T(8,128)(2,1)S(1)} collective-permute-done((bf16[2,144,128]{2,1,0:T(8,128)(2,1)S(1)}, bf16[2,144,128]{2,1,0:T(8,128)(2,1)S(1)}, u32[]{:S(2)}, u32[]{:S(2)}) %collective-permute-start.11) | collective-permute-done | bytes 73760 | tf_op jit(solution)/shard_map/ppermute | solution.py:526
  50.4 1.7 %collective-permute-done.12.refs_2_ = bf16[2,144,128]{2,1,0:T(8,128)(2,1)S(1)} collective-permute-done((bf16[2,144,128]{2,1,0:T(8,128)(2,1)S(1)}, bf16[2,144,128]{2,1,0:T(8,128)(2,1)S(1)}, u32[]{:S(2)}, u32[]{:S(2)}) %collective-permute-start.12) | collective-permute-done | bytes 73760 | tf_op jit(solution)/shard_map/ppermute | solution.py:526
  52.1 0.4 collective-permute-done.13.refs_3_
  52.5 0.1 collective-permute-start.16
  52.6 0.9 %collective-permute-start.15 = (bf16[2,144,128]{2,1,0:T(8,128)(2,1)S(1)}, bf16[2,144,128]{2,1,0:T(8,128)(2,1)S(1)}, u32[]{:S(2)}, u32[]{:S(2)}) collective-permute-start(bf16[2,144,128]{2,1,0:T(8,128)(2,1)S(1)} %share.1.mine_ref), channel_id=1, source_target_pairs={{0,8},{8,0},{16,24},{24,16},{1,9},{9,1},{17,25},{25,17},{2,10},{10... | collective-permute-start | bytes 221192 | tf_op jit(solution)/shard_map/ppermute | solution.py:520
  53.5 1.2 %collective-permute-start.14 = (bf16[2,144,128]{2,1,0:T(8,128)(2,1)S(1)}, bf16[2,144,128]{2,1,0:T(8,128)(2,1)S(1)}, u32[]{:S(2)}, u32[]{:S(2)}) collective-permute-start(bf16[2,144,128]{2,1,0:T(8,128)(2,1)S(1)} %share.1.mine_ref), channel_id=1, source_target_pairs={{0,16},{8,24},{16,0},{24,8},{1,17},{9,25},{17,1},{25,9},{2,18},{10... | collective-permute-start | bytes 221192 | tf_op jit(solution)/shard_map/ppermute | solution.py:520
  54.7 1.1 %input_conv.1 = bf16[2,4,32,128]{3,2,1,0:T(8,128)(2,1)} custom-call(bf16[2,6,32,768]{3,2,1,0:T(8,128)(2,1)S(1)} %get-tuple-element.65.moved_ref, bf16[9,128,256]{2,1,0:T(8,128)(2,1)S(1)} %copy-done), custom_call_target="tpu_custom_call" | custom-call | flops 150994944 | bytes 1245184 | tf_op jit(solution)/shard_map/input_conv/pallas_call | solution.py:50
  55.8 0.9 %collective-permute-done.16.both_ref = bf16[2,144,128]{2,1,0:T(8,128)(2,1)S(1)} collective-permute-done((bf16[2,144,128]{2,1,0:T(8,128)(2,1)S(1)}, bf16[2,144,128]{2,1,0:T(8,128)(2,1)S(1)}, u32[]{:S(2)}, u32[]{:S(2)}) %collective-permute-start.16) | collective-permute-done | bytes 73760 | tf_op jit(solution)/shard_map/ppermute | solution.py:520
  56.7 0.0 collective-permute-done.15.core_ref
  56.7 1.6 %collective-permute-done.14.cross_ref = bf16[2,144,128]{2,1,0:T(8,128)(2,1)S(1)} collective-permute-done((bf16[2,144,128]{2,1,0:T(8,128)(2,1)S(1)}, bf16[2,144,128]{2,1,0:T(8,128)(2,1)S(1)}, u32[]{:S(2)}, u32[]{:S(2)}) %collective-permute-start.14) | collective-permute-done | bytes 73760 | tf_op jit(solution)/shard_map/ppermute | solution.py:520
  58.3 0.8 %join_halves.1 = (f32[288,128]{1,0:T(8,128)}, f32[576,128]{1,0:T(8,128)}) custom-call(bf16[2,144,128]{2,1,0:T(8,128)(2,1)S(1)} %share.1.mine_ref, bf16[2,144,128]{2,1,0:T(8,128)(2,1)S(1)} %collective-permute-done.14.cross_ref, bf16[2,144,128]{2,1,0:T(8,128)(2,1)S(1)} %collective-permute-done.15.core_ref, ...), custom_call_target="tpu_custom_call" | custom-call | bytes 737280 | tf_op jit(solution)/shard_map/join_halves/pallas_call | solution.py:50
  (3 shorter events, 0.0 us)
Async XLA Ops:
  1.9 8.7 %collective-permute-start.2 = (bf16[2,4,32,256]{3,2,1,0:T(8,128)(2,1)}, bf16[2,4,32,256]{3,2,1,0:T(8,128)(2,1)S(1)}, u32[]{:S(2)}, u32[]{:S(2)}) collective-permute-start(bf16[2,4,32,256]{3,2,1,0:T(8,128)(2,1)} %first_far.1), channel_id=1, source_target_pairs={{0,16},{8,24},{16,0},{24,8},{1,17},{9,25},{17,1},{25,9},{2,18},{10... | collective-permute-start | bytes 393224 | tf_op jit(solution)/shard_map/ppermute | solution.py:520
  4.9 6.6 %collective-permute-start = (bf16[10,24,128]{2,1,0:T(8,128)(2,1)S(1)}, bf16[10,24,128]{2,1,0:T(8,128)(2,1)S(1)}, u32[]{:S(2)}, u32[]{:S(2)}) collective-permute-start(bf16[10,24,128]{2,1,0:T(8,128)(2,1)S(1)} %get-tuple-element.44), channel_id=1, source_target_pairs={{0,1},{1,2},{2,3},{3,0},{4,5},{5,6},{6,7},{7,4},{8,9},{9,10},{10,1... | collective-permute-start | bytes 184328 | tf_op jit(solution)/shard_map/ppermute | solution.py:526
  6.5 5.0 %collective-permute-start.1 = (bf16[10,24,128]{2,1,0:T(8,128)(2,1)S(1)}, bf16[10,24,128]{2,1,0:T(8,128)(2,1)S(1)}, u32[]{:S(2)}, u32[]{:S(2)}) collective-permute-start(bf16[10,24,128]{2,1,0:T(8,128)(2,1)S(1)} %get-tuple-element.45), channel_id=1, source_target_pairs={{0,3},{1,0},{2,1},{3,2},{4,7},{5,4},{6,5},{7,6},{8,11},{9,8},{10,9... | collective-permute-start | bytes 184328 | tf_op jit(solution)/shard_map/ppermute | solution.py:526
  12.5 1.9 %collective-permute-start.3 = (bf16[4,6,40,256]{3,2,1,0:T(8,128)(2,1)S(1)}, bf16[4,6,40,256]{3,2,1,0:T(8,128)(2,1)S(1)}, u32[]{:S(2)}, u32[]{:S(2)}) collective-permute-start(bf16[4,6,40,256]{3,2,1,0:T(8,128)(2,1)S(1)} %head_conv.3), channel_id=1, source_target_pairs={{0,8},{8,0},{16,24},{24,16},{1,9},{9,1},{17,25},{25,17},{2,10},{10... | collective-permute-start | bytes 1474568 | tf_op jit(solution)/shard_map/ppermute | solution.py:520
  14.7 11.7 %collective-permute-start.4 = (bf16[2,6,40,256]{3,2,1,0:T(8,128)(2,1)S(1)}, bf16[2,6,40,256]{3,2,1,0:T(8,128)(2,1)S(1)}, u32[]{:S(2)}, u32[]{:S(2)}) collective-permute-start(bf16[2,6,40,256]{3,2,1,0:T(8,128)(2,1)S(1)} %get-tuple-element.56), channel_id=1, source_target_pairs={{0,16},{8,24},{16,0},{24,8},{1,17},{9,25},{17,1},{25,9},{2,18},{10... | collective-permute-start | bytes 737288 | tf_op jit(solution)/shard_map/ppermute | solution.py:520
  15.2 11.3 %collective-permute-start.5 = (bf16[2,6,40,256]{3,2,1,0:T(8,128)(2,1)S(1)}, bf16[2,6,40,256]{3,2,1,0:T(8,128)(2,1)S(1)}, u32[]{:S(2)}, u32[]{:S(2)}) collective-permute-start(bf16[2,6,40,256]{3,2,1,0:T(8,128)(2,1)S(1)} %get-tuple-element.57), channel_id=1, source_target_pairs={{0,4},{4,0},{1,5},{5,1},{2,6},{6,2},{3,7},{7,3},{8,12},{12,8},{9,1... | collective-permute-start | bytes 737288 | tf_op jit(solution)/shard_map/ppermute | solution.py:520
  16.8 9.6 %collective-permute-start.6 = (bf16[2,3,40,256]{3,2,1,0:T(8,128)(2,1)S(1)}, bf16[2,3,40,256]{3,2,1,0:T(8,128)(2,1)S(1)}, u32[]{:S(2)}, u32[]{:S(2)}) collective-permute-start(bf16[2,3,40,256]{3,2,1,0:T(8,128)(2,1)S(1)} %get-tuple-element.58), channel_id=1, source_target_pairs={{0,20},{4,16},{8,28},{12,24},{16,4},{20,0},{24,12},{28,8},{1,21},{... | collective-permute-start | bytes 368648 | tf_op jit(solution)/shard_map/ppermute | solution.py:537
  26.8 4.9 %collective-permute-start.8 = (bf16[2,6,40,128]{3,2,1,0:T(8,128)(2,1)S(1)}, bf16[2,6,40,128]{3,2,1,0:T(8,128)(2,1)S(1)}, u32[]{:S(2)}, u32[]{:S(2)}) collective-permute-start(bf16[2,6,40,128]{3,2,1,0:T(8,128)(2,1)S(1)} %get-tuple-element.68), channel_id=1, source_target_pairs={{0,16},{8,24},{16,0},{24,8},{1,17},{9,25},{17,1},{25,9},{2,18},{10... | collective-permute-start | bytes 368648 | tf_op jit(solution)/shard_map/ppermute | solution.py:520
  29.2 3.3 %collective-permute-start.7 = (bf16[9,128,128]{2,1,0:T(8,128)(2,1)S(1)}, bf16[9,128,128]{2,1,0:T(8,128)(2,1)S(1)}, u32[]{:S(2)}, u32[]{:S(2)}) collective-permute-start(bf16[9,128,128]{2,1,0:T(8,128)(2,1)S(1)} %get-tuple-element.67), channel_id=1, source_target_pairs={{0,8},{8,0},{16,24},{24,16},{1,9},{9,1},{17,25},{25,17},{2,10},{10... | collective-permute-start | bytes 884744 | tf_op jit(solution)/shard_map/ppermute | solution.py:520
  32.4 1.6 %collective-permute-start.9 = (bf16[8,144,128]{2,1,0:T(8,128)(2,1)S(1)}, bf16[8,144,128]{2,1,0:T(8,128)(2,1)S(1)}, u32[]{:S(2)}, u32[]{:S(2)}) collective-permute-start(bf16[8,144,128]{2,1,0:T(8,128)(2,1)S(1)} %get-tuple-element.72), channel_id=1, source_target_pairs={{0,8},{8,0},{16,24},{24,16},{1,9},{9,1},{17,25},{25,17},{2,10},{10... | collective-permute-start | bytes 884744 | tf_op jit(solution)/shard_map/ppermute | solution.py:520
  34.1 20.6 %copy-start = (bf16[9,128,256]{2,1,0:T(8,128)(2,1)S(1)}, bf16[9,128,256]{2,1,0:T(8,128)(2,1)}, u32[]{:S(2)}) copy-start(bf16[9,128,256]{2,1,0:T(8,128)(2,1)} %w_first_ref.1) | copy-start | bytes 1769476
  34.2 9.1 %collective-permute-start.10 = (bf16[2,4,144,128]{3,2,1,0:T(8,128)(2,1)S(1)}, bf16[2,4,144,128]{3,2,1,0:T(8,128)(2,1)S(1)}, u32[]{:S(2)}, u32[]{:S(2)}) collective-permute-start(bf16[2,4,144,128]{3,2,1,0:T(8,128)(2,1)S(1)} %other_band.1), channel_id=1, source_target_pairs={{0,4},{4,0},{1,5},{5,1},{2,6},{6,2},{3,7},{7,3},{8,12},{12,8},{9,1... | collective-permute-start | bytes 884744 | tf_op jit(solution)/shard_map/ppermute | solution.py:520
  43.4 7.0 %collective-permute-start.11 = (bf16[2,144,128]{2,1,0:T(8,128)(2,1)S(1)}, bf16[2,144,128]{2,1,0:T(8,128)(2,1)S(1)}, u32[]{:S(2)}, u32[]{:S(2)}) collective-permute-start(bf16[2,144,128]{2,1,0:T(8,128)(2,1)S(1)} %get-tuple-element.74), channel_id=1, source_target_pairs={{0,1},{1,2},{2,3},{3,0},{4,5},{5,6},{6,7},{7,4},{8,9},{9,10},{10,1... | collective-permute-start | bytes 221192 | tf_op jit(solution)/shard_map/ppermute | solution.py:526
  44.4 7.6 %collective-permute-start.12 = (bf16[2,144,128]{2,1,0:T(8,128)(2,1)S(1)}, bf16[2,144,128]{2,1,0:T(8,128)(2,1)S(1)}, u32[]{:S(2)}, u32[]{:S(2)}) collective-permute-start(bf16[2,144,128]{2,1,0:T(8,128)(2,1)S(1)} %get-tuple-element.75), channel_id=1, source_target_pairs={{0,2},{1,3},{2,0},{3,1},{4,6},{5,7},{6,4},{7,5},{8,10},{9,11},{10,... | collective-permute-start | bytes 221192 | tf_op jit(solution)/shard_map/ppermute | solution.py:526
  47.3 5.2 %collective-permute-start.13 = (bf16[2,144,128]{2,1,0:T(8,128)(2,1)S(1)}, bf16[2,144,128]{2,1,0:T(8,128)(2,1)S(1)}, u32[]{:S(2)}, u32[]{:S(2)}) collective-permute-start(bf16[2,144,128]{2,1,0:T(8,128)(2,1)S(1)} %get-tuple-element.76), channel_id=1, source_target_pairs={{0,3},{1,0},{2,1},{3,2},{4,7},{5,4},{6,5},{7,6},{8,11},{9,8},{10,9... | collective-permute-start | bytes 221192 | tf_op jit(solution)/shard_map/ppermute | solution.py:526
  52.5 4.2 %collective-permute-start.16 = (bf16[2,144,128]{2,1,0:T(8,128)(2,1)S(1)}, bf16[2,144,128]{2,1,0:T(8,128)(2,1)S(1)}, u32[]{:S(2)}, u32[]{:S(2)}) collective-permute-start(bf16[2,144,128]{2,1,0:T(8,128)(2,1)S(1)} %share.1.mine_ref), channel_id=1, source_target_pairs={{0,24},{8,16},{16,8},{24,0},{1,25},{9,17},{17,9},{25,1},{2,26},{10... | collective-permute-start | bytes 221192 | tf_op jit(solution)/shard_map/ppermute | solution.py:520
  52.6 4.1 %collective-permute-start.15 = (bf16[2,144,128]{2,1,0:T(8,128)(2,1)S(1)}, bf16[2,144,128]{2,1,0:T(8,128)(2,1)S(1)}, u32[]{:S(2)}, u32[]{:S(2)}) collective-permute-start(bf16[2,144,128]{2,1,0:T(8,128)(2,1)S(1)} %share.1.mine_ref), channel_id=1, source_target_pairs={{0,8},{8,0},{16,24},{24,16},{1,9},{9,1},{17,25},{25,17},{2,10},{10... | collective-permute-start | bytes 221192 | tf_op jit(solution)/shard_map/ppermute | solution.py:520
  53.5 4.8 %collective-permute-start.14 = (bf16[2,144,128]{2,1,0:T(8,128)(2,1)S(1)}, bf16[2,144,128]{2,1,0:T(8,128)(2,1)S(1)}, u32[]{:S(2)}, u32[]{:S(2)}) collective-permute-start(bf16[2,144,128]{2,1,0:T(8,128)(2,1)S(1)} %share.1.mine_ref), channel_id=1, source_target_pairs={{0,16},{8,24},{16,0},{24,8},{1,17},{9,25},{17,1},{25,9},{2,18},{10... | collective-permute-start | bytes 221192 | tf_op jit(solution)/shard_map/ppermute | solution.py:520

commit v3 on v2

--- a/solution.py
+++ b/solution.py
@@ -55,11 +55,12 @@
         out_specs=[pl.BlockSpec(memory_space=pltpu.VMEM)] * len(out_shape),
         scratch_shapes=list(scratch),
         compiler_params=pltpu.CompilerParams(vmem_limit_bytes=VMEM_BYTES),
-        cost_estimate=pl.CostEstimate(flops=flops, bytes_accessed=touched, transcendentals=0),
+        cost_estimate=pl.CostEstimate(flops=1, bytes_accessed=1, transcendentals=0),
     )(*arrays)
 
 
-def pack_kernel(grads_far, second_far, first_far, right_ref, left_ref, grads_near, second_near, first_near, edges, edges_wide, packed, sems):
+def pack_kernel(with_tile, grads_far, second_far, first_far, input_far, right_ref, left_ref, *refs):
+    grads_near, second_near, first_near, edges, edges_wide, packed, sems, tile_sems = refs[-8:]
     heads, batch, height, breadth, _ = grads_far.shape
     samples = second_far.shape[0]
     rows = 6 * height
@@ -70,6 +71,13 @@
             source = far.at[:, :, :, columns, :] if j == 0 else far.at[:, :, columns, :]
             copies.append(pltpu.make_async_copy(source, near.at[side], sems.at[side, j]))
             copies[-1].start()
+    tile_copies = []
+    if with_tile:
+        for j, far in enumerate((second_far, second_far, first_far, first_far, input_far)):
+            source = far.at[:, :, :, pl.ds(LANES * (j % 2), LANES)] if j < 4 else far
+            target = refs[0].at[j] if j < 2 else refs[1].at[j - 2]
+            tile_copies.append(pltpu.make_async_copy(source, target, tile_sems.at[j]))
+            tile_copies[-1].start()
     for copy in copies:
         copy.wait()
     for side, out_ref in ((0, right_ref), (1, left_ref)):
@@ -102,17 +110,20 @@
                         half, pl.ds((j * samples + s) * height * 8 + inner, height, stride=8), :
                     ]
         out_ref[...] = packed[...].astype(BF).reshape(out_ref.shape)
-
-
-def pack(head_grads, pre_second, pre_first):
+    for copy in tile_copies:
+        copy.wait()
+
+
+def pack(head_grads, pre_second, pre_first, encoder_input, with_tile):
     heads, batch, height, _, _ = head_grads.shape
     samples = pre_second.shape[0]
     shape = jax.ShapeDtypeStruct((batch + samples, 6 * height, LANES), BF)
+    tiles = [jax.ShapeDtypeStruct((count,) + encoder_input.shape, BF) for count in (2, 3)]
     return run(
         "pack_columns",
-        pack_kernel,
-        [shape, shape],
-        [head_grads, pre_second, pre_first],
+        functools.partial(pack_kernel, with_tile),
+        [shape, shape] + tiles * with_tile,
+        [head_grads, pre_second, pre_first, encoder_input],
         [
             pltpu.VMEM((2, heads, batch, height, 16, LANES), BF),
             pltpu.VMEM((2, samples, height, 16, 2 * LANES), BF),
@@ -121,6 +132,7 @@
             pltpu.VMEM((2, 2 * samples * height * 8, LANES), F32),
             pltpu.VMEM(((batch + samples) * 6 * height, LANES), F32),
             pltpu.SemaphoreType.DMA((2, 3)),
+            pltpu.SemaphoreType.DMA((5,)),
         ],
         far=True,
     )
@@ -141,7 +153,7 @@
     return run("stage", stage_kernel, shapes, list(arrays), [pltpu.SemaphoreType.DMA((len(arrays),))], far=True, flops=1 << 30)
 
 
-def heads_kernel(other_core, grads_ref, low_ref, high_ref, weights_ref, out_ref, wide, shifted, total):
+def heads_kernel(other_core, other_chip, samples, grads_ref, low_ref, high_ref, weights_ref, out_ref, wide, shifted, total):
     heads, batch, height, breadth, _ = grads_ref.shape
     slots, _, kept, depth = out_ref.shape
     pitch = kept + 16
@@ -149,8 +161,8 @@
     core, chip = core_and_chip()
     core = 1 - core if other_core else core
     for slot in range(slots):
-        group = chip if slot < slots // 2 else 1 - chip
-        b = (2 * group + core) * (slots // 2) + slot % (slots // 2)
+        group = 1 - chip if other_chip != (slot >= samples) else chip
+        b = (2 * group + core) * samples + slot % samples
         low = low_ref[b].astype(F32)
         high = high_ref[b].astype(F32)
         for r in range(height):
@@ -179,18 +191,21 @@
             total[:, :height] = part
         else:
             total[:, 1 + u : 1 + u + height] += part
-    out_ref[...] = total[...].astype(BF)
-
-
-def head_conv(other_core, head_grads, low, high, head_weights, samples):
+    if out_ref.shape[1] == height + 2:
+        out_ref[...] = total[...].astype(BF)
+    else:
+        out_ref[...] = total[:, pl.ds(1 - lax.axis_index("lat"), height + 1)].astype(BF)
+
+
+def head_conv(other_core, other_chip, head_grads, low, high, head_weights, slots, rows):
+    samples = head_grads.shape[1] // lax.axis_size("lead")
     heads, batch, height, breadth, _ = head_grads.shape
     depth = head_weights.shape[2]
     kept = breadth + 2 * EDGE
-    slots = 2 * samples
     return run(
         "head_conv",
-        functools.partial(heads_kernel, other_core),
-        [jax.ShapeDtypeStruct((slots, height + 2, kept, depth), BF)],
+        functools.partial(heads_kernel, other_core, other_chip, samples),
+        [jax.ShapeDtypeStruct((slots, rows, kept, depth), BF)],
         [head_grads, low, high, head_weights],
         [
             pltpu.VMEM((heads, slots * height * (kept + 16), LANES), F32),
@@ -253,31 +268,37 @@
     )
 
 
-def spread_kernel(mine_ref, got_ref, second_ref, first_ref, own_ref, cross_ref, *strips):
-    samples = own_ref.shape[0]
+def goes_down(way, ways):
+    return 1 - lax.axis_index("lat") if ways == 1 else 1 - way
+
+
+def cross_kernel(mine_ref, got_ref, cross_ref, *strips):
+    height = mine_ref.shape[1] - 2
+    cross_ref[...] = (mine_ref[...].astype(F32) + got_ref[...].astype(F32)).astype(BF)
+    for way, corner_ref in enumerate(strips):
+        corner_ref[...] = cross_ref[:, pl.ds((height - 1) * goes_down(way, len(strips)), 3)]
+
+
+def own_kernel(mine_ref, got_ref, second_ref, first_ref, own_ref, *strips):
     height = second_ref.shape[1]
-    total = mine_ref[...].astype(F32) + got_ref[...].astype(F32)
-    total = total.astype(BF)
-    own_ref[...] = total[:samples]
-    cross_ref[...] = total[samples:]
-    for way in range(len(strips) // 2):
-        line_ref, corner_ref = strips[2 * way], strips[2 * way + 1]
-        down = 1 - lax.axis_index("lat") if len(strips) == 2 else 1 - way
+    own_ref[...] = (mine_ref[...].astype(F32) + got_ref[...].astype(F32)).astype(BF)
+    for way, line_ref in enumerate(strips):
+        down = goes_down(way, len(strips))
         line_ref[:, 0:3] = own_ref[:, pl.ds((height - 1) * down, 3)]
-        corner_ref[...] = cross_ref[:, pl.ds((height - 1) * down, 3)]
         line_ref[:, 3:5] = second_ref[:, pl.ds((height - 2) * down, 2)]
         line_ref[:, 5:6] = first_ref[:, pl.ds((height - 1) * down, 1)]
 
 
-def spread(mine, got, second, first, ways):
-    slots, rows, kept, depth = mine.shape
-    samples = slots // 2
-    whole = jax.ShapeDtypeStruct((samples, rows, kept, depth), BF)
-    strips = [
-        jax.ShapeDtypeStruct((samples, 6, kept, depth), BF),
-        jax.ShapeDtypeStruct((samples, 3, kept, depth), BF),
-    ] * ways
-    return run("core_sum", spread_kernel, [whole, whole] + strips, [mine, got, second, first])
+def spread_cross(mine, got, ways):
+    samples, _, kept, depth = mine.shape
+    strip = jax.ShapeDtypeStruct((samples, 3, kept, depth), BF)
+    return run("core_sum_cross", cross_kernel, [jax.ShapeDtypeStruct(mine.shape, BF)] + [strip] * ways, [mine, got])
+
+
+def spread_own(mine, got, second, first, ways):
+    samples, _, kept, depth = mine.shape
+    strip = jax.ShapeDtypeStruct((samples, 6, kept, depth), BF)
+    return run("core_sum_own", own_kernel, [jax.ShapeDtypeStruct(mine.shape, BF)] + [strip] * ways, [mine, got, second, first])
 
 
 def latent_kernel(ways, bands, own_ref, cross_ref, *refs):
@@ -453,22 +474,24 @@
 
 
 def other_band_kernel(*refs):
-    terms, out_ref = refs[:-1], refs[-1]
     band = 1 - lax.rem(lax.axis_index("lat"), 2)
-    for layer in range(2):
-        parts = [t[band].astype(F32) for t in terms[layer * len(terms) // 2 : (layer + 1) * len(terms) // 2]]
-        out_ref[layer] = sum(parts[1:], parts[0]).astype(BF)
+    parts = [t[band].astype(F32) for t in refs[:-1]]
+    refs[-1][...] = sum(parts[1:], parts[0]).astype(BF)
+
+
+def partner(index, step, count):
+    return index ^ step if count & (count - 1) == 0 else (index + step) % count
 
 
 def own_band_kernel(*refs):
     columns = refs[0].shape[1]
-    terms, came, outs = refs[: -columns - 1], refs[-columns - 1], refs[-columns:]
+    terms, came, outs = refs[: -columns - 2], refs[-columns - 2 : -columns], refs[-columns:]
     band, lon = lax.rem(lax.axis_index("lat"), 2), lax.axis_index("lon")
     for step in range(columns):
-        block = lax.rem(lon + step, columns)
+        block = partner(lon, step, columns)
         for layer in range(2):
             parts = [t[band, block].astype(F32) for t in terms[layer * len(terms) // 2 : (layer + 1) * len(terms) // 2]]
-            outs[step][layer] = sum(parts, came[layer, block].astype(F32)).astype(BF)
+            outs[step][layer] = sum(parts, came[layer][block].astype(F32)).astype(BF)
 
 
 def sum_kernel(*refs):
@@ -501,18 +524,22 @@
     )[0]
 
 
-def join_kernel(mine_ref, cross_ref, core_ref, both_ref, first_ref, second_ref):
-    core, chip = core_and_chip()
+def chips_kernel(mine_ref, cross_ref, out_ref):
+    _, chip = core_and_chip()
+    out_ref[0] = (mine_ref[0].astype(F32) + cross_ref[0].astype(F32)).astype(BF)
+    out_ref[1] = jnp.where(chip == 0, mine_ref[1], cross_ref[1])
+    out_ref[2] = jnp.where(chip == 0, cross_ref[1], mine_ref[1])
+
+
+def cores_kernel(mine_ref, other_ref, first_ref, second_ref):
+    core, _ = core_and_chip()
     rows = mine_ref.shape[1]
-    here = mine_ref[0].astype(F32) + cross_ref[0].astype(F32)
-    there = core_ref[0].astype(F32) + both_ref[0].astype(F32)
-    first_ref[pl.ds(0, rows, stride=2), :] = jnp.where(core == 0, here, there)
-    first_ref[pl.ds(1, rows, stride=2), :] = jnp.where(core == 0, there, here)
-    mine, cross, other, both = (ref[1].astype(F32) for ref in (mine_ref, cross_ref, core_ref, both_ref))
+    mine, other = (ref[...].astype(F32) for ref in (mine_ref, other_ref))
     for part in range(2):
-        near, far = jnp.where(core == part, mine, other), jnp.where(core == part, cross, both)
-        second_ref[pl.ds(2 * rows * part, rows, stride=2), :] = jnp.where(chip == 0, near, far)
-        second_ref[pl.ds(2 * rows * part + 1, rows, stride=2), :] = jnp.where(chip == 0, far, near)
+        value = jnp.where(core == part, mine, other)
+        first_ref[pl.ds(part, rows, stride=2), :] = value[0]
+        second_ref[pl.ds(2 * rows * part, rows, stride=2), :] = value[1]
+        second_ref[pl.ds(2 * rows * part + 1, rows, stride=2), :] = value[2]
 
 
 def swap(array, axis, flip):
@@ -537,13 +564,330 @@
     return lax.ppermute(array, ("lead", "lat"), pairs)
 
 
-def per_device(head_grads, head_weights, encoder_input, pre_first, pre_second, w_first, w_second):
+def other_band(terms, columns):
+    shape = (columns, terms[0].size // LANES // columns // 2, LANES)
+    return run("other_band", other_band_kernel, [jax.ShapeDtypeStruct(shape, BF)], [t.reshape(2, *shape) for t in terms])[0]
+
+
+def pairwise(terms, bands):
+    lat = lax.axis_index("lat")
+    total = sum(t.reshape(-1, LANES).astype(F32) for t in terms).astype(BF)
+    left = bands
+    while left > 2:
+        left //= 2
+        bit = (lat // left) % 2
+        halves = total.reshape(2, -1, LANES)
+        send = lax.dynamic_index_in_dim(halves, 1 - bit, 0, keepdims=False)
+        keep = lax.dynamic_index_in_dim(halves, bit, 0, keepdims=False)
+        total = (keep.astype(F32) + swap(send, "lat", left).astype(F32)).astype(BF)
+    return total
+
+
+def near_kernel(second_ref, first_ref, low_ref, high_ref, slope_second, slope_first, halo_ref, wide, cells):
+    samples, height, breadth, depth = second_ref.shape
+    kept = breadth + 2 * EDGE
+    batch = low_ref.shape[0] - samples
+    for ref, width, first_cell, slope_ref in ((second_ref, 2, 0, slope_second), (first_ref, 1, 4 * height, slope_first)):
+        wide[...] = jnp.zeros(wide.shape, F32)
+        for s in range(samples):
+            for r in range(height):
+                at = (s * height + r) * kept + EDGE
+                for half in range(2):
+                    wide[half, at : at + breadth, :] = ref[s, r, :, half * LANES : (half + 1) * LANES].astype(F32)
+            for side, packed_ref in ((0, low_ref), (1, high_ref)):
+                packed = packed_ref[batch + s].astype(F32)
+                for col in range(width):
+                    for half in range(2):
+                        here = ((col if width == 2 else 2) * 2 + half) * height
+                        value = packed[here : here + height]
+                        at = s * height * kept + EDGE + col + (breadth if side else -width)
+                        wide[half, pl.ds(at, height, stride=kept), :] = value
+                        at = first_cell + (side * width + col) * height
+                        cells[s, at : at + height, half * LANES : (half + 1) * LANES] = value
+        value = jnp.concatenate([wide[0], wide[1]], axis=1)
+        slope_ref[...] = gelu_slope(value).reshape(slope_ref.shape)
+    halo_ref[...] = cells[...].astype(BF)
+
+
+def near_parts(pre_second, pre_first, low, high):
+    samples, height, breadth, depth = pre_second.shape
+    kept = breadth + 2 * EDGE
+    slope = jax.ShapeDtypeStruct((samples, height, kept, depth), F32)
+    return run(
+        "near_parts",
+        near_kernel,
+        [slope, slope, jax.ShapeDtypeStruct((samples, 6 * height, depth), BF)],
+        [pre_second, pre_first, low, high],
+        [pltpu.VMEM((2, samples * height * kept, LANES), F32), pltpu.VMEM((samples, 6 * height, depth), F32)],
+    )
+
+
+def far_kernel(first_ref, input_ref, tile_second, tile_ref, slope_second, slope_first, act_out, input_out, wide, act, cells):
+    samples, height, breadth, depth = first_ref.shape
+    kept = breadth + 2 * EDGE
+    lat = lax.axis_index("lat")
+    for source_ref, slope_ref in ((tile_second, slope_second), (tile_ref, slope_first)):
+        wide[...] = jnp.zeros(wide.shape, F32)
+        for s in range(samples):
+            for half in range(2):
+                for r in range(height):
+                    at = (s * height + r) * kept + EDGE
+                    wide[half, at : at + breadth, :] = source_ref[half, s, r].astype(F32)
+        value = jnp.concatenate([wide[0], wide[1]], axis=1)
+        slope_ref[...] = gelu_slope(value).reshape(slope_ref.shape)
+    own, other = pl.ds(height * lat, height), pl.ds(height * (1 - lat), height)
+    act[:, own] = gelu_value(first_ref[...].astype(F32))
+    act[:, other] = jnp.concatenate([gelu_value(tile_ref[half].astype(F32)) for half in range(2)], axis=-1)
+    cells[:, own] = input_ref[...].astype(F32)
+    cells[:, other] = tile_ref[2].astype(F32)
+    act_out[...] = act[...].reshape(act_out.shape[1], depth).T.astype(BF)
+    input_out[...] = cells[...].reshape(input_out.shape[1], input_out.shape[0]).T.astype(BF)
+
+
+def far_parts(pre_first, encoder_input, tile_second, tile):
+    samples, height, breadth, depth = pre_first.shape
+    channels = encoder_input.shape[3]
+    kept = breadth + 2 * EDGE
+    cells = 2 * samples * height * breadth
+    slope = jax.ShapeDtypeStruct((samples, height, kept, depth), F32)
+    return run(
+        "far_parts",
+        far_kernel,
+        [slope, slope, jax.ShapeDtypeStruct((depth, cells), BF), jax.ShapeDtypeStruct((channels, cells), BF)],
+        [pre_first, encoder_input, tile_second, tile],
+        [
+            pltpu.VMEM((2, samples * height * kept, LANES), F32),
+            pltpu.VMEM((samples, 2 * height, breadth, depth), F32),
+            pltpu.VMEM((samples, 2 * height, breadth, channels), F32),
+        ],
+    )
+
+
+def put_slopes(slope, near_ref, far_ref, halo_ref, width, first_cell):
+    samples, height, kept, _ = near_ref.shape
+    lat = lax.axis_index("lat")
+    other = pl.ds(height * (1 - lat), height)
+    slope[:, pl.ds(height * lat, height)] = near_ref[...]
+    slope[:, other] = far_ref[...]
+    for s in range(samples):
+        beside = gelu_slope(halo_ref[s].astype(F32))
+        for side in range(2):
+            for col in range(width):
+                here = first_cell + (side * width + col) * height
+                at = kept - EDGE + col if side else EDGE - width + col
+                slope[s, other, at, :] = beside[here : here + height]
+
+
+def globe_kernel(own_ref, cross_ref, line_ref, corner_ref, near_ref, far_ref, halo_ref, cat_ref, moved_ref, latent, slope, wide):
+    samples, rows, kept, depth = own_ref.shape
+    height = rows - 1
+    tall = 2 * height
+    breadth = kept - 2 * EDGE
+    lat = lax.axis_index("lat")
+    own = 8 + EDGE
+    latent[...] = jnp.zeros(latent.shape, F32)
+    latent[:, pl.ds((height - 1) * lat, rows)] = own_ref[...].astype(F32) + cross_ref[...].astype(F32)
+    latent[:, pl.ds((height - 1) * (1 - lat), rows)] += line_ref[...].astype(F32) + corner_ref[...].astype(F32)
+    put_slopes(slope, near_ref, far_ref, halo_ref, 2, 0)
+    wide[:, :, 8 : 8 + kept, :] = (latent[...] * slope[...]).astype(BF).astype(F32)
+    for v in STEPS:
+        lanes = slice((v + 1) * depth, (v + 2) * depth)
+        cat_ref[:, 1 : 1 + tall, :, lanes] = wide[:, :, 8 - v : 8 - v + kept + 8, :].astype(BF)
+        moved_ref[v + 1, :, 1 : 1 + tall] = wide[:, :, own - v : own - v + breadth, :].astype(BF)
+    for row in (0, tall + 1):
+        cat_ref[:, row] = jnp.zeros(cat_ref.shape[:1] + cat_ref.shape[2:], BF)
+        moved_ref[:, :, row] = jnp.zeros(moved_ref.shape[:2] + moved_ref.shape[3:], BF)
+
+
+def globe(own, cross, line, angle, near, far, halo):
+    samples, rows, kept, depth = own.shape
+    tall, breadth = 2 * (rows - 1), kept - 2 * EDGE
+    return run(
+        "latent_grads",
+        globe_kernel,
+        [
+            jax.ShapeDtypeStruct((samples, tall + 2, kept + 8, 3 * depth), BF),
+            jax.ShapeDtypeStruct((3, samples, tall + 2, breadth, depth), BF),
+        ],
+        [own, cross, line, angle, near, far, halo],
+        [
+            pltpu.VMEM((samples, tall, kept, depth), F32),
+            pltpu.VMEM((samples, tall, kept, depth), F32),
+            pltpu.VMEM((samples, tall, kept + 24, depth), F32),
+        ],
+    )
+
+
+def band_rows(norm_factor, left_ref, moved_ref, mine_ref, other_ref):
+    channels, cells = left_ref.shape
+    _, samples, padded, breadth, depth = moved_ref.shape
+    tall = padded - 2
+    lat = lax.axis_index("lat")
+    core, _ = core_and_chip()
+    half = channels // 2
+
+    def put(left, u, v, start, size):
+        right = moved_ref[v + 1, :, pl.ds(1 - u, tall)].reshape(cells, depth)
+        part = dot_plain(left, right) * norm_factor
+        lower, upper = part[:, :LANES], part[:, LANES:]
+        here = pl.ds(pl.multiple_of(start, half), size)
+        mine_ref[here, :] = jnp.where(core == 0, lower, upper).astype(BF)
+        other_ref[here, :] = jnp.where(core == 0, upper, lower).astype(BF)
+
+    for j in range(4):
+        (u0, v0), (u1, v1) = (divmod(k, 3) for k in (j, 5 + j))
+        put(left_ref[...], u0 - 1 + lat * (u1 - u0), v0 - 1 + lat * (v1 - v0), lat * half + j * channels, channels)
+    put(left_ref[pl.ds(pl.multiple_of(lat * half, half), half), :], 0, 0, (1 - lat) * 4 * channels, half)
+
+
+def second_band_kernel(norm_factor, moved_ref, act_ref, mine_ref, other_ref):
+    band_rows(norm_factor, act_ref, moved_ref, mine_ref, other_ref)
+
+
+def first_band_kernel(norm_factor, cat_ref, near_ref, far_ref, halo_ref, input_ref, weights_ref, moved_ref, mine_ref, other_ref, slope, wide):
+    samples, padded, broad, triple = cat_ref.shape
+    tall, kept, depth = padded - 2, broad - 8, triple // 3
+    height = tall // 2
+    breadth = kept - 2 * EDGE
+    lat = lax.axis_index("lat")
+    own = 8 + EDGE
+    put_slopes(slope, near_ref, far_ref, halo_ref, 1, 4 * height)
+    linear = None
+    for u in STEPS:
+        weights = jnp.concatenate([weights_ref[3 * (u + 1) + (v + 1)] for v in STEPS], axis=1)
+        part = dot_last(cat_ref[:, 1 - u : 1 - u + tall].reshape(samples * tall * broad, triple), weights)
+        linear = part if linear is None else linear + part
+    linear = linear.reshape(samples, tall, broad, depth)[:, :, :kept]
+    wide[:, :, 8 : 8 + kept, :] = (linear * slope[...]).astype(BF).astype(F32)
+    for v in STEPS:
+        moved_ref[v + 1, :, 1 : 1 + tall] = wide[:, :, own - v : own - v + breadth, :].astype(BF)
+    for row in (0, tall + 1):
+        moved_ref[:, :, row] = jnp.zeros(moved_ref.shape[:2] + moved_ref.shape[3:], BF)
+    band_rows(norm_factor, input_ref, moved_ref, mine_ref, other_ref)
+
+
+def second_band(norm_factor, moved, act):
+    half = jax.ShapeDtypeStruct((9 * act.shape[0] // 2, LANES), BF)
+    return run("second_weight_grads", functools.partial(second_band_kernel, norm_factor), [half, half], [moved, act])
+
+
+def first_band(norm_factor, cat, near, far, halo, cells_in, w_second):
+    samples, padded, broad, triple = cat.shape
+    tall, kept, depth = padded - 2, broad - 8, triple // 3
+    breadth = kept - 2 * EDGE
+    half = jax.ShapeDtypeStruct((9 * cells_in.shape[0] // 2, LANES), BF)
+    return run(
+        "encoder_grads",
+        functools.partial(first_band_kernel, norm_factor),
+        [jax.ShapeDtypeStruct((3, samples, padded, breadth, depth), BF), half, half],
+        [cat, near, far, halo, cells_in, w_second],
+        [pltpu.VMEM((samples, tall, kept, depth), F32), pltpu.VMEM((samples, tall, kept + 16, depth), F32)],
+    )
+
+
+def input_band_kernel(moved_ref, w_first_ref, out_ref):
+    samples, height, breadth, channels = out_ref.shape
+    depth = moved_ref.shape[4]
+    lat = lax.axis_index("lat")
+    total = None
+    for u in STEPS:
+        weights = jnp.concatenate([w_first_ref[3 * (u + 1) + (v + 1)] for v in STEPS], axis=1)
+        left = [moved_ref[v + 1, :, pl.ds(height * lat + 1 - u, height)].reshape(-1, depth) for v in STEPS]
+        part = dot_last(jnp.concatenate(left, axis=1), weights)
+        total = part if total is None else total + part
+    out_ref[...] = total.astype(BF).reshape(out_ref.shape)
+
+
+def blocks_kernel(first_mine, first_got, second_mine, second_got, *outs):
+    lon = lax.axis_index("lon")
+    rows = first_mine.shape[1]
+    for step, out_ref in enumerate(outs):
+        block = partner(lon, step, len(outs))
+        out_ref[:rows] = (first_mine[block].astype(F32) + first_got[block].astype(F32)).astype(BF)
+        out_ref[rows:] = (second_mine[block].astype(F32) + second_got[block].astype(F32)).astype(BF)
+
+
+def halves_kernel(mine_ref, other_ref, first_ref, second_ref):
+    core, _ = core_and_chip()
+    mine, other = mine_ref[...].astype(F32), other_ref[...].astype(F32)
+    rows = mine.shape[0] // 3
+    for part in range(2):
+        value = jnp.where(core == part, mine, other)
+        first_ref[pl.ds(part, rows, stride=2), :] = value[:rows]
+        second_ref[pl.ds(part, 2 * rows, stride=2), :] = value[rows:]
+
+
+def to_partner(array, step):
+    count = lax.axis_size("lon")
+    return lax.ppermute(array, "lon", [(partner(i, step, count), i) for i in range(count)])
+
+
+def two_bands(head_grads, head_weights, encoder_input, pre_first, pre_second, w_first, w_second, norm_factor):
+    samples, height, breadth, _ = encoder_input.shape
+    columns = lax.axis_size("lon")
+    to_right, to_left, tile_second, tile = pack(head_grads, pre_second, pre_first, encoder_input, True)
+    low = around(to_right, "lon", 1)
+    high = around(to_left, "lon", -1)
+    tile_second = swap(tile_second, "lat", 1)
+    head_grads, head_weights, w_second, pre_second, pre_first, encoder_input = stage(
+        head_grads, head_weights, w_second, pre_second, pre_first, encoder_input
+    )
+    tile = swap(tile, "lat", 1)
+    low, high, tile_second, tile = lax.optimization_barrier((low, high, tile_second, tile))
+    heads_of = functools.partial(
+        head_conv,
+        head_grads=head_grads,
+        low=low,
+        high=high,
+        head_weights=head_weights,
+        slots=2 * samples,
+        rows=height + 1,
+    )
+    got = swap(heads_of(True, False), "lead", 1)
+    near_second, near_first, halo = near_parts(pre_second, pre_first, low, high)
+    mine = heads_of(False, False)
+    got, halo = lax.optimization_barrier((got, halo))
+    halo = swap(halo, "lat", 1)
+    part_shape = jax.ShapeDtypeStruct((samples,) + mine.shape[1:], BF)
+    own, cross = run("core_sum", core_sum_kernel, [part_shape, part_shape], [mine, got])
+    cross_got, line_got, corner_got = swap(cross, "lead", 2), swap(own, "lat", 1), corner(cross, None)
+    far_second, far_first, act, cells_in = far_parts(pre_first, encoder_input, tile_second, tile)
+
+    cat, moved = globe(own, cross_got, line_got, corner_got, near_second, far_second, halo)
+    second_mine, second_other = second_band(norm_factor, moved, act)
+    second_got = swap(second_other, "lead", 1)
+    moved_first, first_mine, first_other = first_band(norm_factor, cat, near_first, far_first, halo, cells_in, w_second)
+    first_got = swap(first_other, "lead", 1)
+    input_grad = run(
+        "input_conv", input_band_kernel, [jax.ShapeDtypeStruct(encoder_input.shape, BF)], [moved_first, w_first]
+    )[0]
+
+    blocks = [t.reshape(columns, -1, LANES) for t in (first_mine, first_got, second_mine, second_got)]
+    rows = blocks[0].shape[1]
+    share_shape = jax.ShapeDtypeStruct((3 * rows, LANES), BF)
+    shares = run("blocks", blocks_kernel, [share_shape] * columns, blocks)
+    parts = [to_partner(shares[step], step) for step in range(1, columns)]
+    share = run("share", sum_kernel, [share_shape], [shares[0], *parts])[0]
+    both = run("chips", sum_kernel, [share_shape], [share, swap(share, "lead", 2)])[0]
+    result_first, result_second = run(
+        "cores",
+        halves_kernel,
+        [jax.ShapeDtypeStruct((2 * rows, LANES), F32), jax.ShapeDtypeStruct((4 * rows, LANES), F32)],
+        [both, swap(both, "lead", 1)],
+    )
+    return input_grad, result_first.reshape(-1), result_second.reshape(-1)
+
+
+def core_sum_kernel(mine_ref, got_ref, own_ref, cross_ref):
+    samples = own_ref.shape[0]
+    for ref, part in ((own_ref, slice(0, samples)), (cross_ref, slice(samples, 2 * samples))):
+        ref[...] = (mine_ref[part].astype(F32) + got_ref[part].astype(F32)).astype(BF)
+
+
+def general(head_grads, head_weights, encoder_input, pre_first, pre_second, w_first, w_second, norm_factor):
     samples, height, breadth, _ = encoder_input.shape
     bands, columns = lax.axis_size("lat"), lax.axis_size("lon")
-    cells_total = samples * lax.axis_size("lead") * height * bands * breadth * columns
-    norm_factor = 1.0 / math.sqrt(cells_total)
-
-    to_right, to_left = pack(head_grads, pre_second, pre_first)
+    to_right, to_left = pack(head_grads, pre_second, pre_first, encoder_input, False)
     to_right, to_left, to_cross = lax.optimization_barrier((to_right, to_left, pre_first))
     low = around(to_right, "lon", 1)
     high = around(to_left, "lon", -1)
@@ -553,20 +897,18 @@
     )
     low, high, act_got = lax.optimization_barrier((low, high, act_got))
 
-    theirs = head_conv(True, head_grads, low, high, head_weights, samples)
-    got = swap(theirs, "lead", 1)
-    mine = head_conv(False, head_grads, low, high, head_weights, samples)
+    steps = [1, -1]
+    heads_of = functools.partial(head_conv, head_grads=head_grads, high=high, head_weights=head_weights, slots=samples, rows=height + 2)
+    got_cross = swap(heads_of(True, True, low=low), "lead", 1)
+    got_own = swap(heads_of(True, False, low=low), "lead", 1)
+    cross, *angles = spread_cross(heads_of(False, True, low=low), got_cross, len(steps))
+    low_later, cross, *angles = lax.optimization_barrier((low, cross, *angles))
+    cross = swap(cross, "lead", 2)
+    angles = [corner(angle, step) for angle, step in zip(angles, steps)]
     second, first, slope_second, slope_first, act, cells_in = saved(pre_second, pre_first, encoder_input, low, high)
-
-    steps = [None] if bands == 2 else [1, -1]
-    spreads = spread(mine, got, second, first, len(steps))
-    own = spreads[0]
-    cross = swap(spreads[1], "lead", 2)
-    strips = []
-    for way, step in enumerate(steps):
-        line, angle = spreads[2 + 2 * way], spreads[3 + 2 * way]
-        strips.append(swap(line, "lat", 1) if step is None else around(line, "lat", step, False))
-        strips.append(corner(angle, step))
+    own, *lines = spread_own(heads_of(False, False, low=low_later), got_own, second, first, len(steps))
+    lines = [swap(line, "lat", 1) if step is None else around(line, "lat", step, False) for line, step in zip(lines, steps)]
+    strips = [strip for pair in zip(lines, angles) for strip in pair]
 
     grad, away, slope = latent_grads(len(steps), bands, own, cross, strips, slope_second, slope_first)
     grad_got = swap(away, "lead", 2)
@@ -576,37 +918,33 @@
     second_mine, second_other = second_grads(norm_factor, bands * columns, grad, grad_got, act, act_got)
     second_got = swap(second_other, "lead", 1)
 
-    terms = [[first_mine, first_got], [second_mine, second_got]]
-    left = bands
-    if left > 2:
-        lat = lax.axis_index("lat")
-        summed = jnp.stack([a.reshape(-1, LANES).astype(F32) + b.reshape(-1, LANES).astype(F32) for a, b in terms])
-        summed = summed.astype(BF)
-        while left > 2:
-            left //= 2
-            bit = (lat // left) % 2
-            parts = summed.reshape(2, 2, -1, LANES)
-            send = lax.dynamic_index_in_dim(parts, 1 - bit, 1, keepdims=False)
-            keep = lax.dynamic_index_in_dim(parts, bit, 1, keepdims=False)
-            summed = (keep.astype(F32) + swap(send, "lat", left).astype(F32)).astype(BF)
-        terms = [[summed[0]], [summed[1]]]
-    blocks = [t.reshape(2, columns, -1, LANES) for ts in terms for t in ts]
-    shape = blocks[0].shape
-    rows = shape[2]
-    sent = run("other_band", other_band_kernel, [jax.ShapeDtypeStruct(shape, BF)], blocks)[0]
-    came = swap(sent, "lat", 1)
+    first_terms = [pairwise([first_mine, first_got], bands)]
+    second_terms = [pairwise([second_mine, second_got], bands)]
+    first_came = swap(other_band(first_terms, columns), "lat", 1)
+    second_came = swap(other_band(second_terms, columns), "lat", 1)
+    blocks = [t.reshape(2, columns, -1, LANES) for t in first_terms + second_terms]
+    rows = blocks[0].shape[2]
     share_shape = jax.ShapeDtypeStruct((2, rows, LANES), BF)
-    shares = run("own_band", own_band_kernel, [share_shape] * columns, blocks + [came])
-    parts = [around(shares[step], "lon", step) for step in range(1, columns)]
+    shares = run("own_band", own_band_kernel, [share_shape] * columns, blocks + [first_came, second_came])
+    parts = [to_partner(shares[step], step) for step in range(1, columns)]
     share = run("share", sum_kernel, [share_shape], [shares[0], *parts])[0]
-    peers = [swap(share, "lead", flip) for flip in (2, 1, 3)]
+    both = run("chips", chips_kernel, [jax.ShapeDtypeStruct((3, rows, LANES), BF)], [share, swap(share, "lead", 2)])[0]
     result_first, result_second = run(
-        "join_halves",
-        join_kernel,
+        "cores",
+        cores_kernel,
         [jax.ShapeDtypeStruct((2 * rows, LANES), F32), jax.ShapeDtypeStruct((4 * rows, LANES), F32)],
-        [share, *peers],
+        [both, swap(both, "lead", 1)],
     )
     return input_grad, result_first.reshape(-1), result_second.reshape(-1)
+
+
+def per_device(head_grads, head_weights, encoder_input, pre_first, pre_second, w_first, w_second):
+    samples, height, breadth, channels = encoder_input.shape
+    bands, columns = lax.axis_size("lat"), lax.axis_size("lon")
+    cells_total = samples * lax.axis_size("lead") * height * bands * breadth * columns
+    norm_factor = 1.0 / math.sqrt(cells_total)
+    plan = two_bands if bands == 2 and 9 * channels // (bands * columns) % 16 == 0 else general
+    return plan(head_grads, head_weights, encoder_input, pre_first, pre_second, w_first, w_second, norm_factor)
 
 
 def solution(mesh):

time: 59.3 us -> 54.7 us (0.922)
  waiting for transfers between devices: 28.2 us -> 22.3 us
  Pallas kernels: 10.8 us -> 12.3 us
    ppermute x0 -> x3, waiting for transfers between devices: none -> 8.91 us  [to_partner(): lax.ppermute(array, 'lon', [(partner(i, step, count), i) for i in range(c...]
    ppermute x1, waiting for transfers between devices: 8.19 us -> 0.01 us  [corner(): return lax.ppermute(array, ('lead', 'lat'), pairs)]
    ppermute x5 -> x2, starting transfers between devices: 8.61 us -> 4.03 us  [around(): return lax.ppermute(array, axis, pairs)]
    ppermute x0 -> x3, starting transfers between devices: none -> 4.47 us  [to_partner(): lax.ppermute(array, 'lon', [(partner(i, step, count), i) for i in range(c...]
    ppermute x5 -> x2, waiting for transfers between devices: 5.01 us -> 0.98 us  [around(): return lax.ppermute(array, axis, pairs)]
    ppermute x11 -> x10, waiting for transfers between devices: 15 us -> 12.4 us  [swap(): return lax.ppermute(array, axis, [(i, i ^ flip) for i in range(count)])]
    pallas_call x15, Pallas kernels: 10.8 us -> 12.3 us  [run(): pl.pallas_call(kernel, name=name, out_shape=out_shape, in_specs=specs, ou...]
    ppermute x11 -> x10, starting transfers between devices: 9.26 us -> 9.33 us  [swap(): return lax.ppermute(array, axis, [(i, i ^ flip) for i in range(count)])]
  transfers between devices with their start and end apart: 17 -> 16, of which waited for: 11 -> 10; matrix products, arithmetic and copies ran while one was open for 0% -> 0% of each run, Pallas kernels for 12% -> 13%
where the time goes in v3:
time: 54.7 us; the launch traced here: 54.6 us
  waiting for transfers between devices  22.3 us (41%)
  starting transfers between devices  19.3 us (35%)
  Pallas kernels  12.3 us (22%)
  between operations  0.75 us (1%)
    ppermute x10, waiting for transfers between devices, swap(): return lax.ppermute(array, axis, [(i, i ^ flip) for i in range(count)])  12.4 us
    pallas_call x15, Pallas kernels, run(): pl.pallas_call(kernel, name=name, out_shape=out_shape, in_specs=specs, ou...  12.3 us
    ppermute x10, starting transfers between devices, swap(): return lax.ppermute(array, axis, [(i, i ^ flip) for i in range(count)])  9.33 us
    ppermute x3, waiting for transfers between devices, to_partner(): lax.ppermute(array, 'lon', [(partner(i, step, count), i) for i in range(c...  8.91 us
    ppermute x3, starting transfers between devices, to_partner(): lax.ppermute(array, 'lon', [(partner(i, step, count), i) for i in range(c...  4.47 us
    ppermute x2, starting transfers between devices, around(): return lax.ppermute(array, axis, pairs)  4.03 us
    ppermute x1, starting transfers between devices, corner(): return lax.ppermute(array, ('lead', 'lat'), pairs)  1.44 us
  transfers between devices with their start and end apart: 16, of which 10 were waited for; matrix products, arithmetic and copies ran while one was open for 0% of the time, Pallas kernels for 13%

profile of v3, /device:TPU:0, one launch (start us, length us, event | category | flops | bytes accessed | tf_op | source)
XLA Modules:
  0.0 54.6 jit_solution(1539146001344301598)
XLA Ops:
  0.6 1.4 %pack_columns.1 = (bf16[10,24,128]{2,1,0:T(8,128)(2,1)S(1)}, bf16[10,24,128]{2,1,0:T(8,128)(2,1)S(1)}, bf16[2,2,4,32,128]{4,3,2,1,0:T(8,128)(2,1)S(1)}, bf16[3,2,4,32,128]{4,3,2,1,0:T(8,128)(2,1)S(1)}) custom-call(bf16[2,8,4,32,128]{4,3,2,1,0:T(8,128)(2,1)} %grads_far.1, bf16[2,4,32,256]{3,2,1,0:T(8,128)(2,1)} %second_far.1, ...), custom_call_target="tpu_custom_call" | custom-call | flops 1 | bytes 1 | tf_op jit(solution)/shard_map/pack_columns/pallas_call | solution.py:50
  2.0 3.0 %collective-permute-start.3 = (bf16[3,2,4,32,128]{4,3,2,1,0:T(8,128)(2,1)S(1)}, bf16[3,2,4,32,128]{4,3,2,1,0:T(8,128)(2,1)S(1)}, u32[]{:S(2)}, u32[]{:S(2)}) collective-permute-start(bf16[3,2,4,32,128]{4,3,2,1,0:T(8,128)(2,1)S(1)} %get-tuple-element.45), channel_id=1, source_target_pairs={{0,4},{4,0},{1,5},{5,1},{2,6},{6,2},{3,7},{7,3},{8,12},{12,8},{9,1... | collective-permute-start | bytes 589832 | tf_op jit(solution)/shard_map/ppermute | solution.py:547
  5.1 0.1 collective-permute-start.2
  5.2 2.0 %collective-permute-start = (bf16[10,24,128]{2,1,0:T(8,128)(2,1)S(1)}, bf16[10,24,128]{2,1,0:T(8,128)(2,1)S(1)}, u32[]{:S(2)}, u32[]{:S(2)}) collective-permute-start(bf16[10,24,128]{2,1,0:T(8,128)(2,1)S(1)} %get-tuple-element.42), channel_id=1, source_target_pairs={{0,1},{1,2},{2,3},{3,0},{4,5},{5,6},{6,7},{7,4},{8,9},{9,10},{10,1... | collective-permute-start | bytes 184328 | tf_op jit(solution)/shard_map/ppermute | solution.py:553
  7.2 2.0 %collective-permute-start.1 = (bf16[10,24,128]{2,1,0:T(8,128)(2,1)S(1)}, bf16[10,24,128]{2,1,0:T(8,128)(2,1)S(1)}, u32[]{:S(2)}, u32[]{:S(2)}) collective-permute-start(bf16[10,24,128]{2,1,0:T(8,128)(2,1)S(1)} %get-tuple-element.43), channel_id=1, source_target_pairs={{0,3},{1,0},{2,1},{3,2},{4,7},{5,4},{6,5},{7,6},{8,11},{9,8},{10,9... | collective-permute-start | bytes 184328 | tf_op jit(solution)/shard_map/ppermute | solution.py:553
  9.2 1.9 %stage.1 = (bf16[2,8,4,32,128]{4,3,2,1,0:T(8,128)(2,1)S(1)}, bf16[2,9,256,128]{3,2,1,0:T(8,128)(2,1)S(1)}, bf16[9,256,256]{2,1,0:T(8,128)(2,1)S(1)}, bf16[2,4,32...) custom-call(bf16[2,8,4,32,128]{4,3,2,1,0:T(8,128)(2,1)} %grads_far.1, ...), custom_call_target="tpu_custom_call" | custom-call | flops 1 | bytes 1 | tf_op jit(solution)/shard_map/stage/pallas_call | solution.py:50
  11.1 0.9 %collective-permute-done.low_ref = bf16[10,24,128]{2,1,0:T(8,128)(2,1)S(1)} collective-permute-done((bf16[10,24,128]{2,1,0:T(8,128)(2,1)S(1)}, bf16[10,24,128]{2,1,0:T(8,128)(2,1)S(1)}, u32[]{:S(2)}, u32[]{:S(2)}) %collective-permute-start) | collective-permute-done | bytes 61472 | tf_op jit(solution)/shard_map/ppermute | solution.py:553
  12.0 0.0 collective-permute-done.1.high_ref
  12.0 0.7 %collective-permute-done.2.tile_second = bf16[2,2,4,32,128]{4,3,2,1,0:T(8,128)(2,1)S(1)} collective-permute-done((bf16[2,2,4,32,128]{4,3,2,1,0:T(8,128)(2,1)S(1)}, bf16[2,2,4,32,128]{4,3,2,1,0:T(8,128)(2,1)S(1)}, u32[]{:S(2)}, u32[]{:S(2)}) %collective-permute-start.2) | collective-permute-done | bytes 131104 | tf_op jit(solution)/shard_map/ppermute | solution.py:547
  12.8 0.0 collective-permute-done.3.tile_ref
  12.8 1.1 %head_conv.3 = bf16[4,5,40,256]{3,2,1,0:T(8,128)(2,1)S(1)} custom-call(bf16[2,8,4,32,128]{4,3,2,1,0:T(8,128)(2,1)S(1)} %get-tuple-element.41.grads_ref, bf16[10,24,128]{2,1,0:T(8,128)(2,1)S(1)} %collective-permute-done.low_ref, bf16[10,24,128]{2,1,0:T(8,128)(2,1)S(1)} %collective-permute-done.1.high_ref, ...), custom_call_target="tpu_custom_call" | custom-call | flops 1 | bytes 1 | tf_op jit(solution)/shard_map/head_conv/pallas_call | solution.py:50
  13.9 0.1 collective-permute-start.4
  14.0 1.1 %head_conv.2.mine_ref = bf16[4,5,40,256]{3,2,1,0:T(8,128)(2,1)S(1)} custom-call(bf16[2,8,4,32,128]{4,3,2,1,0:T(8,128)(2,1)S(1)} %get-tuple-element.41.grads_ref, bf16[10,24,128]{2,1,0:T(8,128)(2,1)S(1)} %collective-permute-done.low_ref, bf16[10,24,128]{2,1,0:T(8,128)(2,1)S(1)} %collective-permute-done.1.high_ref, ...), custom_call_target="tpu_custom_call" | custom-call | flops 1 | bytes 1 | tf_op jit(solution)/shard_map/head_conv/pallas_call | solution.py:50
  15.2 0.4 near_parts.1
  15.6 0.2 collective-permute-done.4.got_ref
  15.8 0.1 core_sum.1
  15.8 1.8 %collective-permute-start.6 = (bf16[2,5,40,256]{3,2,1,0:T(8,128)(2,1)S(1)}, bf16[2,5,40,256]{3,2,1,0:T(8,128)(2,1)S(1)}, u32[]{:S(2)}, u32[]{:S(2)}) collective-permute-start(bf16[2,5,40,256]{3,2,1,0:T(8,128)(2,1)S(1)} %get-tuple-element.53.own_ref), channel_id=1, source_target_pairs={{0,4},{4,0},{1,5},{5,1},{2,6},{6,2},{3,7},{7,3},{8,12},{12,8},{9,1... | collective-permute-start | bytes 614408 | tf_op jit(solution)/shard_map/ppermute | solution.py:547
  17.6 1.4 %collective-permute-start.7 = (bf16[2,5,40,256]{3,2,1,0:T(8,128)(2,1)S(1)}, bf16[2,5,40,256]{3,2,1,0:T(8,128)(2,1)S(1)}, u32[]{:S(2)}, u32[]{:S(2)}) collective-permute-start(bf16[2,5,40,256]{3,2,1,0:T(8,128)(2,1)S(1)} %get-tuple-element.54), channel_id=1, source_target_pairs={{0,20},{4,16},{8,28},{12,24},{16,4},{20,0},{24,12},{28,8},{1,21},{... | collective-permute-start | bytes 614408 | tf_op jit(solution)/shard_map/ppermute | solution.py:564
  19.1 0.3 collective-permute-start.5
  19.4 1.7 %collective-permute-start.8 = (bf16[2,24,256]{2,1,0:T(8,128)(2,1)S(1)}, bf16[2,24,256]{2,1,0:T(8,128)(2,1)S(1)}, u32[]{:S(2)}, u32[]{:S(2)}) collective-permute-start(bf16[2,24,256]{2,1,0:T(8,128)(2,1)S(1)} %get-tuple-element.60), channel_id=1, source_target_pairs={{0,4},{4,0},{1,5},{5,1},{2,6},{6,2},{3,7},{7,3},{8,12},{12,8},{9,1... | collective-permute-start | bytes 73736 | tf_op jit(solution)/shard_map/ppermute | solution.py:547
  21.1 0.7 %far_parts.1 = (f32[2,4,40,256]{3,2,1,0:T(8,128)S(1)}, f32[2,4,40,256]{3,2,1,0:T(8,128)S(1)}, bf16[256,512]{1,0:T(8,128)(2,1)S(1)}, bf16[128,512]{1,0:T(8,128)(2,1)S(1)}) custom-call(bf16[2,4,32,256]{3,2,1,0:T(8,128)(2,1)S(1)} %get-tuple-element.50.first_ref, bf16[2,4,32,128]{3,2,1,0:T(8,128)(2,1)S(1)} %get-tuple-element.56.input_ref, ...), custom_call_target="tpu_custom_call" | custom-call | flops 1 | bytes 1 | tf_op jit(solution)/shard_map/far_parts/pallas_call | solution.py:50
  21.8 6.3 %collective-permute-done.8.halo_ref = bf16[2,24,256]{2,1,0:T(8,128)(2,1)S(1)} collective-permute-done((bf16[2,24,256]{2,1,0:T(8,128)(2,1)S(1)}, bf16[2,24,256]{2,1,0:T(8,128)(2,1)S(1)}, u32[]{:S(2)}, u32[]{:S(2)}) %collective-permute-start.8) | collective-permute-done | bytes 24608 | tf_op jit(solution)/shard_map/ppermute | solution.py:547
  28.2 0.0 collective-permute-done.6.line_ref
  28.2 0.0 collective-permute-done.7.corner_ref
  28.2 0.8 %collective-permute-done.5.cross_ref = bf16[2,5,40,256]{3,2,1,0:T(8,128)(2,1)S(1)} collective-permute-done((bf16[2,5,40,256]{3,2,1,0:T(8,128)(2,1)S(1)}, bf16[2,5,40,256]{3,2,1,0:T(8,128)(2,1)S(1)}, u32[]{:S(2)}, u32[]{:S(2)}) %collective-permute-start.5) | collective-permute-done | bytes 204832 | tf_op jit(solution)/shard_map/ppermute | solution.py:547
  28.9 1.0 %latent_grads.1 = (bf16[2,10,48,768]{3,2,1,0:T(8,128)(2,1)S(1)}, bf16[3,2,10,32,256]{4,3,2,1,0:T(8,128)(2,1)S(1)}) custom-call(bf16[2,5,40,256]{3,2,1,0:T(8,128)(2,1)S(1)} %get-tuple-element.53.own_ref, bf16[2,5,40,256]{3,2,1,0:T(8,128)(2,1)S(1)} %collective-permute-done.5.cross_ref, bf16[2,5,40,256]{3,2,1,0:T(8,128)(2,1)S(1)} %collective-permute-done.6.line_ref, ...), custom_call_target="tpu_custom_call" | custom-call | flops 1 | bytes 1 | tf_op jit(solution)/shard_map/latent_grads/pallas_call | solution.py:50
  29.9 0.5 second_weight_grads.1
  30.4 0.1 collective-permute-start.10
  30.5 2.0 %encoder_grads.1 = (bf16[3,2,10,32,256]{4,3,2,1,0:T(8,128)(2,1)S(1)}, bf16[576,128]{1,0:T(8,128)(2,1)S(1)}, bf16[576,128]{1,0:T(8,128)(2,1)S(1)}) custom-call(bf16[2,10,48,768]{3,2,1,0:T(8,128)(2,1)S(1)} %get-tuple-element.61.cat_ref, f32[2,4,40,256]{3,2,1,0:T(8,128)S(1)} %get-tuple-element.62.near_ref, f32[2,4,40,256]{3,2,1,0:T(8,128)S(1)} %get-tuple-element.63.far_ref, ...), custom_call_target="tpu_custom_call" | custom-call | flops 1 | bytes 1 | tf_op jit(solution)/shard_map/encoder_grads/pallas_call | solution.py:50
  32.4 0.0 copy-start
  32.4 0.6 %collective-permute-start.9 = (bf16[576,128]{1,0:T(8,128)(2,1)S(1)}, bf16[576,128]{1,0:T(8,128)(2,1)S(1)}, u32[]{:S(2)}, u32[]{:S(2)}) collective-permute-start(bf16[576,128]{1,0:T(8,128)(2,1)S(1)} %get-tuple-element.68), channel_id=1, source_target_pairs={{0,8},{8,0},{16,24},{24,16},{1,9},{9,1},{17,25},{25,17},{2,10},{10... | collective-permute-start | bytes 442376 | tf_op jit(solution)/shard_map/ppermute | solution.py:547
  33.0 1.0 %collective-permute-done.9 = bf16[576,128]{1,0:T(8,128)(2,1)S(1)} collective-permute-done((bf16[576,128]{1,0:T(8,128)(2,1)S(1)}, bf16[576,128]{1,0:T(8,128)(2,1)S(1)}, u32[]{:S(2)}, u32[]{:S(2)}) %collective-permute-start.9) | collective-permute-done | bytes 147488 | tf_op jit(solution)/shard_map/ppermute | solution.py:547
  34.0 0.0 collective-permute-done.10
  34.0 0.1 blocks.1
  34.1 1.8 %collective-permute-start.11 = (bf16[432,128]{1,0:T(8,128)(2,1)S(1)}, bf16[432,128]{1,0:T(8,128)(2,1)S(1)}, u32[]{:S(2)}, u32[]{:S(2)}) collective-permute-start(bf16[432,128]{1,0:T(8,128)(2,1)S(1)} %get-tuple-element.74), channel_id=1, source_target_pairs={{1,0},{0,1},{3,2},{2,3},{5,4},{4,5},{7,6},{6,7},{9,8},{8,9},{11,10... | collective-permute-start | bytes 331784 | tf_op jit(solution)/shard_map/ppermute | solution.py:822
  35.9 2.6 %collective-permute-start.12 = (bf16[432,128]{1,0:T(8,128)(2,1)S(1)}, bf16[432,128]{1,0:T(8,128)(2,1)S(1)}, u32[]{:S(2)}, u32[]{:S(2)}) collective-permute-start(bf16[432,128]{1,0:T(8,128)(2,1)S(1)} %get-tuple-element.75), channel_id=1, source_target_pairs={{2,0},{3,1},{0,2},{1,3},{6,4},{7,5},{4,6},{5,7},{10,8},{11,9},{8,1... | collective-permute-start | bytes 331784 | tf_op jit(solution)/shard_map/ppermute | solution.py:822
  38.5 0.1 collective-permute-start.13
  38.6 0.9 %collective-permute-done.11.refs_1_ = bf16[432,128]{1,0:T(8,128)(2,1)S(1)} collective-permute-done((bf16[432,128]{1,0:T(8,128)(2,1)S(1)}, bf16[432,128]{1,0:T(8,128)(2,1)S(1)}, u32[]{:S(2)}, u32[]{:S(2)}) %collective-permute-start.11) | collective-permute-done | bytes 110624 | tf_op jit(solution)/shard_map/ppermute | solution.py:822
  39.5 8.0 %collective-permute-done.12.refs_2_ = bf16[432,128]{1,0:T(8,128)(2,1)S(1)} collective-permute-done((bf16[432,128]{1,0:T(8,128)(2,1)S(1)}, bf16[432,128]{1,0:T(8,128)(2,1)S(1)}, u32[]{:S(2)}, u32[]{:S(2)}) %collective-permute-start.12) | collective-permute-done | bytes 110624 | tf_op jit(solution)/shard_map/ppermute | solution.py:822
  47.5 0.0 collective-permute-done.13.refs_3_
  47.5 0.1 share.1.refs_0_
  47.6 1.6 %collective-permute-start.14 = (bf16[432,128]{1,0:T(8,128)(2,1)S(1)}, bf16[432,128]{1,0:T(8,128)(2,1)S(1)}, u32[]{:S(2)}, u32[]{:S(2)}) collective-permute-start(bf16[432,128]{1,0:T(8,128)(2,1)S(1)} %share.1.refs_0_), channel_id=1, source_target_pairs={{0,16},{8,24},{16,0},{24,8},{1,17},{9,25},{17,1},{25,9},{2,18},{10... | collective-permute-start | bytes 331784 | tf_op jit(solution)/shard_map/ppermute | solution.py:547
  49.2 3.2 %collective-permute-done.14.refs_1_ = bf16[432,128]{1,0:T(8,128)(2,1)S(1)} collective-permute-done((bf16[432,128]{1,0:T(8,128)(2,1)S(1)}, bf16[432,128]{1,0:T(8,128)(2,1)S(1)}, u32[]{:S(2)}, u32[]{:S(2)}) %collective-permute-start.14) | collective-permute-done | bytes 110624 | tf_op jit(solution)/shard_map/ppermute | solution.py:547
  52.4 0.1 collective-permute-start.15
  52.5 0.0 copy-done
  52.5 1.1 %input_conv.1 = bf16[2,4,32,128]{3,2,1,0:T(8,128)(2,1)} custom-call(bf16[3,2,10,32,256]{4,3,2,1,0:T(8,128)(2,1)S(1)} %get-tuple-element.66.moved_ref, bf16[9,128,256]{2,1,0:T(8,128)(2,1)S(1)} %copy-done), custom_call_target="tpu_custom_call" | custom-call | flops 1 | bytes 1 | tf_op jit(solution)/shard_map/input_conv/pallas_call | solution.py:50
  53.6 0.2 collective-permute-done.15.other_ref
  53.8 0.8 %cores.1 = (f32[288,128]{1,0:T(8,128)}, f32[576,128]{1,0:T(8,128)}) custom-call(bf16[432,128]{1,0:T(8,128)(2,1)S(1)} %chips.1.mine_ref, bf16[432,128]{1,0:T(8,128)(2,1)S(1)} %collective-permute-done.15.other_ref), custom_call_target="tpu_custom_call" | custom-call | flops 1 | bytes 1 | tf_op jit(solution)/shard_map/cores/pallas_call | solution.py:50
  (1 shorter events, 0.0 us)
Async XLA Ops:
  2.0 10.7 %collective-permute-start.3 = (bf16[3,2,4,32,128]{4,3,2,1,0:T(8,128)(2,1)S(1)}, bf16[3,2,4,32,128]{4,3,2,1,0:T(8,128)(2,1)S(1)}, u32[]{:S(2)}, u32[]{:S(2)}) collective-permute-start(bf16[3,2,4,32,128]{4,3,2,1,0:T(8,128)(2,1)S(1)} %get-tuple-element.45), channel_id=1, source_target_pairs={{0,4},{4,0},{1,5},{5,1},{2,6},{6,2},{3,7},{7,3},{8,12},{12,8},{9,1... | collective-permute-start | bytes 589832 | tf_op jit(solution)/shard_map/ppermute | solution.py:547
  5.1 7.7 %collective-permute-start.2 = (bf16[2,2,4,32,128]{4,3,2,1,0:T(8,128)(2,1)S(1)}, bf16[2,2,4,32,128]{4,3,2,1,0:T(8,128)(2,1)S(1)}, u32[]{:S(2)}, u32[]{:S(2)}) collective-permute-start(bf16[2,2,4,32,128]{4,3,2,1,0:T(8,128)(2,1)S(1)} %get-tuple-element.44), channel_id=1, source_target_pairs={{0,4},{4,0},{1,5},{5,1},{2,6},{6,2},{3,7},{7,3},{8,12},{12,8},{9,1... | collective-permute-start | bytes 393224 | tf_op jit(solution)/shard_map/ppermute | solution.py:547
  5.2 6.8 %collective-permute-start = (bf16[10,24,128]{2,1,0:T(8,128)(2,1)S(1)}, bf16[10,24,128]{2,1,0:T(8,128)(2,1)S(1)}, u32[]{:S(2)}, u32[]{:S(2)}) collective-permute-start(bf16[10,24,128]{2,1,0:T(8,128)(2,1)S(1)} %get-tuple-element.42), channel_id=1, source_target_pairs={{0,1},{1,2},{2,3},{3,0},{4,5},{5,6},{6,7},{7,4},{8,9},{9,10},{10,1... | collective-permute-start | bytes 184328 | tf_op jit(solution)/shard_map/ppermute | solution.py:553
  7.2 4.9 %collective-permute-start.1 = (bf16[10,24,128]{2,1,0:T(8,128)(2,1)S(1)}, bf16[10,24,128]{2,1,0:T(8,128)(2,1)S(1)}, u32[]{:S(2)}, u32[]{:S(2)}) collective-permute-start(bf16[10,24,128]{2,1,0:T(8,128)(2,1)S(1)} %get-tuple-element.43), channel_id=1, source_target_pairs={{0,3},{1,0},{2,1},{3,2},{4,7},{5,4},{6,5},{7,6},{8,11},{9,8},{10,9... | collective-permute-start | bytes 184328 | tf_op jit(solution)/shard_map/ppermute | solution.py:553
  13.9 1.8 %collective-permute-start.4 = (bf16[4,5,40,256]{3,2,1,0:T(8,128)(2,1)S(1)}, bf16[4,5,40,256]{3,2,1,0:T(8,128)(2,1)S(1)}, u32[]{:S(2)}, u32[]{:S(2)}) collective-permute-start(bf16[4,5,40,256]{3,2,1,0:T(8,128)(2,1)S(1)} %head_conv.3), channel_id=1, source_target_pairs={{0,8},{8,0},{16,24},{24,16},{1,9},{9,1},{17,25},{25,17},{2,10},{10... | collective-permute-start | bytes 1228808 | tf_op jit(solution)/shard_map/ppermute | solution.py:547
  15.8 12.3 %collective-permute-start.6 = (bf16[2,5,40,256]{3,2,1,0:T(8,128)(2,1)S(1)}, bf16[2,5,40,256]{3,2,1,0:T(8,128)(2,1)S(1)}, u32[]{:S(2)}, u32[]{:S(2)}) collective-permute-start(bf16[2,5,40,256]{3,2,1,0:T(8,128)(2,1)S(1)} %get-tuple-element.53.own_ref), channel_id=1, source_target_pairs={{0,4},{4,0},{1,5},{5,1},{2,6},{6,2},{3,7},{7,3},{8,12},{12,8},{9,1... | collective-permute-start | bytes 614408 | tf_op jit(solution)/shard_map/ppermute | solution.py:547
  17.6 10.5 %collective-permute-start.7 = (bf16[2,5,40,256]{3,2,1,0:T(8,128)(2,1)S(1)}, bf16[2,5,40,256]{3,2,1,0:T(8,128)(2,1)S(1)}, u32[]{:S(2)}, u32[]{:S(2)}) collective-permute-start(bf16[2,5,40,256]{3,2,1,0:T(8,128)(2,1)S(1)} %get-tuple-element.54), channel_id=1, source_target_pairs={{0,20},{4,16},{8,28},{12,24},{16,4},{20,0},{24,12},{28,8},{1,21},{... | collective-permute-start | bytes 614408 | tf_op jit(solution)/shard_map/ppermute | solution.py:564
  19.1 9.8 %collective-permute-start.5 = (bf16[2,5,40,256]{3,2,1,0:T(8,128)(2,1)S(1)}, bf16[2,5,40,256]{3,2,1,0:T(8,128)(2,1)S(1)}, u32[]{:S(2)}, u32[]{:S(2)}) collective-permute-start(bf16[2,5,40,256]{3,2,1,0:T(8,128)(2,1)S(1)} %get-tuple-element.54), channel_id=1, source_target_pairs={{0,16},{8,24},{16,0},{24,8},{1,17},{9,25},{17,1},{25,9},{2,18},{10... | collective-permute-start | bytes 614408 | tf_op jit(solution)/shard_map/ppermute | solution.py:547
  19.4 8.8 %collective-permute-start.8 = (bf16[2,24,256]{2,1,0:T(8,128)(2,1)S(1)}, bf16[2,24,256]{2,1,0:T(8,128)(2,1)S(1)}, u32[]{:S(2)}, u32[]{:S(2)}) collective-permute-start(bf16[2,24,256]{2,1,0:T(8,128)(2,1)S(1)} %get-tuple-element.60), channel_id=1, source_target_pairs={{0,4},{4,0},{1,5},{5,1},{2,6},{6,2},{3,7},{7,3},{8,12},{12,8},{9,1... | collective-permute-start | bytes 73736 | tf_op jit(solution)/shard_map/ppermute | solution.py:547
  30.4 3.6 %collective-permute-start.10 = (bf16[1152,128]{1,0:T(8,128)(2,1)S(1)}, bf16[1152,128]{1,0:T(8,128)(2,1)S(1)}, u32[]{:S(2)}, u32[]{:S(2)}) collective-permute-start(bf16[1152,128]{1,0:T(8,128)(2,1)S(1)} %get-tuple-element.72), channel_id=1, source_target_pairs={{0,8},{8,0},{16,24},{24,16},{1,9},{9,1},{17,25},{25,17},{2,10},{10... | collective-permute-start | bytes 884744 | tf_op jit(solution)/shard_map/ppermute | solution.py:547
  32.4 20.1 %copy-start = (bf16[9,128,256]{2,1,0:T(8,128)(2,1)S(1)}, bf16[9,128,256]{2,1,0:T(8,128)(2,1)}, u32[]{:S(2)}) copy-start(bf16[9,128,256]{2,1,0:T(8,128)(2,1)} %w_first_ref.1) | copy-start | bytes 1769476
  32.4 1.6 %collective-permute-start.9 = (bf16[576,128]{1,0:T(8,128)(2,1)S(1)}, bf16[576,128]{1,0:T(8,128)(2,1)S(1)}, u32[]{:S(2)}, u32[]{:S(2)}) collective-permute-start(bf16[576,128]{1,0:T(8,128)(2,1)S(1)} %get-tuple-element.68), channel_id=1, source_target_pairs={{0,8},{8,0},{16,24},{24,16},{1,9},{9,1},{17,25},{25,17},{2,10},{10... | collective-permute-start | bytes 442376 | tf_op jit(solution)/shard_map/ppermute | solution.py:547
  34.1 5.4 %collective-permute-start.11 = (bf16[432,128]{1,0:T(8,128)(2,1)S(1)}, bf16[432,128]{1,0:T(8,128)(2,1)S(1)}, u32[]{:S(2)}, u32[]{:S(2)}) collective-permute-start(bf16[432,128]{1,0:T(8,128)(2,1)S(1)} %get-tuple-element.74), channel_id=1, source_target_pairs={{1,0},{0,1},{3,2},{2,3},{5,4},{4,5},{7,6},{6,7},{9,8},{8,9},{11,10... | collective-permute-start | bytes 331784 | tf_op jit(solution)/shard_map/ppermute | solution.py:822
  35.9 11.6 %collective-permute-start.12 = (bf16[432,128]{1,0:T(8,128)(2,1)S(1)}, bf16[432,128]{1,0:T(8,128)(2,1)S(1)}, u32[]{:S(2)}, u32[]{:S(2)}) collective-permute-start(bf16[432,128]{1,0:T(8,128)(2,1)S(1)} %get-tuple-element.75), channel_id=1, source_target_pairs={{2,0},{3,1},{0,2},{1,3},{6,4},{7,5},{4,6},{5,7},{10,8},{11,9},{8,1... | collective-permute-start | bytes 331784 | tf_op jit(solution)/shard_map/ppermute | solution.py:822
  38.5 9.0 %collective-permute-start.13 = (bf16[432,128]{1,0:T(8,128)(2,1)S(1)}, bf16[432,128]{1,0:T(8,128)(2,1)S(1)}, u32[]{:S(2)}, u32[]{:S(2)}) collective-permute-start(bf16[432,128]{1,0:T(8,128)(2,1)S(1)} %get-tuple-element.76), channel_id=1, source_target_pairs={{3,0},{2,1},{1,2},{0,3},{7,4},{6,5},{5,6},{4,7},{11,8},{10,9},{9,1... | collective-permute-start | bytes 331784 | tf_op jit(solution)/shard_map/ppermute | solution.py:822
  47.6 4.8 %collective-permute-start.14 = (bf16[432,128]{1,0:T(8,128)(2,1)S(1)}, bf16[432,128]{1,0:T(8,128)(2,1)S(1)}, u32[]{:S(2)}, u32[]{:S(2)}) collective-permute-start(bf16[432,128]{1,0:T(8,128)(2,1)S(1)} %share.1.refs_0_), channel_id=1, source_target_pairs={{0,16},{8,24},{16,0},{24,8},{1,17},{9,25},{17,1},{25,9},{2,18},{10... | collective-permute-start | bytes 331784 | tf_op jit(solution)/shard_map/ppermute | solution.py:547
  52.4 1.4 %collective-permute-start.15 = (bf16[432,128]{1,0:T(8,128)(2,1)S(1)}, bf16[432,128]{1,0:T(8,128)(2,1)S(1)}, u32[]{:S(2)}, u32[]{:S(2)}) collective-permute-start(bf16[432,128]{1,0:T(8,128)(2,1)S(1)} %chips.1.mine_ref), channel_id=1, source_target_pairs={{0,8},{8,0},{16,24},{24,16},{1,9},{9,1},{17,25},{25,17},{2,10},{10... | collective-permute-start | bytes 331784 | tf_op jit(solution)/shard_map/ppermute | solution.py:547

commit v4 on v3

--- a/solution.py
+++ b/solution.py
@@ -59,8 +59,7 @@
     )(*arrays)
 
 
-def pack_kernel(with_tile, grads_far, second_far, first_far, input_far, right_ref, left_ref, *refs):
-    grads_near, second_near, first_near, edges, edges_wide, packed, sems, tile_sems = refs[-8:]
+def pack_kernel(grads_far, second_far, first_far, right_ref, left_ref, grads_near, second_near, first_near, edges, edges_wide, packed, sems):
     heads, batch, height, breadth, _ = grads_far.shape
     samples = second_far.shape[0]
     rows = 6 * height
@@ -71,13 +70,6 @@
             source = far.at[:, :, :, columns, :] if j == 0 else far.at[:, :, columns, :]
             copies.append(pltpu.make_async_copy(source, near.at[side], sems.at[side, j]))
             copies[-1].start()
-    tile_copies = []
-    if with_tile:
-        for j, far in enumerate((second_far, second_far, first_far, first_far, input_far)):
-            source = far.at[:, :, :, pl.ds(LANES * (j % 2), LANES)] if j < 4 else far
-            target = refs[0].at[j] if j < 2 else refs[1].at[j - 2]
-            tile_copies.append(pltpu.make_async_copy(source, target, tile_sems.at[j]))
-            tile_copies[-1].start()
     for copy in copies:
         copy.wait()
     for side, out_ref in ((0, right_ref), (1, left_ref)):
@@ -110,20 +102,17 @@
                         half, pl.ds((j * samples + s) * height * 8 + inner, height, stride=8), :
                     ]
         out_ref[...] = packed[...].astype(BF).reshape(out_ref.shape)
-    for copy in tile_copies:
-        copy.wait()
-
-
-def pack(head_grads, pre_second, pre_first, encoder_input, with_tile):
+
+
+def pack(head_grads, pre_second, pre_first):
     heads, batch, height, _, _ = head_grads.shape
     samples = pre_second.shape[0]
     shape = jax.ShapeDtypeStruct((batch + samples, 6 * height, LANES), BF)
-    tiles = [jax.ShapeDtypeStruct((count,) + encoder_input.shape, BF) for count in (2, 3)]
     return run(
         "pack_columns",
-        functools.partial(pack_kernel, with_tile),
-        [shape, shape] + tiles * with_tile,
-        [head_grads, pre_second, pre_first, encoder_input],
+        pack_kernel,
+        [shape, shape],
+        [head_grads, pre_second, pre_first],
         [
             pltpu.VMEM((2, heads, batch, height, 16, LANES), BF),
             pltpu.VMEM((2, samples, height, 16, 2 * LANES), BF),
@@ -132,7 +121,6 @@
             pltpu.VMEM((2, 2 * samples * height * 8, LANES), F32),
             pltpu.VMEM(((batch + samples) * 6 * height, LANES), F32),
             pltpu.SemaphoreType.DMA((2, 3)),
-            pltpu.SemaphoreType.DMA((5,)),
         ],
         far=True,
     )
@@ -583,7 +571,7 @@
     return total
 
 
-def near_kernel(second_ref, first_ref, low_ref, high_ref, slope_second, slope_first, halo_ref, wide, cells):
+def near_kernel(second_ref, first_ref, input_ref, low_ref, high_ref, slope_second, slope_first, halo_ref, wide, cells):
     samples, height, breadth, depth = second_ref.shape
     kept = breadth + 2 * EDGE
     batch = low_ref.shape[0] - samples
@@ -606,59 +594,57 @@
                         cells[s, at : at + height, half * LANES : (half + 1) * LANES] = value
         value = jnp.concatenate([wide[0], wide[1]], axis=1)
         slope_ref[...] = gelu_slope(value).reshape(slope_ref.shape)
-    halo_ref[...] = cells[...].astype(BF)
-
-
-def near_parts(pre_second, pre_first, low, high):
+    halo_ref[:, : cells.shape[1]] = cells[...].astype(BF)
+    half = height // 2
+    for part in range(2):
+        values = input_ref[:, part * half : (part + 1) * half].reshape(samples, half * breadth, LANES)
+        halo_ref[:, cells.shape[1] :, part * LANES : (part + 1) * LANES] = values
+
+
+def near_parts(pre_second, pre_first, encoder_input, low, high):
     samples, height, breadth, depth = pre_second.shape
     kept = breadth + 2 * EDGE
     slope = jax.ShapeDtypeStruct((samples, height, kept, depth), F32)
     return run(
         "near_parts",
         near_kernel,
-        [slope, slope, jax.ShapeDtypeStruct((samples, 6 * height, depth), BF)],
-        [pre_second, pre_first, low, high],
+        [slope, slope, jax.ShapeDtypeStruct((samples, 6 * height + height * breadth // 2, depth), BF)],
+        [pre_second, pre_first, encoder_input, low, high],
         [pltpu.VMEM((2, samples * height * kept, LANES), F32), pltpu.VMEM((samples, 6 * height, depth), F32)],
     )
 
 
-def far_kernel(first_ref, input_ref, tile_second, tile_ref, slope_second, slope_first, act_out, input_out, wide, act, cells):
+def far_kernel(first_ref, tile_second, tile_first, slope_second, slope_first, act_out, wide, act):
     samples, height, breadth, depth = first_ref.shape
     kept = breadth + 2 * EDGE
     lat = lax.axis_index("lat")
-    for source_ref, slope_ref in ((tile_second, slope_second), (tile_ref, slope_first)):
+    for source_ref, slope_ref in ((tile_second, slope_second), (tile_first, slope_first)):
         wide[...] = jnp.zeros(wide.shape, F32)
         for s in range(samples):
             for half in range(2):
                 for r in range(height):
                     at = (s * height + r) * kept + EDGE
-                    wide[half, at : at + breadth, :] = source_ref[half, s, r].astype(F32)
+                    wide[half, at : at + breadth, :] = source_ref[s, r, :, half * LANES : (half + 1) * LANES].astype(F32)
         value = jnp.concatenate([wide[0], wide[1]], axis=1)
         slope_ref[...] = gelu_slope(value).reshape(slope_ref.shape)
     own, other = pl.ds(height * lat, height), pl.ds(height * (1 - lat), height)
     act[:, own] = gelu_value(first_ref[...].astype(F32))
-    act[:, other] = jnp.concatenate([gelu_value(tile_ref[half].astype(F32)) for half in range(2)], axis=-1)
-    cells[:, own] = input_ref[...].astype(F32)
-    cells[:, other] = tile_ref[2].astype(F32)
+    act[:, other] = gelu_value(tile_first[...].astype(F32))
     act_out[...] = act[...].reshape(act_out.shape[1], depth).T.astype(BF)
-    input_out[...] = cells[...].reshape(input_out.shape[1], input_out.shape[0]).T.astype(BF)
-
-
-def far_parts(pre_first, encoder_input, tile_second, tile):
+
+
+def far_parts(pre_first, tile_second, tile_first):
     samples, height, breadth, depth = pre_first.shape
-    channels = encoder_input.shape[3]
     kept = breadth + 2 * EDGE
-    cells = 2 * samples * height * breadth
     slope = jax.ShapeDtypeStruct((samples, height, kept, depth), F32)
     return run(
         "far_parts",
         far_kernel,
-        [slope, slope, jax.ShapeDtypeStruct((depth, cells), BF), jax.ShapeDtypeStruct((channels, cells), BF)],
-        [pre_first, encoder_input, tile_second, tile],
+        [slope, slope, jax.ShapeDtypeStruct((depth, 2 * samples * height * breadth), BF)],
+        [pre_first, tile_second, tile_first],
         [
             pltpu.VMEM((2, samples * height * kept, LANES), F32),
             pltpu.VMEM((samples, 2 * height, breadth, depth), F32),
-            pltpu.VMEM((samples, 2 * height, breadth, channels), F32),
         ],
     )
 
@@ -678,38 +664,42 @@
                 slope[s, other, at, :] = beside[here : here + height]
 
 
-def globe_kernel(own_ref, cross_ref, line_ref, corner_ref, near_ref, far_ref, halo_ref, cat_ref, moved_ref, latent, slope, wide):
-    samples, rows, kept, depth = own_ref.shape
+def globe_kernel(near_ref, far_ref, halo_ref, *refs):
+    cat_ref, moved_ref, latent, slope, wide = refs[-5:]
+    samples = near_ref.shape[0]
+    totals, lines = refs[:samples], refs[samples : 2 * samples]
+    rows, kept, depth = totals[0].shape
     height = rows - 1
     tall = 2 * height
     breadth = kept - 2 * EDGE
     lat = lax.axis_index("lat")
     own = 8 + EDGE
     latent[...] = jnp.zeros(latent.shape, F32)
-    latent[:, pl.ds((height - 1) * lat, rows)] = own_ref[...].astype(F32) + cross_ref[...].astype(F32)
-    latent[:, pl.ds((height - 1) * (1 - lat), rows)] += line_ref[...].astype(F32) + corner_ref[...].astype(F32)
+    for s in range(samples):
+        latent[s, pl.ds((height - 1) * lat, rows)] = totals[s][...].astype(F32)
+        latent[s, pl.ds((height - 1) * (1 - lat), rows)] += lines[s][...].astype(F32)
     put_slopes(slope, near_ref, far_ref, halo_ref, 2, 0)
     wide[:, :, 8 : 8 + kept, :] = (latent[...] * slope[...]).astype(BF).astype(F32)
     for v in STEPS:
         lanes = slice((v + 1) * depth, (v + 2) * depth)
-        cat_ref[:, 1 : 1 + tall, :, lanes] = wide[:, :, 8 - v : 8 - v + kept + 8, :].astype(BF)
+        cat_ref[:, 1 : 1 + tall, :, lanes] = wide[:, :, 8 - v : 8 - v + kept, :].astype(BF)
         moved_ref[v + 1, :, 1 : 1 + tall] = wide[:, :, own - v : own - v + breadth, :].astype(BF)
     for row in (0, tall + 1):
         cat_ref[:, row] = jnp.zeros(cat_ref.shape[:1] + cat_ref.shape[2:], BF)
         moved_ref[:, :, row] = jnp.zeros(moved_ref.shape[:2] + moved_ref.shape[3:], BF)
 
 
-def globe(own, cross, line, angle, near, far, halo):
-    samples, rows, kept, depth = own.shape
+def globe(totals, lines, near, far, halo):
+    samples, (rows, kept, depth) = len(totals), totals[0].shape
     tall, breadth = 2 * (rows - 1), kept - 2 * EDGE
     return run(
         "latent_grads",
         globe_kernel,
         [
-            jax.ShapeDtypeStruct((samples, tall + 2, kept + 8, 3 * depth), BF),
+            jax.ShapeDtypeStruct((samples, tall + 2, kept, 3 * depth), BF),
             jax.ShapeDtypeStruct((3, samples, tall + 2, breadth, depth), BF),
         ],
-        [own, cross, line, angle, near, far, halo],
+        [near, far, halo, *totals, *lines],
         [
             pltpu.VMEM((samples, tall, kept, depth), F32),
             pltpu.VMEM((samples, tall, kept, depth), F32),
@@ -718,8 +708,8 @@
     )
 
 
-def band_rows(norm_factor, left_ref, moved_ref, mine_ref, other_ref):
-    channels, cells = left_ref.shape
+def band_rows(norm_factor, left_all, moved_ref, mine_ref, other_ref):
+    channels, cells = left_all.shape
     _, samples, padded, breadth, depth = moved_ref.shape
     tall = padded - 2
     lat = lax.axis_index("lat")
@@ -736,17 +726,17 @@
 
     for j in range(4):
         (u0, v0), (u1, v1) = (divmod(k, 3) for k in (j, 5 + j))
-        put(left_ref[...], u0 - 1 + lat * (u1 - u0), v0 - 1 + lat * (v1 - v0), lat * half + j * channels, channels)
-    put(left_ref[pl.ds(pl.multiple_of(lat * half, half), half), :], 0, 0, (1 - lat) * 4 * channels, half)
+        put(left_all, u0 - 1 + lat * (u1 - u0), v0 - 1 + lat * (v1 - v0), lat * half + j * channels, channels)
+    put(jnp.where(lat == 0, left_all[:half], left_all[half:]), 0, 0, (1 - lat) * 4 * channels, half)
 
 
 def second_band_kernel(norm_factor, moved_ref, act_ref, mine_ref, other_ref):
-    band_rows(norm_factor, act_ref, moved_ref, mine_ref, other_ref)
-
-
-def first_band_kernel(norm_factor, cat_ref, near_ref, far_ref, halo_ref, input_ref, weights_ref, moved_ref, mine_ref, other_ref, slope, wide):
+    band_rows(norm_factor, act_ref[...], moved_ref, mine_ref, other_ref)
+
+
+def first_band_kernel(norm_factor, cat_ref, near_ref, far_ref, halo_ref, input_ref, weights_ref, moved_ref, mine_ref, other_ref, slope, wide, cells):
     samples, padded, broad, triple = cat_ref.shape
-    tall, kept, depth = padded - 2, broad - 8, triple // 3
+    tall, kept, depth = padded - 2, broad, triple // 3
     height = tall // 2
     breadth = kept - 2 * EDGE
     lat = lax.axis_index("lat")
@@ -757,13 +747,18 @@
         weights = jnp.concatenate([weights_ref[3 * (u + 1) + (v + 1)] for v in STEPS], axis=1)
         part = dot_last(cat_ref[:, 1 - u : 1 - u + tall].reshape(samples * tall * broad, triple), weights)
         linear = part if linear is None else linear + part
-    linear = linear.reshape(samples, tall, broad, depth)[:, :, :kept]
+    linear = linear.reshape(samples, tall, broad, depth)
     wide[:, :, 8 : 8 + kept, :] = (linear * slope[...]).astype(BF).astype(F32)
     for v in STEPS:
         moved_ref[v + 1, :, 1 : 1 + tall] = wide[:, :, own - v : own - v + breadth, :].astype(BF)
     for row in (0, tall + 1):
         moved_ref[:, :, row] = jnp.zeros(moved_ref.shape[:2] + moved_ref.shape[3:], BF)
-    band_rows(norm_factor, input_ref, moved_ref, mine_ref, other_ref)
+    cells[:, pl.ds(height * lat, height)] = input_ref[...].astype(F32)
+    half = height // 2
+    for part in range(2):
+        values = halo_ref[:, 6 * height :, part * LANES : (part + 1) * LANES].astype(F32)
+        cells[:, pl.ds(height * (1 - lat) + part * half, half)] = values.reshape(samples, half, breadth, LANES)
+    band_rows(norm_factor, cells[...].reshape(samples * tall * breadth, LANES).T.astype(BF), moved_ref, mine_ref, other_ref)
 
 
 def second_band(norm_factor, moved, act):
@@ -771,17 +766,21 @@
     return run("second_weight_grads", functools.partial(second_band_kernel, norm_factor), [half, half], [moved, act])
 
 
-def first_band(norm_factor, cat, near, far, halo, cells_in, w_second):
+def first_band(norm_factor, cat, near, far, halo, encoder_input, w_second):
     samples, padded, broad, triple = cat.shape
-    tall, kept, depth = padded - 2, broad - 8, triple // 3
+    tall, kept, depth = padded - 2, broad, triple // 3
     breadth = kept - 2 * EDGE
-    half = jax.ShapeDtypeStruct((9 * cells_in.shape[0] // 2, LANES), BF)
+    half = jax.ShapeDtypeStruct((9 * encoder_input.shape[3] // 2, LANES), BF)
     return run(
         "encoder_grads",
         functools.partial(first_band_kernel, norm_factor),
         [jax.ShapeDtypeStruct((3, samples, padded, breadth, depth), BF), half, half],
-        [cat, near, far, halo, cells_in, w_second],
-        [pltpu.VMEM((samples, tall, kept, depth), F32), pltpu.VMEM((samples, tall, kept + 16, depth), F32)],
+        [cat, near, far, halo, encoder_input, w_second],
+        [
+            pltpu.VMEM((samples, tall, kept, depth), F32),
+            pltpu.VMEM((samples, tall, kept + 16, depth), F32),
+            pltpu.VMEM((samples, tall, breadth, LANES), F32),
+        ],
     )
 
 
@@ -825,15 +824,14 @@
 def two_bands(head_grads, head_weights, encoder_input, pre_first, pre_second, w_first, w_second, norm_factor):
     samples, height, breadth, _ = encoder_input.shape
     columns = lax.axis_size("lon")
-    to_right, to_left, tile_second, tile = pack(head_grads, pre_second, pre_first, encoder_input, True)
+    tiles = [swap(array, "lat", 1) for array in (pre_second, pre_first)]
+    to_right, to_left = pack(head_grads, pre_second, pre_first)
     low = around(to_right, "lon", 1)
     high = around(to_left, "lon", -1)
-    tile_second = swap(tile_second, "lat", 1)
     head_grads, head_weights, w_second, pre_second, pre_first, encoder_input = stage(
         head_grads, head_weights, w_second, pre_second, pre_first, encoder_input
     )
-    tile = swap(tile, "lat", 1)
-    low, high, tile_second, tile = lax.optimization_barrier((low, high, tile_second, tile))
+    low, high, *tiles = lax.optimization_barrier((low, high, *tiles))
     heads_of = functools.partial(
         head_conv,
         head_grads=head_grads,
@@ -844,19 +842,21 @@
         rows=height + 1,
     )
     got = swap(heads_of(True, False), "lead", 1)
-    near_second, near_first, halo = near_parts(pre_second, pre_first, low, high)
+    near_second, near_first, halo = near_parts(pre_second, pre_first, encoder_input, low, high)
     mine = heads_of(False, False)
-    got, halo = lax.optimization_barrier((got, halo))
     halo = swap(halo, "lat", 1)
-    part_shape = jax.ShapeDtypeStruct((samples,) + mine.shape[1:], BF)
-    own, cross = run("core_sum", core_sum_kernel, [part_shape, part_shape], [mine, got])
-    cross_got, line_got, corner_got = swap(cross, "lead", 2), swap(own, "lat", 1), corner(cross, None)
-    far_second, far_first, act, cells_in = far_parts(pre_first, encoder_input, tile_second, tile)
-
-    cat, moved = globe(own, cross_got, line_got, corner_got, near_second, far_second, halo)
+    part_shape = jax.ShapeDtypeStruct(mine.shape[1:], BF)
+    parts = run("core_sum", core_sum_kernel, [part_shape] * (2 * samples), [mine, got])
+    cross = [swap(part, "lead", 2) for part in parts[samples:]]
+    cross[0], halo = lax.optimization_barrier((cross[0], halo))
+    totals = [run("chip_sum", sum_kernel, [part_shape], [parts[s], cross[s]])[0] for s in range(samples)]
+    lines = [swap(total, "lat", 1) for total in totals]
+    far_second, far_first, act = far_parts(pre_first, *tiles)
+
+    cat, moved = globe(totals, lines, near_second, far_second, halo)
     second_mine, second_other = second_band(norm_factor, moved, act)
     second_got = swap(second_other, "lead", 1)
-    moved_first, first_mine, first_other = first_band(norm_factor, cat, near_first, far_first, halo, cells_in, w_second)
+    moved_first, first_mine, first_other = first_band(norm_factor, cat, near_first, far_first, halo, encoder_input, w_second)
     first_got = swap(first_other, "lead", 1)
     input_grad = run(
         "input_conv", input_band_kernel, [jax.ShapeDtypeStruct(encoder_input.shape, BF)], [moved_first, w_first]
@@ -866,7 +866,7 @@
     rows = blocks[0].shape[1]
     share_shape = jax.ShapeDtypeStruct((3 * rows, LANES), BF)
     shares = run("blocks", blocks_kernel, [share_shape] * columns, blocks)
-    parts = [to_partner(shares[step], step) for step in range(1, columns)]
+    parts = [to_partner(shares[step], step) for step in [*range(2, columns), 1]]
     share = run("share", sum_kernel, [share_shape], [shares[0], *parts])[0]
     both = run("chips", sum_kernel, [share_shape], [share, swap(share, "lead", 2)])[0]
     result_first, result_second = run(
@@ -878,16 +878,15 @@
     return input_grad, result_first.reshape(-1), result_second.reshape(-1)
 
 
-def core_sum_kernel(mine_ref, got_ref, own_ref, cross_ref):
-    samples = own_ref.shape[0]
-    for ref, part in ((own_ref, slice(0, samples)), (cross_ref, slice(samples, 2 * samples))):
-        ref[...] = (mine_ref[part].astype(F32) + got_ref[part].astype(F32)).astype(BF)
+def core_sum_kernel(mine_ref, got_ref, *outs):
+    for slot, out_ref in enumerate(outs):
+        out_ref[...] = (mine_ref[slot].astype(F32) + got_ref[slot].astype(F32)).astype(BF)
 
 
 def general(head_grads, head_weights, encoder_input, pre_first, pre_second, w_first, w_second, norm_factor):
     samples, height, breadth, _ = encoder_input.shape
     bands, columns = lax.axis_size("lat"), lax.axis_size("lon")
-    to_right, to_left = pack(head_grads, pre_second, pre_first, encoder_input, False)
+    to_right, to_left = pack(head_grads, pre_second, pre_first)
     to_right, to_left, to_cross = lax.optimization_barrier((to_right, to_left, pre_first))
     low = around(to_right, "lon", 1)
     high = around(to_left, "lon", -1)
@@ -926,7 +925,7 @@
     rows = blocks[0].shape[2]
     share_shape = jax.ShapeDtypeStruct((2, rows, LANES), BF)
     shares = run("own_band", own_band_kernel, [share_shape] * columns, blocks + [first_came, second_came])
-    parts = [to_partner(shares[step], step) for step in range(1, columns)]
+    parts = [to_partner(shares[step], step) for step in [*range(2, columns), 1]]
     share = run("share", sum_kernel, [share_shape], [shares[0], *parts])[0]
     both = run("chips", chips_kernel, [jax.ShapeDtypeStruct((3, rows, LANES), BF)], [share, swap(share, "lead", 2)])[0]
     result_first, result_second = run(

time: 54.7 us -> 52.2 us (0.954)
  waiting for transfers between devices: 22.3 us -> 18.7 us
  starting transfers between devices: 19.3 us -> 20.7 us
    ppermute x10 -> x12, starting transfers between devices: 9.33 us -> 12.6 us  [swap(): return lax.ppermute(array, axis, [(i, i ^ flip) for i in range(count)])]
    ppermute x10 -> x12, waiting for transfers between devices: 12.4 us -> 9.18 us  [swap(): return lax.ppermute(array, axis, [(i, i ^ flip) for i in range(count)])]
    ppermute x1 -> x0, starting transfers between devices: 1.44 us -> none  [corner(): return lax.ppermute(array, ('lead', 'lat'), pairs)]
    ppermute x3, starting transfers between devices: 4.47 us -> 3.88 us  [to_partner(): lax.ppermute(array, 'lon', [(partner(i, step, count), i) for i in range(c...]
    pallas_call x15 -> x17, Pallas kernels: 12.3 us -> 11.9 us  [run(): pl.pallas_call(kernel, name=name, out_shape=out_shape, in_specs=specs, ou...]
  transfers between devices with their start and end apart: 16 -> 17, of which waited for: 10 -> 10; matrix products, arithmetic and copies ran while one was open for 0% -> 0% of each run, Pallas kernels for 13% -> 16%
where the time goes in v4:
time: 52.2 us; the launch traced here: 52 us
  starting transfers between devices  20.7 us (40%)
  waiting for transfers between devices  18.7 us (36%)
  Pallas kernels  11.9 us (23%)
  between operations  0.76 us (1%)
    ppermute x12, starting transfers between devices, swap(): return lax.ppermute(array, axis, [(i, i ^ flip) for i in range(count)])  12.6 us
    pallas_call x17, Pallas kernels, run(): pl.pallas_call(kernel, name=name, out_shape=out_shape, in_specs=specs, ou...  11.9 us
    ppermute x12, waiting for transfers between devices, swap(): return lax.ppermute(array, axis, [(i, i ^ flip) for i in range(count)])  9.18 us
    ppermute x3, waiting for transfers between devices, to_partner(): lax.ppermute(array, 'lon', [(partner(i, step, count), i) for i in range(c...  8.59 us
    ppermute x2, starting transfers between devices, around(): return lax.ppermute(array, axis, pairs)  4.15 us
    ppermute x3, starting transfers between devices, to_partner(): lax.ppermute(array, 'lon', [(partner(i, step, count), i) for i in range(c...  3.88 us
  transfers between devices with their start and end apart: 17, of which 10 were waited for; matrix products, arithmetic and copies ran while one was open for 0% of the time, Pallas kernels for 16%

profile of v4, /device:TPU:0, one launch (start us, length us, event | category | flops | bytes accessed | tf_op | source)
XLA Modules:
  0.0 52.0 jit_solution(915846981501474732)
XLA Ops:
  0.6 3.0 %collective-permute-start.2 = (bf16[2,4,32,256]{3,2,1,0:T(8,128)(2,1)}, bf16[2,4,32,256]{3,2,1,0:T(8,128)(2,1)S(1)}, u32[]{:S(2)}, u32[]{:S(2)}) collective-permute-start(bf16[2,4,32,256]{3,2,1,0:T(8,128)(2,1)} %second_far.1), channel_id=1, source_target_pairs={{0,4},{4,0},{1,5},{5,1},{2,6},{6,2},{3,7},{7,3},{8,12},{12,8},{9,1... | collective-permute-start | bytes 393224 | tf_op jit(solution)/shard_map/ppermute | solution.py:535
  3.7 0.1 collective-permute-start.3
  3.7 1.3 %pack_columns.1 = (bf16[10,24,128]{2,1,0:T(8,128)(2,1)S(1)}, bf16[10,24,128]{2,1,0:T(8,128)(2,1)S(1)}) custom-call(bf16[2,8,4,32,128]{4,3,2,1,0:T(8,128)(2,1)} %grads_far.1, bf16[2,4,32,256]{3,2,1,0:T(8,128)(2,1)} %second_far.1, bf16[2,4,32,256]{3,2,1,0:T(8,128)(2,1)} %first_far.1), custom_call_target="tpu_custom_call" | custom-call | flops 1 | bytes 1 | tf_op jit(solution)/shard_map/pack_columns/pallas_call | solution.py:50
  5.0 2.1 %collective-permute-start = (bf16[10,24,128]{2,1,0:T(8,128)(2,1)S(1)}, bf16[10,24,128]{2,1,0:T(8,128)(2,1)S(1)}, u32[]{:S(2)}, u32[]{:S(2)}) collective-permute-start(bf16[10,24,128]{2,1,0:T(8,128)(2,1)S(1)} %get-tuple-element.43), channel_id=1, source_target_pairs={{0,1},{1,2},{2,3},{3,0},{4,5},{5,6},{6,7},{7,4},{8,9},{9,10},{10,1... | collective-permute-start | bytes 184328 | tf_op jit(solution)/shard_map/ppermute | solution.py:541
  7.1 2.1 %collective-permute-start.1 = (bf16[10,24,128]{2,1,0:T(8,128)(2,1)S(1)}, bf16[10,24,128]{2,1,0:T(8,128)(2,1)S(1)}, u32[]{:S(2)}, u32[]{:S(2)}) collective-permute-start(bf16[10,24,128]{2,1,0:T(8,128)(2,1)S(1)} %get-tuple-element.44), channel_id=1, source_target_pairs={{0,3},{1,0},{2,1},{3,2},{4,7},{5,4},{6,5},{7,6},{8,11},{9,8},{10,9... | collective-permute-start | bytes 184328 | tf_op jit(solution)/shard_map/ppermute | solution.py:541
  9.2 1.9 %stage.1 = (bf16[2,8,4,32,128]{4,3,2,1,0:T(8,128)(2,1)S(1)}, bf16[2,9,256,128]{3,2,1,0:T(8,128)(2,1)S(1)}, bf16[9,256,256]{2,1,0:T(8,128)(2,1)S(1)}, bf16[2,4,32...) custom-call(bf16[2,8,4,32,128]{4,3,2,1,0:T(8,128)(2,1)} %grads_far.1, ...), custom_call_target="tpu_custom_call" | custom-call | flops 1 | bytes 1 | tf_op jit(solution)/shard_map/stage/pallas_call | solution.py:50
  11.0 0.9 %collective-permute-done.low_ref = bf16[10,24,128]{2,1,0:T(8,128)(2,1)S(1)} collective-permute-done((bf16[10,24,128]{2,1,0:T(8,128)(2,1)S(1)}, bf16[10,24,128]{2,1,0:T(8,128)(2,1)S(1)}, u32[]{:S(2)}, u32[]{:S(2)}) %collective-permute-start) | collective-permute-done | bytes 61472 | tf_op jit(solution)/shard_map/ppermute | solution.py:541
  11.9 0.0 collective-permute-done.1.high_ref
  12.0 0.0 collective-permute-done.2.tile_second
  12.0 0.0 collective-permute-done.3.tile_first
  12.0 1.1 %head_conv.3 = bf16[4,5,40,256]{3,2,1,0:T(8,128)(2,1)S(1)} custom-call(bf16[2,8,4,32,128]{4,3,2,1,0:T(8,128)(2,1)S(1)} %get-tuple-element.51.grads_ref, bf16[10,24,128]{2,1,0:T(8,128)(2,1)S(1)} %collective-permute-done.low_ref, bf16[10,24,128]{2,1,0:T(8,128)(2,1)S(1)} %collective-permute-done.1.high_ref, ...), custom_call_target="tpu_custom_call" | custom-call | flops 1 | bytes 1 | tf_op jit(solution)/shard_map/head_conv/pallas_call | solution.py:50
  13.1 0.1 collective-permute-start.4
  13.2 1.1 %head_conv.2.mine_ref = bf16[4,5,40,256]{3,2,1,0:T(8,128)(2,1)S(1)} custom-call(bf16[2,8,4,32,128]{4,3,2,1,0:T(8,128)(2,1)S(1)} %get-tuple-element.51.grads_ref, bf16[10,24,128]{2,1,0:T(8,128)(2,1)S(1)} %collective-permute-done.low_ref, bf16[10,24,128]{2,1,0:T(8,128)(2,1)S(1)} %collective-permute-done.1.high_ref, ...), custom_call_target="tpu_custom_call" | custom-call | flops 1 | bytes 1 | tf_op jit(solution)/shard_map/head_conv/pallas_call | solution.py:50
  14.3 0.6 %collective-permute-done.4.got_ref = bf16[4,5,40,256]{3,2,1,0:T(8,128)(2,1)S(1)} collective-permute-done((bf16[4,5,40,256]{3,2,1,0:T(8,128)(2,1)S(1)}, bf16[4,5,40,256]{3,2,1,0:T(8,128)(2,1)S(1)}, u32[]{:S(2)}, u32[]{:S(2)}) %collective-permute-start.4) | collective-permute-done | bytes 409632 | tf_op jit(solution)/shard_map/ppermute | solution.py:535
  14.9 0.1 core_sum.1
  15.0 1.7 %collective-permute-start.7 = (bf16[5,40,256]{2,1,0:T(8,128)(2,1)S(1)}, bf16[5,40,256]{2,1,0:T(8,128)(2,1)S(1)}, u32[]{:S(2)}, u32[]{:S(2)}) collective-permute-start(bf16[5,40,256]{2,1,0:T(8,128)(2,1)S(1)} %get-tuple-element.59), channel_id=1, source_target_pairs={{0,16},{8,24},{16,0},{24,8},{1,17},{9,25},{17,1},{25,9},{2,18},{10... | collective-permute-start | bytes 307208 | tf_op jit(solution)/shard_map/ppermute | solution.py:535
  16.7 0.4 collective-permute-start.5
  17.1 0.4 near_parts.1
  17.5 1.7 %collective-permute-start.6 = (bf16[2,88,256]{2,1,0:T(8,128)(2,1)S(1)}, bf16[2,88,256]{2,1,0:T(8,128)(2,1)S(1)}, u32[]{:S(2)}, u32[]{:S(2)}) collective-permute-start(bf16[2,88,256]{2,1,0:T(8,128)(2,1)S(1)} %get-tuple-element.54), channel_id=1, source_target_pairs={{0,4},{4,0},{1,5},{5,1},{2,6},{6,2},{3,7},{7,3},{8,12},{12,8},{9,1... | collective-permute-start | bytes 270344 | tf_op jit(solution)/shard_map/ppermute | solution.py:535
  19.3 1.5 %collective-permute-done.7.refs_1_ = bf16[5,40,256]{2,1,0:T(8,128)(2,1)S(1)} collective-permute-done((bf16[5,40,256]{2,1,0:T(8,128)(2,1)S(1)}, bf16[5,40,256]{2,1,0:T(8,128)(2,1)S(1)}, u32[]{:S(2)}, u32[]{:S(2)}) %collective-permute-start.7) | collective-permute-done | bytes 102432 | tf_op jit(solution)/shard_map/ppermute | solution.py:535
  20.8 1.7 %collective-permute-start.9 = (bf16[5,40,256]{2,1,0:T(8,128)(2,1)S(1)}, bf16[5,40,256]{2,1,0:T(8,128)(2,1)S(1)}, u32[]{:S(2)}, u32[]{:S(2)}) collective-permute-start(bf16[5,40,256]{2,1,0:T(8,128)(2,1)S(1)} %chip_sum.3.refs_1_), channel_id=1, source_target_pairs={{0,4},{4,0},{1,5},{5,1},{2,6},{6,2},{3,7},{7,3},{8,12},{12,8},{9,1... | collective-permute-start | bytes 307208 | tf_op jit(solution)/shard_map/ppermute | solution.py:535
  22.6 0.0 collective-permute-done.6.halo_ref
  22.6 0.0 collective-permute-done.5.refs_1_
  22.6 1.5 %collective-permute-start.8 = (bf16[5,40,256]{2,1,0:T(8,128)(2,1)S(1)}, bf16[5,40,256]{2,1,0:T(8,128)(2,1)S(1)}, u32[]{:S(2)}, u32[]{:S(2)}) collective-permute-start(bf16[5,40,256]{2,1,0:T(8,128)(2,1)S(1)} %chip_sum.2.refs_0_), channel_id=1, source_target_pairs={{0,4},{4,0},{1,5},{5,1},{2,6},{6,2},{3,7},{7,3},{8,12},{12,8},{9,1... | collective-permute-start | bytes 307208 | tf_op jit(solution)/shard_map/ppermute | solution.py:535
  24.1 0.6 %far_parts.1 = (f32[2,4,40,256]{3,2,1,0:T(8,128)S(1)}, f32[2,4,40,256]{3,2,1,0:T(8,128)S(1)}, bf16[256,512]{1,0:T(8,128)(2,1)S(1)}) custom-call(bf16[2,4,32,256]{3,2,1,0:T(8,128)(2,1)S(1)} %get-tuple-element.41.first_ref, bf16[2,4,32,256]{3,2,1,0:T(8,128)(2,1)S(1)} %collective-permute-done.2.tile_second, ...), custom_call_target="tpu_custom_call" | custom-call | flops 1 | bytes 1 | tf_op jit(solution)/shard_map/far_parts/pallas_call | solution.py:50
  24.7 1.7 %collective-permute-done.9.refs_3_ = bf16[5,40,256]{2,1,0:T(8,128)(2,1)S(1)} collective-permute-done((bf16[5,40,256]{2,1,0:T(8,128)(2,1)S(1)}, bf16[5,40,256]{2,1,0:T(8,128)(2,1)S(1)}, u32[]{:S(2)}, u32[]{:S(2)}) %collective-permute-start.9) | collective-permute-done | bytes 102432 | tf_op jit(solution)/shard_map/ppermute | solution.py:535
  26.4 1.1 %collective-permute-done.8.refs_2_ = bf16[5,40,256]{2,1,0:T(8,128)(2,1)S(1)} collective-permute-done((bf16[5,40,256]{2,1,0:T(8,128)(2,1)S(1)}, bf16[5,40,256]{2,1,0:T(8,128)(2,1)S(1)}, u32[]{:S(2)}, u32[]{:S(2)}) %collective-permute-start.8) | collective-permute-done | bytes 102432 | tf_op jit(solution)/shard_map/ppermute | solution.py:535
  27.5 0.8 %latent_grads.1 = (bf16[2,10,40,768]{3,2,1,0:T(8,128)(2,1)S(1)}, bf16[3,2,10,32,256]{4,3,2,1,0:T(8,128)(2,1)S(1)}) custom-call(f32[2,4,40,256]{3,2,1,0:T(8,128)S(1)} %get-tuple-element.47.near_ref, f32[2,4,40,256]{3,2,1,0:T(8,128)S(1)} %get-tuple-element.50.far_ref, bf16[2,88,256]{2,1,0:T(8,128)(2,1)S(1)} %collective-permute-done.6.halo_ref, ...), custom_call_target="tpu_custom_call" | custom-call | flops 1 | bytes 1 | tf_op jit(solution)/shard_map/latent_grads/pallas_call | solution.py:50
  28.3 0.5 second_weight_grads.1
  28.8 0.1 collective-permute-start.11
  28.9 1.8 %encoder_grads.1 = (bf16[3,2,10,32,256]{4,3,2,1,0:T(8,128)(2,1)S(1)}, bf16[576,128]{1,0:T(8,128)(2,1)S(1)}, bf16[576,128]{1,0:T(8,128)(2,1)S(1)}) custom-call(bf16[2,10,40,768]{3,2,1,0:T(8,128)(2,1)S(1)} %get-tuple-element.60.cat_ref, f32[2,4,40,256]{3,2,1,0:T(8,128)S(1)} %get-tuple-element.61.near_ref, f32[2,4,40,256]{3,2,1,0:T(8,128)S(1)} %get-tuple-element.62.far_ref, ...), custom_call_target="tpu_custom_call" | custom-call | flops 1 | bytes 1 | tf_op jit(solution)/shard_map/encoder_grads/pallas_call | solution.py:50
  30.8 0.0 copy-start
  30.8 0.6 %collective-permute-start.10 = (bf16[576,128]{1,0:T(8,128)(2,1)S(1)}, bf16[576,128]{1,0:T(8,128)(2,1)S(1)}, u32[]{:S(2)}, u32[]{:S(2)}) collective-permute-start(bf16[576,128]{1,0:T(8,128)(2,1)S(1)} %get-tuple-element.66), channel_id=1, source_target_pairs={{0,8},{8,0},{16,24},{24,16},{1,9},{9,1},{17,25},{25,17},{2,10},{10... | collective-permute-start | bytes 442376 | tf_op jit(solution)/shard_map/ppermute | solution.py:535
  31.3 1.0 %collective-permute-done.10 = bf16[576,128]{1,0:T(8,128)(2,1)S(1)} collective-permute-done((bf16[576,128]{1,0:T(8,128)(2,1)S(1)}, bf16[576,128]{1,0:T(8,128)(2,1)S(1)}, u32[]{:S(2)}, u32[]{:S(2)}) %collective-permute-start.10) | collective-permute-done | bytes 147488 | tf_op jit(solution)/shard_map/ppermute | solution.py:535
  32.3 0.0 collective-permute-done.11
  32.3 0.1 blocks.1
  32.5 2.0 %collective-permute-start.12 = (bf16[432,128]{1,0:T(8,128)(2,1)S(1)}, bf16[432,128]{1,0:T(8,128)(2,1)S(1)}, u32[]{:S(2)}, u32[]{:S(2)}) collective-permute-start(bf16[432,128]{1,0:T(8,128)(2,1)S(1)} %get-tuple-element.72), channel_id=1, source_target_pairs={{2,0},{3,1},{0,2},{1,3},{6,4},{7,5},{4,6},{5,7},{10,8},{11,9},{8,1... | collective-permute-start | bytes 331784 | tf_op jit(solution)/shard_map/ppermute | solution.py:821
  34.5 1.5 %collective-permute-start.13 = (bf16[432,128]{1,0:T(8,128)(2,1)S(1)}, bf16[432,128]{1,0:T(8,128)(2,1)S(1)}, u32[]{:S(2)}, u32[]{:S(2)}) collective-permute-start(bf16[432,128]{1,0:T(8,128)(2,1)S(1)} %get-tuple-element.73), channel_id=1, source_target_pairs={{3,0},{2,1},{1,2},{0,3},{7,4},{6,5},{5,6},{4,7},{11,8},{10,9},{9,1... | collective-permute-start | bytes 331784 | tf_op jit(solution)/shard_map/ppermute | solution.py:821
  35.9 0.4 collective-permute-start.14
  36.3 7.8 %collective-permute-done.12.refs_1_ = bf16[432,128]{1,0:T(8,128)(2,1)S(1)} collective-permute-done((bf16[432,128]{1,0:T(8,128)(2,1)S(1)}, bf16[432,128]{1,0:T(8,128)(2,1)S(1)}, u32[]{:S(2)}, u32[]{:S(2)}) %collective-permute-start.12) | collective-permute-done | bytes 110624 | tf_op jit(solution)/shard_map/ppermute | solution.py:821
  44.1 0.8 %collective-permute-done.14.refs_3_ = bf16[432,128]{1,0:T(8,128)(2,1)S(1)} collective-permute-done((bf16[432,128]{1,0:T(8,128)(2,1)S(1)}, bf16[432,128]{1,0:T(8,128)(2,1)S(1)}, u32[]{:S(2)}, u32[]{:S(2)}) %collective-permute-start.14) | collective-permute-done | bytes 110624 | tf_op jit(solution)/shard_map/ppermute | solution.py:821
  44.9 0.1 share.1.refs_0_
  45.0 1.7 %collective-permute-start.15 = (bf16[432,128]{1,0:T(8,128)(2,1)S(1)}, bf16[432,128]{1,0:T(8,128)(2,1)S(1)}, u32[]{:S(2)}, u32[]{:S(2)}) collective-permute-start(bf16[432,128]{1,0:T(8,128)(2,1)S(1)} %share.1.refs_0_), channel_id=1, source_target_pairs={{0,16},{8,24},{16,0},{24,8},{1,17},{9,25},{17,1},{25,9},{2,18},{10... | collective-permute-start | bytes 331784 | tf_op jit(solution)/shard_map/ppermute | solution.py:535
  46.7 3.1 %collective-permute-done.15.refs_1_ = bf16[432,128]{1,0:T(8,128)(2,1)S(1)} collective-permute-done((bf16[432,128]{1,0:T(8,128)(2,1)S(1)}, bf16[432,128]{1,0:T(8,128)(2,1)S(1)}, u32[]{:S(2)}, u32[]{:S(2)}) %collective-permute-start.15) | collective-permute-done | bytes 110624 | tf_op jit(solution)/shard_map/ppermute | solution.py:535
  49.8 0.1 collective-permute-start.16
  49.9 1.1 %input_conv.1 = bf16[2,4,32,128]{3,2,1,0:T(8,128)(2,1)} custom-call(bf16[3,2,10,32,256]{4,3,2,1,0:T(8,128)(2,1)S(1)} %get-tuple-element.64.moved_ref, bf16[9,128,256]{2,1,0:T(8,128)(2,1)S(1)} %copy-done), custom_call_target="tpu_custom_call" | custom-call | flops 1 | bytes 1 | tf_op jit(solution)/shard_map/input_conv/pallas_call | solution.py:50
  51.0 0.2 collective-permute-done.16.other_ref
  51.2 0.8 %cores.1 = (f32[288,128]{1,0:T(8,128)}, f32[576,128]{1,0:T(8,128)}) custom-call(bf16[432,128]{1,0:T(8,128)(2,1)S(1)} %chips.1.mine_ref, bf16[432,128]{1,0:T(8,128)(2,1)S(1)} %collective-permute-done.16.other_ref), custom_call_target="tpu_custom_call" | custom-call | flops 1 | bytes 1 | tf_op jit(solution)/shard_map/cores/pallas_call | solution.py:50
  (5 shorter events, 0.1 us)
Async XLA Ops:
  0.6 11.3 %collective-permute-start.2 = (bf16[2,4,32,256]{3,2,1,0:T(8,128)(2,1)}, bf16[2,4,32,256]{3,2,1,0:T(8,128)(2,1)S(1)}, u32[]{:S(2)}, u32[]{:S(2)}) collective-permute-start(bf16[2,4,32,256]{3,2,1,0:T(8,128)(2,1)} %second_far.1), channel_id=1, source_target_pairs={{0,4},{4,0},{1,5},{5,1},{2,6},{6,2},{3,7},{7,3},{8,12},{12,8},{9,1... | collective-permute-start | bytes 393224 | tf_op jit(solution)/shard_map/ppermute | solution.py:535
  3.7 8.3 %collective-permute-start.3 = (bf16[2,4,32,256]{3,2,1,0:T(8,128)(2,1)}, bf16[2,4,32,256]{3,2,1,0:T(8,128)(2,1)S(1)}, u32[]{:S(2)}, u32[]{:S(2)}) collective-permute-start(bf16[2,4,32,256]{3,2,1,0:T(8,128)(2,1)} %first_far.1), channel_id=1, source_target_pairs={{0,4},{4,0},{1,5},{5,1},{2,6},{6,2},{3,7},{7,3},{8,12},{12,8},{9,1... | collective-permute-start | bytes 393224 | tf_op jit(solution)/shard_map/ppermute | solution.py:535
  5.0 6.9 %collective-permute-start = (bf16[10,24,128]{2,1,0:T(8,128)(2,1)S(1)}, bf16[10,24,128]{2,1,0:T(8,128)(2,1)S(1)}, u32[]{:S(2)}, u32[]{:S(2)}) collective-permute-start(bf16[10,24,128]{2,1,0:T(8,128)(2,1)S(1)} %get-tuple-element.43), channel_id=1, source_target_pairs={{0,1},{1,2},{2,3},{3,0},{4,5},{5,6},{6,7},{7,4},{8,9},{9,10},{10,1... | collective-permute-start | bytes 184328 | tf_op jit(solution)/shard_map/ppermute | solution.py:541
  7.1 4.9 %collective-permute-start.1 = (bf16[10,24,128]{2,1,0:T(8,128)(2,1)S(1)}, bf16[10,24,128]{2,1,0:T(8,128)(2,1)S(1)}, u32[]{:S(2)}, u32[]{:S(2)}) collective-permute-start(bf16[10,24,128]{2,1,0:T(8,128)(2,1)S(1)} %get-tuple-element.44), channel_id=1, source_target_pairs={{0,3},{1,0},{2,1},{3,2},{4,7},{5,4},{6,5},{7,6},{8,11},{9,8},{10,9... | collective-permute-start | bytes 184328 | tf_op jit(solution)/shard_map/ppermute | solution.py:541
  13.1 1.8 %collective-permute-start.4 = (bf16[4,5,40,256]{3,2,1,0:T(8,128)(2,1)S(1)}, bf16[4,5,40,256]{3,2,1,0:T(8,128)(2,1)S(1)}, u32[]{:S(2)}, u32[]{:S(2)}) collective-permute-start(bf16[4,5,40,256]{3,2,1,0:T(8,128)(2,1)S(1)} %head_conv.3), channel_id=1, source_target_pairs={{0,8},{8,0},{16,24},{24,16},{1,9},{9,1},{17,25},{25,17},{2,10},{10... | collective-permute-start | bytes 1228808 | tf_op jit(solution)/shard_map/ppermute | solution.py:535
  15.0 5.8 %collective-permute-start.7 = (bf16[5,40,256]{2,1,0:T(8,128)(2,1)S(1)}, bf16[5,40,256]{2,1,0:T(8,128)(2,1)S(1)}, u32[]{:S(2)}, u32[]{:S(2)}) collective-permute-start(bf16[5,40,256]{2,1,0:T(8,128)(2,1)S(1)} %get-tuple-element.59), channel_id=1, source_target_pairs={{0,16},{8,24},{16,0},{24,8},{1,17},{9,25},{17,1},{25,9},{2,18},{10... | collective-permute-start | bytes 307208 | tf_op jit(solution)/shard_map/ppermute | solution.py:535
  16.7 5.8 %collective-permute-start.5 = (bf16[5,40,256]{2,1,0:T(8,128)(2,1)S(1)}, bf16[5,40,256]{2,1,0:T(8,128)(2,1)S(1)}, u32[]{:S(2)}, u32[]{:S(2)}) collective-permute-start(bf16[5,40,256]{2,1,0:T(8,128)(2,1)S(1)} %get-tuple-element.53), channel_id=1, source_target_pairs={{0,16},{8,24},{16,0},{24,8},{1,17},{9,25},{17,1},{25,9},{2,18},{10... | collective-permute-start | bytes 307208 | tf_op jit(solution)/shard_map/ppermute | solution.py:535
  17.5 5.0 %collective-permute-start.6 = (bf16[2,88,256]{2,1,0:T(8,128)(2,1)S(1)}, bf16[2,88,256]{2,1,0:T(8,128)(2,1)S(1)}, u32[]{:S(2)}, u32[]{:S(2)}) collective-permute-start(bf16[2,88,256]{2,1,0:T(8,128)(2,1)S(1)} %get-tuple-element.54), channel_id=1, source_target_pairs={{0,4},{4,0},{1,5},{5,1},{2,6},{6,2},{3,7},{7,3},{8,12},{12,8},{9,1... | collective-permute-start | bytes 270344 | tf_op jit(solution)/shard_map/ppermute | solution.py:535
  20.8 5.6 %collective-permute-start.9 = (bf16[5,40,256]{2,1,0:T(8,128)(2,1)S(1)}, bf16[5,40,256]{2,1,0:T(8,128)(2,1)S(1)}, u32[]{:S(2)}, u32[]{:S(2)}) collective-permute-start(bf16[5,40,256]{2,1,0:T(8,128)(2,1)S(1)} %chip_sum.3.refs_1_), channel_id=1, source_target_pairs={{0,4},{4,0},{1,5},{5,1},{2,6},{6,2},{3,7},{7,3},{8,12},{12,8},{9,1... | collective-permute-start | bytes 307208 | tf_op jit(solution)/shard_map/ppermute | solution.py:535
  22.6 4.9 %collective-permute-start.8 = (bf16[5,40,256]{2,1,0:T(8,128)(2,1)S(1)}, bf16[5,40,256]{2,1,0:T(8,128)(2,1)S(1)}, u32[]{:S(2)}, u32[]{:S(2)}) collective-permute-start(bf16[5,40,256]{2,1,0:T(8,128)(2,1)S(1)} %chip_sum.2.refs_0_), channel_id=1, source_target_pairs={{0,4},{4,0},{1,5},{5,1},{2,6},{6,2},{3,7},{7,3},{8,12},{12,8},{9,1... | collective-permute-start | bytes 307208 | tf_op jit(solution)/shard_map/ppermute | solution.py:535
  28.8 3.5 %collective-permute-start.11 = (bf16[1152,128]{1,0:T(8,128)(2,1)S(1)}, bf16[1152,128]{1,0:T(8,128)(2,1)S(1)}, u32[]{:S(2)}, u32[]{:S(2)}) collective-permute-start(bf16[1152,128]{1,0:T(8,128)(2,1)S(1)} %get-tuple-element.70), channel_id=1, source_target_pairs={{0,8},{8,0},{16,24},{24,16},{1,9},{9,1},{17,25},{25,17},{2,10},{10... | collective-permute-start | bytes 884744 | tf_op jit(solution)/shard_map/ppermute | solution.py:535
  30.8 19.1 %copy-start = (bf16[9,128,256]{2,1,0:T(8,128)(2,1)S(1)}, bf16[9,128,256]{2,1,0:T(8,128)(2,1)}, u32[]{:S(2)}) copy-start(bf16[9,128,256]{2,1,0:T(8,128)(2,1)} %w_first_ref.1) | copy-start | bytes 1769476
  30.8 1.6 %collective-permute-start.10 = (bf16[576,128]{1,0:T(8,128)(2,1)S(1)}, bf16[576,128]{1,0:T(8,128)(2,1)S(1)}, u32[]{:S(2)}, u32[]{:S(2)}) collective-permute-start(bf16[576,128]{1,0:T(8,128)(2,1)S(1)} %get-tuple-element.66), channel_id=1, source_target_pairs={{0,8},{8,0},{16,24},{24,16},{1,9},{9,1},{17,25},{25,17},{2,10},{10... | collective-permute-start | bytes 442376 | tf_op jit(solution)/shard_map/ppermute | solution.py:535
  32.5 11.6 %collective-permute-start.12 = (bf16[432,128]{1,0:T(8,128)(2,1)S(1)}, bf16[432,128]{1,0:T(8,128)(2,1)S(1)}, u32[]{:S(2)}, u32[]{:S(2)}) collective-permute-start(bf16[432,128]{1,0:T(8,128)(2,1)S(1)} %get-tuple-element.72), channel_id=1, source_target_pairs={{2,0},{3,1},{0,2},{1,3},{6,4},{7,5},{4,6},{5,7},{10,8},{11,9},{8,1... | collective-permute-start | bytes 331784 | tf_op jit(solution)/shard_map/ppermute | solution.py:821
  34.5 9.6 %collective-permute-start.13 = (bf16[432,128]{1,0:T(8,128)(2,1)S(1)}, bf16[432,128]{1,0:T(8,128)(2,1)S(1)}, u32[]{:S(2)}, u32[]{:S(2)}) collective-permute-start(bf16[432,128]{1,0:T(8,128)(2,1)S(1)} %get-tuple-element.73), channel_id=1, source_target_pairs={{3,0},{2,1},{1,2},{0,3},{7,4},{6,5},{5,6},{4,7},{11,8},{10,9},{9,1... | collective-permute-start | bytes 331784 | tf_op jit(solution)/shard_map/ppermute | solution.py:821
  35.9 9.0 %collective-permute-start.14 = (bf16[432,128]{1,0:T(8,128)(2,1)S(1)}, bf16[432,128]{1,0:T(8,128)(2,1)S(1)}, u32[]{:S(2)}, u32[]{:S(2)}) collective-permute-start(bf16[432,128]{1,0:T(8,128)(2,1)S(1)} %get-tuple-element.74), channel_id=1, source_target_pairs={{1,0},{0,1},{3,2},{2,3},{5,4},{4,5},{7,6},{6,7},{9,8},{8,9},{11,10... | collective-permute-start | bytes 331784 | tf_op jit(solution)/shard_map/ppermute | solution.py:821
  45.0 4.8 %collective-permute-start.15 = (bf16[432,128]{1,0:T(8,128)(2,1)S(1)}, bf16[432,128]{1,0:T(8,128)(2,1)S(1)}, u32[]{:S(2)}, u32[]{:S(2)}) collective-permute-start(bf16[432,128]{1,0:T(8,128)(2,1)S(1)} %share.1.refs_0_), channel_id=1, source_target_pairs={{0,16},{8,24},{16,0},{24,8},{1,17},{9,25},{17,1},{25,9},{2,18},{10... | collective-permute-start | bytes 331784 | tf_op jit(solution)/shard_map/ppermute | solution.py:535
  49.8 1.4 %collective-permute-start.16 = (bf16[432,128]{1,0:T(8,128)(2,1)S(1)}, bf16[432,128]{1,0:T(8,128)(2,1)S(1)}, u32[]{:S(2)}, u32[]{:S(2)}) collective-permute-start(bf16[432,128]{1,0:T(8,128)(2,1)S(1)} %chips.1.mine_ref), channel_id=1, source_target_pairs={{0,8},{8,0},{16,24},{24,16},{1,9},{9,1},{17,25},{25,17},{2,10},{10... | collective-permute-start | bytes 331784 | tf_op jit(solution)/shard_map/ppermute | solution.py:535

commit v5 on v4

--- a/solution.py
+++ b/solution.py
@@ -141,7 +141,7 @@
     return run("stage", stage_kernel, shapes, list(arrays), [pltpu.SemaphoreType.DMA((len(arrays),))], far=True, flops=1 << 30)
 
 
-def heads_kernel(other_core, other_chip, samples, grads_ref, low_ref, high_ref, weights_ref, out_ref, wide, shifted, total):
+def heads_kernel(other_core, other_chip, sample, samples, grads_ref, low_ref, high_ref, weights_ref, out_ref, wide, shifted, total):
     heads, batch, height, breadth, _ = grads_ref.shape
     slots, _, kept, depth = out_ref.shape
     pitch = kept + 16
@@ -149,8 +149,11 @@
     core, chip = core_and_chip()
     core = 1 - core if other_core else core
     for slot in range(slots):
-        group = 1 - chip if other_chip != (slot >= samples) else chip
-        b = (2 * group + core) * samples + slot % samples
+        if sample is None:
+            group, s = 1 - chip if other_chip else chip, slot
+        else:
+            group, s = 1 - chip if slot % 2 else chip, sample + slot // 2
+        b = (2 * group + core) * samples + s
         low = low_ref[b].astype(F32)
         high = high_ref[b].astype(F32)
         for r in range(height):
@@ -185,14 +188,14 @@
         out_ref[...] = total[:, pl.ds(1 - lax.axis_index("lat"), height + 1)].astype(BF)
 
 
-def head_conv(other_core, other_chip, head_grads, low, high, head_weights, slots, rows):
+def head_conv(other_core, other_chip, sample, head_grads, low, high, head_weights, slots, rows):
     samples = head_grads.shape[1] // lax.axis_size("lead")
     heads, batch, height, breadth, _ = head_grads.shape
     depth = head_weights.shape[2]
     kept = breadth + 2 * EDGE
     return run(
         "head_conv",
-        functools.partial(heads_kernel, other_core, other_chip, samples),
+        functools.partial(heads_kernel, other_core, other_chip, sample, samples),
         [jax.ShapeDtypeStruct((slots, rows, kept, depth), BF)],
         [head_grads, low, high, head_weights],
         [
@@ -649,150 +652,163 @@
     )
 
 
-def put_slopes(slope, near_ref, far_ref, halo_ref, width, first_cell):
-    samples, height, kept, _ = near_ref.shape
+def put_slopes(sample, slope, near_ref, far_ref, halo_ref, width, first_cell):
+    _, height, kept, _ = near_ref.shape
     lat = lax.axis_index("lat")
     other = pl.ds(height * (1 - lat), height)
-    slope[:, pl.ds(height * lat, height)] = near_ref[...]
-    slope[:, other] = far_ref[...]
-    for s in range(samples):
-        beside = gelu_slope(halo_ref[s].astype(F32))
-        for side in range(2):
-            for col in range(width):
-                here = first_cell + (side * width + col) * height
-                at = kept - EDGE + col if side else EDGE - width + col
-                slope[s, other, at, :] = beside[here : here + height]
-
-
-def globe_kernel(near_ref, far_ref, halo_ref, *refs):
-    cat_ref, moved_ref, latent, slope, wide = refs[-5:]
-    samples = near_ref.shape[0]
-    totals, lines = refs[:samples], refs[samples : 2 * samples]
-    rows, kept, depth = totals[0].shape
+    slope[pl.ds(height * lat, height)] = near_ref[sample]
+    slope[other] = far_ref[sample]
+    beside = gelu_slope(halo_ref[sample, : 6 * height].astype(F32))
+    for side in range(2):
+        for col in range(width):
+            here = first_cell + (side * width + col) * height
+            at = kept - EDGE + col if side else EDGE - width + col
+            slope[other, at, :] = beside[here : here + height]
+
+
+def globe_kernel(sample, near_ref, far_ref, halo_ref, total_ref, line_ref, cat_ref, moved_ref, latent, slope, wide):
+    rows, kept, depth = total_ref.shape
     height = rows - 1
     tall = 2 * height
     breadth = kept - 2 * EDGE
     lat = lax.axis_index("lat")
     own = 8 + EDGE
     latent[...] = jnp.zeros(latent.shape, F32)
-    for s in range(samples):
-        latent[s, pl.ds((height - 1) * lat, rows)] = totals[s][...].astype(F32)
-        latent[s, pl.ds((height - 1) * (1 - lat), rows)] += lines[s][...].astype(F32)
-    put_slopes(slope, near_ref, far_ref, halo_ref, 2, 0)
-    wide[:, :, 8 : 8 + kept, :] = (latent[...] * slope[...]).astype(BF).astype(F32)
+    latent[pl.ds((height - 1) * lat, rows)] = total_ref[...].astype(F32)
+    latent[pl.ds((height - 1) * (1 - lat), rows)] += line_ref[...].astype(F32)
+    put_slopes(sample, slope, near_ref, far_ref, halo_ref, 2, 0)
+    wide[:, 8 : 8 + kept, :] = (latent[...] * slope[...]).astype(BF).astype(F32)
     for v in STEPS:
         lanes = slice((v + 1) * depth, (v + 2) * depth)
-        cat_ref[:, 1 : 1 + tall, :, lanes] = wide[:, :, 8 - v : 8 - v + kept, :].astype(BF)
-        moved_ref[v + 1, :, 1 : 1 + tall] = wide[:, :, own - v : own - v + breadth, :].astype(BF)
+        cat_ref[1 : 1 + tall, :, lanes] = wide[:, 8 - v : 8 - v + kept, :].astype(BF)
+        moved_ref[v + 1, 1 : 1 + tall] = wide[:, own - v : own - v + breadth, :].astype(BF)
     for row in (0, tall + 1):
-        cat_ref[:, row] = jnp.zeros(cat_ref.shape[:1] + cat_ref.shape[2:], BF)
-        moved_ref[:, :, row] = jnp.zeros(moved_ref.shape[:2] + moved_ref.shape[3:], BF)
-
-
-def globe(totals, lines, near, far, halo):
-    samples, (rows, kept, depth) = len(totals), totals[0].shape
+        cat_ref[row] = jnp.zeros(cat_ref.shape[1:], BF)
+        moved_ref[:, row] = jnp.zeros(moved_ref.shape[:1] + moved_ref.shape[2:], BF)
+
+
+def globe(sample, total, line, near, far, halo):
+    rows, kept, depth = total.shape
     tall, breadth = 2 * (rows - 1), kept - 2 * EDGE
     return run(
         "latent_grads",
-        globe_kernel,
+        functools.partial(globe_kernel, sample),
         [
-            jax.ShapeDtypeStruct((samples, tall + 2, kept, 3 * depth), BF),
-            jax.ShapeDtypeStruct((3, samples, tall + 2, breadth, depth), BF),
+            jax.ShapeDtypeStruct((tall + 2, kept, 3 * depth), BF),
+            jax.ShapeDtypeStruct((3, tall + 2, breadth, depth), BF),
         ],
-        [near, far, halo, *totals, *lines],
+        [near, far, halo, total, line],
         [
-            pltpu.VMEM((samples, tall, kept, depth), F32),
-            pltpu.VMEM((samples, tall, kept, depth), F32),
-            pltpu.VMEM((samples, tall, kept + 24, depth), F32),
+            pltpu.VMEM((tall, kept, depth), F32),
+            pltpu.VMEM((tall, kept, depth), F32),
+            pltpu.VMEM((tall, kept + 24, depth), F32),
         ],
     )
 
 
-def band_rows(norm_factor, left_all, moved_ref, mine_ref, other_ref):
-    channels, cells = left_all.shape
-    _, samples, padded, breadth, depth = moved_ref.shape
+def band_rows(norm_factor, lefts, moved, mine_ref, other_ref):
+    channels, cells = lefts[0].shape
+    _, padded, breadth, depth = moved[0].shape
     tall = padded - 2
     lat = lax.axis_index("lat")
     core, _ = core_and_chip()
     half = channels // 2
 
-    def put(left, u, v, start, size):
-        right = moved_ref[v + 1, :, pl.ds(1 - u, tall)].reshape(cells, depth)
-        part = dot_plain(left, right) * norm_factor
-        lower, upper = part[:, :LANES], part[:, LANES:]
+    def put(parts, u, v, start, size):
+        total = None
+        for left, ref in zip(parts, moved):
+            part = dot_plain(left, ref[v + 1, pl.ds(1 - u, tall)].reshape(cells, depth))
+            total = part if total is None else total + part
+        total = total * norm_factor
+        lower, upper = total[:, :LANES], total[:, LANES:]
         here = pl.ds(pl.multiple_of(start, half), size)
         mine_ref[here, :] = jnp.where(core == 0, lower, upper).astype(BF)
         other_ref[here, :] = jnp.where(core == 0, upper, lower).astype(BF)
 
     for j in range(4):
         (u0, v0), (u1, v1) = (divmod(k, 3) for k in (j, 5 + j))
-        put(left_all, u0 - 1 + lat * (u1 - u0), v0 - 1 + lat * (v1 - v0), lat * half + j * channels, channels)
-    put(jnp.where(lat == 0, left_all[:half], left_all[half:]), 0, 0, (1 - lat) * 4 * channels, half)
-
-
-def second_band_kernel(norm_factor, moved_ref, act_ref, mine_ref, other_ref):
-    band_rows(norm_factor, act_ref[...], moved_ref, mine_ref, other_ref)
-
-
-def first_band_kernel(norm_factor, cat_ref, near_ref, far_ref, halo_ref, input_ref, weights_ref, moved_ref, mine_ref, other_ref, slope, wide, cells):
-    samples, padded, broad, triple = cat_ref.shape
-    tall, kept, depth = padded - 2, broad, triple // 3
-    height = tall // 2
+        put(lefts, u0 - 1 + lat * (u1 - u0), v0 - 1 + lat * (v1 - v0), lat * half + j * channels, channels)
+    put([jnp.where(lat == 0, left[:half], left[half:]) for left in lefts], 0, 0, (1 - lat) * 4 * channels, half)
+
+
+def second_band_kernel(norm_factor, act_ref, *refs):
+    moved, (mine_ref, other_ref) = refs[:-2], refs[-2:]
+    cells = act_ref.shape[1] // len(moved)
+    lefts = [act_ref[:, s * cells : (s + 1) * cells] for s in range(len(moved))]
+    band_rows(norm_factor, lefts, moved, mine_ref, other_ref)
+
+
+def second_band(norm_factor, act, moved):
+    half = jax.ShapeDtypeStruct((9 * act.shape[0] // 2, LANES), BF)
+    return run("second_weight_grads", functools.partial(second_band_kernel, norm_factor), [half, half], [act, *moved])
+
+
+def first_kernel(sample, cat_ref, near_ref, far_ref, halo_ref, weights_ref, moved_ref, slope, wide):
+    padded, kept, triple = cat_ref.shape
+    tall, depth = padded - 2, triple // 3
     breadth = kept - 2 * EDGE
-    lat = lax.axis_index("lat")
     own = 8 + EDGE
-    put_slopes(slope, near_ref, far_ref, halo_ref, 1, 4 * height)
+    put_slopes(sample, slope, near_ref, far_ref, halo_ref, 1, 2 * tall)
     linear = None
     for u in STEPS:
         weights = jnp.concatenate([weights_ref[3 * (u + 1) + (v + 1)] for v in STEPS], axis=1)
-        part = dot_last(cat_ref[:, 1 - u : 1 - u + tall].reshape(samples * tall * broad, triple), weights)
+        part = dot_last(cat_ref[1 - u : 1 - u + tall].reshape(tall * kept, triple), weights)
         linear = part if linear is None else linear + part
-    linear = linear.reshape(samples, tall, broad, depth)
-    wide[:, :, 8 : 8 + kept, :] = (linear * slope[...]).astype(BF).astype(F32)
+    wide[:, 8 : 8 + kept, :] = (linear.reshape(tall, kept, depth) * slope[...]).astype(BF).astype(F32)
     for v in STEPS:
-        moved_ref[v + 1, :, 1 : 1 + tall] = wide[:, :, own - v : own - v + breadth, :].astype(BF)
+        moved_ref[v + 1, 1 : 1 + tall] = wide[:, own - v : own - v + breadth, :].astype(BF)
     for row in (0, tall + 1):
-        moved_ref[:, :, row] = jnp.zeros(moved_ref.shape[:2] + moved_ref.shape[3:], BF)
+        moved_ref[:, row] = jnp.zeros(moved_ref.shape[:1] + moved_ref.shape[2:], BF)
+
+
+def first_grad(sample, cat, near, far, halo, w_second):
+    padded, kept, triple = cat.shape
+    tall, depth = padded - 2, triple // 3
+    return run(
+        "second_conv",
+        functools.partial(first_kernel, sample),
+        [jax.ShapeDtypeStruct((3, padded, kept - 2 * EDGE, depth), BF)],
+        [cat, near, far, halo, w_second],
+        [pltpu.VMEM((tall, kept, depth), F32), pltpu.VMEM((tall, kept + 16, depth), F32)],
+    )[0]
+
+
+def first_band_kernel(norm_factor, halo_ref, input_ref, *refs):
+    moved, (mine_ref, other_ref, cells) = refs[:-3], refs[-3:]
+    samples, height, breadth, channels = input_ref.shape
+    lat = lax.axis_index("lat")
     cells[:, pl.ds(height * lat, height)] = input_ref[...].astype(F32)
     half = height // 2
     for part in range(2):
         values = halo_ref[:, 6 * height :, part * LANES : (part + 1) * LANES].astype(F32)
         cells[:, pl.ds(height * (1 - lat) + part * half, half)] = values.reshape(samples, half, breadth, LANES)
-    band_rows(norm_factor, cells[...].reshape(samples * tall * breadth, LANES).T.astype(BF), moved_ref, mine_ref, other_ref)
-
-
-def second_band(norm_factor, moved, act):
-    half = jax.ShapeDtypeStruct((9 * act.shape[0] // 2, LANES), BF)
-    return run("second_weight_grads", functools.partial(second_band_kernel, norm_factor), [half, half], [moved, act])
-
-
-def first_band(norm_factor, cat, near, far, halo, encoder_input, w_second):
-    samples, padded, broad, triple = cat.shape
-    tall, kept, depth = padded - 2, broad, triple // 3
-    breadth = kept - 2 * EDGE
-    half = jax.ShapeDtypeStruct((9 * encoder_input.shape[3] // 2, LANES), BF)
-    return run(
-        "encoder_grads",
+    lefts = [cells[s].reshape(2 * height * breadth, channels).T.astype(BF) for s in range(samples)]
+    band_rows(norm_factor, lefts, moved, mine_ref, other_ref)
+
+
+def first_band(norm_factor, halo, encoder_input, moved):
+    samples, height, breadth, channels = encoder_input.shape
+    half = jax.ShapeDtypeStruct((9 * channels // 2, LANES), BF)
+    return run(
+        "first_weight_grads",
         functools.partial(first_band_kernel, norm_factor),
-        [jax.ShapeDtypeStruct((3, samples, padded, breadth, depth), BF), half, half],
-        [cat, near, far, halo, encoder_input, w_second],
-        [
-            pltpu.VMEM((samples, tall, kept, depth), F32),
-            pltpu.VMEM((samples, tall, kept + 16, depth), F32),
-            pltpu.VMEM((samples, tall, breadth, LANES), F32),
-        ],
-    )
-
-
-def input_band_kernel(moved_ref, w_first_ref, out_ref):
-    samples, height, breadth, channels = out_ref.shape
-    depth = moved_ref.shape[4]
+        [half, half],
+        [halo, encoder_input, *moved],
+        [pltpu.VMEM((samples, 2 * height, breadth, channels), F32)],
+    )
+
+
+def input_band_kernel(w_first_ref, *refs):
+    moved, out_ref = refs[:-1], refs[-1]
+    _, height, breadth, channels = out_ref.shape
+    depth = moved[0].shape[3]
     lat = lax.axis_index("lat")
     total = None
     for u in STEPS:
         weights = jnp.concatenate([w_first_ref[3 * (u + 1) + (v + 1)] for v in STEPS], axis=1)
-        left = [moved_ref[v + 1, :, pl.ds(height * lat + 1 - u, height)].reshape(-1, depth) for v in STEPS]
-        part = dot_last(jnp.concatenate(left, axis=1), weights)
+        here = pl.ds(height * lat + 1 - u, height)
+        left = [jnp.concatenate([ref[v + 1, here].reshape(-1, depth) for v in STEPS], axis=1) for ref in moved]
+        part = dot_last(jnp.concatenate(left, axis=0), weights)
         total = part if total is None else total + part
     out_ref[...] = total.astype(BF).reshape(out_ref.shape)
 
@@ -841,25 +857,32 @@
         slots=2 * samples,
         rows=height + 1,
     )
-    got = swap(heads_of(True, False), "lead", 1)
+    everyone = range(samples)
+    got = swap(heads_of(True, False, 0), "lead", 1)
+    part_shape = jax.ShapeDtypeStruct(got.shape[1:], BF)
+    parts = run("core_sum", core_sum_kernel, [part_shape] * (2 * samples), [heads_of(False, False, 0), got])
+    own, cross = parts[0::2], [swap(part, "lead", 2) for part in parts[1::2]]
     near_second, near_first, halo = near_parts(pre_second, pre_first, encoder_input, low, high)
-    mine = heads_of(False, False)
     halo = swap(halo, "lat", 1)
-    part_shape = jax.ShapeDtypeStruct(mine.shape[1:], BF)
-    parts = run("core_sum", core_sum_kernel, [part_shape] * (2 * samples), [mine, got])
-    cross = [swap(part, "lead", 2) for part in parts[samples:]]
-    cross[0], halo = lax.optimization_barrier((cross[0], halo))
-    totals = [run("chip_sum", sum_kernel, [part_shape], [parts[s], cross[s]])[0] for s in range(samples)]
+    cross[-1], halo = lax.optimization_barrier((cross[-1], halo))
+    totals = [run("chip_sum", sum_kernel, [part_shape], [own[s], cross[s]])[0] for s in everyone]
     lines = [swap(total, "lat", 1) for total in totals]
     far_second, far_first, act = far_parts(pre_first, *tiles)
 
-    cat, moved = globe(totals, lines, near_second, far_second, halo)
-    second_mine, second_other = second_band(norm_factor, moved, act)
+    moved_second, moved_first = [], []
+    for s in everyone:
+        cat, moved = globe(s, totals[s], lines[s], near_second, far_second, halo)
+        moved_second.append(moved)
+        if s < samples - 1:
+            moved_first.append(first_grad(s, cat, near_first, far_first, halo, w_second))
+            near_second, moved_first[s] = lax.optimization_barrier((near_second, moved_first[s]))
+    second_mine, second_other = second_band(norm_factor, act, moved_second)
     second_got = swap(second_other, "lead", 1)
-    moved_first, first_mine, first_other = first_band(norm_factor, cat, near_first, far_first, halo, encoder_input, w_second)
+    moved_first.append(first_grad(samples - 1, cat, near_first, far_first, halo, w_second))
+    first_mine, first_other = first_band(norm_factor, halo, encoder_input, moved_first)
     first_got = swap(first_other, "lead", 1)
     input_grad = run(
-        "input_conv", input_band_kernel, [jax.ShapeDtypeStruct(encoder_input.shape, BF)], [moved_first, w_first]
+        "input_conv", input_band_kernel, [jax.ShapeDtypeStruct(encoder_input.shape, BF)], [w_first, *moved_first]
     )[0]
 
     blocks = [t.reshape(columns, -1, LANES) for t in (first_mine, first_got, second_mine, second_got)]
@@ -898,14 +921,14 @@
 
     steps = [1, -1]
     heads_of = functools.partial(head_conv, head_grads=head_grads, high=high, head_weights=head_weights, slots=samples, rows=height + 2)
-    got_cross = swap(heads_of(True, True, low=low), "lead", 1)
-    got_own = swap(heads_of(True, False, low=low), "lead", 1)
-    cross, *angles = spread_cross(heads_of(False, True, low=low), got_cross, len(steps))
+    got_cross = swap(heads_of(True, True, None, low=low), "lead", 1)
+    got_own = swap(heads_of(True, False, None, low=low), "lead", 1)
+    cross, *angles = spread_cross(heads_of(False, True, None, low=low), got_cross, len(steps))
     low_later, cross, *angles = lax.optimization_barrier((low, cross, *angles))
     cross = swap(cross, "lead", 2)
     angles = [corner(angle, step) for angle, step in zip(angles, steps)]
     second, first, slope_second, slope_first, act, cells_in = saved(pre_second, pre_first, encoder_input, low, high)
-    own, *lines = spread_own(heads_of(False, False, low=low_later), got_own, second, first, len(steps))
+    own, *lines = spread_own(heads_of(False, False, None, low=low_later), got_own, second, first, len(steps))
     lines = [swap(line, "lat", 1) if step is None else around(line, "lat", step, False) for line, step in zip(lines, steps)]
     strips = [strip for pair in zip(lines, angles) for strip in pair]
 

time: 52.2 us -> 51 us (0.977)
  waiting for transfers between devices: 18.7 us -> 17.6 us
    ppermute x12, waiting for transfers between devices: 9.18 us -> 8.08 us  [swap(): return lax.ppermute(array, axis, [(i, i ^ flip) for i in range(count)])]
    pallas_call x17 -> x20, Pallas kernels: 11.9 us -> 11.8 us  [run(): pl.pallas_call(kernel, name=name, out_shape=out_shape, in_specs=specs, ou...]
  transfers between devices with their start and end apart: 17 -> 17, of which waited for: 10 -> 9; matrix products, arithmetic and copies ran while one was open for 0% -> 0% of each run, Pallas kernels for 16% -> 17%
where the time goes in v5:
time: 51 us; the launch traced here: 50.9 us
  starting transfers between devices  20.7 us (41%)
  waiting for transfers between devices  17.6 us (35%)
  Pallas kernels  11.8 us (23%)
  between operations  0.79 us (2%)
    ppermute x12, starting transfers between devices, swap(): return lax.ppermute(array, axis, [(i, i ^ flip) for i in range(count)])  12.7 us
    pallas_call x20, Pallas kernels, run(): pl.pallas_call(kernel, name=name, out_shape=out_shape, in_specs=specs, ou...  11.8 us
    ppermute x3, waiting for transfers between devices, to_partner(): lax.ppermute(array, 'lon', [(partner(i, step, count), i) for i in range(c...  8.58 us
    ppermute x12, waiting for transfers between devices, swap(): return lax.ppermute(array, axis, [(i, i ^ flip) for i in range(count)])  8.08 us
    ppermute x2, starting transfers between devices, around(): return lax.ppermute(array, axis, pairs)  4.15 us
    ppermute x3, starting transfers between devices, to_partner(): lax.ppermute(array, 'lon', [(partner(i, step, count), i) for i in range(c...  3.89 us
  transfers between devices with their start and end apart: 17, of which 9 were waited for; matrix products, arithmetic and copies ran while one was open for 0% of the time, Pallas kernels for 17%

profile of v5, /device:TPU:0, one launch (start us, length us, event | category | flops | bytes accessed | tf_op | source)
XLA Modules:
  0.0 50.9 jit_solution(7112980321076772960)
XLA Ops:
  0.6 3.0 %collective-permute-start.3 = (bf16[2,4,32,256]{3,2,1,0:T(8,128)(2,1)}, bf16[2,4,32,256]{3,2,1,0:T(8,128)(2,1)S(1)}, u32[]{:S(2)}, u32[]{:S(2)}) collective-permute-start(bf16[2,4,32,256]{3,2,1,0:T(8,128)(2,1)} %first_far.1), channel_id=1, source_target_pairs={{0,4},{4,0},{1,5},{5,1},{2,6},{6,2},{3,7},{7,3},{8,12},{12,8},{9,1... | collective-permute-start | bytes 393224 | tf_op jit(solution)/shard_map/ppermute | solution.py:538
  3.7 0.1 collective-permute-start.2
  3.7 1.3 %pack_columns.1 = (bf16[10,24,128]{2,1,0:T(8,128)(2,1)S(1)}, bf16[10,24,128]{2,1,0:T(8,128)(2,1)S(1)}) custom-call(bf16[2,8,4,32,128]{4,3,2,1,0:T(8,128)(2,1)} %grads_far.1, bf16[2,4,32,256]{3,2,1,0:T(8,128)(2,1)} %second_far.1, bf16[2,4,32,256]{3,2,1,0:T(8,128)(2,1)} %first_far.1), custom_call_target="tpu_custom_call" | custom-call | flops 1 | bytes 1 | tf_op jit(solution)/shard_map/pack_columns/pallas_call | solution.py:50
  5.0 2.1 %collective-permute-start = (bf16[10,24,128]{2,1,0:T(8,128)(2,1)S(1)}, bf16[10,24,128]{2,1,0:T(8,128)(2,1)S(1)}, u32[]{:S(2)}, u32[]{:S(2)}) collective-permute-start(bf16[10,24,128]{2,1,0:T(8,128)(2,1)S(1)} %get-tuple-element.46), channel_id=1, source_target_pairs={{0,1},{1,2},{2,3},{3,0},{4,5},{5,6},{6,7},{7,4},{8,9},{9,10},{10,1... | collective-permute-start | bytes 184328 | tf_op jit(solution)/shard_map/ppermute | solution.py:544
  7.1 2.1 %collective-permute-start.1 = (bf16[10,24,128]{2,1,0:T(8,128)(2,1)S(1)}, bf16[10,24,128]{2,1,0:T(8,128)(2,1)S(1)}, u32[]{:S(2)}, u32[]{:S(2)}) collective-permute-start(bf16[10,24,128]{2,1,0:T(8,128)(2,1)S(1)} %get-tuple-element.47), channel_id=1, source_target_pairs={{0,3},{1,0},{2,1},{3,2},{4,7},{5,4},{6,5},{7,6},{8,11},{9,8},{10,9... | collective-permute-start | bytes 184328 | tf_op jit(solution)/shard_map/ppermute | solution.py:544
  9.2 1.9 %stage.1 = (bf16[2,8,4,32,128]{4,3,2,1,0:T(8,128)(2,1)S(1)}, bf16[2,9,256,128]{3,2,1,0:T(8,128)(2,1)S(1)}, bf16[9,256,256]{2,1,0:T(8,128)(2,1)S(1)}, bf16[2,4,32...) custom-call(bf16[2,8,4,32,128]{4,3,2,1,0:T(8,128)(2,1)} %grads_far.1, ...), custom_call_target="tpu_custom_call" | custom-call | flops 1 | bytes 1 | tf_op jit(solution)/shard_map/stage/pallas_call | solution.py:50
  11.0 0.9 %collective-permute-done.low_ref = bf16[10,24,128]{2,1,0:T(8,128)(2,1)S(1)} collective-permute-done((bf16[10,24,128]{2,1,0:T(8,128)(2,1)S(1)}, bf16[10,24,128]{2,1,0:T(8,128)(2,1)S(1)}, u32[]{:S(2)}, u32[]{:S(2)}) %collective-permute-start) | collective-permute-done | bytes 61472 | tf_op jit(solution)/shard_map/ppermute | solution.py:544
  11.9 0.0 collective-permute-done.1.high_ref
  12.0 0.0 collective-permute-done.3.tile_first
  12.0 0.0 collective-permute-done.2.tile_second
  12.0 1.1 %head_conv.3 = bf16[4,5,40,256]{3,2,1,0:T(8,128)(2,1)S(1)} custom-call(bf16[2,8,4,32,128]{4,3,2,1,0:T(8,128)(2,1)S(1)} %get-tuple-element.54.grads_ref, bf16[10,24,128]{2,1,0:T(8,128)(2,1)S(1)} %collective-permute-done.low_ref, bf16[10,24,128]{2,1,0:T(8,128)(2,1)S(1)} %collective-permute-done.1.high_ref, ...), custom_call_target="tpu_custom_call" | custom-call | flops 1 | bytes 1 | tf_op jit(solution)/shard_map/head_conv/pallas_call | solution.py:50
  13.1 0.1 collective-permute-start.4
  13.2 1.1 %head_conv.2.mine_ref = bf16[4,5,40,256]{3,2,1,0:T(8,128)(2,1)S(1)} custom-call(bf16[2,8,4,32,128]{4,3,2,1,0:T(8,128)(2,1)S(1)} %get-tuple-element.54.grads_ref, bf16[10,24,128]{2,1,0:T(8,128)(2,1)S(1)} %collective-permute-done.low_ref, bf16[10,24,128]{2,1,0:T(8,128)(2,1)S(1)} %collective-permute-done.1.high_ref, ...), custom_call_target="tpu_custom_call" | custom-call | flops 1 | bytes 1 | tf_op jit(solution)/shard_map/head_conv/pallas_call | solution.py:50
  14.3 0.6 %collective-permute-done.4.got_ref = bf16[4,5,40,256]{3,2,1,0:T(8,128)(2,1)S(1)} collective-permute-done((bf16[4,5,40,256]{3,2,1,0:T(8,128)(2,1)S(1)}, bf16[4,5,40,256]{3,2,1,0:T(8,128)(2,1)S(1)}, u32[]{:S(2)}, u32[]{:S(2)}) %collective-permute-start.4) | collective-permute-done | bytes 409632 | tf_op jit(solution)/shard_map/ppermute | solution.py:538
  14.9 0.1 core_sum.1
  15.0 1.7 %collective-permute-start.7 = (bf16[5,40,256]{2,1,0:T(8,128)(2,1)S(1)}, bf16[5,40,256]{2,1,0:T(8,128)(2,1)S(1)}, u32[]{:S(2)}, u32[]{:S(2)}) collective-permute-start(bf16[5,40,256]{2,1,0:T(8,128)(2,1)S(1)} %get-tuple-element.60), channel_id=1, source_target_pairs={{0,16},{8,24},{16,0},{24,8},{1,17},{9,25},{17,1},{25,9},{2,18},{10... | collective-permute-start | bytes 307208 | tf_op jit(solution)/shard_map/ppermute | solution.py:538
  16.7 0.4 collective-permute-start.5
  17.1 0.4 near_parts.1
  17.5 1.7 %collective-permute-start.6 = (bf16[2,88,256]{2,1,0:T(8,128)(2,1)S(1)}, bf16[2,88,256]{2,1,0:T(8,128)(2,1)S(1)}, u32[]{:S(2)}, u32[]{:S(2)}) collective-permute-start(bf16[2,88,256]{2,1,0:T(8,128)(2,1)S(1)} %get-tuple-element.57), channel_id=1, source_target_pairs={{0,4},{4,0},{1,5},{5,1},{2,6},{6,2},{3,7},{7,3},{8,12},{12,8},{9,1... | collective-permute-start | bytes 270344 | tf_op jit(solution)/shard_map/ppermute | solution.py:538
  19.3 1.5 %collective-permute-done.7.refs_1_ = bf16[5,40,256]{2,1,0:T(8,128)(2,1)S(1)} collective-permute-done((bf16[5,40,256]{2,1,0:T(8,128)(2,1)S(1)}, bf16[5,40,256]{2,1,0:T(8,128)(2,1)S(1)}, u32[]{:S(2)}, u32[]{:S(2)}) %collective-permute-start.7) | collective-permute-done | bytes 102432 | tf_op jit(solution)/shard_map/ppermute | solution.py:538
  20.8 1.7 %collective-permute-start.8 = (bf16[5,40,256]{2,1,0:T(8,128)(2,1)S(1)}, bf16[5,40,256]{2,1,0:T(8,128)(2,1)S(1)}, u32[]{:S(2)}, u32[]{:S(2)}) collective-permute-start(bf16[5,40,256]{2,1,0:T(8,128)(2,1)S(1)} %chip_sum.2.total_ref), channel_id=1, source_target_pairs={{0,4},{4,0},{1,5},{5,1},{2,6},{6,2},{3,7},{7,3},{8,12},{12,8},{9,1... | collective-permute-start | bytes 307208 | tf_op jit(solution)/shard_map/ppermute | solution.py:538
  22.6 0.0 collective-permute-done.6.halo_ref
  22.6 1.5 %collective-permute-start.9 = (bf16[5,40,256]{2,1,0:T(8,128)(2,1)S(1)}, bf16[5,40,256]{2,1,0:T(8,128)(2,1)S(1)}, u32[]{:S(2)}, u32[]{:S(2)}) collective-permute-start(bf16[5,40,256]{2,1,0:T(8,128)(2,1)S(1)} %chip_sum.3.total_ref), channel_id=1, source_target_pairs={{0,4},{4,0},{1,5},{5,1},{2,6},{6,2},{3,7},{7,3},{8,12},{12,8},{9,1... | collective-permute-start | bytes 307208 | tf_op jit(solution)/shard_map/ppermute | solution.py:538
  24.1 0.6 %far_parts.1 = (f32[2,4,40,256]{3,2,1,0:T(8,128)S(1)}, f32[2,4,40,256]{3,2,1,0:T(8,128)S(1)}, bf16[256,512]{1,0:T(8,128)(2,1)S(1)}) custom-call(bf16[2,4,32,256]{3,2,1,0:T(8,128)(2,1)S(1)} %get-tuple-element.44.first_ref, bf16[2,4,32,256]{3,2,1,0:T(8,128)(2,1)S(1)} %collective-permute-done.2.tile_second, ...), custom_call_target="tpu_custom_call" | custom-call | flops 1 | bytes 1 | tf_op jit(solution)/shard_map/far_parts/pallas_call | solution.py:50
  24.7 1.7 %collective-permute-done.8.line_ref = bf16[5,40,256]{2,1,0:T(8,128)(2,1)S(1)} collective-permute-done((bf16[5,40,256]{2,1,0:T(8,128)(2,1)S(1)}, bf16[5,40,256]{2,1,0:T(8,128)(2,1)S(1)}, u32[]{:S(2)}, u32[]{:S(2)}) %collective-permute-start.8) | collective-permute-done | bytes 102432 | tf_op jit(solution)/shard_map/ppermute | solution.py:538
  26.4 0.4 latent_grads.2
  26.8 0.7 %second_conv.2.refs_0_ = bf16[3,10,32,256]{3,2,1,0:T(8,128)(2,1)S(1)} custom-call(bf16[10,40,768]{2,1,0:T(8,128)(2,1)S(1)} %get-tuple-element.61.cat_ref, f32[2,4,40,256]{3,2,1,0:T(8,128)S(1)} %get-tuple-element.62.near_ref, f32[2,4,40,256]{3,2,1,0:T(8,128)S(1)} %get-tuple-element.63.far_ref, bf16[2,88,256]{2,1,0:T(8,128)(2,1)S(1)} %collective-permute-done.6.halo_ref, ...), custom_call_target="tpu_custom_call" | custom-call | flops 1 | bytes 1 | tf_op jit(solution)/shard_map/second_conv/pallas_call | solution.py:50
  27.5 0.4 latent_grads.3
  27.9 0.5 second_weight_grads.1
  28.4 0.1 collective-permute-start.11
  28.5 0.7 %second_conv.3.refs_1_ = bf16[3,10,32,256]{3,2,1,0:T(8,128)(2,1)S(1)} custom-call(bf16[10,40,768]{2,1,0:T(8,128)(2,1)S(1)} %get-tuple-element.69.cat_ref, f32[2,4,40,256]{3,2,1,0:T(8,128)S(1)} %get-tuple-element.62.near_ref, f32[2,4,40,256]{3,2,1,0:T(8,128)S(1)} %get-tuple-element.63.far_ref, bf16[2,88,256]{2,1,0:T(8,128)(2,1)S(1)} %collective-permute-done.6.halo_ref, ...), custom_call_target="tpu_custom_call" | custom-call | flops 1 | bytes 1 | tf_op jit(solution)/shard_map/second_conv/pallas_call | solution.py:50
  29.2 0.4 first_weight_grads.1
  29.6 0.0 copy-start
  29.6 0.6 %collective-permute-start.10 = (bf16[576,128]{1,0:T(8,128)(2,1)S(1)}, bf16[576,128]{1,0:T(8,128)(2,1)S(1)}, u32[]{:S(2)}, u32[]{:S(2)}) collective-permute-start(bf16[576,128]{1,0:T(8,128)(2,1)S(1)} %get-tuple-element.71), channel_id=1, source_target_pairs={{0,8},{8,0},{16,24},{24,16},{1,9},{9,1},{17,25},{25,17},{2,10},{10... | collective-permute-start | bytes 442376 | tf_op jit(solution)/shard_map/ppermute | solution.py:538
  30.2 1.0 %collective-permute-done.10 = bf16[576,128]{1,0:T(8,128)(2,1)S(1)} collective-permute-done((bf16[576,128]{1,0:T(8,128)(2,1)S(1)}, bf16[576,128]{1,0:T(8,128)(2,1)S(1)}, u32[]{:S(2)}, u32[]{:S(2)}) %collective-permute-start.10) | collective-permute-done | bytes 147488 | tf_op jit(solution)/shard_map/ppermute | solution.py:538
  31.2 0.1 blocks.1
  31.3 2.0 %collective-permute-start.12 = (bf16[432,128]{1,0:T(8,128)(2,1)S(1)}, bf16[432,128]{1,0:T(8,128)(2,1)S(1)}, u32[]{:S(2)}, u32[]{:S(2)}) collective-permute-start(bf16[432,128]{1,0:T(8,128)(2,1)S(1)} %get-tuple-element.78), channel_id=1, source_target_pairs={{2,0},{3,1},{0,2},{1,3},{6,4},{7,5},{4,6},{5,7},{10,8},{11,9},{8,1... | collective-permute-start | bytes 331784 | tf_op jit(solution)/shard_map/ppermute | solution.py:837
  33.3 1.5 %collective-permute-start.13 = (bf16[432,128]{1,0:T(8,128)(2,1)S(1)}, bf16[432,128]{1,0:T(8,128)(2,1)S(1)}, u32[]{:S(2)}, u32[]{:S(2)}) collective-permute-start(bf16[432,128]{1,0:T(8,128)(2,1)S(1)} %get-tuple-element.79), channel_id=1, source_target_pairs={{3,0},{2,1},{1,2},{0,3},{7,4},{6,5},{5,6},{4,7},{11,8},{10,9},{9,1... | collective-permute-start | bytes 331784 | tf_op jit(solution)/shard_map/ppermute | solution.py:837
  34.8 0.4 collective-permute-start.14
  35.2 7.7 %collective-permute-done.12.refs_1_ = bf16[432,128]{1,0:T(8,128)(2,1)S(1)} collective-permute-done((bf16[432,128]{1,0:T(8,128)(2,1)S(1)}, bf16[432,128]{1,0:T(8,128)(2,1)S(1)}, u32[]{:S(2)}, u32[]{:S(2)}) %collective-permute-start.12) | collective-permute-done | bytes 110624 | tf_op jit(solution)/shard_map/ppermute | solution.py:837
  43.0 0.8 %collective-permute-done.14.refs_3_ = bf16[432,128]{1,0:T(8,128)(2,1)S(1)} collective-permute-done((bf16[432,128]{1,0:T(8,128)(2,1)S(1)}, bf16[432,128]{1,0:T(8,128)(2,1)S(1)}, u32[]{:S(2)}, u32[]{:S(2)}) %collective-permute-start.14) | collective-permute-done | bytes 110624 | tf_op jit(solution)/shard_map/ppermute | solution.py:837
  43.8 0.1 share.1.refs_0_
  43.8 1.7 %collective-permute-start.15 = (bf16[432,128]{1,0:T(8,128)(2,1)S(1)}, bf16[432,128]{1,0:T(8,128)(2,1)S(1)}, u32[]{:S(2)}, u32[]{:S(2)}) collective-permute-start(bf16[432,128]{1,0:T(8,128)(2,1)S(1)} %share.1.refs_0_), channel_id=1, source_target_pairs={{0,16},{8,24},{16,0},{24,8},{1,17},{9,25},{17,1},{25,9},{2,18},{10... | collective-permute-start | bytes 331784 | tf_op jit(solution)/shard_map/ppermute | solution.py:538
  45.6 3.1 %collective-permute-done.15.refs_1_ = bf16[432,128]{1,0:T(8,128)(2,1)S(1)} collective-permute-done((bf16[432,128]{1,0:T(8,128)(2,1)S(1)}, bf16[432,128]{1,0:T(8,128)(2,1)S(1)}, u32[]{:S(2)}, u32[]{:S(2)}) %collective-permute-start.15) | collective-permute-done | bytes 110624 | tf_op jit(solution)/shard_map/ppermute | solution.py:538
  48.7 0.1 collective-permute-start.16
  48.8 1.1 %input_conv.1 = bf16[2,4,32,128]{3,2,1,0:T(8,128)(2,1)} custom-call(bf16[9,128,256]{2,1,0:T(8,128)(2,1)S(1)} %copy-done, bf16[3,10,32,256]{3,2,1,0:T(8,128)(2,1)S(1)} %second_conv.2.refs_0_, bf16[3,10,32,256]{3,2,1,0:T(8,128)(2,1)S(1)} %second_conv.3.refs_1_), custom_call_target="tpu_custom_call" | custom-call | flops 1 | bytes 1 | tf_op jit(solution)/shard_map/input_conv/pallas_call | solution.py:50
  49.9 0.2 collective-permute-done.16.other_ref
  50.1 0.8 %cores.1 = (f32[288,128]{1,0:T(8,128)}, f32[576,128]{1,0:T(8,128)}) custom-call(bf16[432,128]{1,0:T(8,128)(2,1)S(1)} %chips.1.mine_ref, bf16[432,128]{1,0:T(8,128)(2,1)S(1)} %collective-permute-done.16.other_ref), custom_call_target="tpu_custom_call" | custom-call | flops 1 | bytes 1 | tf_op jit(solution)/shard_map/cores/pallas_call | solution.py:50
  (8 shorter events, 0.1 us)
Async XLA Ops:
  0.6 11.3 %collective-permute-start.3 = (bf16[2,4,32,256]{3,2,1,0:T(8,128)(2,1)}, bf16[2,4,32,256]{3,2,1,0:T(8,128)(2,1)S(1)}, u32[]{:S(2)}, u32[]{:S(2)}) collective-permute-start(bf16[2,4,32,256]{3,2,1,0:T(8,128)(2,1)} %first_far.1), channel_id=1, source_target_pairs={{0,4},{4,0},{1,5},{5,1},{2,6},{6,2},{3,7},{7,3},{8,12},{12,8},{9,1... | collective-permute-start | bytes 393224 | tf_op jit(solution)/shard_map/ppermute | solution.py:538
  3.7 8.3 %collective-permute-start.2 = (bf16[2,4,32,256]{3,2,1,0:T(8,128)(2,1)}, bf16[2,4,32,256]{3,2,1,0:T(8,128)(2,1)S(1)}, u32[]{:S(2)}, u32[]{:S(2)}) collective-permute-start(bf16[2,4,32,256]{3,2,1,0:T(8,128)(2,1)} %second_far.1), channel_id=1, source_target_pairs={{0,4},{4,0},{1,5},{5,1},{2,6},{6,2},{3,7},{7,3},{8,12},{12,8},{9,1... | collective-permute-start | bytes 393224 | tf_op jit(solution)/shard_map/ppermute | solution.py:538
  5.0 6.9 %collective-permute-start = (bf16[10,24,128]{2,1,0:T(8,128)(2,1)S(1)}, bf16[10,24,128]{2,1,0:T(8,128)(2,1)S(1)}, u32[]{:S(2)}, u32[]{:S(2)}) collective-permute-start(bf16[10,24,128]{2,1,0:T(8,128)(2,1)S(1)} %get-tuple-element.46), channel_id=1, source_target_pairs={{0,1},{1,2},{2,3},{3,0},{4,5},{5,6},{6,7},{7,4},{8,9},{9,10},{10,1... | collective-permute-start | bytes 184328 | tf_op jit(solution)/shard_map/ppermute | solution.py:544
  7.1 4.9 %collective-permute-start.1 = (bf16[10,24,128]{2,1,0:T(8,128)(2,1)S(1)}, bf16[10,24,128]{2,1,0:T(8,128)(2,1)S(1)}, u32[]{:S(2)}, u32[]{:S(2)}) collective-permute-start(bf16[10,24,128]{2,1,0:T(8,128)(2,1)S(1)} %get-tuple-element.47), channel_id=1, source_target_pairs={{0,3},{1,0},{2,1},{3,2},{4,7},{5,4},{6,5},{7,6},{8,11},{9,8},{10,9... | collective-permute-start | bytes 184328 | tf_op jit(solution)/shard_map/ppermute | solution.py:544
  13.1 1.8 %collective-permute-start.4 = (bf16[4,5,40,256]{3,2,1,0:T(8,128)(2,1)S(1)}, bf16[4,5,40,256]{3,2,1,0:T(8,128)(2,1)S(1)}, u32[]{:S(2)}, u32[]{:S(2)}) collective-permute-start(bf16[4,5,40,256]{3,2,1,0:T(8,128)(2,1)S(1)} %head_conv.3), channel_id=1, source_target_pairs={{0,8},{8,0},{16,24},{24,16},{1,9},{9,1},{17,25},{25,17},{2,10},{10... | collective-permute-start | bytes 1228808 | tf_op jit(solution)/shard_map/ppermute | solution.py:538
  15.0 5.8 %collective-permute-start.7 = (bf16[5,40,256]{2,1,0:T(8,128)(2,1)S(1)}, bf16[5,40,256]{2,1,0:T(8,128)(2,1)S(1)}, u32[]{:S(2)}, u32[]{:S(2)}) collective-permute-start(bf16[5,40,256]{2,1,0:T(8,128)(2,1)S(1)} %get-tuple-element.60), channel_id=1, source_target_pairs={{0,16},{8,24},{16,0},{24,8},{1,17},{9,25},{17,1},{25,9},{2,18},{10... | collective-permute-start | bytes 307208 | tf_op jit(solution)/shard_map/ppermute | solution.py:538
  16.7 5.9 %collective-permute-start.5 = (bf16[5,40,256]{2,1,0:T(8,128)(2,1)S(1)}, bf16[5,40,256]{2,1,0:T(8,128)(2,1)S(1)}, u32[]{:S(2)}, u32[]{:S(2)}) collective-permute-start(bf16[5,40,256]{2,1,0:T(8,128)(2,1)S(1)} %get-tuple-element.56), channel_id=1, source_target_pairs={{0,16},{8,24},{16,0},{24,8},{1,17},{9,25},{17,1},{25,9},{2,18},{10... | collective-permute-start | bytes 307208 | tf_op jit(solution)/shard_map/ppermute | solution.py:538
  17.5 5.0 %collective-permute-start.6 = (bf16[2,88,256]{2,1,0:T(8,128)(2,1)S(1)}, bf16[2,88,256]{2,1,0:T(8,128)(2,1)S(1)}, u32[]{:S(2)}, u32[]{:S(2)}) collective-permute-start(bf16[2,88,256]{2,1,0:T(8,128)(2,1)S(1)} %get-tuple-element.57), channel_id=1, source_target_pairs={{0,4},{4,0},{1,5},{5,1},{2,6},{6,2},{3,7},{7,3},{8,12},{12,8},{9,1... | collective-permute-start | bytes 270344 | tf_op jit(solution)/shard_map/ppermute | solution.py:538
  20.8 5.6 %collective-permute-start.8 = (bf16[5,40,256]{2,1,0:T(8,128)(2,1)S(1)}, bf16[5,40,256]{2,1,0:T(8,128)(2,1)S(1)}, u32[]{:S(2)}, u32[]{:S(2)}) collective-permute-start(bf16[5,40,256]{2,1,0:T(8,128)(2,1)S(1)} %chip_sum.2.total_ref), channel_id=1, source_target_pairs={{0,4},{4,0},{1,5},{5,1},{2,6},{6,2},{3,7},{7,3},{8,12},{12,8},{9,1... | collective-permute-start | bytes 307208 | tf_op jit(solution)/shard_map/ppermute | solution.py:538
  22.6 4.9 %collective-permute-start.9 = (bf16[5,40,256]{2,1,0:T(8,128)(2,1)S(1)}, bf16[5,40,256]{2,1,0:T(8,128)(2,1)S(1)}, u32[]{:S(2)}, u32[]{:S(2)}) collective-permute-start(bf16[5,40,256]{2,1,0:T(8,128)(2,1)S(1)} %chip_sum.3.total_ref), channel_id=1, source_target_pairs={{0,4},{4,0},{1,5},{5,1},{2,6},{6,2},{3,7},{7,3},{8,12},{12,8},{9,1... | collective-permute-start | bytes 307208 | tf_op jit(solution)/shard_map/ppermute | solution.py:538
  28.4 2.8 %collective-permute-start.11 = (bf16[1152,128]{1,0:T(8,128)(2,1)S(1)}, bf16[1152,128]{1,0:T(8,128)(2,1)S(1)}, u32[]{:S(2)}, u32[]{:S(2)}) collective-permute-start(bf16[1152,128]{1,0:T(8,128)(2,1)S(1)} %get-tuple-element.76), channel_id=1, source_target_pairs={{0,8},{8,0},{16,24},{24,16},{1,9},{9,1},{17,25},{25,17},{2,10},{10... | collective-permute-start | bytes 884744 | tf_op jit(solution)/shard_map/ppermute | solution.py:538
  29.6 19.1 %copy-start = (bf16[9,128,256]{2,1,0:T(8,128)(2,1)S(1)}, bf16[9,128,256]{2,1,0:T(8,128)(2,1)}, u32[]{:S(2)}) copy-start(bf16[9,128,256]{2,1,0:T(8,128)(2,1)} %w_first_ref.1) | copy-start | bytes 1769476
  29.6 1.6 %collective-permute-start.10 = (bf16[576,128]{1,0:T(8,128)(2,1)S(1)}, bf16[576,128]{1,0:T(8,128)(2,1)S(1)}, u32[]{:S(2)}, u32[]{:S(2)}) collective-permute-start(bf16[576,128]{1,0:T(8,128)(2,1)S(1)} %get-tuple-element.71), channel_id=1, source_target_pairs={{0,8},{8,0},{16,24},{24,16},{1,9},{9,1},{17,25},{25,17},{2,10},{10... | collective-permute-start | bytes 442376 | tf_op jit(solution)/shard_map/ppermute | solution.py:538
  31.3 11.6 %collective-permute-start.12 = (bf16[432,128]{1,0:T(8,128)(2,1)S(1)}, bf16[432,128]{1,0:T(8,128)(2,1)S(1)}, u32[]{:S(2)}, u32[]{:S(2)}) collective-permute-start(bf16[432,128]{1,0:T(8,128)(2,1)S(1)} %get-tuple-element.78), channel_id=1, source_target_pairs={{2,0},{3,1},{0,2},{1,3},{6,4},{7,5},{4,6},{5,7},{10,8},{11,9},{8,1... | collective-permute-start | bytes 331784 | tf_op jit(solution)/shard_map/ppermute | solution.py:837
  33.3 9.6 %collective-permute-start.13 = (bf16[432,128]{1,0:T(8,128)(2,1)S(1)}, bf16[432,128]{1,0:T(8,128)(2,1)S(1)}, u32[]{:S(2)}, u32[]{:S(2)}) collective-permute-start(bf16[432,128]{1,0:T(8,128)(2,1)S(1)} %get-tuple-element.79), channel_id=1, source_target_pairs={{3,0},{2,1},{1,2},{0,3},{7,4},{6,5},{5,6},{4,7},{11,8},{10,9},{9,1... | collective-permute-start | bytes 331784 | tf_op jit(solution)/shard_map/ppermute | solution.py:837
  34.8 9.0 %collective-permute-start.14 = (bf16[432,128]{1,0:T(8,128)(2,1)S(1)}, bf16[432,128]{1,0:T(8,128)(2,1)S(1)}, u32[]{:S(2)}, u32[]{:S(2)}) collective-permute-start(bf16[432,128]{1,0:T(8,128)(2,1)S(1)} %get-tuple-element.80), channel_id=1, source_target_pairs={{1,0},{0,1},{3,2},{2,3},{5,4},{4,5},{7,6},{6,7},{9,8},{8,9},{11,10... | collective-permute-start | bytes 331784 | tf_op jit(solution)/shard_map/ppermute | solution.py:837
  43.8 4.8 %collective-permute-start.15 = (bf16[432,128]{1,0:T(8,128)(2,1)S(1)}, bf16[432,128]{1,0:T(8,128)(2,1)S(1)}, u32[]{:S(2)}, u32[]{:S(2)}) collective-permute-start(bf16[432,128]{1,0:T(8,128)(2,1)S(1)} %share.1.refs_0_), channel_id=1, source_target_pairs={{0,16},{8,24},{16,0},{24,8},{1,17},{9,25},{17,1},{25,9},{2,18},{10... | collective-permute-start | bytes 331784 | tf_op jit(solution)/shard_map/ppermute | solution.py:538
  48.7 1.4 %collective-permute-start.16 = (bf16[432,128]{1,0:T(8,128)(2,1)S(1)}, bf16[432,128]{1,0:T(8,128)(2,1)S(1)}, u32[]{:S(2)}, u32[]{:S(2)}) collective-permute-start(bf16[432,128]{1,0:T(8,128)(2,1)S(1)} %chips.1.mine_ref), channel_id=1, source_target_pairs={{0,8},{8,0},{16,24},{24,16},{1,9},{9,1},{17,25},{25,17},{2,10},{10... | collective-permute-start | bytes 331784 | tf_op jit(solution)/shard_map/ppermute | solution.py:538

commit v6 on v5

--- a/solution.py
+++ b/solution.py
@@ -207,6 +207,109 @@
     )[0]
 
 
+def inside_kernel(samples, grads_ref, weights_ref, total_ref, wide, shifted):
+    heads, _, height, breadth, _ = grads_ref.shape
+    slots, _, kept, depth = total_ref.shape
+    pitch = kept + 16
+    own = 8 + EDGE
+    core, chip = core_and_chip()
+    blank = jnp.zeros((height, LANES), F32)
+    for slot in range(slots):
+        group, s = 1 - chip if slot % 2 else chip, slot // 2
+        b = (2 * group + 1 - core) * samples + s
+        for h in range(heads):
+            for r in range(height):
+                at = (slot * height + r) * pitch + own
+                wide[h, at : at + breadth, :] = grads_ref[h, b, r].astype(F32)
+            for col in range(3):
+                at = slot * height * pitch + own + col
+                wide[h, pl.ds(at - 3, height, stride=pitch), :] = blank
+                wide[h, pl.ds(at + breadth, height, stride=pitch), :] = blank
+            for v in STEPS:
+                starts = [(slot * height + r) * pitch + 8 - v for r in range(height)]
+                moved = jnp.concatenate([wide[h, at : at + kept, :] for at in starts], axis=0).astype(BF)
+                lane = ((v + 1) * heads + h) * LANES
+                shifted[slot * height * kept : (slot + 1) * height * kept, lane : lane + LANES] = moved
+    total_ref[:, height:, :, :] = jnp.zeros((slots, 2, kept, depth), F32)
+    for u in STEPS:
+        weights = jnp.concatenate(
+            [weights_ref[h, 3 * (u + 1) + (v + 1)] for v in STEPS for h in range(heads)], axis=1
+        )
+        part = dot_last(shifted[...], weights).reshape(slots, height, kept, depth)
+        if u == -1:
+            total_ref[:, :height] = part
+        else:
+            total_ref[:, 1 + u : 1 + u + height] += part
+
+
+def edges_kernel(samples, inside_ref, low_ref, high_ref, weights_ref, out_ref, wide, shifted, total):
+    slots, rows, kept, depth = inside_ref.shape
+    height, heads, pitch = rows - 2, weights_ref.shape[0], 24
+    core, chip = core_and_chip()
+    wide[...] = jnp.zeros(wide.shape, F32)
+    for side, packed_ref in ((0, low_ref), (1, high_ref)):
+        for slot in range(slots):
+            group, s = 1 - chip if slot % 2 else chip, slot // 2
+            packed = packed_ref[(2 * group + 1 - core) * samples + s].astype(F32)
+            first = (side * slots + slot) * height
+            for h in range(heads):
+                for col in range(3):
+                    here = (col * 2 + h) * height
+                    at = first * pitch + 9 + 3 * side + col
+                    wide[h, pl.ds(at, height, stride=pitch), :] = packed[here : here + height]
+                for v in STEPS:
+                    starts = [(first + r) * pitch + 8 - v for r in range(height)]
+                    moved = jnp.concatenate([wide[h, at : at + 8, :] for at in starts], axis=0).astype(BF)
+                    lane = ((v + 1) * heads + h) * LANES
+                    shifted[first * 8 : (first + height) * 8, lane : lane + LANES] = moved
+    for u in STEPS:
+        weights = jnp.concatenate(
+            [weights_ref[h, 3 * (u + 1) + (v + 1)] for v in STEPS for h in range(heads)], axis=1
+        )
+        part = dot_last(shifted[...], weights).reshape(2, slots, height, 8, depth)
+        if u == -1:
+            total[:, :, :height] = part
+            total[:, :, height:] = jnp.zeros((2, slots, 2, 8, depth), F32)
+        else:
+            total[:, :, 1 + u : 1 + u + height] += part
+    here = pl.ds(1 - lax.axis_index("lat"), height + 1)
+    out_ref[:, :, 8 : kept - 8] = inside_ref[:, here, 8 : kept - 8].astype(BF)
+    for side, columns in enumerate((slice(0, 8), slice(kept - 8, kept))):
+        out_ref[:, :, columns] = (inside_ref[:, here, columns] + total[side, :, here]).astype(BF)
+
+
+def inside_conv(head_grads, head_weights, slots):
+    samples = head_grads.shape[1] // lax.axis_size("lead")
+    heads, _, height, breadth, _ = head_grads.shape
+    kept = breadth + 2 * EDGE
+    return run(
+        "head_conv_inside",
+        functools.partial(inside_kernel, samples),
+        [jax.ShapeDtypeStruct((slots, height + 2, kept, head_weights.shape[2]), F32)],
+        [head_grads, head_weights],
+        [
+            pltpu.VMEM((heads, slots * height * (kept + 16), LANES), F32),
+            pltpu.VMEM((slots * height * kept, 3 * heads * LANES), BF),
+        ],
+    )[0]
+
+
+def edges_conv(inside, low, high, head_weights):
+    slots, rows, kept, depth = inside.shape
+    samples, heads, height = slots // 2, head_weights.shape[0], rows - 2
+    return run(
+        "head_conv_edges",
+        functools.partial(edges_kernel, samples),
+        [jax.ShapeDtypeStruct((slots, rows - 1, kept, depth), BF)],
+        [inside, low, high, head_weights],
+        [
+            pltpu.VMEM((heads, 2 * slots * height * 24, LANES), F32),
+            pltpu.VMEM((2 * slots * height * 8, 3 * heads * LANES), BF),
+            pltpu.VMEM((2, slots, rows, 8, depth), F32),
+        ],
+    )[0]
+
+
 def saved_kernel(second_ref, first_ref, input_ref, low_ref, high_ref, second_out, first_out, slope_second, slope_first, act_out, input_out, wide):
     samples, height, breadth, depth = second_ref.shape
     kept = breadth + 2 * EDGE
@@ -847,7 +950,8 @@
     head_grads, head_weights, w_second, pre_second, pre_first, encoder_input = stage(
         head_grads, head_weights, w_second, pre_second, pre_first, encoder_input
     )
-    low, high, *tiles = lax.optimization_barrier((low, high, *tiles))
+    inside = inside_conv(head_grads, head_weights, 2 * samples)
+    low, high, inside, *tiles = lax.optimization_barrier((low, high, inside, *tiles))
     heads_of = functools.partial(
         head_conv,
         head_grads=head_grads,
@@ -858,11 +962,13 @@
         rows=height + 1,
     )
     everyone = range(samples)
-    got = swap(heads_of(True, False, 0), "lead", 1)
+    got = swap(edges_conv(inside, low, high, head_weights), "lead", 1)
     part_shape = jax.ShapeDtypeStruct(got.shape[1:], BF)
     parts = run("core_sum", core_sum_kernel, [part_shape] * (2 * samples), [heads_of(False, False, 0), got])
-    own, cross = parts[0::2], [swap(part, "lead", 2) for part in parts[1::2]]
+    own, cross = parts[0::2], list(parts[1::2])
     near_second, near_first, halo = near_parts(pre_second, pre_first, encoder_input, low, high)
+    cross[-1], halo = lax.optimization_barrier((cross[-1], halo))
+    cross = [swap(part, "lead", 2) for part in cross]
     halo = swap(halo, "lat", 1)
     cross[-1], halo = lax.optimization_barrier((cross[-1], halo))
     totals = [run("chip_sum", sum_kernel, [part_shape], [own[s], cross[s]])[0] for s in everyone]
@@ -889,7 +995,7 @@
     rows = blocks[0].shape[1]
     share_shape = jax.ShapeDtypeStruct((3 * rows, LANES), BF)
     shares = run("blocks", blocks_kernel, [share_shape] * columns, blocks)
-    parts = [to_partner(shares[step], step) for step in [*range(2, columns), 1]]
+    parts = [to_partner(shares[step], step) for step in ((2, 1, 3) if columns == 4 else range(1, columns))]
     share = run("share", sum_kernel, [share_shape], [shares[0], *parts])[0]
     both = run("chips", sum_kernel, [share_shape], [share, swap(share, "lead", 2)])[0]
     result_first, result_second = run(
@@ -948,7 +1054,7 @@
     rows = blocks[0].shape[2]
     share_shape = jax.ShapeDtypeStruct((2, rows, LANES), BF)
     shares = run("own_band", own_band_kernel, [share_shape] * columns, blocks + [first_came, second_came])
-    parts = [to_partner(shares[step], step) for step in [*range(2, columns), 1]]
+    parts = [to_partner(shares[step], step) for step in ((2, 1, 3) if columns == 4 else range(1, columns))]
     share = run("share", sum_kernel, [share_shape], [shares[0], *parts])[0]
     both = run("chips", chips_kernel, [jax.ShapeDtypeStruct((3, rows, LANES), BF)], [share, swap(share, "lead", 2)])[0]
     result_first, result_second = run(

time: 51 us -> 50.1 us (0.982); the launches traced: 50.9 us -> 49.4 us
  waiting for transfers between devices: 17.6 us -> 14.3 us
  starting transfers between devices: 20.7 us -> 21.9 us
    ppermute x3, waiting for transfers between devices: 8.58 us -> 7.18 us  [to_partner(): lax.ppermute(array, 'lon', [(partner(i, step, count), i) for i in range(c...]
    ppermute x12, waiting for transfers between devices: 8.08 us -> 7.16 us  [swap(): return lax.ppermute(array, axis, [(i, i ^ flip) for i in range(count)])]
    ppermute x2, waiting for transfers between devices: 0.91 us -> 0.01 us  [around(): return lax.ppermute(array, axis, pairs)]
    ppermute x12, starting transfers between devices: 12.7 us -> 13.3 us  [swap(): return lax.ppermute(array, axis, [(i, i ^ flip) for i in range(count)])]
    ppermute x3, starting transfers between devices: 3.89 us -> 4.47 us  [to_partner(): lax.ppermute(array, 'lon', [(partner(i, step, count), i) for i in range(c...]
    pallas_call x20 -> x21, Pallas kernels: 11.8 us -> 12.3 us  [run(): pl.pallas_call(kernel, name=name, out_shape=out_shape, in_specs=specs, ou...]
  transfers between devices with their start and end apart: 17 -> 17, of which waited for: 9 -> 9; matrix products, arithmetic and copies ran while one was open for 0% -> 0% of each run, Pallas kernels for 17% -> 20%
where the time goes in v6:
time: 50.1 us; the launch traced here: 49.4 us
  starting transfers between devices  21.9 us (44%)
  waiting for transfers between devices  14.3 us (29%)
  Pallas kernels  12.3 us (25%)
  between operations  0.82 us (2%)
    ppermute x12, starting transfers between devices, swap(): return lax.ppermute(array, axis, [(i, i ^ flip) for i in range(count)])  13.3 us
    pallas_call x21, Pallas kernels, run(): pl.pallas_call(kernel, name=name, out_shape=out_shape, in_specs=specs, ou...  12.3 us
    ppermute x3, waiting for transfers between devices, to_partner(): lax.ppermute(array, 'lon', [(partner(i, step, count), i) for i in range(c...  7.18 us
    ppermute x12, waiting for transfers between devices, swap(): return lax.ppermute(array, axis, [(i, i ^ flip) for i in range(count)])  7.16 us
    ppermute x3, starting transfers between devices, to_partner(): lax.ppermute(array, 'lon', [(partner(i, step, count), i) for i in range(c...  4.47 us
    ppermute x2, starting transfers between devices, around(): return lax.ppermute(array, axis, pairs)  4.15 us
  transfers between devices with their start and end apart: 17, of which 9 were waited for; matrix products, arithmetic and copies ran while one was open for 0% of the time, Pallas kernels for 20%

profile of v6, /device:TPU:0, one launch (start us, length us, event | category | flops | bytes accessed | tf_op | source)
XLA Modules:
  0.0 49.4 jit_solution(8730495229019659496)
XLA Ops:
  0.6 3.0 %collective-permute-start.3 = (bf16[2,4,32,256]{3,2,1,0:T(8,128)(2,1)}, bf16[2,4,32,256]{3,2,1,0:T(8,128)(2,1)S(1)}, u32[]{:S(2)}, u32[]{:S(2)}) collective-permute-start(bf16[2,4,32,256]{3,2,1,0:T(8,128)(2,1)} %first_far.1), channel_id=1, source_target_pairs={{0,4},{4,0},{1,5},{5,1},{2,6},{6,2},{3,7},{7,3},{8,12},{12,8},{9,1... | collective-permute-start | bytes 393224 | tf_op jit(solution)/shard_map/ppermute | solution.py:641
  3.7 0.1 collective-permute-start.2
  3.7 1.3 %pack_columns.1 = (bf16[10,24,128]{2,1,0:T(8,128)(2,1)S(1)}, bf16[10,24,128]{2,1,0:T(8,128)(2,1)S(1)}) custom-call(bf16[2,8,4,32,128]{4,3,2,1,0:T(8,128)(2,1)} %grads_far.1, bf16[2,4,32,256]{3,2,1,0:T(8,128)(2,1)} %second_far.1, bf16[2,4,32,256]{3,2,1,0:T(8,128)(2,1)} %first_far.1), custom_call_target="tpu_custom_call" | custom-call | flops 1 | bytes 1 | tf_op jit(solution)/shard_map/pack_columns/pallas_call | solution.py:50
  5.0 2.1 %collective-permute-start = (bf16[10,24,128]{2,1,0:T(8,128)(2,1)S(1)}, bf16[10,24,128]{2,1,0:T(8,128)(2,1)S(1)}, u32[]{:S(2)}, u32[]{:S(2)}) collective-permute-start(bf16[10,24,128]{2,1,0:T(8,128)(2,1)S(1)} %get-tuple-element.49), channel_id=1, source_target_pairs={{0,1},{1,2},{2,3},{3,0},{4,5},{5,6},{6,7},{7,4},{8,9},{9,10},{10,1... | collective-permute-start | bytes 184328 | tf_op jit(solution)/shard_map/ppermute | solution.py:647
  7.1 2.1 %collective-permute-start.1 = (bf16[10,24,128]{2,1,0:T(8,128)(2,1)S(1)}, bf16[10,24,128]{2,1,0:T(8,128)(2,1)S(1)}, u32[]{:S(2)}, u32[]{:S(2)}) collective-permute-start(bf16[10,24,128]{2,1,0:T(8,128)(2,1)S(1)} %get-tuple-element.50), channel_id=1, source_target_pairs={{0,3},{1,0},{2,1},{3,2},{4,7},{5,4},{6,5},{7,6},{8,11},{9,8},{10,9... | collective-permute-start | bytes 184328 | tf_op jit(solution)/shard_map/ppermute | solution.py:647
  9.2 1.9 %stage.1 = (bf16[2,8,4,32,128]{4,3,2,1,0:T(8,128)(2,1)S(1)}, bf16[2,9,256,128]{3,2,1,0:T(8,128)(2,1)S(1)}, bf16[9,256,256]{2,1,0:T(8,128)(2,1)S(1)}, bf16[2,4,32...) custom-call(bf16[2,8,4,32,128]{4,3,2,1,0:T(8,128)(2,1)} %grads_far.1, ...), custom_call_target="tpu_custom_call" | custom-call | flops 1 | bytes 1 | tf_op jit(solution)/shard_map/stage/pallas_call | solution.py:50
  11.0 1.0 %head_conv_inside.1.inside_ref = f32[4,6,40,256]{3,2,1,0:T(8,128)S(1)} custom-call(bf16[2,8,4,32,128]{4,3,2,1,0:T(8,128)(2,1)S(1)} %get-tuple-element.51.grads_ref, bf16[2,9,256,128]{3,2,1,0:T(8,128)(2,1)S(1)} %get-tuple-element.52.weights_ref), custom_call_target="tpu_custom_call" | custom-call | flops 1 | bytes 1 | tf_op jit(solution)/shard_map/head_conv_inside/pallas_call | solution.py:50
  12.1 0.0 collective-permute-done.low_ref
  12.1 0.0 collective-permute-done.2.tile_second
  12.1 0.6 %head_conv_edges.1 = bf16[4,5,40,256]{3,2,1,0:T(8,128)(2,1)S(1)} custom-call(f32[4,6,40,256]{3,2,1,0:T(8,128)S(1)} %head_conv_inside.1.inside_ref, bf16[10,24,128]{2,1,0:T(8,128)(2,1)S(1)} %collective-permute-done.low_ref, bf16[10,24,128]{2,1,0:T(8,128)(2,1)S(1)} %collective-permute-done.1.high_ref, bf16[2,9,256,128]{3,2,1,0:T(8,128)(2,1)S(1)} %get-tuple-element.52.weights_ref), custom_call_target="tpu_custom_call" | custom-call | flops 1 | bytes 1 | tf_op jit(solution)/shard_map/head_conv_edges/pallas_call | solution.py:50
  12.7 0.1 collective-permute-start.4
  12.8 1.1 %head_conv.1.mine_ref = bf16[4,5,40,256]{3,2,1,0:T(8,128)(2,1)S(1)} custom-call(bf16[2,8,4,32,128]{4,3,2,1,0:T(8,128)(2,1)S(1)} %get-tuple-element.51.grads_ref, bf16[10,24,128]{2,1,0:T(8,128)(2,1)S(1)} %collective-permute-done.low_ref, bf16[10,24,128]{2,1,0:T(8,128)(2,1)S(1)} %collective-permute-done.1.high_ref, ...), custom_call_target="tpu_custom_call" | custom-call | flops 1 | bytes 1 | tf_op jit(solution)/shard_map/head_conv/pallas_call | solution.py:50
  13.9 0.6 %collective-permute-done.4.got_ref = bf16[4,5,40,256]{3,2,1,0:T(8,128)(2,1)S(1)} collective-permute-done((bf16[4,5,40,256]{3,2,1,0:T(8,128)(2,1)S(1)}, bf16[4,5,40,256]{3,2,1,0:T(8,128)(2,1)S(1)}, u32[]{:S(2)}, u32[]{:S(2)}) %collective-permute-start.4) | collective-permute-done | bytes 409632 | tf_op jit(solution)/shard_map/ppermute | solution.py:641
  14.5 0.1 core_sum.1
  14.6 1.7 %collective-permute-start.7 = (bf16[5,40,256]{2,1,0:T(8,128)(2,1)S(1)}, bf16[5,40,256]{2,1,0:T(8,128)(2,1)S(1)}, u32[]{:S(2)}, u32[]{:S(2)}) collective-permute-start(bf16[5,40,256]{2,1,0:T(8,128)(2,1)S(1)} %get-tuple-element.66), channel_id=1, source_target_pairs={{0,16},{8,24},{16,0},{24,8},{1,17},{9,25},{17,1},{25,9},{2,18},{10... | collective-permute-start | bytes 307208 | tf_op jit(solution)/shard_map/ppermute | solution.py:641
  16.3 0.4 near_parts.1
  16.8 0.4 collective-permute-start.5
  17.2 1.7 %collective-permute-start.6 = (bf16[2,88,256]{2,1,0:T(8,128)(2,1)S(1)}, bf16[2,88,256]{2,1,0:T(8,128)(2,1)S(1)}, u32[]{:S(2)}, u32[]{:S(2)}) collective-permute-start(bf16[2,88,256]{2,1,0:T(8,128)(2,1)S(1)} %get-tuple-element.63), channel_id=1, source_target_pairs={{0,4},{4,0},{1,5},{5,1},{2,6},{6,2},{3,7},{7,3},{8,12},{12,8},{9,1... | collective-permute-start | bytes 270344 | tf_op jit(solution)/shard_map/ppermute | solution.py:641
  18.9 1.0 %collective-permute-done.7.refs_1_ = bf16[5,40,256]{2,1,0:T(8,128)(2,1)S(1)} collective-permute-done((bf16[5,40,256]{2,1,0:T(8,128)(2,1)S(1)}, bf16[5,40,256]{2,1,0:T(8,128)(2,1)S(1)}, u32[]{:S(2)}, u32[]{:S(2)}) %collective-permute-start.7) | collective-permute-done | bytes 102432 | tf_op jit(solution)/shard_map/ppermute | solution.py:641
  20.0 1.9 %collective-permute-start.8 = (bf16[5,40,256]{2,1,0:T(8,128)(2,1)S(1)}, bf16[5,40,256]{2,1,0:T(8,128)(2,1)S(1)}, u32[]{:S(2)}, u32[]{:S(2)}) collective-permute-start(bf16[5,40,256]{2,1,0:T(8,128)(2,1)S(1)} %chip_sum.2.total_ref), channel_id=1, source_target_pairs={{0,4},{4,0},{1,5},{5,1},{2,6},{6,2},{3,7},{7,3},{8,12},{12,8},{9,1... | collective-permute-start | bytes 307208 | tf_op jit(solution)/shard_map/ppermute | solution.py:641
  21.9 0.0 collective-permute-done.6.halo_ref
  21.9 1.7 %collective-permute-start.9 = (bf16[5,40,256]{2,1,0:T(8,128)(2,1)S(1)}, bf16[5,40,256]{2,1,0:T(8,128)(2,1)S(1)}, u32[]{:S(2)}, u32[]{:S(2)}) collective-permute-start(bf16[5,40,256]{2,1,0:T(8,128)(2,1)S(1)} %chip_sum.3.total_ref), channel_id=1, source_target_pairs={{0,4},{4,0},{1,5},{5,1},{2,6},{6,2},{3,7},{7,3},{8,12},{12,8},{9,1... | collective-permute-start | bytes 307208 | tf_op jit(solution)/shard_map/ppermute | solution.py:641
  23.7 0.6 %far_parts.1 = (f32[2,4,40,256]{3,2,1,0:T(8,128)S(1)}, f32[2,4,40,256]{3,2,1,0:T(8,128)S(1)}, bf16[256,512]{1,0:T(8,128)(2,1)S(1)}) custom-call(bf16[2,4,32,256]{3,2,1,0:T(8,128)(2,1)S(1)} %get-tuple-element.47.first_ref, bf16[2,4,32,256]{3,2,1,0:T(8,128)(2,1)S(1)} %collective-permute-done.2.tile_second, ...), custom_call_target="tpu_custom_call" | custom-call | flops 1 | bytes 1 | tf_op jit(solution)/shard_map/far_parts/pallas_call | solution.py:50
  24.3 1.1 %collective-permute-done.8.line_ref = bf16[5,40,256]{2,1,0:T(8,128)(2,1)S(1)} collective-permute-done((bf16[5,40,256]{2,1,0:T(8,128)(2,1)S(1)}, bf16[5,40,256]{2,1,0:T(8,128)(2,1)S(1)}, u32[]{:S(2)}, u32[]{:S(2)}) %collective-permute-start.8) | collective-permute-done | bytes 102432 | tf_op jit(solution)/shard_map/ppermute | solution.py:641
  25.5 0.4 latent_grads.2
  25.8 0.7 %second_conv.2.refs_0_ = bf16[3,10,32,256]{3,2,1,0:T(8,128)(2,1)S(1)} custom-call(bf16[10,40,768]{2,1,0:T(8,128)(2,1)S(1)} %get-tuple-element.67.cat_ref, f32[2,4,40,256]{3,2,1,0:T(8,128)S(1)} %get-tuple-element.68.near_ref, f32[2,4,40,256]{3,2,1,0:T(8,128)S(1)} %get-tuple-element.69.far_ref, bf16[2,88,256]{2,1,0:T(8,128)(2,1)S(1)} %collective-permute-done.6.halo_ref, ...), custom_call_target="tpu_custom_call" | custom-call | flops 1 | bytes 1 | tf_op jit(solution)/shard_map/second_conv/pallas_call | solution.py:50
  26.6 0.3 collective-permute-done.9.line_ref
  26.9 0.4 latent_grads.3
  27.3 0.5 %second_weight_grads.1 = (bf16[1152,128]{1,0:T(8,128)(2,1)S(1)}, bf16[1152,128]{1,0:T(8,128)(2,1)S(1)}) custom-call(bf16[256,512]{1,0:T(8,128)(2,1)S(1)} %get-tuple-element.78.act_ref, bf16[3,10,32,256]{3,2,1,0:T(8,128)(2,1)S(1)} %get-tuple-element.79.refs_0_, bf16[3,10,32,256]{3,2,1,0:T(8,128)(2,1)S(1)} %get-tuple-element.80.refs_1_), custom_call_target="tpu_custom_call" | custom-call | flops 1 | bytes 1 | tf_op jit(solution)/shard_map/second_weight_grads/pallas_call | solution.py:50
  27.8 0.1 collective-permute-start.11
  27.8 0.7 %second_conv.3.refs_1_ = bf16[3,10,32,256]{3,2,1,0:T(8,128)(2,1)S(1)} custom-call(bf16[10,40,768]{2,1,0:T(8,128)(2,1)S(1)} %get-tuple-element.75.cat_ref, f32[2,4,40,256]{3,2,1,0:T(8,128)S(1)} %get-tuple-element.68.near_ref, f32[2,4,40,256]{3,2,1,0:T(8,128)S(1)} %get-tuple-element.69.far_ref, bf16[2,88,256]{2,1,0:T(8,128)(2,1)S(1)} %collective-permute-done.6.halo_ref, ...), custom_call_target="tpu_custom_call" | custom-call | flops 1 | bytes 1 | tf_op jit(solution)/shard_map/second_conv/pallas_call | solution.py:50
  28.6 0.4 first_weight_grads.1
  29.0 0.0 copy-start
  29.0 0.6 %collective-permute-start.10 = (bf16[576,128]{1,0:T(8,128)(2,1)S(1)}, bf16[576,128]{1,0:T(8,128)(2,1)S(1)}, u32[]{:S(2)}, u32[]{:S(2)}) collective-permute-start(bf16[576,128]{1,0:T(8,128)(2,1)S(1)} %get-tuple-element.77), channel_id=1, source_target_pairs={{0,8},{8,0},{16,24},{24,16},{1,9},{9,1},{17,25},{25,17},{2,10},{10... | collective-permute-start | bytes 442376 | tf_op jit(solution)/shard_map/ppermute | solution.py:641
  29.6 1.0 %collective-permute-done.10 = bf16[576,128]{1,0:T(8,128)(2,1)S(1)} collective-permute-done((bf16[576,128]{1,0:T(8,128)(2,1)S(1)}, bf16[576,128]{1,0:T(8,128)(2,1)S(1)}, u32[]{:S(2)}, u32[]{:S(2)}) %collective-permute-start.10) | collective-permute-done | bytes 147488 | tf_op jit(solution)/shard_map/ppermute | solution.py:641
  30.6 0.1 blocks.1
  30.7 2.1 %collective-permute-start.12 = (bf16[432,128]{1,0:T(8,128)(2,1)S(1)}, bf16[432,128]{1,0:T(8,128)(2,1)S(1)}, u32[]{:S(2)}, u32[]{:S(2)}) collective-permute-start(bf16[432,128]{1,0:T(8,128)(2,1)S(1)} %get-tuple-element.84), channel_id=1, source_target_pairs={{2,0},{3,1},{0,2},{1,3},{6,4},{7,5},{4,6},{5,7},{10,8},{11,9},{8,1... | collective-permute-start | bytes 331784 | tf_op jit(solution)/shard_map/ppermute | solution.py:940
  32.7 1.7 %collective-permute-start.13 = (bf16[432,128]{1,0:T(8,128)(2,1)S(1)}, bf16[432,128]{1,0:T(8,128)(2,1)S(1)}, u32[]{:S(2)}, u32[]{:S(2)}) collective-permute-start(bf16[432,128]{1,0:T(8,128)(2,1)S(1)} %get-tuple-element.85), channel_id=1, source_target_pairs={{1,0},{0,1},{3,2},{2,3},{5,4},{4,5},{7,6},{6,7},{9,8},{8,9},{11,10... | collective-permute-start | bytes 331784 | tf_op jit(solution)/shard_map/ppermute | solution.py:940
  34.4 0.7 %collective-permute-start.14 = (bf16[432,128]{1,0:T(8,128)(2,1)S(1)}, bf16[432,128]{1,0:T(8,128)(2,1)S(1)}, u32[]{:S(2)}, u32[]{:S(2)}) collective-permute-start(bf16[432,128]{1,0:T(8,128)(2,1)S(1)} %get-tuple-element.86), channel_id=1, source_target_pairs={{3,0},{2,1},{1,2},{0,3},{7,4},{6,5},{5,6},{4,7},{11,8},{10,9},{9,1... | collective-permute-start | bytes 331784 | tf_op jit(solution)/shard_map/ppermute | solution.py:940
  35.1 5.2 %collective-permute-done.12.refs_1_ = bf16[432,128]{1,0:T(8,128)(2,1)S(1)} collective-permute-done((bf16[432,128]{1,0:T(8,128)(2,1)S(1)}, bf16[432,128]{1,0:T(8,128)(2,1)S(1)}, u32[]{:S(2)}, u32[]{:S(2)}) %collective-permute-start.12) | collective-permute-done | bytes 110624 | tf_op jit(solution)/shard_map/ppermute | solution.py:940
  40.3 2.0 %collective-permute-done.14.refs_3_ = bf16[432,128]{1,0:T(8,128)(2,1)S(1)} collective-permute-done((bf16[432,128]{1,0:T(8,128)(2,1)S(1)}, bf16[432,128]{1,0:T(8,128)(2,1)S(1)}, u32[]{:S(2)}, u32[]{:S(2)}) %collective-permute-start.14) | collective-permute-done | bytes 110624 | tf_op jit(solution)/shard_map/ppermute | solution.py:940
  42.3 0.1 share.1.refs_0_
  42.4 1.9 %collective-permute-start.15 = (bf16[432,128]{1,0:T(8,128)(2,1)S(1)}, bf16[432,128]{1,0:T(8,128)(2,1)S(1)}, u32[]{:S(2)}, u32[]{:S(2)}) collective-permute-start(bf16[432,128]{1,0:T(8,128)(2,1)S(1)} %share.1.refs_0_), channel_id=1, source_target_pairs={{0,16},{8,24},{16,0},{24,8},{1,17},{9,25},{17,1},{25,9},{2,18},{10... | collective-permute-start | bytes 331784 | tf_op jit(solution)/shard_map/ppermute | solution.py:641
  44.3 2.9 %collective-permute-done.15.refs_1_ = bf16[432,128]{1,0:T(8,128)(2,1)S(1)} collective-permute-done((bf16[432,128]{1,0:T(8,128)(2,1)S(1)}, bf16[432,128]{1,0:T(8,128)(2,1)S(1)}, u32[]{:S(2)}, u32[]{:S(2)}) %collective-permute-start.15) | collective-permute-done | bytes 110624 | tf_op jit(solution)/shard_map/ppermute | solution.py:641
  47.2 0.1 collective-permute-start.16
  47.3 1.1 %input_conv.1 = bf16[2,4,32,128]{3,2,1,0:T(8,128)(2,1)} custom-call(bf16[9,128,256]{2,1,0:T(8,128)(2,1)S(1)} %copy-done, bf16[3,10,32,256]{3,2,1,0:T(8,128)(2,1)S(1)} %second_conv.2.refs_0_, bf16[3,10,32,256]{3,2,1,0:T(8,128)(2,1)S(1)} %second_conv.3.refs_1_), custom_call_target="tpu_custom_call" | custom-call | flops 1 | bytes 1 | tf_op jit(solution)/shard_map/input_conv/pallas_call | solution.py:50
  48.4 0.2 collective-permute-done.16.other_ref
  48.6 0.8 %cores.1 = (f32[288,128]{1,0:T(8,128)}, f32[576,128]{1,0:T(8,128)}) custom-call(bf16[432,128]{1,0:T(8,128)(2,1)S(1)} %chips.1.mine_ref, bf16[432,128]{1,0:T(8,128)(2,1)S(1)} %collective-permute-done.16.other_ref), custom_call_target="tpu_custom_call" | custom-call | flops 1 | bytes 1 | tf_op jit(solution)/shard_map/cores/pallas_call | solution.py:50
  (9 shorter events, 0.1 us)
Async XLA Ops:
  0.6 11.4 %collective-permute-start.3 = (bf16[2,4,32,256]{3,2,1,0:T(8,128)(2,1)}, bf16[2,4,32,256]{3,2,1,0:T(8,128)(2,1)S(1)}, u32[]{:S(2)}, u32[]{:S(2)}) collective-permute-start(bf16[2,4,32,256]{3,2,1,0:T(8,128)(2,1)} %first_far.1), channel_id=1, source_target_pairs={{0,4},{4,0},{1,5},{5,1},{2,6},{6,2},{3,7},{7,3},{8,12},{12,8},{9,1... | collective-permute-start | bytes 393224 | tf_op jit(solution)/shard_map/ppermute | solution.py:641
  3.7 8.4 %collective-permute-start.2 = (bf16[2,4,32,256]{3,2,1,0:T(8,128)(2,1)}, bf16[2,4,32,256]{3,2,1,0:T(8,128)(2,1)S(1)}, u32[]{:S(2)}, u32[]{:S(2)}) collective-permute-start(bf16[2,4,32,256]{3,2,1,0:T(8,128)(2,1)} %second_far.1), channel_id=1, source_target_pairs={{0,4},{4,0},{1,5},{5,1},{2,6},{6,2},{3,7},{7,3},{8,12},{12,8},{9,1... | collective-permute-start | bytes 393224 | tf_op jit(solution)/shard_map/ppermute | solution.py:641
  5.0 7.0 %collective-permute-start = (bf16[10,24,128]{2,1,0:T(8,128)(2,1)S(1)}, bf16[10,24,128]{2,1,0:T(8,128)(2,1)S(1)}, u32[]{:S(2)}, u32[]{:S(2)}) collective-permute-start(bf16[10,24,128]{2,1,0:T(8,128)(2,1)S(1)} %get-tuple-element.49), channel_id=1, source_target_pairs={{0,1},{1,2},{2,3},{3,0},{4,5},{5,6},{6,7},{7,4},{8,9},{9,10},{10,1... | collective-permute-start | bytes 184328 | tf_op jit(solution)/shard_map/ppermute | solution.py:647
  7.1 5.0 %collective-permute-start.1 = (bf16[10,24,128]{2,1,0:T(8,128)(2,1)S(1)}, bf16[10,24,128]{2,1,0:T(8,128)(2,1)S(1)}, u32[]{:S(2)}, u32[]{:S(2)}) collective-permute-start(bf16[10,24,128]{2,1,0:T(8,128)(2,1)S(1)} %get-tuple-element.50), channel_id=1, source_target_pairs={{0,3},{1,0},{2,1},{3,2},{4,7},{5,4},{6,5},{7,6},{8,11},{9,8},{10,9... | collective-permute-start | bytes 184328 | tf_op jit(solution)/shard_map/ppermute | solution.py:647
  12.7 1.8 %collective-permute-start.4 = (bf16[4,5,40,256]{3,2,1,0:T(8,128)(2,1)S(1)}, bf16[4,5,40,256]{3,2,1,0:T(8,128)(2,1)S(1)}, u32[]{:S(2)}, u32[]{:S(2)}) collective-permute-start(bf16[4,5,40,256]{3,2,1,0:T(8,128)(2,1)S(1)} %head_conv_edges.1), channel_id=1, source_target_pairs={{0,8},{8,0},{16,24},{24,16},{1,9},{9,1},{17,25},{25,17},{2,10},{10... | collective-permute-start | bytes 1228808 | tf_op jit(solution)/shard_map/ppermute | solution.py:641
  14.6 5.3 %collective-permute-start.7 = (bf16[5,40,256]{2,1,0:T(8,128)(2,1)S(1)}, bf16[5,40,256]{2,1,0:T(8,128)(2,1)S(1)}, u32[]{:S(2)}, u32[]{:S(2)}) collective-permute-start(bf16[5,40,256]{2,1,0:T(8,128)(2,1)S(1)} %get-tuple-element.66), channel_id=1, source_target_pairs={{0,16},{8,24},{16,0},{24,8},{1,17},{9,25},{17,1},{25,9},{2,18},{10... | collective-permute-start | bytes 307208 | tf_op jit(solution)/shard_map/ppermute | solution.py:641
  16.8 5.1 %collective-permute-start.5 = (bf16[5,40,256]{2,1,0:T(8,128)(2,1)S(1)}, bf16[5,40,256]{2,1,0:T(8,128)(2,1)S(1)}, u32[]{:S(2)}, u32[]{:S(2)}) collective-permute-start(bf16[5,40,256]{2,1,0:T(8,128)(2,1)S(1)} %get-tuple-element.62), channel_id=1, source_target_pairs={{0,16},{8,24},{16,0},{24,8},{1,17},{9,25},{17,1},{25,9},{2,18},{10... | collective-permute-start | bytes 307208 | tf_op jit(solution)/shard_map/ppermute | solution.py:641
  17.2 4.7 %collective-permute-start.6 = (bf16[2,88,256]{2,1,0:T(8,128)(2,1)S(1)}, bf16[2,88,256]{2,1,0:T(8,128)(2,1)S(1)}, u32[]{:S(2)}, u32[]{:S(2)}) collective-permute-start(bf16[2,88,256]{2,1,0:T(8,128)(2,1)S(1)} %get-tuple-element.63), channel_id=1, source_target_pairs={{0,4},{4,0},{1,5},{5,1},{2,6},{6,2},{3,7},{7,3},{8,12},{12,8},{9,1... | collective-permute-start | bytes 270344 | tf_op jit(solution)/shard_map/ppermute | solution.py:641
  20.0 5.5 %collective-permute-start.8 = (bf16[5,40,256]{2,1,0:T(8,128)(2,1)S(1)}, bf16[5,40,256]{2,1,0:T(8,128)(2,1)S(1)}, u32[]{:S(2)}, u32[]{:S(2)}) collective-permute-start(bf16[5,40,256]{2,1,0:T(8,128)(2,1)S(1)} %chip_sum.2.total_ref), channel_id=1, source_target_pairs={{0,4},{4,0},{1,5},{5,1},{2,6},{6,2},{3,7},{7,3},{8,12},{12,8},{9,1... | collective-permute-start | bytes 307208 | tf_op jit(solution)/shard_map/ppermute | solution.py:641
  21.9 4.9 %collective-permute-start.9 = (bf16[5,40,256]{2,1,0:T(8,128)(2,1)S(1)}, bf16[5,40,256]{2,1,0:T(8,128)(2,1)S(1)}, u32[]{:S(2)}, u32[]{:S(2)}) collective-permute-start(bf16[5,40,256]{2,1,0:T(8,128)(2,1)S(1)} %chip_sum.3.total_ref), channel_id=1, source_target_pairs={{0,4},{4,0},{1,5},{5,1},{2,6},{6,2},{3,7},{7,3},{8,12},{12,8},{9,1... | collective-permute-start | bytes 307208 | tf_op jit(solution)/shard_map/ppermute | solution.py:641
  27.8 2.8 %collective-permute-start.11 = (bf16[1152,128]{1,0:T(8,128)(2,1)S(1)}, bf16[1152,128]{1,0:T(8,128)(2,1)S(1)}, u32[]{:S(2)}, u32[]{:S(2)}) collective-permute-start(bf16[1152,128]{1,0:T(8,128)(2,1)S(1)} %get-tuple-element.82), channel_id=1, source_target_pairs={{0,8},{8,0},{16,24},{24,16},{1,9},{9,1},{17,25},{25,17},{2,10},{10... | collective-permute-start | bytes 884744 | tf_op jit(solution)/shard_map/ppermute | solution.py:641
  29.0 18.3 %copy-start = (bf16[9,128,256]{2,1,0:T(8,128)(2,1)S(1)}, bf16[9,128,256]{2,1,0:T(8,128)(2,1)}, u32[]{:S(2)}) copy-start(bf16[9,128,256]{2,1,0:T(8,128)(2,1)} %w_first_ref.1) | copy-start | bytes 1769476
  29.0 1.6 %collective-permute-start.10 = (bf16[576,128]{1,0:T(8,128)(2,1)S(1)}, bf16[576,128]{1,0:T(8,128)(2,1)S(1)}, u32[]{:S(2)}, u32[]{:S(2)}) collective-permute-start(bf16[576,128]{1,0:T(8,128)(2,1)S(1)} %get-tuple-element.77), channel_id=1, source_target_pairs={{0,8},{8,0},{16,24},{24,16},{1,9},{9,1},{17,25},{25,17},{2,10},{10... | collective-permute-start | bytes 442376 | tf_op jit(solution)/shard_map/ppermute | solution.py:641
  30.7 9.6 %collective-permute-start.12 = (bf16[432,128]{1,0:T(8,128)(2,1)S(1)}, bf16[432,128]{1,0:T(8,128)(2,1)S(1)}, u32[]{:S(2)}, u32[]{:S(2)}) collective-permute-start(bf16[432,128]{1,0:T(8,128)(2,1)S(1)} %get-tuple-element.84), channel_id=1, source_target_pairs={{2,0},{3,1},{0,2},{1,3},{6,4},{7,5},{4,6},{5,7},{10,8},{11,9},{8,1... | collective-permute-start | bytes 331784 | tf_op jit(solution)/shard_map/ppermute | solution.py:940
  32.7 7.6 %collective-permute-start.13 = (bf16[432,128]{1,0:T(8,128)(2,1)S(1)}, bf16[432,128]{1,0:T(8,128)(2,1)S(1)}, u32[]{:S(2)}, u32[]{:S(2)}) collective-permute-start(bf16[432,128]{1,0:T(8,128)(2,1)S(1)} %get-tuple-element.85), channel_id=1, source_target_pairs={{1,0},{0,1},{3,2},{2,3},{5,4},{4,5},{7,6},{6,7},{9,8},{8,9},{11,10... | collective-permute-start | bytes 331784 | tf_op jit(solution)/shard_map/ppermute | solution.py:940
  34.4 7.9 %collective-permute-start.14 = (bf16[432,128]{1,0:T(8,128)(2,1)S(1)}, bf16[432,128]{1,0:T(8,128)(2,1)S(1)}, u32[]{:S(2)}, u32[]{:S(2)}) collective-permute-start(bf16[432,128]{1,0:T(8,128)(2,1)S(1)} %get-tuple-element.86), channel_id=1, source_target_pairs={{3,0},{2,1},{1,2},{0,3},{7,4},{6,5},{5,6},{4,7},{11,8},{10,9},{9,1... | collective-permute-start | bytes 331784 | tf_op jit(solution)/shard_map/ppermute | solution.py:940
  42.4 4.8 %collective-permute-start.15 = (bf16[432,128]{1,0:T(8,128)(2,1)S(1)}, bf16[432,128]{1,0:T(8,128)(2,1)S(1)}, u32[]{:S(2)}, u32[]{:S(2)}) collective-permute-start(bf16[432,128]{1,0:T(8,128)(2,1)S(1)} %share.1.refs_0_), channel_id=1, source_target_pairs={{0,16},{8,24},{16,0},{24,8},{1,17},{9,25},{17,1},{25,9},{2,18},{10... | collective-permute-start | bytes 331784 | tf_op jit(solution)/shard_map/ppermute | solution.py:641
  47.2 1.4 %collective-permute-start.16 = (bf16[432,128]{1,0:T(8,128)(2,1)S(1)}, bf16[432,128]{1,0:T(8,128)(2,1)S(1)}, u32[]{:S(2)}, u32[]{:S(2)}) collective-permute-start(bf16[432,128]{1,0:T(8,128)(2,1)S(1)} %chips.1.mine_ref), channel_id=1, source_target_pairs={{0,8},{8,0},{16,24},{24,16},{1,9},{9,1},{17,25},{25,17},{2,10},{10... | collective-permute-start | bytes 331784 | tf_op jit(solution)/shard_map/ppermute | solution.py:641

commit v7 on v6

--- a/solution.py
+++ b/solution.py
@@ -59,7 +59,8 @@
     )(*arrays)
 
 
-def pack_kernel(grads_far, second_far, first_far, right_ref, left_ref, grads_near, second_near, first_near, edges, edges_wide, packed, sems):
+def pack_kernel(with_tile, grads_far, second_far, first_far, right_ref, left_ref, *refs):
+    grads_near, second_near, first_near, edges, edges_wide, packed, sems, tile_sems = refs[-8:]
     heads, batch, height, breadth, _ = grads_far.shape
     samples = second_far.shape[0]
     rows = 6 * height
@@ -70,6 +71,11 @@
             source = far.at[:, :, :, columns, :] if j == 0 else far.at[:, :, columns, :]
             copies.append(pltpu.make_async_copy(source, near.at[side], sems.at[side, j]))
             copies[-1].start()
+    tile_copies = []
+    if with_tile:
+        for j, far in enumerate((second_far, first_far)):
+            tile_copies.append(pltpu.make_async_copy(far, refs[0].at[j], tile_sems.at[j]))
+            tile_copies[-1].start()
     for copy in copies:
         copy.wait()
     for side, out_ref in ((0, right_ref), (1, left_ref)):
@@ -77,11 +83,11 @@
         grads_ref, second_ref, first_ref = grads_near.at[side], second_near.at[side], first_near.at[side]
         for h in range(heads):
             for b in range(batch):
-                block = grads_ref[h, b, :, start : start + 8, :].astype(F32)
+                block = grads_ref[h, b].astype(F32)[:, start : start + 8, :]
                 edges[(h * batch + b) * height * 8 : (h * batch + b + 1) * height * 8, :] = block.reshape(height * 8, LANES)
         for j, ref in enumerate((second_ref, first_ref)):
             for s in range(samples):
-                block = ref[s, :, start : start + 8, :].astype(F32)
+                block = ref[s].astype(F32)[:, start : start + 8, :]
                 at = (j * samples + s) * height * 8
                 for half in range(2):
                     lanes = slice(half * LANES, (half + 1) * LANES)
@@ -101,26 +107,29 @@
                     packed[at : at + height, :] = edges_wide[
                         half, pl.ds((j * samples + s) * height * 8 + inner, height, stride=8), :
                     ]
-        out_ref[...] = packed[...].astype(BF).reshape(out_ref.shape)
-
-
-def pack(head_grads, pre_second, pre_first):
+        out_ref[...] = packed[: (batch + samples) * rows].astype(BF).reshape(out_ref.shape)
+    for copy in tile_copies:
+        copy.wait()
+
+
+def pack(head_grads, pre_second, pre_first, with_tile):
     heads, batch, height, _, _ = head_grads.shape
     samples = pre_second.shape[0]
     shape = jax.ShapeDtypeStruct((batch + samples, 6 * height, LANES), BF)
     return run(
         "pack_columns",
-        pack_kernel,
-        [shape, shape],
+        functools.partial(pack_kernel, with_tile),
+        [shape, shape] + [jax.ShapeDtypeStruct((2,) + pre_second.shape, BF)] * with_tile,
         [head_grads, pre_second, pre_first],
         [
             pltpu.VMEM((2, heads, batch, height, 16, LANES), BF),
             pltpu.VMEM((2, samples, height, 16, 2 * LANES), BF),
             pltpu.VMEM((2, samples, height, 16, 2 * LANES), BF),
-            pltpu.VMEM((heads * batch * height * 8, LANES), F32),
-            pltpu.VMEM((2, 2 * samples * height * 8, LANES), F32),
-            pltpu.VMEM(((batch + samples) * 6 * height, LANES), F32),
+            pltpu.VMEM((heads * batch * height * 8 + 64, LANES), F32),
+            pltpu.VMEM((2, 2 * samples * height * 8 + 64, LANES), F32),
+            pltpu.VMEM(((batch + samples) * 6 * height + 16, LANES), F32),
             pltpu.SemaphoreType.DMA((2, 3)),
+            pltpu.SemaphoreType.DMA((2,)),
         ],
         far=True,
     )
@@ -199,7 +208,7 @@
         [jax.ShapeDtypeStruct((slots, rows, kept, depth), BF)],
         [head_grads, low, high, head_weights],
         [
-            pltpu.VMEM((heads, slots * height * (kept + 16), LANES), F32),
+            pltpu.VMEM((heads, (slots * height + 8) * (kept + 16), LANES), F32),
             pltpu.VMEM((slots * height * kept, 3 * heads * LANES), BF),
             pltpu.VMEM((slots, height + 2, kept, depth), F32),
         ],
@@ -247,6 +256,7 @@
     height, heads, pitch = rows - 2, weights_ref.shape[0], 24
     core, chip = core_and_chip()
     wide[...] = jnp.zeros(wide.shape, F32)
+    total[...] = inside_ref[...]
     for side, packed_ref in ((0, low_ref), (1, high_ref)):
         for slot in range(slots):
             group, s = 1 - chip if slot % 2 else chip, slot // 2
@@ -267,15 +277,9 @@
             [weights_ref[h, 3 * (u + 1) + (v + 1)] for v in STEPS for h in range(heads)], axis=1
         )
         part = dot_last(shifted[...], weights).reshape(2, slots, height, 8, depth)
-        if u == -1:
-            total[:, :, :height] = part
-            total[:, :, height:] = jnp.zeros((2, slots, 2, 8, depth), F32)
-        else:
-            total[:, :, 1 + u : 1 + u + height] += part
-    here = pl.ds(1 - lax.axis_index("lat"), height + 1)
-    out_ref[:, :, 8 : kept - 8] = inside_ref[:, here, 8 : kept - 8].astype(BF)
-    for side, columns in enumerate((slice(0, 8), slice(kept - 8, kept))):
-        out_ref[:, :, columns] = (inside_ref[:, here, columns] + total[side, :, here]).astype(BF)
+        total[:, 1 + u : 1 + u + height, :8] += part[0]
+        total[:, 1 + u : 1 + u + height, kept - 8 :] += part[1]
+    out_ref[...] = total[:, pl.ds(1 - lax.axis_index("lat"), height + 1)].astype(BF)
 
 
 def inside_conv(head_grads, head_weights, slots):
@@ -288,7 +292,7 @@
         [jax.ShapeDtypeStruct((slots, height + 2, kept, head_weights.shape[2]), F32)],
         [head_grads, head_weights],
         [
-            pltpu.VMEM((heads, slots * height * (kept + 16), LANES), F32),
+            pltpu.VMEM((heads, (slots * height + 8) * (kept + 16), LANES), F32),
             pltpu.VMEM((slots * height * kept, 3 * heads * LANES), BF),
         ],
     )[0]
@@ -303,9 +307,9 @@
         [jax.ShapeDtypeStruct((slots, rows - 1, kept, depth), BF)],
         [inside, low, high, head_weights],
         [
-            pltpu.VMEM((heads, 2 * slots * height * 24, LANES), F32),
+            pltpu.VMEM((heads, (2 * slots * height + 8) * 24, LANES), F32),
             pltpu.VMEM((2 * slots * height * 8, 3 * heads * LANES), BF),
-            pltpu.VMEM((2, slots, rows, 8, depth), F32),
+            pltpu.VMEM((slots, rows, kept, depth), F32),
         ],
     )[0]
 
@@ -333,7 +337,7 @@
                     at = s * height * kept + EDGE + col
                     wide[half, pl.ds(at - width, height, stride=kept), :] = low[here : here + height]
                     wide[half, pl.ds(at + breadth, height, stride=kept), :] = high[here : here + height]
-        value = jnp.concatenate([wide[0], wide[1]], axis=1)
+        value = jnp.concatenate([wide[half, : samples * height * kept] for half in range(2)], axis=1)
         out_ref[...] = value.astype(BF).reshape(out_ref.shape)
         slope_ref[...] = gelu_slope(value).reshape(slope_ref.shape)
     active = gelu_value(first_ref[...].astype(F32).reshape(samples * height * breadth, depth)).astype(BF).astype(F32)
@@ -358,7 +362,7 @@
             jax.ShapeDtypeStruct((encoder_input.shape[3], cells), BF),
         ],
         [pre_second, pre_first, encoder_input, low, high],
-        [pltpu.VMEM((2, samples * height * kept, LANES), F32)],
+        [pltpu.VMEM((2, (samples * height + 8) * kept, LANES), F32)],
     )
 
 
@@ -698,13 +702,13 @@
                         wide[half, pl.ds(at, height, stride=kept), :] = value
                         at = first_cell + (side * width + col) * height
                         cells[s, at : at + height, half * LANES : (half + 1) * LANES] = value
-        value = jnp.concatenate([wide[0], wide[1]], axis=1)
+        value = jnp.concatenate([wide[half, : samples * height * kept] for half in range(2)], axis=1)
         slope_ref[...] = gelu_slope(value).reshape(slope_ref.shape)
-    halo_ref[:, : cells.shape[1]] = cells[...].astype(BF)
     half = height // 2
     for part in range(2):
         values = input_ref[:, part * half : (part + 1) * half].reshape(samples, half * breadth, LANES)
-        halo_ref[:, cells.shape[1] :, part * LANES : (part + 1) * LANES] = values
+        halo_ref[:, : half * breadth, part * LANES : (part + 1) * LANES] = values
+    halo_ref[:, half * breadth :] = cells[:, : 6 * height].astype(BF)
 
 
 def near_parts(pre_second, pre_first, encoder_input, low, high):
@@ -716,15 +720,18 @@
         near_kernel,
         [slope, slope, jax.ShapeDtypeStruct((samples, 6 * height + height * breadth // 2, depth), BF)],
         [pre_second, pre_first, encoder_input, low, high],
-        [pltpu.VMEM((2, samples * height * kept, LANES), F32), pltpu.VMEM((samples, 6 * height, depth), F32)],
-    )
-
-
-def far_kernel(first_ref, tile_second, tile_first, slope_second, slope_first, act_out, wide, act):
+        [
+            pltpu.VMEM((2, (samples * height + 8) * kept, LANES), F32),
+            pltpu.VMEM((samples, 6 * height + 8, depth), F32),
+        ],
+    )
+
+
+def far_kernel(first_ref, tile_ref, slope_second, slope_first, act_out, wide, act):
     samples, height, breadth, depth = first_ref.shape
     kept = breadth + 2 * EDGE
     lat = lax.axis_index("lat")
-    for source_ref, slope_ref in ((tile_second, slope_second), (tile_first, slope_first)):
+    for source_ref, slope_ref in ((tile_ref.at[0], slope_second), (tile_ref.at[1], slope_first)):
         wide[...] = jnp.zeros(wide.shape, F32)
         for s in range(samples):
             for half in range(2):
@@ -735,11 +742,11 @@
         slope_ref[...] = gelu_slope(value).reshape(slope_ref.shape)
     own, other = pl.ds(height * lat, height), pl.ds(height * (1 - lat), height)
     act[:, own] = gelu_value(first_ref[...].astype(F32))
-    act[:, other] = gelu_value(tile_first[...].astype(F32))
+    act[:, other] = gelu_value(tile_ref[1].astype(F32))
     act_out[...] = act[...].reshape(act_out.shape[1], depth).T.astype(BF)
 
 
-def far_parts(pre_first, tile_second, tile_first):
+def far_parts(pre_first, tile):
     samples, height, breadth, depth = pre_first.shape
     kept = breadth + 2 * EDGE
     slope = jax.ShapeDtypeStruct((samples, height, kept, depth), F32)
@@ -747,7 +754,7 @@
         "far_parts",
         far_kernel,
         [slope, slope, jax.ShapeDtypeStruct((depth, 2 * samples * height * breadth), BF)],
-        [pre_first, tile_second, tile_first],
+        [pre_first, tile],
         [
             pltpu.VMEM((2, samples * height * kept, LANES), F32),
             pltpu.VMEM((samples, 2 * height, breadth, depth), F32),
@@ -761,7 +768,7 @@
     other = pl.ds(height * (1 - lat), height)
     slope[pl.ds(height * lat, height)] = near_ref[sample]
     slope[other] = far_ref[sample]
-    beside = gelu_slope(halo_ref[sample, : 6 * height].astype(F32))
+    beside = gelu_slope(halo_ref[sample, halo_ref.shape[1] - 6 * height :].astype(F32))
     for side in range(2):
         for col in range(width):
             here = first_cell + (side * width + col) * height
@@ -883,7 +890,7 @@
     cells[:, pl.ds(height * lat, height)] = input_ref[...].astype(F32)
     half = height // 2
     for part in range(2):
-        values = halo_ref[:, 6 * height :, part * LANES : (part + 1) * LANES].astype(F32)
+        values = halo_ref[:, : half * breadth, part * LANES : (part + 1) * LANES].astype(F32)
         cells[:, pl.ds(height * (1 - lat) + part * half, half)] = values.reshape(samples, half, breadth, LANES)
     lefts = [cells[s].reshape(2 * height * breadth, channels).T.astype(BF) for s in range(samples)]
     band_rows(norm_factor, lefts, moved, mine_ref, other_ref)
@@ -943,15 +950,15 @@
 def two_bands(head_grads, head_weights, encoder_input, pre_first, pre_second, w_first, w_second, norm_factor):
     samples, height, breadth, _ = encoder_input.shape
     columns = lax.axis_size("lon")
-    tiles = [swap(array, "lat", 1) for array in (pre_second, pre_first)]
-    to_right, to_left = pack(head_grads, pre_second, pre_first)
+    to_right, to_left, tile = pack(head_grads, pre_second, pre_first, True)
+    tile = swap(tile, "lat", 1)
     low = around(to_right, "lon", 1)
     high = around(to_left, "lon", -1)
     head_grads, head_weights, w_second, pre_second, pre_first, encoder_input = stage(
         head_grads, head_weights, w_second, pre_second, pre_first, encoder_input
     )
     inside = inside_conv(head_grads, head_weights, 2 * samples)
-    low, high, inside, *tiles = lax.optimization_barrier((low, high, inside, *tiles))
+    low, high, inside, tile = lax.optimization_barrier((low, high, inside, tile))
     heads_of = functools.partial(
         head_conv,
         head_grads=head_grads,
@@ -973,7 +980,7 @@
     cross[-1], halo = lax.optimization_barrier((cross[-1], halo))
     totals = [run("chip_sum", sum_kernel, [part_shape], [own[s], cross[s]])[0] for s in everyone]
     lines = [swap(total, "lat", 1) for total in totals]
-    far_second, far_first, act = far_parts(pre_first, *tiles)
+    far_second, far_first, act = far_parts(pre_first, tile)
 
     moved_second, moved_first = [], []
     for s in everyone:
@@ -1015,7 +1022,7 @@
 def general(head_grads, head_weights, encoder_input, pre_first, pre_second, w_first, w_second, norm_factor):
     samples, height, breadth, _ = encoder_input.shape
     bands, columns = lax.axis_size("lat"), lax.axis_size("lon")
-    to_right, to_left = pack(head_grads, pre_second, pre_first)
+    to_right, to_left = pack(head_grads, pre_second, pre_first, False)
     to_right, to_left, to_cross = lax.optimization_barrier((to_right, to_left, pre_first))
     low = around(to_right, "lon", 1)
     high = around(to_left, "lon", -1)

time: 50.1 us -> 50.3 us (level)
  waiting for transfers between devices: 14.3 us -> 16.5 us
  starting transfers between devices: 21.9 us -> 19.9 us
    ppermute x12 -> x11, waiting for transfers between devices: 7.16 us -> 8.96 us  [swap(): return lax.ppermute(array, axis, [(i, i ^ flip) for i in range(count)])]
    ppermute x12 -> x11, starting transfers between devices: 13.3 us -> 11.6 us  [swap(): return lax.ppermute(array, axis, [(i, i ^ flip) for i in range(count)])]
  transfers between devices with their start and end apart: 17 -> 16, of which waited for: 9 -> 10; matrix products, arithmetic and copies ran while one was open for 0% -> 0% of each run, Pallas kernels for 20% -> 17%
where the time goes in v7:
time: 50.3 us; the launch traced here: 49.6 us
  starting transfers between devices  19.9 us (40%)
  waiting for transfers between devices  16.5 us (33%)
  Pallas kernels  12.4 us (25%)
  between operations  0.81 us (2%)
    pallas_call x21, Pallas kernels, run(): pl.pallas_call(kernel, name=name, out_shape=out_shape, in_specs=specs, ou...  12.4 us
    ppermute x11, starting transfers between devices, swap(): return lax.ppermute(array, axis, [(i, i ^ flip) for i in range(count)])  11.6 us
    ppermute x11, waiting for transfers between devices, swap(): return lax.ppermute(array, axis, [(i, i ^ flip) for i in range(count)])  8.96 us
    ppermute x3, waiting for transfers between devices, to_partner(): lax.ppermute(array, 'lon', [(partner(i, step, count), i) for i in range(c...  7.51 us
    ppermute x3, starting transfers between devices, to_partner(): lax.ppermute(array, 'lon', [(partner(i, step, count), i) for i in range(c...  4.47 us
    ppermute x2, starting transfers between devices, around(): return lax.ppermute(array, axis, pairs)  3.82 us
  transfers between devices with their start and end apart: 16, of which 10 were waited for; matrix products, arithmetic and copies ran while one was open for 0% of the time, Pallas kernels for 17%

profile of v7, /device:TPU:0, one launch (start us, length us, event | category | flops | bytes accessed | tf_op | source)
XLA Modules:
  0.0 49.6 jit_solution(11260943909367475830)
XLA Ops:
  0.6 1.3 %pack_columns.1 = (bf16[10,24,128]{2,1,0:T(8,128)(2,1)S(1)}, bf16[10,24,128]{2,1,0:T(8,128)(2,1)S(1)}, bf16[2,2,4,32,256]{4,3,2,1,0:T(8,128)(2,1)S(1)}) custom-call(bf16[2,8,4,32,128]{4,3,2,1,0:T(8,128)(2,1)} %grads_far.1, bf16[2,4,32,256]{3,2,1,0:T(8,128)(2,1)} %second_far.1, bf16[2,4,32,256]{3,2,1,0:T(8,128)(2,1)} %first_far.1), custom_call_target="tpu_custom_call" | custom-call | flops 1 | bytes 1 | tf_op jit(solution)/shard_map/pack_columns/pallas_call | solution.py:50
  2.0 3.0 %collective-permute-start.2 = (bf16[2,2,4,32,256]{4,3,2,1,0:T(8,128)(2,1)S(1)}, bf16[2,2,4,32,256]{4,3,2,1,0:T(8,128)(2,1)S(1)}, u32[]{:S(2)}, u32[]{:S(2)}) collective-permute-start(bf16[2,2,4,32,256]{4,3,2,1,0:T(8,128)(2,1)S(1)} %get-tuple-element.53), channel_id=1, source_target_pairs={{0,4},{4,0},{1,5},{5,1},{2,6},{6,2},{3,7},{7,3},{8,12},{12,8},{9,1... | collective-permute-start | bytes 786440 | tf_op jit(solution)/shard_map/ppermute | solution.py:645
  5.0 1.6 %collective-permute-start = (bf16[10,24,128]{2,1,0:T(8,128)(2,1)S(1)}, bf16[10,24,128]{2,1,0:T(8,128)(2,1)S(1)}, u32[]{:S(2)}, u32[]{:S(2)}) collective-permute-start(bf16[10,24,128]{2,1,0:T(8,128)(2,1)S(1)} %get-tuple-element.49), channel_id=1, source_target_pairs={{0,1},{1,2},{2,3},{3,0},{4,5},{5,6},{6,7},{7,4},{8,9},{9,10},{10,1... | collective-permute-start | bytes 184328 | tf_op jit(solution)/shard_map/ppermute | solution.py:651
  6.6 2.2 %collective-permute-start.1 = (bf16[10,24,128]{2,1,0:T(8,128)(2,1)S(1)}, bf16[10,24,128]{2,1,0:T(8,128)(2,1)S(1)}, u32[]{:S(2)}, u32[]{:S(2)}) collective-permute-start(bf16[10,24,128]{2,1,0:T(8,128)(2,1)S(1)} %get-tuple-element.50), channel_id=1, source_target_pairs={{0,3},{1,0},{2,1},{3,2},{4,7},{5,4},{6,5},{7,6},{8,11},{9,8},{10,9... | collective-permute-start | bytes 184328 | tf_op jit(solution)/shard_map/ppermute | solution.py:651
  8.8 1.9 %stage.1 = (bf16[2,8,4,32,128]{4,3,2,1,0:T(8,128)(2,1)S(1)}, bf16[2,9,256,128]{3,2,1,0:T(8,128)(2,1)S(1)}, bf16[9,256,256]{2,1,0:T(8,128)(2,1)S(1)}, bf16[2,4,32...) custom-call(bf16[2,8,4,32,128]{4,3,2,1,0:T(8,128)(2,1)} %grads_far.1, ...), custom_call_target="tpu_custom_call" | custom-call | flops 1 | bytes 1 | tf_op jit(solution)/shard_map/stage/pallas_call | solution.py:50
  10.7 1.0 %head_conv_inside.1.inside_ref = f32[4,6,40,256]{3,2,1,0:T(8,128)S(1)} custom-call(bf16[2,8,4,32,128]{4,3,2,1,0:T(8,128)(2,1)S(1)} %get-tuple-element.51.grads_ref, bf16[2,9,256,128]{3,2,1,0:T(8,128)(2,1)S(1)} %get-tuple-element.52.weights_ref), custom_call_target="tpu_custom_call" | custom-call | flops 1 | bytes 1 | tf_op jit(solution)/shard_map/head_conv_inside/pallas_call | solution.py:50
  11.7 0.0 collective-permute-done.low_ref
  11.7 0.0 collective-permute-done.2.tile_ref
  11.7 0.6 %head_conv_edges.1 = bf16[4,5,40,256]{3,2,1,0:T(8,128)(2,1)S(1)} custom-call(f32[4,6,40,256]{3,2,1,0:T(8,128)S(1)} %head_conv_inside.1.inside_ref, bf16[10,24,128]{2,1,0:T(8,128)(2,1)S(1)} %collective-permute-done.low_ref, bf16[10,24,128]{2,1,0:T(8,128)(2,1)S(1)} %collective-permute-done.1.high_ref, bf16[2,9,256,128]{3,2,1,0:T(8,128)(2,1)S(1)} %get-tuple-element.52.weights_ref), custom_call_target="tpu_custom_call" | custom-call | flops 1 | bytes 1 | tf_op jit(solution)/shard_map/head_conv_edges/pallas_call | solution.py:50
  12.4 0.1 collective-permute-start.3
  12.5 1.1 %head_conv.1.mine_ref = bf16[4,5,40,256]{3,2,1,0:T(8,128)(2,1)S(1)} custom-call(bf16[2,8,4,32,128]{4,3,2,1,0:T(8,128)(2,1)S(1)} %get-tuple-element.51.grads_ref, bf16[10,24,128]{2,1,0:T(8,128)(2,1)S(1)} %collective-permute-done.low_ref, bf16[10,24,128]{2,1,0:T(8,128)(2,1)S(1)} %collective-permute-done.1.high_ref, ...), custom_call_target="tpu_custom_call" | custom-call | flops 1 | bytes 1 | tf_op jit(solution)/shard_map/head_conv/pallas_call | solution.py:50
  13.6 0.6 %collective-permute-done.3.got_ref = bf16[4,5,40,256]{3,2,1,0:T(8,128)(2,1)S(1)} collective-permute-done((bf16[4,5,40,256]{3,2,1,0:T(8,128)(2,1)S(1)}, bf16[4,5,40,256]{3,2,1,0:T(8,128)(2,1)S(1)}, u32[]{:S(2)}, u32[]{:S(2)}) %collective-permute-start.3) | collective-permute-done | bytes 409632 | tf_op jit(solution)/shard_map/ppermute | solution.py:645
  14.2 0.1 core_sum.1
  14.3 1.6 %collective-permute-start.6 = (bf16[5,40,256]{2,1,0:T(8,128)(2,1)S(1)}, bf16[5,40,256]{2,1,0:T(8,128)(2,1)S(1)}, u32[]{:S(2)}, u32[]{:S(2)}) collective-permute-start(bf16[5,40,256]{2,1,0:T(8,128)(2,1)S(1)} %get-tuple-element.66), channel_id=1, source_target_pairs={{0,16},{8,24},{16,0},{24,8},{1,17},{9,25},{17,1},{25,9},{2,18},{10... | collective-permute-start | bytes 307208 | tf_op jit(solution)/shard_map/ppermute | solution.py:645
  15.8 0.4 near_parts.1
  16.3 0.6 %collective-permute-start.4 = (bf16[5,40,256]{2,1,0:T(8,128)(2,1)S(1)}, bf16[5,40,256]{2,1,0:T(8,128)(2,1)S(1)}, u32[]{:S(2)}, u32[]{:S(2)}) collective-permute-start(bf16[5,40,256]{2,1,0:T(8,128)(2,1)S(1)} %get-tuple-element.62), channel_id=1, source_target_pairs={{0,16},{8,24},{16,0},{24,8},{1,17},{9,25},{17,1},{25,9},{2,18},{10... | collective-permute-start | bytes 307208 | tf_op jit(solution)/shard_map/ppermute | solution.py:645
  16.9 1.3 %collective-permute-start.5 = (bf16[2,88,256]{2,1,0:T(8,128)(2,1)S(1)}, bf16[2,88,256]{2,1,0:T(8,128)(2,1)S(1)}, u32[]{:S(2)}, u32[]{:S(2)}) collective-permute-start(bf16[2,88,256]{2,1,0:T(8,128)(2,1)S(1)} %get-tuple-element.63), channel_id=1, source_target_pairs={{0,4},{4,0},{1,5},{5,1},{2,6},{6,2},{3,7},{7,3},{8,12},{12,8},{9,1... | collective-permute-start | bytes 270344 | tf_op jit(solution)/shard_map/ppermute | solution.py:645
  18.2 1.6 %collective-permute-done.6.refs_1_ = bf16[5,40,256]{2,1,0:T(8,128)(2,1)S(1)} collective-permute-done((bf16[5,40,256]{2,1,0:T(8,128)(2,1)S(1)}, bf16[5,40,256]{2,1,0:T(8,128)(2,1)S(1)}, u32[]{:S(2)}, u32[]{:S(2)}) %collective-permute-start.6) | collective-permute-done | bytes 102432 | tf_op jit(solution)/shard_map/ppermute | solution.py:645
  19.8 1.4 %collective-permute-start.7 = (bf16[5,40,256]{2,1,0:T(8,128)(2,1)S(1)}, bf16[5,40,256]{2,1,0:T(8,128)(2,1)S(1)}, u32[]{:S(2)}, u32[]{:S(2)}) collective-permute-start(bf16[5,40,256]{2,1,0:T(8,128)(2,1)S(1)} %chip_sum.2.total_ref), channel_id=1, source_target_pairs={{0,4},{4,0},{1,5},{5,1},{2,6},{6,2},{3,7},{7,3},{8,12},{12,8},{9,1... | collective-permute-start | bytes 307208 | tf_op jit(solution)/shard_map/ppermute | solution.py:645
  21.2 0.4 collective-permute-done.5.halo_ref
  21.6 1.4 %collective-permute-start.8 = (bf16[5,40,256]{2,1,0:T(8,128)(2,1)S(1)}, bf16[5,40,256]{2,1,0:T(8,128)(2,1)S(1)}, u32[]{:S(2)}, u32[]{:S(2)}) collective-permute-start(bf16[5,40,256]{2,1,0:T(8,128)(2,1)S(1)} %chip_sum.3.total_ref), channel_id=1, source_target_pairs={{0,4},{4,0},{1,5},{5,1},{2,6},{6,2},{3,7},{7,3},{8,12},{12,8},{9,1... | collective-permute-start | bytes 307208 | tf_op jit(solution)/shard_map/ppermute | solution.py:645
  23.0 0.6 %far_parts.1 = (f32[2,4,40,256]{3,2,1,0:T(8,128)S(1)}, f32[2,4,40,256]{3,2,1,0:T(8,128)S(1)}, bf16[256,512]{1,0:T(8,128)(2,1)S(1)}) custom-call(bf16[2,4,32,256]{3,2,1,0:T(8,128)(2,1)S(1)} %get-tuple-element.47.first_ref, bf16[2,2,4,32,256]{4,3,2,1,0:T(8,128)(2,1)S(1)} %collective-permute-done.2.tile_ref), custom_call_target="tpu_custom_call" | custom-call | flops 1 | bytes 1 | tf_op jit(solution)/shard_map/far_parts/pallas_call | solution.py:50
  23.6 1.8 %collective-permute-done.7.line_ref = bf16[5,40,256]{2,1,0:T(8,128)(2,1)S(1)} collective-permute-done((bf16[5,40,256]{2,1,0:T(8,128)(2,1)S(1)}, bf16[5,40,256]{2,1,0:T(8,128)(2,1)S(1)}, u32[]{:S(2)}, u32[]{:S(2)}) %collective-permute-start.7) | collective-permute-done | bytes 102432 | tf_op jit(solution)/shard_map/ppermute | solution.py:645
  25.4 0.4 latent_grads.2
  25.8 0.7 %second_conv.2.refs_0_ = bf16[3,10,32,256]{3,2,1,0:T(8,128)(2,1)S(1)} custom-call(bf16[10,40,768]{2,1,0:T(8,128)(2,1)S(1)} %get-tuple-element.67.cat_ref, f32[2,4,40,256]{3,2,1,0:T(8,128)S(1)} %get-tuple-element.68.near_ref, f32[2,4,40,256]{3,2,1,0:T(8,128)S(1)} %get-tuple-element.69.far_ref, bf16[2,88,256]{2,1,0:T(8,128)(2,1)S(1)} %collective-permute-done.5.halo_ref, ...), custom_call_target="tpu_custom_call" | custom-call | flops 1 | bytes 1 | tf_op jit(solution)/shard_map/second_conv/pallas_call | solution.py:50
  26.5 0.2 collective-permute-done.8.line_ref
  26.7 0.4 latent_grads.3
  27.1 0.5 %second_weight_grads.1 = (bf16[1152,128]{1,0:T(8,128)(2,1)S(1)}, bf16[1152,128]{1,0:T(8,128)(2,1)S(1)}) custom-call(bf16[256,512]{1,0:T(8,128)(2,1)S(1)} %get-tuple-element.78.act_ref, bf16[3,10,32,256]{3,2,1,0:T(8,128)(2,1)S(1)} %get-tuple-element.79.refs_0_, bf16[3,10,32,256]{3,2,1,0:T(8,128)(2,1)S(1)} %get-tuple-element.80.refs_1_), custom_call_target="tpu_custom_call" | custom-call | flops 1 | bytes 1 | tf_op jit(solution)/shard_map/second_weight_grads/pallas_call | solution.py:50
  27.6 0.1 collective-permute-start.10
  27.7 0.7 %second_conv.3.refs_1_ = bf16[3,10,32,256]{3,2,1,0:T(8,128)(2,1)S(1)} custom-call(bf16[10,40,768]{2,1,0:T(8,128)(2,1)S(1)} %get-tuple-element.75.cat_ref, f32[2,4,40,256]{3,2,1,0:T(8,128)S(1)} %get-tuple-element.68.near_ref, f32[2,4,40,256]{3,2,1,0:T(8,128)S(1)} %get-tuple-element.69.far_ref, bf16[2,88,256]{2,1,0:T(8,128)(2,1)S(1)} %collective-permute-done.5.halo_ref, ...), custom_call_target="tpu_custom_call" | custom-call | flops 1 | bytes 1 | tf_op jit(solution)/shard_map/second_conv/pallas_call | solution.py:50
  28.4 0.4 first_weight_grads.1
  28.8 0.0 copy-start
  28.8 0.6 %collective-permute-start.9 = (bf16[576,128]{1,0:T(8,128)(2,1)S(1)}, bf16[576,128]{1,0:T(8,128)(2,1)S(1)}, u32[]{:S(2)}, u32[]{:S(2)}) collective-permute-start(bf16[576,128]{1,0:T(8,128)(2,1)S(1)} %get-tuple-element.77), channel_id=1, source_target_pairs={{0,8},{8,0},{16,24},{24,16},{1,9},{9,1},{17,25},{25,17},{2,10},{10... | collective-permute-start | bytes 442376 | tf_op jit(solution)/shard_map/ppermute | solution.py:645
  29.4 1.0 %collective-permute-done.9 = bf16[576,128]{1,0:T(8,128)(2,1)S(1)} collective-permute-done((bf16[576,128]{1,0:T(8,128)(2,1)S(1)}, bf16[576,128]{1,0:T(8,128)(2,1)S(1)}, u32[]{:S(2)}, u32[]{:S(2)}) %collective-permute-start.9) | collective-permute-done | bytes 147488 | tf_op jit(solution)/shard_map/ppermute | solution.py:645
  30.4 0.1 blocks.1
  30.5 2.5 %collective-permute-start.11 = (bf16[432,128]{1,0:T(8,128)(2,1)S(1)}, bf16[432,128]{1,0:T(8,128)(2,1)S(1)}, u32[]{:S(2)}, u32[]{:S(2)}) collective-permute-start(bf16[432,128]{1,0:T(8,128)(2,1)S(1)} %get-tuple-element.84), channel_id=1, source_target_pairs={{2,0},{3,1},{0,2},{1,3},{6,4},{7,5},{4,6},{5,7},{10,8},{11,9},{8,1... | collective-permute-start | bytes 331784 | tf_op jit(solution)/shard_map/ppermute | solution.py:947
  33.0 1.6 %collective-permute-start.12 = (bf16[432,128]{1,0:T(8,128)(2,1)S(1)}, bf16[432,128]{1,0:T(8,128)(2,1)S(1)}, u32[]{:S(2)}, u32[]{:S(2)}) collective-permute-start(bf16[432,128]{1,0:T(8,128)(2,1)S(1)} %get-tuple-element.85), channel_id=1, source_target_pairs={{1,0},{0,1},{3,2},{2,3},{5,4},{4,5},{7,6},{6,7},{9,8},{8,9},{11,10... | collective-permute-start | bytes 331784 | tf_op jit(solution)/shard_map/ppermute | solution.py:947
  34.5 0.4 collective-permute-start.13
  35.0 5.0 %collective-permute-done.11.refs_1_ = bf16[432,128]{1,0:T(8,128)(2,1)S(1)} collective-permute-done((bf16[432,128]{1,0:T(8,128)(2,1)S(1)}, bf16[432,128]{1,0:T(8,128)(2,1)S(1)}, u32[]{:S(2)}, u32[]{:S(2)}) %collective-permute-start.11) | collective-permute-done | bytes 110624 | tf_op jit(solution)/shard_map/ppermute | solution.py:947
  40.0 0.0 collective-permute-done.12.refs_2_
  40.0 2.5 %collective-permute-done.13.refs_3_ = bf16[432,128]{1,0:T(8,128)(2,1)S(1)} collective-permute-done((bf16[432,128]{1,0:T(8,128)(2,1)S(1)}, bf16[432,128]{1,0:T(8,128)(2,1)S(1)}, u32[]{:S(2)}, u32[]{:S(2)}) %collective-permute-start.13) | collective-permute-done | bytes 110624 | tf_op jit(solution)/shard_map/ppermute | solution.py:947
  42.5 0.1 share.1.refs_0_
  42.5 1.6 %collective-permute-start.14 = (bf16[432,128]{1,0:T(8,128)(2,1)S(1)}, bf16[432,128]{1,0:T(8,128)(2,1)S(1)}, u32[]{:S(2)}, u32[]{:S(2)}) collective-permute-start(bf16[432,128]{1,0:T(8,128)(2,1)S(1)} %share.1.refs_0_), channel_id=1, source_target_pairs={{0,16},{8,24},{16,0},{24,8},{1,17},{9,25},{17,1},{25,9},{2,18},{10... | collective-permute-start | bytes 331784 | tf_op jit(solution)/shard_map/ppermute | solution.py:645
  44.2 3.2 %collective-permute-done.14.refs_1_ = bf16[432,128]{1,0:T(8,128)(2,1)S(1)} collective-permute-done((bf16[432,128]{1,0:T(8,128)(2,1)S(1)}, bf16[432,128]{1,0:T(8,128)(2,1)S(1)}, u32[]{:S(2)}, u32[]{:S(2)}) %collective-permute-start.14) | collective-permute-done | bytes 110624 | tf_op jit(solution)/shard_map/ppermute | solution.py:645
  47.4 0.1 collective-permute-start.15
  47.5 1.1 %input_conv.1 = bf16[2,4,32,128]{3,2,1,0:T(8,128)(2,1)} custom-call(bf16[9,128,256]{2,1,0:T(8,128)(2,1)S(1)} %copy-done, bf16[3,10,32,256]{3,2,1,0:T(8,128)(2,1)S(1)} %second_conv.2.refs_0_, bf16[3,10,32,256]{3,2,1,0:T(8,128)(2,1)S(1)} %second_conv.3.refs_1_), custom_call_target="tpu_custom_call" | custom-call | flops 1 | bytes 1 | tf_op jit(solution)/shard_map/input_conv/pallas_call | solution.py:50
  48.6 0.2 collective-permute-done.15.other_ref
  48.8 0.8 %cores.1 = (f32[288,128]{1,0:T(8,128)}, f32[576,128]{1,0:T(8,128)}) custom-call(bf16[432,128]{1,0:T(8,128)(2,1)S(1)} %chips.1.mine_ref, bf16[432,128]{1,0:T(8,128)(2,1)S(1)} %collective-permute-done.15.other_ref), custom_call_target="tpu_custom_call" | custom-call | flops 1 | bytes 1 | tf_op jit(solution)/shard_map/cores/pallas_call | solution.py:50
  (7 shorter events, 0.1 us)
Async XLA Ops:
  2.0 9.8 %collective-permute-start.2 = (bf16[2,2,4,32,256]{4,3,2,1,0:T(8,128)(2,1)S(1)}, bf16[2,2,4,32,256]{4,3,2,1,0:T(8,128)(2,1)S(1)}, u32[]{:S(2)}, u32[]{:S(2)}) collective-permute-start(bf16[2,2,4,32,256]{4,3,2,1,0:T(8,128)(2,1)S(1)} %get-tuple-element.53), channel_id=1, source_target_pairs={{0,4},{4,0},{1,5},{5,1},{2,6},{6,2},{3,7},{7,3},{8,12},{12,8},{9,1... | collective-permute-start | bytes 786440 | tf_op jit(solution)/shard_map/ppermute | solution.py:645
  5.0 6.7 %collective-permute-start = (bf16[10,24,128]{2,1,0:T(8,128)(2,1)S(1)}, bf16[10,24,128]{2,1,0:T(8,128)(2,1)S(1)}, u32[]{:S(2)}, u32[]{:S(2)}) collective-permute-start(bf16[10,24,128]{2,1,0:T(8,128)(2,1)S(1)} %get-tuple-element.49), channel_id=1, source_target_pairs={{0,1},{1,2},{2,3},{3,0},{4,5},{5,6},{6,7},{7,4},{8,9},{9,10},{10,1... | collective-permute-start | bytes 184328 | tf_op jit(solution)/shard_map/ppermute | solution.py:651
  6.6 5.2 %collective-permute-start.1 = (bf16[10,24,128]{2,1,0:T(8,128)(2,1)S(1)}, bf16[10,24,128]{2,1,0:T(8,128)(2,1)S(1)}, u32[]{:S(2)}, u32[]{:S(2)}) collective-permute-start(bf16[10,24,128]{2,1,0:T(8,128)(2,1)S(1)} %get-tuple-element.50), channel_id=1, source_target_pairs={{0,3},{1,0},{2,1},{3,2},{4,7},{5,4},{6,5},{7,6},{8,11},{9,8},{10,9... | collective-permute-start | bytes 184328 | tf_op jit(solution)/shard_map/ppermute | solution.py:651
  12.4 1.8 %collective-permute-start.3 = (bf16[4,5,40,256]{3,2,1,0:T(8,128)(2,1)S(1)}, bf16[4,5,40,256]{3,2,1,0:T(8,128)(2,1)S(1)}, u32[]{:S(2)}, u32[]{:S(2)}) collective-permute-start(bf16[4,5,40,256]{3,2,1,0:T(8,128)(2,1)S(1)} %head_conv_edges.1), channel_id=1, source_target_pairs={{0,8},{8,0},{16,24},{24,16},{1,9},{9,1},{17,25},{25,17},{2,10},{10... | collective-permute-start | bytes 1228808 | tf_op jit(solution)/shard_map/ppermute | solution.py:645
  14.3 5.5 %collective-permute-start.6 = (bf16[5,40,256]{2,1,0:T(8,128)(2,1)S(1)}, bf16[5,40,256]{2,1,0:T(8,128)(2,1)S(1)}, u32[]{:S(2)}, u32[]{:S(2)}) collective-permute-start(bf16[5,40,256]{2,1,0:T(8,128)(2,1)S(1)} %get-tuple-element.66), channel_id=1, source_target_pairs={{0,16},{8,24},{16,0},{24,8},{1,17},{9,25},{17,1},{25,9},{2,18},{10... | collective-permute-start | bytes 307208 | tf_op jit(solution)/shard_map/ppermute | solution.py:645
  16.3 5.3 %collective-permute-start.4 = (bf16[5,40,256]{2,1,0:T(8,128)(2,1)S(1)}, bf16[5,40,256]{2,1,0:T(8,128)(2,1)S(1)}, u32[]{:S(2)}, u32[]{:S(2)}) collective-permute-start(bf16[5,40,256]{2,1,0:T(8,128)(2,1)S(1)} %get-tuple-element.62), channel_id=1, source_target_pairs={{0,16},{8,24},{16,0},{24,8},{1,17},{9,25},{17,1},{25,9},{2,18},{10... | collective-permute-start | bytes 307208 | tf_op jit(solution)/shard_map/ppermute | solution.py:645
  16.9 4.7 %collective-permute-start.5 = (bf16[2,88,256]{2,1,0:T(8,128)(2,1)S(1)}, bf16[2,88,256]{2,1,0:T(8,128)(2,1)S(1)}, u32[]{:S(2)}, u32[]{:S(2)}) collective-permute-start(bf16[2,88,256]{2,1,0:T(8,128)(2,1)S(1)} %get-tuple-element.63), channel_id=1, source_target_pairs={{0,4},{4,0},{1,5},{5,1},{2,6},{6,2},{3,7},{7,3},{8,12},{12,8},{9,1... | collective-permute-start | bytes 270344 | tf_op jit(solution)/shard_map/ppermute | solution.py:645
  19.8 5.6 %collective-permute-start.7 = (bf16[5,40,256]{2,1,0:T(8,128)(2,1)S(1)}, bf16[5,40,256]{2,1,0:T(8,128)(2,1)S(1)}, u32[]{:S(2)}, u32[]{:S(2)}) collective-permute-start(bf16[5,40,256]{2,1,0:T(8,128)(2,1)S(1)} %chip_sum.2.total_ref), channel_id=1, source_target_pairs={{0,4},{4,0},{1,5},{5,1},{2,6},{6,2},{3,7},{7,3},{8,12},{12,8},{9,1... | collective-permute-start | bytes 307208 | tf_op jit(solution)/shard_map/ppermute | solution.py:645
  21.6 5.1 %collective-permute-start.8 = (bf16[5,40,256]{2,1,0:T(8,128)(2,1)S(1)}, bf16[5,40,256]{2,1,0:T(8,128)(2,1)S(1)}, u32[]{:S(2)}, u32[]{:S(2)}) collective-permute-start(bf16[5,40,256]{2,1,0:T(8,128)(2,1)S(1)} %chip_sum.3.total_ref), channel_id=1, source_target_pairs={{0,4},{4,0},{1,5},{5,1},{2,6},{6,2},{3,7},{7,3},{8,12},{12,8},{9,1... | collective-permute-start | bytes 307208 | tf_op jit(solution)/shard_map/ppermute | solution.py:645
  27.6 2.8 %collective-permute-start.10 = (bf16[1152,128]{1,0:T(8,128)(2,1)S(1)}, bf16[1152,128]{1,0:T(8,128)(2,1)S(1)}, u32[]{:S(2)}, u32[]{:S(2)}) collective-permute-start(bf16[1152,128]{1,0:T(8,128)(2,1)S(1)} %get-tuple-element.82), channel_id=1, source_target_pairs={{0,8},{8,0},{16,24},{24,16},{1,9},{9,1},{17,25},{25,17},{2,10},{10... | collective-permute-start | bytes 884744 | tf_op jit(solution)/shard_map/ppermute | solution.py:645
  28.8 18.7 %copy-start = (bf16[9,128,256]{2,1,0:T(8,128)(2,1)S(1)}, bf16[9,128,256]{2,1,0:T(8,128)(2,1)}, u32[]{:S(2)}) copy-start(bf16[9,128,256]{2,1,0:T(8,128)(2,1)} %w_first_ref.1) | copy-start | bytes 1769476
  28.8 1.6 %collective-permute-start.9 = (bf16[576,128]{1,0:T(8,128)(2,1)S(1)}, bf16[576,128]{1,0:T(8,128)(2,1)S(1)}, u32[]{:S(2)}, u32[]{:S(2)}) collective-permute-start(bf16[576,128]{1,0:T(8,128)(2,1)S(1)} %get-tuple-element.77), channel_id=1, source_target_pairs={{0,8},{8,0},{16,24},{24,16},{1,9},{9,1},{17,25},{25,17},{2,10},{10... | collective-permute-start | bytes 442376 | tf_op jit(solution)/shard_map/ppermute | solution.py:645
  30.5 9.5 %collective-permute-start.11 = (bf16[432,128]{1,0:T(8,128)(2,1)S(1)}, bf16[432,128]{1,0:T(8,128)(2,1)S(1)}, u32[]{:S(2)}, u32[]{:S(2)}) collective-permute-start(bf16[432,128]{1,0:T(8,128)(2,1)S(1)} %get-tuple-element.84), channel_id=1, source_target_pairs={{2,0},{3,1},{0,2},{1,3},{6,4},{7,5},{4,6},{5,7},{10,8},{11,9},{8,1... | collective-permute-start | bytes 331784 | tf_op jit(solution)/shard_map/ppermute | solution.py:947
  33.0 7.1 %collective-permute-start.12 = (bf16[432,128]{1,0:T(8,128)(2,1)S(1)}, bf16[432,128]{1,0:T(8,128)(2,1)S(1)}, u32[]{:S(2)}, u32[]{:S(2)}) collective-permute-start(bf16[432,128]{1,0:T(8,128)(2,1)S(1)} %get-tuple-element.85), channel_id=1, source_target_pairs={{1,0},{0,1},{3,2},{2,3},{5,4},{4,5},{7,6},{6,7},{9,8},{8,9},{11,10... | collective-permute-start | bytes 331784 | tf_op jit(solution)/shard_map/ppermute | solution.py:947
  34.5 7.9 %collective-permute-start.13 = (bf16[432,128]{1,0:T(8,128)(2,1)S(1)}, bf16[432,128]{1,0:T(8,128)(2,1)S(1)}, u32[]{:S(2)}, u32[]{:S(2)}) collective-permute-start(bf16[432,128]{1,0:T(8,128)(2,1)S(1)} %get-tuple-element.86), channel_id=1, source_target_pairs={{3,0},{2,1},{1,2},{0,3},{7,4},{6,5},{5,6},{4,7},{11,8},{10,9},{9,1... | collective-permute-start | bytes 331784 | tf_op jit(solution)/shard_map/ppermute | solution.py:947
  42.5 4.8 %collective-permute-start.14 = (bf16[432,128]{1,0:T(8,128)(2,1)S(1)}, bf16[432,128]{1,0:T(8,128)(2,1)S(1)}, u32[]{:S(2)}, u32[]{:S(2)}) collective-permute-start(bf16[432,128]{1,0:T(8,128)(2,1)S(1)} %share.1.refs_0_), channel_id=1, source_target_pairs={{0,16},{8,24},{16,0},{24,8},{1,17},{9,25},{17,1},{25,9},{2,18},{10... | collective-permute-start | bytes 331784 | tf_op jit(solution)/shard_map/ppermute | solution.py:645
  47.4 1.4 %collective-permute-start.15 = (bf16[432,128]{1,0:T(8,128)(2,1)S(1)}, bf16[432,128]{1,0:T(8,128)(2,1)S(1)}, u32[]{:S(2)}, u32[]{:S(2)}) collective-permute-start(bf16[432,128]{1,0:T(8,128)(2,1)S(1)} %chips.1.mine_ref), channel_id=1, source_target_pairs={{0,8},{8,0},{16,24},{24,16},{1,9},{9,1},{17,25},{25,17},{2,10},{10... | collective-permute-start | bytes 331784 | tf_op jit(solution)/shard_map/ppermute | solution.py:645

commit v8 on v7

--- a/solution.py
+++ b/solution.py
@@ -59,8 +59,7 @@
     )(*arrays)
 
 
-def pack_kernel(with_tile, grads_far, second_far, first_far, right_ref, left_ref, *refs):
-    grads_near, second_near, first_near, edges, edges_wide, packed, sems, tile_sems = refs[-8:]
+def pack_kernel(grads_far, second_far, first_far, right_ref, left_ref, grads_near, second_near, first_near, edges, edges_wide, packed, sems):
     heads, batch, height, breadth, _ = grads_far.shape
     samples = second_far.shape[0]
     rows = 6 * height
@@ -71,11 +70,6 @@
             source = far.at[:, :, :, columns, :] if j == 0 else far.at[:, :, columns, :]
             copies.append(pltpu.make_async_copy(source, near.at[side], sems.at[side, j]))
             copies[-1].start()
-    tile_copies = []
-    if with_tile:
-        for j, far in enumerate((second_far, first_far)):
-            tile_copies.append(pltpu.make_async_copy(far, refs[0].at[j], tile_sems.at[j]))
-            tile_copies[-1].start()
     for copy in copies:
         copy.wait()
     for side, out_ref in ((0, right_ref), (1, left_ref)):
@@ -108,18 +102,16 @@
                         half, pl.ds((j * samples + s) * height * 8 + inner, height, stride=8), :
                     ]
         out_ref[...] = packed[: (batch + samples) * rows].astype(BF).reshape(out_ref.shape)
-    for copy in tile_copies:
-        copy.wait()
-
-
-def pack(head_grads, pre_second, pre_first, with_tile):
+
+
+def pack(head_grads, pre_second, pre_first):
     heads, batch, height, _, _ = head_grads.shape
     samples = pre_second.shape[0]
     shape = jax.ShapeDtypeStruct((batch + samples, 6 * height, LANES), BF)
     return run(
         "pack_columns",
-        functools.partial(pack_kernel, with_tile),
-        [shape, shape] + [jax.ShapeDtypeStruct((2,) + pre_second.shape, BF)] * with_tile,
+        pack_kernel,
+        [shape, shape],
         [head_grads, pre_second, pre_first],
         [
             pltpu.VMEM((2, heads, batch, height, 16, LANES), BF),
@@ -129,7 +121,6 @@
             pltpu.VMEM((2, 2 * samples * height * 8 + 64, LANES), F32),
             pltpu.VMEM(((batch + samples) * 6 * height + 16, LANES), F32),
             pltpu.SemaphoreType.DMA((2, 3)),
-            pltpu.SemaphoreType.DMA((2,)),
         ],
         far=True,
     )
@@ -727,11 +718,11 @@
     )
 
 
-def far_kernel(first_ref, tile_ref, slope_second, slope_first, act_out, wide, act):
+def far_kernel(first_ref, tile_second, tile_first, slope_second, slope_first, act_out, wide, act):
     samples, height, breadth, depth = first_ref.shape
     kept = breadth + 2 * EDGE
     lat = lax.axis_index("lat")
-    for source_ref, slope_ref in ((tile_ref.at[0], slope_second), (tile_ref.at[1], slope_first)):
+    for source_ref, slope_ref in ((tile_second, slope_second), (tile_first, slope_first)):
         wide[...] = jnp.zeros(wide.shape, F32)
         for s in range(samples):
             for half in range(2):
@@ -742,11 +733,11 @@
         slope_ref[...] = gelu_slope(value).reshape(slope_ref.shape)
     own, other = pl.ds(height * lat, height), pl.ds(height * (1 - lat), height)
     act[:, own] = gelu_value(first_ref[...].astype(F32))
-    act[:, other] = gelu_value(tile_ref[1].astype(F32))
+    act[:, other] = gelu_value(tile_first[...].astype(F32))
     act_out[...] = act[...].reshape(act_out.shape[1], depth).T.astype(BF)
 
 
-def far_parts(pre_first, tile):
+def far_parts(pre_first, tile_second, tile_first):
     samples, height, breadth, depth = pre_first.shape
     kept = breadth + 2 * EDGE
     slope = jax.ShapeDtypeStruct((samples, height, kept, depth), F32)
@@ -754,7 +745,7 @@
         "far_parts",
         far_kernel,
         [slope, slope, jax.ShapeDtypeStruct((depth, 2 * samples * height * breadth), BF)],
-        [pre_first, tile],
+        [pre_first, tile_second, tile_first],
         [
             pltpu.VMEM((2, samples * height * kept, LANES), F32),
             pltpu.VMEM((samples, 2 * height, breadth, depth), F32),
@@ -950,15 +941,15 @@
 def two_bands(head_grads, head_weights, encoder_input, pre_first, pre_second, w_first, w_second, norm_factor):
     samples, height, breadth, _ = encoder_input.shape
     columns = lax.axis_size("lon")
-    to_right, to_left, tile = pack(head_grads, pre_second, pre_first, True)
-    tile = swap(tile, "lat", 1)
+    tiles = [swap(array, "lat", 1) for array in (pre_second, pre_first)]
+    to_right, to_left = pack(head_grads, pre_second, pre_first)
     low = around(to_right, "lon", 1)
     high = around(to_left, "lon", -1)
     head_grads, head_weights, w_second, pre_second, pre_first, encoder_input = stage(
         head_grads, head_weights, w_second, pre_second, pre_first, encoder_input
     )
     inside = inside_conv(head_grads, head_weights, 2 * samples)
-    low, high, inside, tile = lax.optimization_barrier((low, high, inside, tile))
+    low, high, inside, *tiles = lax.optimization_barrier((low, high, inside, *tiles))
     heads_of = functools.partial(
         head_conv,
         head_grads=head_grads,
@@ -980,7 +971,7 @@
     cross[-1], halo = lax.optimization_barrier((cross[-1], halo))
     totals = [run("chip_sum", sum_kernel, [part_shape], [own[s], cross[s]])[0] for s in everyone]
     lines = [swap(total, "lat", 1) for total in totals]
-    far_second, far_first, act = far_parts(pre_first, tile)
+    far_second, far_first, act = far_parts(pre_first, *tiles)
 
     moved_second, moved_first = [], []
     for s in everyone:
@@ -1022,7 +1013,7 @@
 def general(head_grads, head_weights, encoder_input, pre_first, pre_second, w_first, w_second, norm_factor):
     samples, height, breadth, _ = encoder_input.shape
     bands, columns = lax.axis_size("lat"), lax.axis_size("lon")
-    to_right, to_left = pack(head_grads, pre_second, pre_first, False)
+    to_right, to_left = pack(head_grads, pre_second, pre_first)
     to_right, to_left, to_cross = lax.optimization_barrier((to_right, to_left, pre_first))
     low = around(to_right, "lon", 1)
     high = around(to_left, "lon", -1)

time: 50.3 us -> 50.1 us (level)
  waiting for transfers between devices: 16.5 us -> 14.3 us
  starting transfers between devices: 19.9 us -> 22 us
    ppermute x11 -> x12, waiting for transfers between devices: 8.96 us -> 7.15 us  [swap(): return lax.ppermute(array, axis, [(i, i ^ flip) for i in range(count)])]
    ppermute x11 -> x12, starting transfers between devices: 11.6 us -> 13.3 us  [swap(): return lax.ppermute(array, axis, [(i, i ^ flip) for i in range(count)])]
  transfers between devices with their start and end apart: 16 -> 17, of which waited for: 10 -> 10; matrix products, arithmetic and copies ran while one was open for 0% -> 0% of each run, Pallas kernels for 17% -> 20%
where the time goes in v8:
time: 50.1 us; the launch traced here: 49.4 us
  starting transfers between devices  22 us (44%)
  waiting for transfers between devices  14.3 us (29%)
  Pallas kernels  12.3 us (25%)
  between operations  0.82 us (2%)
    ppermute x12, starting transfers between devices, swap(): return lax.ppermute(array, axis, [(i, i ^ flip) for i in range(count)])  13.3 us
    pallas_call x21, Pallas kernels, run(): pl.pallas_call(kernel, name=name, out_shape=out_shape, in_specs=specs, ou...  12.3 us
    ppermute x3, waiting for transfers between devices, to_partner(): lax.ppermute(array, 'lon', [(partner(i, step, count), i) for i in range(c...  7.16 us
    ppermute x12, waiting for transfers between devices, swap(): return lax.ppermute(array, axis, [(i, i ^ flip) for i in range(count)])  7.15 us
    ppermute x3, starting transfers between devices, to_partner(): lax.ppermute(array, 'lon', [(partner(i, step, count), i) for i in range(c...  4.47 us
    ppermute x2, starting transfers between devices, around(): return lax.ppermute(array, axis, pairs)  4.15 us
  transfers between devices with their start and end apart: 17, of which 10 were waited for; matrix products, arithmetic and copies ran while one was open for 0% of the time, Pallas kernels for 20%

profile of v8, /device:TPU:0, one launch (start us, length us, event | category | flops | bytes accessed | tf_op | source)
XLA Modules:
  0.0 49.4 jit_solution(8730385104479534454)
XLA Ops:
  0.6 3.0 %collective-permute-start.3 = (bf16[2,4,32,256]{3,2,1,0:T(8,128)(2,1)}, bf16[2,4,32,256]{3,2,1,0:T(8,128)(2,1)S(1)}, u32[]{:S(2)}, u32[]{:S(2)}) collective-permute-start(bf16[2,4,32,256]{3,2,1,0:T(8,128)(2,1)} %first_far.1), channel_id=1, source_target_pairs={{0,4},{4,0},{1,5},{5,1},{2,6},{6,2},{3,7},{7,3},{8,12},{12,8},{9,1... | collective-permute-start | bytes 393224 | tf_op jit(solution)/shard_map/ppermute | solution.py:636
  3.7 0.1 collective-permute-start.2
  3.7 1.3 %pack_columns.1 = (bf16[10,24,128]{2,1,0:T(8,128)(2,1)S(1)}, bf16[10,24,128]{2,1,0:T(8,128)(2,1)S(1)}) custom-call(bf16[2,8,4,32,128]{4,3,2,1,0:T(8,128)(2,1)} %grads_far.1, bf16[2,4,32,256]{3,2,1,0:T(8,128)(2,1)} %second_far.1, bf16[2,4,32,256]{3,2,1,0:T(8,128)(2,1)} %first_far.1), custom_call_target="tpu_custom_call" | custom-call | flops 1 | bytes 1 | tf_op jit(solution)/shard_map/pack_columns/pallas_call | solution.py:50
  5.0 2.1 %collective-permute-start = (bf16[10,24,128]{2,1,0:T(8,128)(2,1)S(1)}, bf16[10,24,128]{2,1,0:T(8,128)(2,1)S(1)}, u32[]{:S(2)}, u32[]{:S(2)}) collective-permute-start(bf16[10,24,128]{2,1,0:T(8,128)(2,1)S(1)} %get-tuple-element.49), channel_id=1, source_target_pairs={{0,1},{1,2},{2,3},{3,0},{4,5},{5,6},{6,7},{7,4},{8,9},{9,10},{10,1... | collective-permute-start | bytes 184328 | tf_op jit(solution)/shard_map/ppermute | solution.py:642
  7.1 2.1 %collective-permute-start.1 = (bf16[10,24,128]{2,1,0:T(8,128)(2,1)S(1)}, bf16[10,24,128]{2,1,0:T(8,128)(2,1)S(1)}, u32[]{:S(2)}, u32[]{:S(2)}) collective-permute-start(bf16[10,24,128]{2,1,0:T(8,128)(2,1)S(1)} %get-tuple-element.50), channel_id=1, source_target_pairs={{0,3},{1,0},{2,1},{3,2},{4,7},{5,4},{6,5},{7,6},{8,11},{9,8},{10,9... | collective-permute-start | bytes 184328 | tf_op jit(solution)/shard_map/ppermute | solution.py:642
  9.2 1.9 %stage.1 = (bf16[2,8,4,32,128]{4,3,2,1,0:T(8,128)(2,1)S(1)}, bf16[2,9,256,128]{3,2,1,0:T(8,128)(2,1)S(1)}, bf16[9,256,256]{2,1,0:T(8,128)(2,1)S(1)}, bf16[2,4,32...) custom-call(bf16[2,8,4,32,128]{4,3,2,1,0:T(8,128)(2,1)} %grads_far.1, ...), custom_call_target="tpu_custom_call" | custom-call | flops 1 | bytes 1 | tf_op jit(solution)/shard_map/stage/pallas_call | solution.py:50
  11.0 1.0 %head_conv_inside.1.inside_ref = f32[4,6,40,256]{3,2,1,0:T(8,128)S(1)} custom-call(bf16[2,8,4,32,128]{4,3,2,1,0:T(8,128)(2,1)S(1)} %get-tuple-element.51.grads_ref, bf16[2,9,256,128]{3,2,1,0:T(8,128)(2,1)S(1)} %get-tuple-element.52.weights_ref), custom_call_target="tpu_custom_call" | custom-call | flops 1 | bytes 1 | tf_op jit(solution)/shard_map/head_conv_inside/pallas_call | solution.py:50
  12.1 0.0 collective-permute-done.low_ref
  12.1 0.0 collective-permute-done.1.high_ref
  12.1 0.6 %head_conv_edges.1 = bf16[4,5,40,256]{3,2,1,0:T(8,128)(2,1)S(1)} custom-call(f32[4,6,40,256]{3,2,1,0:T(8,128)S(1)} %head_conv_inside.1.inside_ref, bf16[10,24,128]{2,1,0:T(8,128)(2,1)S(1)} %collective-permute-done.low_ref, bf16[10,24,128]{2,1,0:T(8,128)(2,1)S(1)} %collective-permute-done.1.high_ref, bf16[2,9,256,128]{3,2,1,0:T(8,128)(2,1)S(1)} %get-tuple-element.52.weights_ref), custom_call_target="tpu_custom_call" | custom-call | flops 1 | bytes 1 | tf_op jit(solution)/shard_map/head_conv_edges/pallas_call | solution.py:50
  12.7 0.1 collective-permute-start.4
  12.8 1.1 %head_conv.1.mine_ref = bf16[4,5,40,256]{3,2,1,0:T(8,128)(2,1)S(1)} custom-call(bf16[2,8,4,32,128]{4,3,2,1,0:T(8,128)(2,1)S(1)} %get-tuple-element.51.grads_ref, bf16[10,24,128]{2,1,0:T(8,128)(2,1)S(1)} %collective-permute-done.low_ref, bf16[10,24,128]{2,1,0:T(8,128)(2,1)S(1)} %collective-permute-done.1.high_ref, ...), custom_call_target="tpu_custom_call" | custom-call | flops 1 | bytes 1 | tf_op jit(solution)/shard_map/head_conv/pallas_call | solution.py:50
  14.0 0.6 %collective-permute-done.4.got_ref = bf16[4,5,40,256]{3,2,1,0:T(8,128)(2,1)S(1)} collective-permute-done((bf16[4,5,40,256]{3,2,1,0:T(8,128)(2,1)S(1)}, bf16[4,5,40,256]{3,2,1,0:T(8,128)(2,1)S(1)}, u32[]{:S(2)}, u32[]{:S(2)}) %collective-permute-start.4) | collective-permute-done | bytes 409632 | tf_op jit(solution)/shard_map/ppermute | solution.py:636
  14.6 0.1 core_sum.1
  14.6 1.7 %collective-permute-start.7 = (bf16[5,40,256]{2,1,0:T(8,128)(2,1)S(1)}, bf16[5,40,256]{2,1,0:T(8,128)(2,1)S(1)}, u32[]{:S(2)}, u32[]{:S(2)}) collective-permute-start(bf16[5,40,256]{2,1,0:T(8,128)(2,1)S(1)} %get-tuple-element.66), channel_id=1, source_target_pairs={{0,16},{8,24},{16,0},{24,8},{1,17},{9,25},{17,1},{25,9},{2,18},{10... | collective-permute-start | bytes 307208 | tf_op jit(solution)/shard_map/ppermute | solution.py:636
  16.4 0.4 near_parts.1
  16.8 0.4 collective-permute-start.5
  17.2 1.7 %collective-permute-start.6 = (bf16[2,88,256]{2,1,0:T(8,128)(2,1)S(1)}, bf16[2,88,256]{2,1,0:T(8,128)(2,1)S(1)}, u32[]{:S(2)}, u32[]{:S(2)}) collective-permute-start(bf16[2,88,256]{2,1,0:T(8,128)(2,1)S(1)} %get-tuple-element.63), channel_id=1, source_target_pairs={{0,4},{4,0},{1,5},{5,1},{2,6},{6,2},{3,7},{7,3},{8,12},{12,8},{9,1... | collective-permute-start | bytes 270344 | tf_op jit(solution)/shard_map/ppermute | solution.py:636
  18.9 1.0 %collective-permute-done.7.refs_1_ = bf16[5,40,256]{2,1,0:T(8,128)(2,1)S(1)} collective-permute-done((bf16[5,40,256]{2,1,0:T(8,128)(2,1)S(1)}, bf16[5,40,256]{2,1,0:T(8,128)(2,1)S(1)}, u32[]{:S(2)}, u32[]{:S(2)}) %collective-permute-start.7) | collective-permute-done | bytes 102432 | tf_op jit(solution)/shard_map/ppermute | solution.py:636
  20.0 1.9 %collective-permute-start.8 = (bf16[5,40,256]{2,1,0:T(8,128)(2,1)S(1)}, bf16[5,40,256]{2,1,0:T(8,128)(2,1)S(1)}, u32[]{:S(2)}, u32[]{:S(2)}) collective-permute-start(bf16[5,40,256]{2,1,0:T(8,128)(2,1)S(1)} %chip_sum.2.total_ref), channel_id=1, source_target_pairs={{0,4},{4,0},{1,5},{5,1},{2,6},{6,2},{3,7},{7,3},{8,12},{12,8},{9,1... | collective-permute-start | bytes 307208 | tf_op jit(solution)/shard_map/ppermute | solution.py:636
  21.9 0.1 collective-permute-done.6.halo_ref
  22.0 1.7 %collective-permute-start.9 = (bf16[5,40,256]{2,1,0:T(8,128)(2,1)S(1)}, bf16[5,40,256]{2,1,0:T(8,128)(2,1)S(1)}, u32[]{:S(2)}, u32[]{:S(2)}) collective-permute-start(bf16[5,40,256]{2,1,0:T(8,128)(2,1)S(1)} %chip_sum.3.total_ref), channel_id=1, source_target_pairs={{0,4},{4,0},{1,5},{5,1},{2,6},{6,2},{3,7},{7,3},{8,12},{12,8},{9,1... | collective-permute-start | bytes 307208 | tf_op jit(solution)/shard_map/ppermute | solution.py:636
  23.7 0.6 %far_parts.1 = (f32[2,4,40,256]{3,2,1,0:T(8,128)S(1)}, f32[2,4,40,256]{3,2,1,0:T(8,128)S(1)}, bf16[256,512]{1,0:T(8,128)(2,1)S(1)}) custom-call(bf16[2,4,32,256]{3,2,1,0:T(8,128)(2,1)S(1)} %get-tuple-element.47.first_ref, bf16[2,4,32,256]{3,2,1,0:T(8,128)(2,1)S(1)} %collective-permute-done.2.tile_second, ...), custom_call_target="tpu_custom_call" | custom-call | flops 1 | bytes 1 | tf_op jit(solution)/shard_map/far_parts/pallas_call | solution.py:50
  24.4 1.1 %collective-permute-done.8.line_ref = bf16[5,40,256]{2,1,0:T(8,128)(2,1)S(1)} collective-permute-done((bf16[5,40,256]{2,1,0:T(8,128)(2,1)S(1)}, bf16[5,40,256]{2,1,0:T(8,128)(2,1)S(1)}, u32[]{:S(2)}, u32[]{:S(2)}) %collective-permute-start.8) | collective-permute-done | bytes 102432 | tf_op jit(solution)/shard_map/ppermute | solution.py:636
  25.5 0.4 latent_grads.2
  25.9 0.7 %second_conv.2.refs_0_ = bf16[3,10,32,256]{3,2,1,0:T(8,128)(2,1)S(1)} custom-call(bf16[10,40,768]{2,1,0:T(8,128)(2,1)S(1)} %get-tuple-element.67.cat_ref, f32[2,4,40,256]{3,2,1,0:T(8,128)S(1)} %get-tuple-element.68.near_ref, f32[2,4,40,256]{3,2,1,0:T(8,128)S(1)} %get-tuple-element.69.far_ref, bf16[2,88,256]{2,1,0:T(8,128)(2,1)S(1)} %collective-permute-done.6.halo_ref, ...), custom_call_target="tpu_custom_call" | custom-call | flops 1 | bytes 1 | tf_op jit(solution)/shard_map/second_conv/pallas_call | solution.py:50
  26.6 0.3 collective-permute-done.9.line_ref
  26.9 0.4 latent_grads.3
  27.3 0.5 %second_weight_grads.1 = (bf16[1152,128]{1,0:T(8,128)(2,1)S(1)}, bf16[1152,128]{1,0:T(8,128)(2,1)S(1)}) custom-call(bf16[256,512]{1,0:T(8,128)(2,1)S(1)} %get-tuple-element.78.act_ref, bf16[3,10,32,256]{3,2,1,0:T(8,128)(2,1)S(1)} %get-tuple-element.79.refs_0_, bf16[3,10,32,256]{3,2,1,0:T(8,128)(2,1)S(1)} %get-tuple-element.80.refs_1_), custom_call_target="tpu_custom_call" | custom-call | flops 1 | bytes 1 | tf_op jit(solution)/shard_map/second_weight_grads/pallas_call | solution.py:50
  27.8 0.1 collective-permute-start.11
  27.9 0.7 %second_conv.3.refs_1_ = bf16[3,10,32,256]{3,2,1,0:T(8,128)(2,1)S(1)} custom-call(bf16[10,40,768]{2,1,0:T(8,128)(2,1)S(1)} %get-tuple-element.75.cat_ref, f32[2,4,40,256]{3,2,1,0:T(8,128)S(1)} %get-tuple-element.68.near_ref, f32[2,4,40,256]{3,2,1,0:T(8,128)S(1)} %get-tuple-element.69.far_ref, bf16[2,88,256]{2,1,0:T(8,128)(2,1)S(1)} %collective-permute-done.6.halo_ref, ...), custom_call_target="tpu_custom_call" | custom-call | flops 1 | bytes 1 | tf_op jit(solution)/shard_map/second_conv/pallas_call | solution.py:50
  28.6 0.4 first_weight_grads.1
  29.0 0.0 copy-start
  29.0 0.6 %collective-permute-start.10 = (bf16[576,128]{1,0:T(8,128)(2,1)S(1)}, bf16[576,128]{1,0:T(8,128)(2,1)S(1)}, u32[]{:S(2)}, u32[]{:S(2)}) collective-permute-start(bf16[576,128]{1,0:T(8,128)(2,1)S(1)} %get-tuple-element.77), channel_id=1, source_target_pairs={{0,8},{8,0},{16,24},{24,16},{1,9},{9,1},{17,25},{25,17},{2,10},{10... | collective-permute-start | bytes 442376 | tf_op jit(solution)/shard_map/ppermute | solution.py:636
  29.6 1.0 %collective-permute-done.10 = bf16[576,128]{1,0:T(8,128)(2,1)S(1)} collective-permute-done((bf16[576,128]{1,0:T(8,128)(2,1)S(1)}, bf16[576,128]{1,0:T(8,128)(2,1)S(1)}, u32[]{:S(2)}, u32[]{:S(2)}) %collective-permute-start.10) | collective-permute-done | bytes 147488 | tf_op jit(solution)/shard_map/ppermute | solution.py:636
  30.6 0.1 blocks.1
  30.7 2.1 %collective-permute-start.12 = (bf16[432,128]{1,0:T(8,128)(2,1)S(1)}, bf16[432,128]{1,0:T(8,128)(2,1)S(1)}, u32[]{:S(2)}, u32[]{:S(2)}) collective-permute-start(bf16[432,128]{1,0:T(8,128)(2,1)S(1)} %get-tuple-element.84), channel_id=1, source_target_pairs={{2,0},{3,1},{0,2},{1,3},{6,4},{7,5},{4,6},{5,7},{10,8},{11,9},{8,1... | collective-permute-start | bytes 331784 | tf_op jit(solution)/shard_map/ppermute | solution.py:938
  32.8 1.7 %collective-permute-start.13 = (bf16[432,128]{1,0:T(8,128)(2,1)S(1)}, bf16[432,128]{1,0:T(8,128)(2,1)S(1)}, u32[]{:S(2)}, u32[]{:S(2)}) collective-permute-start(bf16[432,128]{1,0:T(8,128)(2,1)S(1)} %get-tuple-element.85), channel_id=1, source_target_pairs={{1,0},{0,1},{3,2},{2,3},{5,4},{4,5},{7,6},{6,7},{9,8},{8,9},{11,10... | collective-permute-start | bytes 331784 | tf_op jit(solution)/shard_map/ppermute | solution.py:938
  34.4 0.7 %collective-permute-start.14 = (bf16[432,128]{1,0:T(8,128)(2,1)S(1)}, bf16[432,128]{1,0:T(8,128)(2,1)S(1)}, u32[]{:S(2)}, u32[]{:S(2)}) collective-permute-start(bf16[432,128]{1,0:T(8,128)(2,1)S(1)} %get-tuple-element.86), channel_id=1, source_target_pairs={{3,0},{2,1},{1,2},{0,3},{7,4},{6,5},{5,6},{4,7},{11,8},{10,9},{9,1... | collective-permute-start | bytes 331784 | tf_op jit(solution)/shard_map/ppermute | solution.py:938
  35.2 5.2 %collective-permute-done.12.refs_1_ = bf16[432,128]{1,0:T(8,128)(2,1)S(1)} collective-permute-done((bf16[432,128]{1,0:T(8,128)(2,1)S(1)}, bf16[432,128]{1,0:T(8,128)(2,1)S(1)}, u32[]{:S(2)}, u32[]{:S(2)}) %collective-permute-start.12) | collective-permute-done | bytes 110624 | tf_op jit(solution)/shard_map/ppermute | solution.py:938
  40.3 2.0 %collective-permute-done.14.refs_3_ = bf16[432,128]{1,0:T(8,128)(2,1)S(1)} collective-permute-done((bf16[432,128]{1,0:T(8,128)(2,1)S(1)}, bf16[432,128]{1,0:T(8,128)(2,1)S(1)}, u32[]{:S(2)}, u32[]{:S(2)}) %collective-permute-start.14) | collective-permute-done | bytes 110624 | tf_op jit(solution)/shard_map/ppermute | solution.py:938
  42.3 0.1 share.1.refs_0_
  42.4 2.0 %collective-permute-start.15 = (bf16[432,128]{1,0:T(8,128)(2,1)S(1)}, bf16[432,128]{1,0:T(8,128)(2,1)S(1)}, u32[]{:S(2)}, u32[]{:S(2)}) collective-permute-start(bf16[432,128]{1,0:T(8,128)(2,1)S(1)} %share.1.refs_0_), channel_id=1, source_target_pairs={{0,16},{8,24},{16,0},{24,8},{1,17},{9,25},{17,1},{25,9},{2,18},{10... | collective-permute-start | bytes 331784 | tf_op jit(solution)/shard_map/ppermute | solution.py:636
  44.4 2.9 %collective-permute-done.15.refs_1_ = bf16[432,128]{1,0:T(8,128)(2,1)S(1)} collective-permute-done((bf16[432,128]{1,0:T(8,128)(2,1)S(1)}, bf16[432,128]{1,0:T(8,128)(2,1)S(1)}, u32[]{:S(2)}, u32[]{:S(2)}) %collective-permute-start.15) | collective-permute-done | bytes 110624 | tf_op jit(solution)/shard_map/ppermute | solution.py:636
  47.2 0.1 collective-permute-start.16
  47.3 1.1 %input_conv.1 = bf16[2,4,32,128]{3,2,1,0:T(8,128)(2,1)} custom-call(bf16[9,128,256]{2,1,0:T(8,128)(2,1)S(1)} %copy-done, bf16[3,10,32,256]{3,2,1,0:T(8,128)(2,1)S(1)} %second_conv.2.refs_0_, bf16[3,10,32,256]{3,2,1,0:T(8,128)(2,1)S(1)} %second_conv.3.refs_1_), custom_call_target="tpu_custom_call" | custom-call | flops 1 | bytes 1 | tf_op jit(solution)/shard_map/input_conv/pallas_call | solution.py:50
  48.4 0.2 collective-permute-done.16.other_ref
  48.6 0.8 %cores.1 = (f32[288,128]{1,0:T(8,128)}, f32[576,128]{1,0:T(8,128)}) custom-call(bf16[432,128]{1,0:T(8,128)(2,1)S(1)} %chips.1.mine_ref, bf16[432,128]{1,0:T(8,128)(2,1)S(1)} %collective-permute-done.16.other_ref), custom_call_target="tpu_custom_call" | custom-call | flops 1 | bytes 1 | tf_op jit(solution)/shard_map/cores/pallas_call | solution.py:50
  (9 shorter events, 0.1 us)
Async XLA Ops:
  0.6 11.4 %collective-permute-start.3 = (bf16[2,4,32,256]{3,2,1,0:T(8,128)(2,1)}, bf16[2,4,32,256]{3,2,1,0:T(8,128)(2,1)S(1)}, u32[]{:S(2)}, u32[]{:S(2)}) collective-permute-start(bf16[2,4,32,256]{3,2,1,0:T(8,128)(2,1)} %first_far.1), channel_id=1, source_target_pairs={{0,4},{4,0},{1,5},{5,1},{2,6},{6,2},{3,7},{7,3},{8,12},{12,8},{9,1... | collective-permute-start | bytes 393224 | tf_op jit(solution)/shard_map/ppermute | solution.py:636
  3.7 8.4 %collective-permute-start.2 = (bf16[2,4,32,256]{3,2,1,0:T(8,128)(2,1)}, bf16[2,4,32,256]{3,2,1,0:T(8,128)(2,1)S(1)}, u32[]{:S(2)}, u32[]{:S(2)}) collective-permute-start(bf16[2,4,32,256]{3,2,1,0:T(8,128)(2,1)} %second_far.1), channel_id=1, source_target_pairs={{0,4},{4,0},{1,5},{5,1},{2,6},{6,2},{3,7},{7,3},{8,12},{12,8},{9,1... | collective-permute-start | bytes 393224 | tf_op jit(solution)/shard_map/ppermute | solution.py:636
  5.0 7.0 %collective-permute-start = (bf16[10,24,128]{2,1,0:T(8,128)(2,1)S(1)}, bf16[10,24,128]{2,1,0:T(8,128)(2,1)S(1)}, u32[]{:S(2)}, u32[]{:S(2)}) collective-permute-start(bf16[10,24,128]{2,1,0:T(8,128)(2,1)S(1)} %get-tuple-element.49), channel_id=1, source_target_pairs={{0,1},{1,2},{2,3},{3,0},{4,5},{5,6},{6,7},{7,4},{8,9},{9,10},{10,1... | collective-permute-start | bytes 184328 | tf_op jit(solution)/shard_map/ppermute | solution.py:642
  7.1 5.0 %collective-permute-start.1 = (bf16[10,24,128]{2,1,0:T(8,128)(2,1)S(1)}, bf16[10,24,128]{2,1,0:T(8,128)(2,1)S(1)}, u32[]{:S(2)}, u32[]{:S(2)}) collective-permute-start(bf16[10,24,128]{2,1,0:T(8,128)(2,1)S(1)} %get-tuple-element.50), channel_id=1, source_target_pairs={{0,3},{1,0},{2,1},{3,2},{4,7},{5,4},{6,5},{7,6},{8,11},{9,8},{10,9... | collective-permute-start | bytes 184328 | tf_op jit(solution)/shard_map/ppermute | solution.py:642
  12.7 1.8 %collective-permute-start.4 = (bf16[4,5,40,256]{3,2,1,0:T(8,128)(2,1)S(1)}, bf16[4,5,40,256]{3,2,1,0:T(8,128)(2,1)S(1)}, u32[]{:S(2)}, u32[]{:S(2)}) collective-permute-start(bf16[4,5,40,256]{3,2,1,0:T(8,128)(2,1)S(1)} %head_conv_edges.1), channel_id=1, source_target_pairs={{0,8},{8,0},{16,24},{24,16},{1,9},{9,1},{17,25},{25,17},{2,10},{10... | collective-permute-start | bytes 1228808 | tf_op jit(solution)/shard_map/ppermute | solution.py:636
  14.6 5.3 %collective-permute-start.7 = (bf16[5,40,256]{2,1,0:T(8,128)(2,1)S(1)}, bf16[5,40,256]{2,1,0:T(8,128)(2,1)S(1)}, u32[]{:S(2)}, u32[]{:S(2)}) collective-permute-start(bf16[5,40,256]{2,1,0:T(8,128)(2,1)S(1)} %get-tuple-element.66), channel_id=1, source_target_pairs={{0,16},{8,24},{16,0},{24,8},{1,17},{9,25},{17,1},{25,9},{2,18},{10... | collective-permute-start | bytes 307208 | tf_op jit(solution)/shard_map/ppermute | solution.py:636
  16.8 5.1 %collective-permute-start.5 = (bf16[5,40,256]{2,1,0:T(8,128)(2,1)S(1)}, bf16[5,40,256]{2,1,0:T(8,128)(2,1)S(1)}, u32[]{:S(2)}, u32[]{:S(2)}) collective-permute-start(bf16[5,40,256]{2,1,0:T(8,128)(2,1)S(1)} %get-tuple-element.62), channel_id=1, source_target_pairs={{0,16},{8,24},{16,0},{24,8},{1,17},{9,25},{17,1},{25,9},{2,18},{10... | collective-permute-start | bytes 307208 | tf_op jit(solution)/shard_map/ppermute | solution.py:636
  17.2 4.7 %collective-permute-start.6 = (bf16[2,88,256]{2,1,0:T(8,128)(2,1)S(1)}, bf16[2,88,256]{2,1,0:T(8,128)(2,1)S(1)}, u32[]{:S(2)}, u32[]{:S(2)}) collective-permute-start(bf16[2,88,256]{2,1,0:T(8,128)(2,1)S(1)} %get-tuple-element.63), channel_id=1, source_target_pairs={{0,4},{4,0},{1,5},{5,1},{2,6},{6,2},{3,7},{7,3},{8,12},{12,8},{9,1... | collective-permute-start | bytes 270344 | tf_op jit(solution)/shard_map/ppermute | solution.py:636
  20.0 5.5 %collective-permute-start.8 = (bf16[5,40,256]{2,1,0:T(8,128)(2,1)S(1)}, bf16[5,40,256]{2,1,0:T(8,128)(2,1)S(1)}, u32[]{:S(2)}, u32[]{:S(2)}) collective-permute-start(bf16[5,40,256]{2,1,0:T(8,128)(2,1)S(1)} %chip_sum.2.total_ref), channel_id=1, source_target_pairs={{0,4},{4,0},{1,5},{5,1},{2,6},{6,2},{3,7},{7,3},{8,12},{12,8},{9,1... | collective-permute-start | bytes 307208 | tf_op jit(solution)/shard_map/ppermute | solution.py:636
  22.0 4.9 %collective-permute-start.9 = (bf16[5,40,256]{2,1,0:T(8,128)(2,1)S(1)}, bf16[5,40,256]{2,1,0:T(8,128)(2,1)S(1)}, u32[]{:S(2)}, u32[]{:S(2)}) collective-permute-start(bf16[5,40,256]{2,1,0:T(8,128)(2,1)S(1)} %chip_sum.3.total_ref), channel_id=1, source_target_pairs={{0,4},{4,0},{1,5},{5,1},{2,6},{6,2},{3,7},{7,3},{8,12},{12,8},{9,1... | collective-permute-start | bytes 307208 | tf_op jit(solution)/shard_map/ppermute | solution.py:636
  27.8 2.8 %collective-permute-start.11 = (bf16[1152,128]{1,0:T(8,128)(2,1)S(1)}, bf16[1152,128]{1,0:T(8,128)(2,1)S(1)}, u32[]{:S(2)}, u32[]{:S(2)}) collective-permute-start(bf16[1152,128]{1,0:T(8,128)(2,1)S(1)} %get-tuple-element.82), channel_id=1, source_target_pairs={{0,8},{8,0},{16,24},{24,16},{1,9},{9,1},{17,25},{25,17},{2,10},{10... | collective-permute-start | bytes 884744 | tf_op jit(solution)/shard_map/ppermute | solution.py:636
  29.0 18.3 %copy-start = (bf16[9,128,256]{2,1,0:T(8,128)(2,1)S(1)}, bf16[9,128,256]{2,1,0:T(8,128)(2,1)}, u32[]{:S(2)}) copy-start(bf16[9,128,256]{2,1,0:T(8,128)(2,1)} %w_first_ref.1) | copy-start | bytes 1769476
  29.0 1.6 %collective-permute-start.10 = (bf16[576,128]{1,0:T(8,128)(2,1)S(1)}, bf16[576,128]{1,0:T(8,128)(2,1)S(1)}, u32[]{:S(2)}, u32[]{:S(2)}) collective-permute-start(bf16[576,128]{1,0:T(8,128)(2,1)S(1)} %get-tuple-element.77), channel_id=1, source_target_pairs={{0,8},{8,0},{16,24},{24,16},{1,9},{9,1},{17,25},{25,17},{2,10},{10... | collective-permute-start | bytes 442376 | tf_op jit(solution)/shard_map/ppermute | solution.py:636
  30.7 9.6 %collective-permute-start.12 = (bf16[432,128]{1,0:T(8,128)(2,1)S(1)}, bf16[432,128]{1,0:T(8,128)(2,1)S(1)}, u32[]{:S(2)}, u32[]{:S(2)}) collective-permute-start(bf16[432,128]{1,0:T(8,128)(2,1)S(1)} %get-tuple-element.84), channel_id=1, source_target_pairs={{2,0},{3,1},{0,2},{1,3},{6,4},{7,5},{4,6},{5,7},{10,8},{11,9},{8,1... | collective-permute-start | bytes 331784 | tf_op jit(solution)/shard_map/ppermute | solution.py:938
  32.8 7.6 %collective-permute-start.13 = (bf16[432,128]{1,0:T(8,128)(2,1)S(1)}, bf16[432,128]{1,0:T(8,128)(2,1)S(1)}, u32[]{:S(2)}, u32[]{:S(2)}) collective-permute-start(bf16[432,128]{1,0:T(8,128)(2,1)S(1)} %get-tuple-element.85), channel_id=1, source_target_pairs={{1,0},{0,1},{3,2},{2,3},{5,4},{4,5},{7,6},{6,7},{9,8},{8,9},{11,10... | collective-permute-start | bytes 331784 | tf_op jit(solution)/shard_map/ppermute | solution.py:938
  34.4 7.9 %collective-permute-start.14 = (bf16[432,128]{1,0:T(8,128)(2,1)S(1)}, bf16[432,128]{1,0:T(8,128)(2,1)S(1)}, u32[]{:S(2)}, u32[]{:S(2)}) collective-permute-start(bf16[432,128]{1,0:T(8,128)(2,1)S(1)} %get-tuple-element.86), channel_id=1, source_target_pairs={{3,0},{2,1},{1,2},{0,3},{7,4},{6,5},{5,6},{4,7},{11,8},{10,9},{9,1... | collective-permute-start | bytes 331784 | tf_op jit(solution)/shard_map/ppermute | solution.py:938
  42.4 4.8 %collective-permute-start.15 = (bf16[432,128]{1,0:T(8,128)(2,1)S(1)}, bf16[432,128]{1,0:T(8,128)(2,1)S(1)}, u32[]{:S(2)}, u32[]{:S(2)}) collective-permute-start(bf16[432,128]{1,0:T(8,128)(2,1)S(1)} %share.1.refs_0_), channel_id=1, source_target_pairs={{0,16},{8,24},{16,0},{24,8},{1,17},{9,25},{17,1},{25,9},{2,18},{10... | collective-permute-start | bytes 331784 | tf_op jit(solution)/shard_map/ppermute | solution.py:636
  47.2 1.4 %collective-permute-start.16 = (bf16[432,128]{1,0:T(8,128)(2,1)S(1)}, bf16[432,128]{1,0:T(8,128)(2,1)S(1)}, u32[]{:S(2)}, u32[]{:S(2)}) collective-permute-start(bf16[432,128]{1,0:T(8,128)(2,1)S(1)} %chips.1.mine_ref), channel_id=1, source_target_pairs={{0,8},{8,0},{16,24},{24,16},{1,9},{9,1},{17,25},{25,17},{2,10},{10... | collective-permute-start | bytes 331784 | tf_op jit(solution)/shard_map/ppermute | solution.py:636

commit v9 on v8

--- a/solution.py
+++ b/solution.py
@@ -242,7 +242,7 @@
             total_ref[:, 1 + u : 1 + u + height] += part
 
 
-def edges_kernel(samples, inside_ref, low_ref, high_ref, weights_ref, out_ref, wide, shifted, total):
+def edges_kernel(samples, inside_ref, low_ref, high_ref, weights_ref, own_out, cross_out, wide, shifted, total):
     slots, rows, kept, depth = inside_ref.shape
     height, heads, pitch = rows - 2, weights_ref.shape[0], 24
     core, chip = core_and_chip()
@@ -270,7 +270,10 @@
         part = dot_last(shifted[...], weights).reshape(2, slots, height, 8, depth)
         total[:, 1 + u : 1 + u + height, :8] += part[0]
         total[:, 1 + u : 1 + u + height, kept - 8 :] += part[1]
-    out_ref[...] = total[:, pl.ds(1 - lax.axis_index("lat"), height + 1)].astype(BF)
+    here = pl.ds(1 - lax.axis_index("lat"), height + 1)
+    for s in range(samples):
+        own_out[s] = total[2 * s, here].astype(BF)
+        cross_out[s] = total[2 * s + 1, here].astype(BF)
 
 
 def inside_conv(head_grads, head_weights, slots):
@@ -295,14 +298,14 @@
     return run(
         "head_conv_edges",
         functools.partial(edges_kernel, samples),
-        [jax.ShapeDtypeStruct((slots, rows - 1, kept, depth), BF)],
+        [jax.ShapeDtypeStruct((samples, rows - 1, kept, depth), BF)] * 2,
         [inside, low, high, head_weights],
         [
             pltpu.VMEM((heads, (2 * slots * height + 8) * 24, LANES), F32),
             pltpu.VMEM((2 * slots * height * 8, 3 * heads * LANES), BF),
             pltpu.VMEM((slots, rows, kept, depth), F32),
         ],
-    )[0]
+    )
 
 
 def saved_kernel(second_ref, first_ref, input_ref, low_ref, high_ref, second_out, first_out, slope_second, slope_first, act_out, input_out, wide):
@@ -953,17 +956,18 @@
     heads_of = functools.partial(
         head_conv,
         head_grads=head_grads,
-        low=low,
         high=high,
         head_weights=head_weights,
-        slots=2 * samples,
+        slots=samples,
         rows=height + 1,
     )
     everyone = range(samples)
-    got = swap(edges_conv(inside, low, high, head_weights), "lead", 1)
-    part_shape = jax.ShapeDtypeStruct(got.shape[1:], BF)
-    parts = run("core_sum", core_sum_kernel, [part_shape] * (2 * samples), [heads_of(False, False, 0), got])
-    own, cross = parts[0::2], list(parts[1::2])
+    own_other, cross_other = edges_conv(inside, low, high, head_weights)
+    cross_got, own_got = swap(cross_other, "lead", 1), swap(own_other, "lead", 1)
+    part_shape = jax.ShapeDtypeStruct(cross_got.shape[1:], BF)
+    cross = run("core_sum", core_sum_kernel, [part_shape] * samples, [heads_of(False, True, None, low=low), cross_got])
+    low_later, *cross = lax.optimization_barrier((low, *cross))
+    own = run("core_sum", core_sum_kernel, [part_shape] * samples, [heads_of(False, False, None, low=low_later), own_got])
     near_second, near_first, halo = near_parts(pre_second, pre_first, encoder_input, low, high)
     cross[-1], halo = lax.optimization_barrier((cross[-1], halo))
     cross = [swap(part, "lead", 2) for part in cross]

time: 50.1 us -> 49.7 us (level)
  waiting for transfers between devices: 14.3 us -> 13.2 us
    ppermute x12 -> x13, waiting for transfers between devices: 7.15 us -> 6.06 us  [swap(): return lax.ppermute(array, axis, [(i, i ^ flip) for i in range(count)])]
    ppermute x12 -> x13, starting transfers between devices: 13.3 us -> 13.9 us  [swap(): return lax.ppermute(array, axis, [(i, i ^ flip) for i in range(count)])]
    pallas_call x21 -> x23, Pallas kernels: 12.3 us -> 12.5 us  [run(): pl.pallas_call(kernel, name=name, out_shape=out_shape, in_specs=specs, ou...]
  transfers between devices with their start and end apart: 17 -> 18, of which waited for: 10 -> 9; matrix products, arithmetic and copies ran while one was open for 0% -> 0% of each run, Pallas kernels for 20% -> 20%
where the time goes in v9:
time: 49.7 us; the launch traced here: 49.1 us
  starting transfers between devices  22.5 us (45%)
  waiting for transfers between devices  13.2 us (27%)
  Pallas kernels  12.5 us (25%)
  between operations  0.84 us (2%)
    ppermute x13, starting transfers between devices, swap(): return lax.ppermute(array, axis, [(i, i ^ flip) for i in range(count)])  13.9 us
    pallas_call x23, Pallas kernels, run(): pl.pallas_call(kernel, name=name, out_shape=out_shape, in_specs=specs, ou...  12.5 us
    ppermute x3, waiting for transfers between devices, to_partner(): lax.ppermute(array, 'lon', [(partner(i, step, count), i) for i in range(c...  7.18 us
    ppermute x13, waiting for transfers between devices, swap(): return lax.ppermute(array, axis, [(i, i ^ flip) for i in range(count)])  6.06 us
    ppermute x3, starting transfers between devices, to_partner(): lax.ppermute(array, 'lon', [(partner(i, step, count), i) for i in range(c...  4.47 us
    ppermute x2, starting transfers between devices, around(): return lax.ppermute(array, axis, pairs)  4.15 us
  transfers between devices with their start and end apart: 18, of which 9 were waited for; matrix products, arithmetic and copies ran while one was open for 0% of the time, Pallas kernels for 20%

profile of v9, /device:TPU:0, one launch (start us, length us, event | category | flops | bytes accessed | tf_op | source)
XLA Modules:
  0.0 49.1 jit_solution(17150718256629163406)
XLA Ops:
  0.6 3.0 %collective-permute-start.3 = (bf16[2,4,32,256]{3,2,1,0:T(8,128)(2,1)}, bf16[2,4,32,256]{3,2,1,0:T(8,128)(2,1)S(1)}, u32[]{:S(2)}, u32[]{:S(2)}) collective-permute-start(bf16[2,4,32,256]{3,2,1,0:T(8,128)(2,1)} %first_far.1), channel_id=1, source_target_pairs={{0,4},{4,0},{1,5},{5,1},{2,6},{6,2},{3,7},{7,3},{8,12},{12,8},{9,1... | collective-permute-start | bytes 393224 | tf_op jit(solution)/shard_map/ppermute | solution.py:639
  3.7 0.1 collective-permute-start.2
  3.7 1.3 %pack_columns.1 = (bf16[10,24,128]{2,1,0:T(8,128)(2,1)S(1)}, bf16[10,24,128]{2,1,0:T(8,128)(2,1)S(1)}) custom-call(bf16[2,8,4,32,128]{4,3,2,1,0:T(8,128)(2,1)} %grads_far.1, bf16[2,4,32,256]{3,2,1,0:T(8,128)(2,1)} %second_far.1, bf16[2,4,32,256]{3,2,1,0:T(8,128)(2,1)} %first_far.1), custom_call_target="tpu_custom_call" | custom-call | flops 1 | bytes 1 | tf_op jit(solution)/shard_map/pack_columns/pallas_call | solution.py:50
  5.0 2.1 %collective-permute-start = (bf16[10,24,128]{2,1,0:T(8,128)(2,1)S(1)}, bf16[10,24,128]{2,1,0:T(8,128)(2,1)S(1)}, u32[]{:S(2)}, u32[]{:S(2)}) collective-permute-start(bf16[10,24,128]{2,1,0:T(8,128)(2,1)S(1)} %get-tuple-element.54), channel_id=1, source_target_pairs={{0,1},{1,2},{2,3},{3,0},{4,5},{5,6},{6,7},{7,4},{8,9},{9,10},{10,1... | collective-permute-start | bytes 184328 | tf_op jit(solution)/shard_map/ppermute | solution.py:645
  7.1 2.1 %collective-permute-start.1 = (bf16[10,24,128]{2,1,0:T(8,128)(2,1)S(1)}, bf16[10,24,128]{2,1,0:T(8,128)(2,1)S(1)}, u32[]{:S(2)}, u32[]{:S(2)}) collective-permute-start(bf16[10,24,128]{2,1,0:T(8,128)(2,1)S(1)} %get-tuple-element.55), channel_id=1, source_target_pairs={{0,3},{1,0},{2,1},{3,2},{4,7},{5,4},{6,5},{7,6},{8,11},{9,8},{10,9... | collective-permute-start | bytes 184328 | tf_op jit(solution)/shard_map/ppermute | solution.py:645
  9.2 1.9 %stage.1 = (bf16[2,8,4,32,128]{4,3,2,1,0:T(8,128)(2,1)S(1)}, bf16[2,9,256,128]{3,2,1,0:T(8,128)(2,1)S(1)}, bf16[9,256,256]{2,1,0:T(8,128)(2,1)S(1)}, bf16[2,4,32...) custom-call(bf16[2,8,4,32,128]{4,3,2,1,0:T(8,128)(2,1)} %grads_far.1, ...), custom_call_target="tpu_custom_call" | custom-call | flops 1 | bytes 1 | tf_op jit(solution)/shard_map/stage/pallas_call | solution.py:50
  11.0 1.0 %head_conv_inside.1.inside_ref = f32[4,6,40,256]{3,2,1,0:T(8,128)S(1)} custom-call(bf16[2,8,4,32,128]{4,3,2,1,0:T(8,128)(2,1)S(1)} %get-tuple-element.56.grads_ref, bf16[2,9,256,128]{3,2,1,0:T(8,128)(2,1)S(1)} %get-tuple-element.57.weights_ref), custom_call_target="tpu_custom_call" | custom-call | flops 1 | bytes 1 | tf_op jit(solution)/shard_map/head_conv_inside/pallas_call | solution.py:50
  12.1 0.6 %head_conv_edges.1 = (bf16[2,5,40,256]{3,2,1,0:T(8,128)(2,1)S(1)}, bf16[2,5,40,256]{3,2,1,0:T(8,128)(2,1)S(1)}) custom-call(f32[4,6,40,256]{3,2,1,0:T(8,128)S(1)} %head_conv_inside.1.inside_ref, bf16[10,24,128]{2,1,0:T(8,128)(2,1)S(1)} %collective-permute-done.low_ref, bf16[10,24,128]{2,1,0:T(8,128)(2,1)S(1)} %collective-permute-done.1.high_ref, ...), custom_call_target="tpu_custom_call" | custom-call | flops 1 | bytes 1 | tf_op jit(solution)/shard_map/head_conv_edges/pallas_call | solution.py:50
  12.7 0.1 collective-permute-start.4
  12.8 0.5 %collective-permute-start.7 = (bf16[2,5,40,256]{3,2,1,0:T(8,128)(2,1)S(1)}, bf16[2,5,40,256]{3,2,1,0:T(8,128)(2,1)S(1)}, u32[]{:S(2)}, u32[]{:S(2)}) collective-permute-start(bf16[2,5,40,256]{3,2,1,0:T(8,128)(2,1)S(1)} %get-tuple-element.74), channel_id=1, source_target_pairs={{0,8},{8,0},{16,24},{24,16},{1,9},{9,1},{17,25},{25,17},{2,10},{10... | collective-permute-start | bytes 614408 | tf_op jit(solution)/shard_map/ppermute | solution.py:639
  13.3 0.7 %head_conv.2.mine_ref = bf16[2,5,40,256]{3,2,1,0:T(8,128)(2,1)S(1)} custom-call(bf16[2,8,4,32,128]{4,3,2,1,0:T(8,128)(2,1)S(1)} %get-tuple-element.56.grads_ref, bf16[10,24,128]{2,1,0:T(8,128)(2,1)S(1)} %collective-permute-done.low_ref, bf16[10,24,128]{2,1,0:T(8,128)(2,1)S(1)} %collective-permute-done.1.high_ref, ...), custom_call_target="tpu_custom_call" | custom-call | flops 1 | bytes 1 | tf_op jit(solution)/shard_map/head_conv/pallas_call | solution.py:50
  14.0 0.3 collective-permute-done.4.got_ref
  14.3 1.7 %collective-permute-start.8 = (bf16[5,40,256]{2,1,0:T(8,128)(2,1)S(1)}, bf16[5,40,256]{2,1,0:T(8,128)(2,1)S(1)}, u32[]{:S(2)}, u32[]{:S(2)}) collective-permute-start(bf16[5,40,256]{2,1,0:T(8,128)(2,1)S(1)} %get-tuple-element.76), channel_id=1, source_target_pairs={{0,16},{8,24},{16,0},{24,8},{1,17},{9,25},{17,1},{25,9},{2,18},{10... | collective-permute-start | bytes 307208 | tf_op jit(solution)/shard_map/ppermute | solution.py:639
  16.0 0.4 near_parts.1
  16.5 0.4 collective-permute-start.5
  16.9 1.7 %collective-permute-start.6 = (bf16[2,88,256]{2,1,0:T(8,128)(2,1)S(1)}, bf16[2,88,256]{2,1,0:T(8,128)(2,1)S(1)}, u32[]{:S(2)}, u32[]{:S(2)}) collective-permute-start(bf16[2,88,256]{2,1,0:T(8,128)(2,1)S(1)} %get-tuple-element.71), channel_id=1, source_target_pairs={{0,4},{4,0},{1,5},{5,1},{2,6},{6,2},{3,7},{7,3},{8,12},{12,8},{9,1... | collective-permute-start | bytes 270344 | tf_op jit(solution)/shard_map/ppermute | solution.py:639
  18.6 0.7 %head_conv.3.mine_ref = bf16[2,5,40,256]{3,2,1,0:T(8,128)(2,1)S(1)} custom-call(bf16[2,8,4,32,128]{4,3,2,1,0:T(8,128)(2,1)S(1)} %get-tuple-element.56.grads_ref, bf16[10,24,128]{2,1,0:T(8,128)(2,1)S(1)} %collective-permute-done.low_ref, bf16[10,24,128]{2,1,0:T(8,128)(2,1)S(1)} %collective-permute-done.1.high_ref, ...), custom_call_target="tpu_custom_call" | custom-call | flops 1 | bytes 1 | tf_op jit(solution)/shard_map/head_conv/pallas_call | solution.py:50
  19.3 0.1 core_sum.3
  19.3 0.3 collective-permute-done.8.refs_1_
  19.6 1.9 %collective-permute-start.9 = (bf16[5,40,256]{2,1,0:T(8,128)(2,1)S(1)}, bf16[5,40,256]{2,1,0:T(8,128)(2,1)S(1)}, u32[]{:S(2)}, u32[]{:S(2)}) collective-permute-start(bf16[5,40,256]{2,1,0:T(8,128)(2,1)S(1)} %chip_sum.2.total_ref), channel_id=1, source_target_pairs={{0,4},{4,0},{1,5},{5,1},{2,6},{6,2},{3,7},{7,3},{8,12},{12,8},{9,1... | collective-permute-start | bytes 307208 | tf_op jit(solution)/shard_map/ppermute | solution.py:639
  21.6 0.0 collective-permute-done.6.halo_ref
  21.6 1.8 %collective-permute-start.10 = (bf16[5,40,256]{2,1,0:T(8,128)(2,1)S(1)}, bf16[5,40,256]{2,1,0:T(8,128)(2,1)S(1)}, u32[]{:S(2)}, u32[]{:S(2)}) collective-permute-start(bf16[5,40,256]{2,1,0:T(8,128)(2,1)S(1)} %chip_sum.3.total_ref), channel_id=1, source_target_pairs={{0,4},{4,0},{1,5},{5,1},{2,6},{6,2},{3,7},{7,3},{8,12},{12,8},{9,1... | collective-permute-start | bytes 307208 | tf_op jit(solution)/shard_map/ppermute | solution.py:639
  23.4 0.6 %far_parts.1 = (f32[2,4,40,256]{3,2,1,0:T(8,128)S(1)}, f32[2,4,40,256]{3,2,1,0:T(8,128)S(1)}, bf16[256,512]{1,0:T(8,128)(2,1)S(1)}) custom-call(bf16[2,4,32,256]{3,2,1,0:T(8,128)(2,1)S(1)} %get-tuple-element.52.first_ref, bf16[2,4,32,256]{3,2,1,0:T(8,128)(2,1)S(1)} %collective-permute-done.2.tile_second, ...), custom_call_target="tpu_custom_call" | custom-call | flops 1 | bytes 1 | tf_op jit(solution)/shard_map/far_parts/pallas_call | solution.py:50
  24.0 1.1 %collective-permute-done.9.line_ref = bf16[5,40,256]{2,1,0:T(8,128)(2,1)S(1)} collective-permute-done((bf16[5,40,256]{2,1,0:T(8,128)(2,1)S(1)}, bf16[5,40,256]{2,1,0:T(8,128)(2,1)S(1)}, u32[]{:S(2)}, u32[]{:S(2)}) %collective-permute-start.9) | collective-permute-done | bytes 102432 | tf_op jit(solution)/shard_map/ppermute | solution.py:639
  25.1 0.4 latent_grads.2
  25.5 0.7 %second_conv.2.refs_0_ = bf16[3,10,32,256]{3,2,1,0:T(8,128)(2,1)S(1)} custom-call(bf16[10,40,768]{2,1,0:T(8,128)(2,1)S(1)} %get-tuple-element.77.cat_ref, f32[2,4,40,256]{3,2,1,0:T(8,128)S(1)} %get-tuple-element.78.near_ref, f32[2,4,40,256]{3,2,1,0:T(8,128)S(1)} %get-tuple-element.79.far_ref, bf16[2,88,256]{2,1,0:T(8,128)(2,1)S(1)} %collective-permute-done.6.halo_ref, ...), custom_call_target="tpu_custom_call" | custom-call | flops 1 | bytes 1 | tf_op jit(solution)/shard_map/second_conv/pallas_call | solution.py:50
  26.2 0.3 collective-permute-done.10.line_ref
  26.6 0.4 latent_grads.3
  26.9 0.5 %second_weight_grads.1 = (bf16[1152,128]{1,0:T(8,128)(2,1)S(1)}, bf16[1152,128]{1,0:T(8,128)(2,1)S(1)}) custom-call(bf16[256,512]{1,0:T(8,128)(2,1)S(1)} %get-tuple-element.88.act_ref, bf16[3,10,32,256]{3,2,1,0:T(8,128)(2,1)S(1)} %get-tuple-element.89.refs_0_, bf16[3,10,32,256]{3,2,1,0:T(8,128)(2,1)S(1)} %get-tuple-element.90.refs_1_), custom_call_target="tpu_custom_call" | custom-call | flops 1 | bytes 1 | tf_op jit(solution)/shard_map/second_weight_grads/pallas_call | solution.py:50
  27.4 0.1 collective-permute-start.12
  27.5 0.7 %second_conv.3.refs_1_ = bf16[3,10,32,256]{3,2,1,0:T(8,128)(2,1)S(1)} custom-call(bf16[10,40,768]{2,1,0:T(8,128)(2,1)S(1)} %get-tuple-element.85.cat_ref, f32[2,4,40,256]{3,2,1,0:T(8,128)S(1)} %get-tuple-element.78.near_ref, f32[2,4,40,256]{3,2,1,0:T(8,128)S(1)} %get-tuple-element.79.far_ref, bf16[2,88,256]{2,1,0:T(8,128)(2,1)S(1)} %collective-permute-done.6.halo_ref, ...), custom_call_target="tpu_custom_call" | custom-call | flops 1 | bytes 1 | tf_op jit(solution)/shard_map/second_conv/pallas_call | solution.py:50
  28.2 0.4 first_weight_grads.1
  28.7 0.0 copy-start
  28.7 0.6 %collective-permute-start.11 = (bf16[576,128]{1,0:T(8,128)(2,1)S(1)}, bf16[576,128]{1,0:T(8,128)(2,1)S(1)}, u32[]{:S(2)}, u32[]{:S(2)}) collective-permute-start(bf16[576,128]{1,0:T(8,128)(2,1)S(1)} %get-tuple-element.87), channel_id=1, source_target_pairs={{0,8},{8,0},{16,24},{24,16},{1,9},{9,1},{17,25},{25,17},{2,10},{10... | collective-permute-start | bytes 442376 | tf_op jit(solution)/shard_map/ppermute | solution.py:639
  29.2 1.0 %collective-permute-done.11 = bf16[576,128]{1,0:T(8,128)(2,1)S(1)} collective-permute-done((bf16[576,128]{1,0:T(8,128)(2,1)S(1)}, bf16[576,128]{1,0:T(8,128)(2,1)S(1)}, u32[]{:S(2)}, u32[]{:S(2)}) %collective-permute-start.11) | collective-permute-done | bytes 147488 | tf_op jit(solution)/shard_map/ppermute | solution.py:639
  30.2 0.1 blocks.1
  30.3 2.1 %collective-permute-start.13 = (bf16[432,128]{1,0:T(8,128)(2,1)S(1)}, bf16[432,128]{1,0:T(8,128)(2,1)S(1)}, u32[]{:S(2)}, u32[]{:S(2)}) collective-permute-start(bf16[432,128]{1,0:T(8,128)(2,1)S(1)} %get-tuple-element.94), channel_id=1, source_target_pairs={{2,0},{3,1},{0,2},{1,3},{6,4},{7,5},{4,6},{5,7},{10,8},{11,9},{8,1... | collective-permute-start | bytes 331784 | tf_op jit(solution)/shard_map/ppermute | solution.py:941
  32.4 1.7 %collective-permute-start.14 = (bf16[432,128]{1,0:T(8,128)(2,1)S(1)}, bf16[432,128]{1,0:T(8,128)(2,1)S(1)}, u32[]{:S(2)}, u32[]{:S(2)}) collective-permute-start(bf16[432,128]{1,0:T(8,128)(2,1)S(1)} %get-tuple-element.95), channel_id=1, source_target_pairs={{1,0},{0,1},{3,2},{2,3},{5,4},{4,5},{7,6},{6,7},{9,8},{8,9},{11,10... | collective-permute-start | bytes 331784 | tf_op jit(solution)/shard_map/ppermute | solution.py:941
  34.1 0.7 %collective-permute-start.15 = (bf16[432,128]{1,0:T(8,128)(2,1)S(1)}, bf16[432,128]{1,0:T(8,128)(2,1)S(1)}, u32[]{:S(2)}, u32[]{:S(2)}) collective-permute-start(bf16[432,128]{1,0:T(8,128)(2,1)S(1)} %get-tuple-element.96), channel_id=1, source_target_pairs={{3,0},{2,1},{1,2},{0,3},{7,4},{6,5},{5,6},{4,7},{11,8},{10,9},{9,1... | collective-permute-start | bytes 331784 | tf_op jit(solution)/shard_map/ppermute | solution.py:941
  34.8 5.2 %collective-permute-done.13.refs_1_ = bf16[432,128]{1,0:T(8,128)(2,1)S(1)} collective-permute-done((bf16[432,128]{1,0:T(8,128)(2,1)S(1)}, bf16[432,128]{1,0:T(8,128)(2,1)S(1)}, u32[]{:S(2)}, u32[]{:S(2)}) %collective-permute-start.13) | collective-permute-done | bytes 110624 | tf_op jit(solution)/shard_map/ppermute | solution.py:941
  40.0 2.0 %collective-permute-done.15.refs_3_ = bf16[432,128]{1,0:T(8,128)(2,1)S(1)} collective-permute-done((bf16[432,128]{1,0:T(8,128)(2,1)S(1)}, bf16[432,128]{1,0:T(8,128)(2,1)S(1)}, u32[]{:S(2)}, u32[]{:S(2)}) %collective-permute-start.15) | collective-permute-done | bytes 110624 | tf_op jit(solution)/shard_map/ppermute | solution.py:941
  42.0 0.1 share.1.refs_0_
  42.1 2.0 %collective-permute-start.16 = (bf16[432,128]{1,0:T(8,128)(2,1)S(1)}, bf16[432,128]{1,0:T(8,128)(2,1)S(1)}, u32[]{:S(2)}, u32[]{:S(2)}) collective-permute-start(bf16[432,128]{1,0:T(8,128)(2,1)S(1)} %share.1.refs_0_), channel_id=1, source_target_pairs={{0,16},{8,24},{16,0},{24,8},{1,17},{9,25},{17,1},{25,9},{2,18},{10... | collective-permute-start | bytes 331784 | tf_op jit(solution)/shard_map/ppermute | solution.py:639
  44.0 2.9 %collective-permute-done.16.refs_1_ = bf16[432,128]{1,0:T(8,128)(2,1)S(1)} collective-permute-done((bf16[432,128]{1,0:T(8,128)(2,1)S(1)}, bf16[432,128]{1,0:T(8,128)(2,1)S(1)}, u32[]{:S(2)}, u32[]{:S(2)}) %collective-permute-start.16) | collective-permute-done | bytes 110624 | tf_op jit(solution)/shard_map/ppermute | solution.py:639
  46.9 0.1 collective-permute-start.17
  47.0 1.1 %input_conv.1 = bf16[2,4,32,128]{3,2,1,0:T(8,128)(2,1)} custom-call(bf16[9,128,256]{2,1,0:T(8,128)(2,1)S(1)} %copy-done, bf16[3,10,32,256]{3,2,1,0:T(8,128)(2,1)S(1)} %second_conv.2.refs_0_, bf16[3,10,32,256]{3,2,1,0:T(8,128)(2,1)S(1)} %second_conv.3.refs_1_), custom_call_target="tpu_custom_call" | custom-call | flops 1 | bytes 1 | tf_op jit(solution)/shard_map/input_conv/pallas_call | solution.py:50
  48.1 0.2 collective-permute-done.17.other_ref
  48.3 0.8 %cores.1 = (f32[288,128]{1,0:T(8,128)}, f32[576,128]{1,0:T(8,128)}) custom-call(bf16[432,128]{1,0:T(8,128)(2,1)S(1)} %chips.1.mine_ref, bf16[432,128]{1,0:T(8,128)(2,1)S(1)} %collective-permute-done.17.other_ref), custom_call_target="tpu_custom_call" | custom-call | flops 1 | bytes 1 | tf_op jit(solution)/shard_map/cores/pallas_call | solution.py:50
  (13 shorter events, 0.2 us)
Async XLA Ops:
  0.6 11.4 %collective-permute-start.3 = (bf16[2,4,32,256]{3,2,1,0:T(8,128)(2,1)}, bf16[2,4,32,256]{3,2,1,0:T(8,128)(2,1)S(1)}, u32[]{:S(2)}, u32[]{:S(2)}) collective-permute-start(bf16[2,4,32,256]{3,2,1,0:T(8,128)(2,1)} %first_far.1), channel_id=1, source_target_pairs={{0,4},{4,0},{1,5},{5,1},{2,6},{6,2},{3,7},{7,3},{8,12},{12,8},{9,1... | collective-permute-start | bytes 393224 | tf_op jit(solution)/shard_map/ppermute | solution.py:639
  3.7 8.4 %collective-permute-start.2 = (bf16[2,4,32,256]{3,2,1,0:T(8,128)(2,1)}, bf16[2,4,32,256]{3,2,1,0:T(8,128)(2,1)S(1)}, u32[]{:S(2)}, u32[]{:S(2)}) collective-permute-start(bf16[2,4,32,256]{3,2,1,0:T(8,128)(2,1)} %second_far.1), channel_id=1, source_target_pairs={{0,4},{4,0},{1,5},{5,1},{2,6},{6,2},{3,7},{7,3},{8,12},{12,8},{9,1... | collective-permute-start | bytes 393224 | tf_op jit(solution)/shard_map/ppermute | solution.py:639
  5.0 7.0 %collective-permute-start = (bf16[10,24,128]{2,1,0:T(8,128)(2,1)S(1)}, bf16[10,24,128]{2,1,0:T(8,128)(2,1)S(1)}, u32[]{:S(2)}, u32[]{:S(2)}) collective-permute-start(bf16[10,24,128]{2,1,0:T(8,128)(2,1)S(1)} %get-tuple-element.54), channel_id=1, source_target_pairs={{0,1},{1,2},{2,3},{3,0},{4,5},{5,6},{6,7},{7,4},{8,9},{9,10},{10,1... | collective-permute-start | bytes 184328 | tf_op jit(solution)/shard_map/ppermute | solution.py:645
  7.1 5.0 %collective-permute-start.1 = (bf16[10,24,128]{2,1,0:T(8,128)(2,1)S(1)}, bf16[10,24,128]{2,1,0:T(8,128)(2,1)S(1)}, u32[]{:S(2)}, u32[]{:S(2)}) collective-permute-start(bf16[10,24,128]{2,1,0:T(8,128)(2,1)S(1)} %get-tuple-element.55), channel_id=1, source_target_pairs={{0,3},{1,0},{2,1},{3,2},{4,7},{5,4},{6,5},{7,6},{8,11},{9,8},{10,9... | collective-permute-start | bytes 184328 | tf_op jit(solution)/shard_map/ppermute | solution.py:645
  12.7 1.5 %collective-permute-start.4 = (bf16[2,5,40,256]{3,2,1,0:T(8,128)(2,1)S(1)}, bf16[2,5,40,256]{3,2,1,0:T(8,128)(2,1)S(1)}, u32[]{:S(2)}, u32[]{:S(2)}) collective-permute-start(bf16[2,5,40,256]{3,2,1,0:T(8,128)(2,1)S(1)} %get-tuple-element.65), channel_id=1, source_target_pairs={{0,8},{8,0},{16,24},{24,16},{1,9},{9,1},{17,25},{25,17},{2,10},{10... | collective-permute-start | bytes 614408 | tf_op jit(solution)/shard_map/ppermute | solution.py:639
  12.8 6.4 %collective-permute-start.7 = (bf16[2,5,40,256]{3,2,1,0:T(8,128)(2,1)S(1)}, bf16[2,5,40,256]{3,2,1,0:T(8,128)(2,1)S(1)}, u32[]{:S(2)}, u32[]{:S(2)}) collective-permute-start(bf16[2,5,40,256]{3,2,1,0:T(8,128)(2,1)S(1)} %get-tuple-element.74), channel_id=1, source_target_pairs={{0,8},{8,0},{16,24},{24,16},{1,9},{9,1},{17,25},{25,17},{2,10},{10... | collective-permute-start | bytes 614408 | tf_op jit(solution)/shard_map/ppermute | solution.py:639
  14.3 5.3 %collective-permute-start.8 = (bf16[5,40,256]{2,1,0:T(8,128)(2,1)S(1)}, bf16[5,40,256]{2,1,0:T(8,128)(2,1)S(1)}, u32[]{:S(2)}, u32[]{:S(2)}) collective-permute-start(bf16[5,40,256]{2,1,0:T(8,128)(2,1)S(1)} %get-tuple-element.76), channel_id=1, source_target_pairs={{0,16},{8,24},{16,0},{24,8},{1,17},{9,25},{17,1},{25,9},{2,18},{10... | collective-permute-start | bytes 307208 | tf_op jit(solution)/shard_map/ppermute | solution.py:639
  16.5 5.1 %collective-permute-start.5 = (bf16[5,40,256]{2,1,0:T(8,128)(2,1)S(1)}, bf16[5,40,256]{2,1,0:T(8,128)(2,1)S(1)}, u32[]{:S(2)}, u32[]{:S(2)}) collective-permute-start(bf16[5,40,256]{2,1,0:T(8,128)(2,1)S(1)} %get-tuple-element.70), channel_id=1, source_target_pairs={{0,16},{8,24},{16,0},{24,8},{1,17},{9,25},{17,1},{25,9},{2,18},{10... | collective-permute-start | bytes 307208 | tf_op jit(solution)/shard_map/ppermute | solution.py:639
  16.9 4.7 %collective-permute-start.6 = (bf16[2,88,256]{2,1,0:T(8,128)(2,1)S(1)}, bf16[2,88,256]{2,1,0:T(8,128)(2,1)S(1)}, u32[]{:S(2)}, u32[]{:S(2)}) collective-permute-start(bf16[2,88,256]{2,1,0:T(8,128)(2,1)S(1)} %get-tuple-element.71), channel_id=1, source_target_pairs={{0,4},{4,0},{1,5},{5,1},{2,6},{6,2},{3,7},{7,3},{8,12},{12,8},{9,1... | collective-permute-start | bytes 270344 | tf_op jit(solution)/shard_map/ppermute | solution.py:639
  19.6 5.5 %collective-permute-start.9 = (bf16[5,40,256]{2,1,0:T(8,128)(2,1)S(1)}, bf16[5,40,256]{2,1,0:T(8,128)(2,1)S(1)}, u32[]{:S(2)}, u32[]{:S(2)}) collective-permute-start(bf16[5,40,256]{2,1,0:T(8,128)(2,1)S(1)} %chip_sum.2.total_ref), channel_id=1, source_target_pairs={{0,4},{4,0},{1,5},{5,1},{2,6},{6,2},{3,7},{7,3},{8,12},{12,8},{9,1... | collective-permute-start | bytes 307208 | tf_op jit(solution)/shard_map/ppermute | solution.py:639
  21.6 5.0 %collective-permute-start.10 = (bf16[5,40,256]{2,1,0:T(8,128)(2,1)S(1)}, bf16[5,40,256]{2,1,0:T(8,128)(2,1)S(1)}, u32[]{:S(2)}, u32[]{:S(2)}) collective-permute-start(bf16[5,40,256]{2,1,0:T(8,128)(2,1)S(1)} %chip_sum.3.total_ref), channel_id=1, source_target_pairs={{0,4},{4,0},{1,5},{5,1},{2,6},{6,2},{3,7},{7,3},{8,12},{12,8},{9,1... | collective-permute-start | bytes 307208 | tf_op jit(solution)/shard_map/ppermute | solution.py:639
  27.4 2.8 %collective-permute-start.12 = (bf16[1152,128]{1,0:T(8,128)(2,1)S(1)}, bf16[1152,128]{1,0:T(8,128)(2,1)S(1)}, u32[]{:S(2)}, u32[]{:S(2)}) collective-permute-start(bf16[1152,128]{1,0:T(8,128)(2,1)S(1)} %get-tuple-element.92), channel_id=1, source_target_pairs={{0,8},{8,0},{16,24},{24,16},{1,9},{9,1},{17,25},{25,17},{2,10},{10... | collective-permute-start | bytes 884744 | tf_op jit(solution)/shard_map/ppermute | solution.py:639
  28.7 18.3 %copy-start = (bf16[9,128,256]{2,1,0:T(8,128)(2,1)S(1)}, bf16[9,128,256]{2,1,0:T(8,128)(2,1)}, u32[]{:S(2)}) copy-start(bf16[9,128,256]{2,1,0:T(8,128)(2,1)} %w_first_ref.1) | copy-start | bytes 1769476
  28.7 1.6 %collective-permute-start.11 = (bf16[576,128]{1,0:T(8,128)(2,1)S(1)}, bf16[576,128]{1,0:T(8,128)(2,1)S(1)}, u32[]{:S(2)}, u32[]{:S(2)}) collective-permute-start(bf16[576,128]{1,0:T(8,128)(2,1)S(1)} %get-tuple-element.87), channel_id=1, source_target_pairs={{0,8},{8,0},{16,24},{24,16},{1,9},{9,1},{17,25},{25,17},{2,10},{10... | collective-permute-start | bytes 442376 | tf_op jit(solution)/shard_map/ppermute | solution.py:639
  30.3 9.6 %collective-permute-start.13 = (bf16[432,128]{1,0:T(8,128)(2,1)S(1)}, bf16[432,128]{1,0:T(8,128)(2,1)S(1)}, u32[]{:S(2)}, u32[]{:S(2)}) collective-permute-start(bf16[432,128]{1,0:T(8,128)(2,1)S(1)} %get-tuple-element.94), channel_id=1, source_target_pairs={{2,0},{3,1},{0,2},{1,3},{6,4},{7,5},{4,6},{5,7},{10,8},{11,9},{8,1... | collective-permute-start | bytes 331784 | tf_op jit(solution)/shard_map/ppermute | solution.py:941
  32.4 7.6 %collective-permute-start.14 = (bf16[432,128]{1,0:T(8,128)(2,1)S(1)}, bf16[432,128]{1,0:T(8,128)(2,1)S(1)}, u32[]{:S(2)}, u32[]{:S(2)}) collective-permute-start(bf16[432,128]{1,0:T(8,128)(2,1)S(1)} %get-tuple-element.95), channel_id=1, source_target_pairs={{1,0},{0,1},{3,2},{2,3},{5,4},{4,5},{7,6},{6,7},{9,8},{8,9},{11,10... | collective-permute-start | bytes 331784 | tf_op jit(solution)/shard_map/ppermute | solution.py:941
  34.1 7.9 %collective-permute-start.15 = (bf16[432,128]{1,0:T(8,128)(2,1)S(1)}, bf16[432,128]{1,0:T(8,128)(2,1)S(1)}, u32[]{:S(2)}, u32[]{:S(2)}) collective-permute-start(bf16[432,128]{1,0:T(8,128)(2,1)S(1)} %get-tuple-element.96), channel_id=1, source_target_pairs={{3,0},{2,1},{1,2},{0,3},{7,4},{6,5},{5,6},{4,7},{11,8},{10,9},{9,1... | collective-permute-start | bytes 331784 | tf_op jit(solution)/shard_map/ppermute | solution.py:941
  42.1 4.8 %collective-permute-start.16 = (bf16[432,128]{1,0:T(8,128)(2,1)S(1)}, bf16[432,128]{1,0:T(8,128)(2,1)S(1)}, u32[]{:S(2)}, u32[]{:S(2)}) collective-permute-start(bf16[432,128]{1,0:T(8,128)(2,1)S(1)} %share.1.refs_0_), channel_id=1, source_target_pairs={{0,16},{8,24},{16,0},{24,8},{1,17},{9,25},{17,1},{25,9},{2,18},{10... | collective-permute-start | bytes 331784 | tf_op jit(solution)/shard_map/ppermute | solution.py:639
  46.9 1.4 %collective-permute-start.17 = (bf16[432,128]{1,0:T(8,128)(2,1)S(1)}, bf16[432,128]{1,0:T(8,128)(2,1)S(1)}, u32[]{:S(2)}, u32[]{:S(2)}) collective-permute-start(bf16[432,128]{1,0:T(8,128)(2,1)S(1)} %chips.1.mine_ref), channel_id=1, source_target_pairs={{0,8},{8,0},{16,24},{24,16},{1,9},{9,1},{17,25},{25,17},{2,10},{10... | collective-permute-start | bytes 331784 | tf_op jit(solution)/shard_map/ppermute | solution.py:639

commit v10 on v9

--- a/solution.py
+++ b/solution.py
@@ -998,8 +998,9 @@
     share_shape = jax.ShapeDtypeStruct((3 * rows, LANES), BF)
     shares = run("blocks", blocks_kernel, [share_shape] * columns, blocks)
     parts = [to_partner(shares[step], step) for step in ((2, 1, 3) if columns == 4 else range(1, columns))]
-    share = run("share", sum_kernel, [share_shape], [shares[0], *parts])[0]
-    both = run("chips", sum_kernel, [share_shape], [share, swap(share, "lead", 2)])[0]
+    early = run("share", sum_kernel, [share_shape], [shares[0], *parts[:-1]])[0]
+    early_got, late_got = swap(early, "lead", 2), swap(parts[-1], "lead", 2)
+    both = run("chips", sum_kernel, [share_shape], [early, parts[-1], early_got, late_got])[0]
     result_first, result_second = run(
         "cores",
         halves_kernel,

time: 49.7 us -> 49.6 us (level)
  starting transfers between devices: 22.5 us -> 24.4 us
  waiting for transfers between devices: 13.2 us -> 11.7 us
    ppermute x3, waiting for transfers between devices: 7.18 us -> 5.19 us  [to_partner(): lax.ppermute(array, 'lon', [(partner(i, step, count), i) for i in range(c...]
    ppermute x13 -> x14, starting transfers between devices: 13.9 us -> 15.7 us  [swap(): return lax.ppermute(array, axis, [(i, i ^ flip) for i in range(count)])]
    ppermute x13 -> x14, waiting for transfers between devices: 6.06 us -> 6.53 us  [swap(): return lax.ppermute(array, axis, [(i, i ^ flip) for i in range(count)])]
  transfers between devices with their start and end apart: 18 -> 19, of which waited for: 9 -> 9; matrix products, arithmetic and copies ran while one was open for 0% -> 0% of each run, Pallas kernels for 20% -> 20%
where the time goes in v10:
time: 49.6 us; the launch traced here: 49.5 us
  starting transfers between devices  24.4 us (49%)
  Pallas kernels  12.5 us (25%)
  waiting for transfers between devices  11.7 us (24%)
  between operations  0.84 us (2%)
    ppermute x14, starting transfers between devices, swap(): return lax.ppermute(array, axis, [(i, i ^ flip) for i in range(count)])  15.7 us
    pallas_call x23, Pallas kernels, run(): pl.pallas_call(kernel, name=name, out_shape=out_shape, in_specs=specs, ou...  12.5 us
    ppermute x14, waiting for transfers between devices, swap(): return lax.ppermute(array, axis, [(i, i ^ flip) for i in range(count)])  6.53 us
    ppermute x3, waiting for transfers between devices, to_partner(): lax.ppermute(array, 'lon', [(partner(i, step, count), i) for i in range(c...  5.19 us
    ppermute x3, starting transfers between devices, to_partner(): lax.ppermute(array, 'lon', [(partner(i, step, count), i) for i in range(c...  4.47 us
    ppermute x2, starting transfers between devices, around(): return lax.ppermute(array, axis, pairs)  4.15 us
  transfers between devices with their start and end apart: 19, of which 9 were waited for; matrix products, arithmetic and copies ran while one was open for 0% of the time, Pallas kernels for 20%

profile of v10, /device:TPU:0, one launch (start us, length us, event | category | flops | bytes accessed | tf_op | source)
XLA Modules:
  0.0 49.5 jit_solution(8706921640652370494)
XLA Ops:
  0.6 3.0 %collective-permute-start.3 = (bf16[2,4,32,256]{3,2,1,0:T(8,128)(2,1)}, bf16[2,4,32,256]{3,2,1,0:T(8,128)(2,1)S(1)}, u32[]{:S(2)}, u32[]{:S(2)}) collective-permute-start(bf16[2,4,32,256]{3,2,1,0:T(8,128)(2,1)} %first_far.1), channel_id=1, source_target_pairs={{0,4},{4,0},{1,5},{5,1},{2,6},{6,2},{3,7},{7,3},{8,12},{12,8},{9,1... | collective-permute-start | bytes 393224 | tf_op jit(solution)/shard_map/ppermute | solution.py:639
  3.7 0.1 collective-permute-start.2
  3.7 1.3 %pack_columns.1 = (bf16[10,24,128]{2,1,0:T(8,128)(2,1)S(1)}, bf16[10,24,128]{2,1,0:T(8,128)(2,1)S(1)}) custom-call(bf16[2,8,4,32,128]{4,3,2,1,0:T(8,128)(2,1)} %grads_far.1, bf16[2,4,32,256]{3,2,1,0:T(8,128)(2,1)} %second_far.1, bf16[2,4,32,256]{3,2,1,0:T(8,128)(2,1)} %first_far.1), custom_call_target="tpu_custom_call" | custom-call | flops 1 | bytes 1 | tf_op jit(solution)/shard_map/pack_columns/pallas_call | solution.py:50
  5.0 2.1 %collective-permute-start = (bf16[10,24,128]{2,1,0:T(8,128)(2,1)S(1)}, bf16[10,24,128]{2,1,0:T(8,128)(2,1)S(1)}, u32[]{:S(2)}, u32[]{:S(2)}) collective-permute-start(bf16[10,24,128]{2,1,0:T(8,128)(2,1)S(1)} %get-tuple-element.54), channel_id=1, source_target_pairs={{0,1},{1,2},{2,3},{3,0},{4,5},{5,6},{6,7},{7,4},{8,9},{9,10},{10,1... | collective-permute-start | bytes 184328 | tf_op jit(solution)/shard_map/ppermute | solution.py:645
  7.1 2.1 %collective-permute-start.1 = (bf16[10,24,128]{2,1,0:T(8,128)(2,1)S(1)}, bf16[10,24,128]{2,1,0:T(8,128)(2,1)S(1)}, u32[]{:S(2)}, u32[]{:S(2)}) collective-permute-start(bf16[10,24,128]{2,1,0:T(8,128)(2,1)S(1)} %get-tuple-element.55), channel_id=1, source_target_pairs={{0,3},{1,0},{2,1},{3,2},{4,7},{5,4},{6,5},{7,6},{8,11},{9,8},{10,9... | collective-permute-start | bytes 184328 | tf_op jit(solution)/shard_map/ppermute | solution.py:645
  9.2 1.9 %stage.1 = (bf16[2,8,4,32,128]{4,3,2,1,0:T(8,128)(2,1)S(1)}, bf16[2,9,256,128]{3,2,1,0:T(8,128)(2,1)S(1)}, bf16[9,256,256]{2,1,0:T(8,128)(2,1)S(1)}, bf16[2,4,32...) custom-call(bf16[2,8,4,32,128]{4,3,2,1,0:T(8,128)(2,1)} %grads_far.1, ...), custom_call_target="tpu_custom_call" | custom-call | flops 1 | bytes 1 | tf_op jit(solution)/shard_map/stage/pallas_call | solution.py:50
  11.0 1.0 %head_conv_inside.1.inside_ref = f32[4,6,40,256]{3,2,1,0:T(8,128)S(1)} custom-call(bf16[2,8,4,32,128]{4,3,2,1,0:T(8,128)(2,1)S(1)} %get-tuple-element.56.grads_ref, bf16[2,9,256,128]{3,2,1,0:T(8,128)(2,1)S(1)} %get-tuple-element.57.weights_ref), custom_call_target="tpu_custom_call" | custom-call | flops 1 | bytes 1 | tf_op jit(solution)/shard_map/head_conv_inside/pallas_call | solution.py:50
  12.1 0.6 %head_conv_edges.1 = (bf16[2,5,40,256]{3,2,1,0:T(8,128)(2,1)S(1)}, bf16[2,5,40,256]{3,2,1,0:T(8,128)(2,1)S(1)}) custom-call(f32[4,6,40,256]{3,2,1,0:T(8,128)S(1)} %head_conv_inside.1.inside_ref, bf16[10,24,128]{2,1,0:T(8,128)(2,1)S(1)} %collective-permute-done.low_ref, bf16[10,24,128]{2,1,0:T(8,128)(2,1)S(1)} %collective-permute-done.1.high_ref, ...), custom_call_target="tpu_custom_call" | custom-call | flops 1 | bytes 1 | tf_op jit(solution)/shard_map/head_conv_edges/pallas_call | solution.py:50
  12.7 0.1 collective-permute-start.4
  12.8 0.5 %collective-permute-start.7 = (bf16[2,5,40,256]{3,2,1,0:T(8,128)(2,1)S(1)}, bf16[2,5,40,256]{3,2,1,0:T(8,128)(2,1)S(1)}, u32[]{:S(2)}, u32[]{:S(2)}) collective-permute-start(bf16[2,5,40,256]{3,2,1,0:T(8,128)(2,1)S(1)} %get-tuple-element.74), channel_id=1, source_target_pairs={{0,8},{8,0},{16,24},{24,16},{1,9},{9,1},{17,25},{25,17},{2,10},{10... | collective-permute-start | bytes 614408 | tf_op jit(solution)/shard_map/ppermute | solution.py:639
  13.3 0.7 %head_conv.2.mine_ref = bf16[2,5,40,256]{3,2,1,0:T(8,128)(2,1)S(1)} custom-call(bf16[2,8,4,32,128]{4,3,2,1,0:T(8,128)(2,1)S(1)} %get-tuple-element.56.grads_ref, bf16[10,24,128]{2,1,0:T(8,128)(2,1)S(1)} %collective-permute-done.low_ref, bf16[10,24,128]{2,1,0:T(8,128)(2,1)S(1)} %collective-permute-done.1.high_ref, ...), custom_call_target="tpu_custom_call" | custom-call | flops 1 | bytes 1 | tf_op jit(solution)/shard_map/head_conv/pallas_call | solution.py:50
  14.0 0.3 collective-permute-done.4.got_ref
  14.3 1.7 %collective-permute-start.8 = (bf16[5,40,256]{2,1,0:T(8,128)(2,1)S(1)}, bf16[5,40,256]{2,1,0:T(8,128)(2,1)S(1)}, u32[]{:S(2)}, u32[]{:S(2)}) collective-permute-start(bf16[5,40,256]{2,1,0:T(8,128)(2,1)S(1)} %get-tuple-element.76), channel_id=1, source_target_pairs={{0,16},{8,24},{16,0},{24,8},{1,17},{9,25},{17,1},{25,9},{2,18},{10... | collective-permute-start | bytes 307208 | tf_op jit(solution)/shard_map/ppermute | solution.py:639
  16.0 0.4 near_parts.1
  16.5 0.4 collective-permute-start.5
  16.9 1.7 %collective-permute-start.6 = (bf16[2,88,256]{2,1,0:T(8,128)(2,1)S(1)}, bf16[2,88,256]{2,1,0:T(8,128)(2,1)S(1)}, u32[]{:S(2)}, u32[]{:S(2)}) collective-permute-start(bf16[2,88,256]{2,1,0:T(8,128)(2,1)S(1)} %get-tuple-element.71), channel_id=1, source_target_pairs={{0,4},{4,0},{1,5},{5,1},{2,6},{6,2},{3,7},{7,3},{8,12},{12,8},{9,1... | collective-permute-start | bytes 270344 | tf_op jit(solution)/shard_map/ppermute | solution.py:639
  18.6 0.7 %head_conv.3.mine_ref = bf16[2,5,40,256]{3,2,1,0:T(8,128)(2,1)S(1)} custom-call(bf16[2,8,4,32,128]{4,3,2,1,0:T(8,128)(2,1)S(1)} %get-tuple-element.56.grads_ref, bf16[10,24,128]{2,1,0:T(8,128)(2,1)S(1)} %collective-permute-done.low_ref, bf16[10,24,128]{2,1,0:T(8,128)(2,1)S(1)} %collective-permute-done.1.high_ref, ...), custom_call_target="tpu_custom_call" | custom-call | flops 1 | bytes 1 | tf_op jit(solution)/shard_map/head_conv/pallas_call | solution.py:50
  19.3 0.1 core_sum.3
  19.3 0.3 collective-permute-done.8.refs_1_
  19.6 1.9 %collective-permute-start.9 = (bf16[5,40,256]{2,1,0:T(8,128)(2,1)S(1)}, bf16[5,40,256]{2,1,0:T(8,128)(2,1)S(1)}, u32[]{:S(2)}, u32[]{:S(2)}) collective-permute-start(bf16[5,40,256]{2,1,0:T(8,128)(2,1)S(1)} %chip_sum.2.total_ref), channel_id=1, source_target_pairs={{0,4},{4,0},{1,5},{5,1},{2,6},{6,2},{3,7},{7,3},{8,12},{12,8},{9,1... | collective-permute-start | bytes 307208 | tf_op jit(solution)/shard_map/ppermute | solution.py:639
  21.6 1.8 %collective-permute-start.10 = (bf16[5,40,256]{2,1,0:T(8,128)(2,1)S(1)}, bf16[5,40,256]{2,1,0:T(8,128)(2,1)S(1)}, u32[]{:S(2)}, u32[]{:S(2)}) collective-permute-start(bf16[5,40,256]{2,1,0:T(8,128)(2,1)S(1)} %chip_sum.3.total_ref), channel_id=1, source_target_pairs={{0,4},{4,0},{1,5},{5,1},{2,6},{6,2},{3,7},{7,3},{8,12},{12,8},{9,1... | collective-permute-start | bytes 307208 | tf_op jit(solution)/shard_map/ppermute | solution.py:639
  23.4 0.6 %far_parts.1 = (f32[2,4,40,256]{3,2,1,0:T(8,128)S(1)}, f32[2,4,40,256]{3,2,1,0:T(8,128)S(1)}, bf16[256,512]{1,0:T(8,128)(2,1)S(1)}) custom-call(bf16[2,4,32,256]{3,2,1,0:T(8,128)(2,1)S(1)} %get-tuple-element.52.first_ref, bf16[2,4,32,256]{3,2,1,0:T(8,128)(2,1)S(1)} %collective-permute-done.2.tile_second, ...), custom_call_target="tpu_custom_call" | custom-call | flops 1 | bytes 1 | tf_op jit(solution)/shard_map/far_parts/pallas_call | solution.py:50
  24.0 1.1 %collective-permute-done.9.line_ref = bf16[5,40,256]{2,1,0:T(8,128)(2,1)S(1)} collective-permute-done((bf16[5,40,256]{2,1,0:T(8,128)(2,1)S(1)}, bf16[5,40,256]{2,1,0:T(8,128)(2,1)S(1)}, u32[]{:S(2)}, u32[]{:S(2)}) %collective-permute-start.9) | collective-permute-done | bytes 102432 | tf_op jit(solution)/shard_map/ppermute | solution.py:639
  25.1 0.4 latent_grads.2
  25.5 0.7 %second_conv.2.refs_0_ = bf16[3,10,32,256]{3,2,1,0:T(8,128)(2,1)S(1)} custom-call(bf16[10,40,768]{2,1,0:T(8,128)(2,1)S(1)} %get-tuple-element.77.cat_ref, f32[2,4,40,256]{3,2,1,0:T(8,128)S(1)} %get-tuple-element.78.near_ref, f32[2,4,40,256]{3,2,1,0:T(8,128)S(1)} %get-tuple-element.79.far_ref, bf16[2,88,256]{2,1,0:T(8,128)(2,1)S(1)} %collective-permute-done.6.halo_ref, ...), custom_call_target="tpu_custom_call" | custom-call | flops 1 | bytes 1 | tf_op jit(solution)/shard_map/second_conv/pallas_call | solution.py:50
  26.2 0.3 collective-permute-done.10.line_ref
  26.6 0.4 latent_grads.3
  26.9 0.5 second_weight_grads.1
  27.4 0.1 collective-permute-start.12
  27.5 0.7 %second_conv.3.refs_1_ = bf16[3,10,32,256]{3,2,1,0:T(8,128)(2,1)S(1)} custom-call(bf16[10,40,768]{2,1,0:T(8,128)(2,1)S(1)} %get-tuple-element.85.cat_ref, f32[2,4,40,256]{3,2,1,0:T(8,128)S(1)} %get-tuple-element.78.near_ref, f32[2,4,40,256]{3,2,1,0:T(8,128)S(1)} %get-tuple-element.79.far_ref, bf16[2,88,256]{2,1,0:T(8,128)(2,1)S(1)} %collective-permute-done.6.halo_ref, ...), custom_call_target="tpu_custom_call" | custom-call | flops 1 | bytes 1 | tf_op jit(solution)/shard_map/second_conv/pallas_call | solution.py:50
  28.2 0.4 first_weight_grads.1
  28.7 0.6 %collective-permute-start.11 = (bf16[576,128]{1,0:T(8,128)(2,1)S(1)}, bf16[576,128]{1,0:T(8,128)(2,1)S(1)}, u32[]{:S(2)}, u32[]{:S(2)}) collective-permute-start(bf16[576,128]{1,0:T(8,128)(2,1)S(1)} %get-tuple-element.87), channel_id=1, source_target_pairs={{0,8},{8,0},{16,24},{24,16},{1,9},{9,1},{17,25},{25,17},{2,10},{10... | collective-permute-start | bytes 442376 | tf_op jit(solution)/shard_map/ppermute | solution.py:639
  29.2 1.0 %collective-permute-done.11 = bf16[576,128]{1,0:T(8,128)(2,1)S(1)} collective-permute-done((bf16[576,128]{1,0:T(8,128)(2,1)S(1)}, bf16[576,128]{1,0:T(8,128)(2,1)S(1)}, u32[]{:S(2)}, u32[]{:S(2)}) %collective-permute-start.11) | collective-permute-done | bytes 147488 | tf_op jit(solution)/shard_map/ppermute | solution.py:639
  30.2 0.1 blocks.1
  30.3 2.1 %collective-permute-start.13 = (bf16[432,128]{1,0:T(8,128)(2,1)S(1)}, bf16[432,128]{1,0:T(8,128)(2,1)S(1)}, u32[]{:S(2)}, u32[]{:S(2)}) collective-permute-start(bf16[432,128]{1,0:T(8,128)(2,1)S(1)} %get-tuple-element.94), channel_id=1, source_target_pairs={{2,0},{3,1},{0,2},{1,3},{6,4},{7,5},{4,6},{5,7},{10,8},{11,9},{8,1... | collective-permute-start | bytes 331784 | tf_op jit(solution)/shard_map/ppermute | solution.py:941
  32.4 1.7 %collective-permute-start.14 = (bf16[432,128]{1,0:T(8,128)(2,1)S(1)}, bf16[432,128]{1,0:T(8,128)(2,1)S(1)}, u32[]{:S(2)}, u32[]{:S(2)}) collective-permute-start(bf16[432,128]{1,0:T(8,128)(2,1)S(1)} %get-tuple-element.95), channel_id=1, source_target_pairs={{1,0},{0,1},{3,2},{2,3},{5,4},{4,5},{7,6},{6,7},{9,8},{8,9},{11,10... | collective-permute-start | bytes 331784 | tf_op jit(solution)/shard_map/ppermute | solution.py:941
  34.1 0.7 %collective-permute-start.15 = (bf16[432,128]{1,0:T(8,128)(2,1)S(1)}, bf16[432,128]{1,0:T(8,128)(2,1)S(1)}, u32[]{:S(2)}, u32[]{:S(2)}) collective-permute-start(bf16[432,128]{1,0:T(8,128)(2,1)S(1)} %get-tuple-element.96), channel_id=1, source_target_pairs={{3,0},{2,1},{1,2},{0,3},{7,4},{6,5},{5,6},{4,7},{11,8},{10,9},{9,1... | collective-permute-start | bytes 331784 | tf_op jit(solution)/shard_map/ppermute | solution.py:941
  34.8 5.2 %collective-permute-done.13.refs_1_ = bf16[432,128]{1,0:T(8,128)(2,1)S(1)} collective-permute-done((bf16[432,128]{1,0:T(8,128)(2,1)S(1)}, bf16[432,128]{1,0:T(8,128)(2,1)S(1)}, u32[]{:S(2)}, u32[]{:S(2)}) %collective-permute-start.13) | collective-permute-done | bytes 110624 | tf_op jit(solution)/shard_map/ppermute | solution.py:941
  40.0 1.9 %collective-permute-start.16 = (bf16[432,128]{1,0:T(8,128)(2,1)S(1)}, bf16[432,128]{1,0:T(8,128)(2,1)S(1)}, u32[]{:S(2)}, u32[]{:S(2)}) collective-permute-start(bf16[432,128]{1,0:T(8,128)(2,1)S(1)} %share.1.refs_0_), channel_id=1, source_target_pairs={{0,16},{8,24},{16,0},{24,8},{1,17},{9,25},{17,1},{25,9},{2,18},{10... | collective-permute-start | bytes 331784 | tf_op jit(solution)/shard_map/ppermute | solution.py:639
  42.0 0.0 collective-permute-done.15.refs_1_
  42.0 1.9 %collective-permute-start.17 = (bf16[432,128]{1,0:T(8,128)(2,1)S(1)}, bf16[432,128]{1,0:T(8,128)(2,1)S(1)}, u32[]{:S(2)}, u32[]{:S(2)}) collective-permute-start(bf16[432,128]{1,0:T(8,128)(2,1)S(1)} %collective-permute-done.15.refs_1_), channel_id=1, source_target_pairs={{0,16},{8,24},{16,0},{24,8},{1,17},{9,25},{17,1},{25,9},{2,18},{10... | collective-permute-start | bytes 331784 | tf_op jit(solution)/shard_map/ppermute | solution.py:639
  43.9 1.5 %collective-permute-done.16.refs_2_ = bf16[432,128]{1,0:T(8,128)(2,1)S(1)} collective-permute-done((bf16[432,128]{1,0:T(8,128)(2,1)S(1)}, bf16[432,128]{1,0:T(8,128)(2,1)S(1)}, u32[]{:S(2)}, u32[]{:S(2)}) %collective-permute-start.16) | collective-permute-done | bytes 110624 | tf_op jit(solution)/shard_map/ppermute | solution.py:639
  45.4 1.9 %collective-permute-done.17.refs_3_ = bf16[432,128]{1,0:T(8,128)(2,1)S(1)} collective-permute-done((bf16[432,128]{1,0:T(8,128)(2,1)S(1)}, bf16[432,128]{1,0:T(8,128)(2,1)S(1)}, u32[]{:S(2)}, u32[]{:S(2)}) %collective-permute-start.17) | collective-permute-done | bytes 110624 | tf_op jit(solution)/shard_map/ppermute | solution.py:639
  47.2 0.1 chips.1.mine_ref
  47.3 0.1 collective-permute-start.18
  47.4 1.1 %input_conv.1 = bf16[2,4,32,128]{3,2,1,0:T(8,128)(2,1)} custom-call(bf16[9,128,256]{2,1,0:T(8,128)(2,1)S(1)} %copy-done, bf16[3,10,32,256]{3,2,1,0:T(8,128)(2,1)S(1)} %second_conv.2.refs_0_, bf16[3,10,32,256]{3,2,1,0:T(8,128)(2,1)S(1)} %second_conv.3.refs_1_), custom_call_target="tpu_custom_call" | custom-call | flops 1 | bytes 1 | tf_op jit(solution)/shard_map/input_conv/pallas_call | solution.py:50
  48.5 0.2 collective-permute-done.18.other_ref
  48.7 0.8 %cores.1 = (f32[288,128]{1,0:T(8,128)}, f32[576,128]{1,0:T(8,128)}) custom-call(bf16[432,128]{1,0:T(8,128)(2,1)S(1)} %chips.1.mine_ref, bf16[432,128]{1,0:T(8,128)(2,1)S(1)} %collective-permute-done.18.other_ref), custom_call_target="tpu_custom_call" | custom-call | flops 1 | bytes 1 | tf_op jit(solution)/shard_map/cores/pallas_call | solution.py:50
  (15 shorter events, 0.2 us)
Async XLA Ops:
  0.6 11.4 %collective-permute-start.3 = (bf16[2,4,32,256]{3,2,1,0:T(8,128)(2,1)}, bf16[2,4,32,256]{3,2,1,0:T(8,128)(2,1)S(1)}, u32[]{:S(2)}, u32[]{:S(2)}) collective-permute-start(bf16[2,4,32,256]{3,2,1,0:T(8,128)(2,1)} %first_far.1), channel_id=1, source_target_pairs={{0,4},{4,0},{1,5},{5,1},{2,6},{6,2},{3,7},{7,3},{8,12},{12,8},{9,1... | collective-permute-start | bytes 393224 | tf_op jit(solution)/shard_map/ppermute | solution.py:639
  3.7 8.4 %collective-permute-start.2 = (bf16[2,4,32,256]{3,2,1,0:T(8,128)(2,1)}, bf16[2,4,32,256]{3,2,1,0:T(8,128)(2,1)S(1)}, u32[]{:S(2)}, u32[]{:S(2)}) collective-permute-start(bf16[2,4,32,256]{3,2,1,0:T(8,128)(2,1)} %second_far.1), channel_id=1, source_target_pairs={{0,4},{4,0},{1,5},{5,1},{2,6},{6,2},{3,7},{7,3},{8,12},{12,8},{9,1... | collective-permute-start | bytes 393224 | tf_op jit(solution)/shard_map/ppermute | solution.py:639
  5.0 7.0 %collective-permute-start = (bf16[10,24,128]{2,1,0:T(8,128)(2,1)S(1)}, bf16[10,24,128]{2,1,0:T(8,128)(2,1)S(1)}, u32[]{:S(2)}, u32[]{:S(2)}) collective-permute-start(bf16[10,24,128]{2,1,0:T(8,128)(2,1)S(1)} %get-tuple-element.54), channel_id=1, source_target_pairs={{0,1},{1,2},{2,3},{3,0},{4,5},{5,6},{6,7},{7,4},{8,9},{9,10},{10,1... | collective-permute-start | bytes 184328 | tf_op jit(solution)/shard_map/ppermute | solution.py:645
  7.1 5.0 %collective-permute-start.1 = (bf16[10,24,128]{2,1,0:T(8,128)(2,1)S(1)}, bf16[10,24,128]{2,1,0:T(8,128)(2,1)S(1)}, u32[]{:S(2)}, u32[]{:S(2)}) collective-permute-start(bf16[10,24,128]{2,1,0:T(8,128)(2,1)S(1)} %get-tuple-element.55), channel_id=1, source_target_pairs={{0,3},{1,0},{2,1},{3,2},{4,7},{5,4},{6,5},{7,6},{8,11},{9,8},{10,9... | collective-permute-start | bytes 184328 | tf_op jit(solution)/shard_map/ppermute | solution.py:645
  12.7 1.5 %collective-permute-start.4 = (bf16[2,5,40,256]{3,2,1,0:T(8,128)(2,1)S(1)}, bf16[2,5,40,256]{3,2,1,0:T(8,128)(2,1)S(1)}, u32[]{:S(2)}, u32[]{:S(2)}) collective-permute-start(bf16[2,5,40,256]{3,2,1,0:T(8,128)(2,1)S(1)} %get-tuple-element.65), channel_id=1, source_target_pairs={{0,8},{8,0},{16,24},{24,16},{1,9},{9,1},{17,25},{25,17},{2,10},{10... | collective-permute-start | bytes 614408 | tf_op jit(solution)/shard_map/ppermute | solution.py:639
  12.8 6.4 %collective-permute-start.7 = (bf16[2,5,40,256]{3,2,1,0:T(8,128)(2,1)S(1)}, bf16[2,5,40,256]{3,2,1,0:T(8,128)(2,1)S(1)}, u32[]{:S(2)}, u32[]{:S(2)}) collective-permute-start(bf16[2,5,40,256]{3,2,1,0:T(8,128)(2,1)S(1)} %get-tuple-element.74), channel_id=1, source_target_pairs={{0,8},{8,0},{16,24},{24,16},{1,9},{9,1},{17,25},{25,17},{2,10},{10... | collective-permute-start | bytes 614408 | tf_op jit(solution)/shard_map/ppermute | solution.py:639
  14.3 5.3 %collective-permute-start.8 = (bf16[5,40,256]{2,1,0:T(8,128)(2,1)S(1)}, bf16[5,40,256]{2,1,0:T(8,128)(2,1)S(1)}, u32[]{:S(2)}, u32[]{:S(2)}) collective-permute-start(bf16[5,40,256]{2,1,0:T(8,128)(2,1)S(1)} %get-tuple-element.76), channel_id=1, source_target_pairs={{0,16},{8,24},{16,0},{24,8},{1,17},{9,25},{17,1},{25,9},{2,18},{10... | collective-permute-start | bytes 307208 | tf_op jit(solution)/shard_map/ppermute | solution.py:639
  16.5 5.1 %collective-permute-start.5 = (bf16[5,40,256]{2,1,0:T(8,128)(2,1)S(1)}, bf16[5,40,256]{2,1,0:T(8,128)(2,1)S(1)}, u32[]{:S(2)}, u32[]{:S(2)}) collective-permute-start(bf16[5,40,256]{2,1,0:T(8,128)(2,1)S(1)} %get-tuple-element.70), channel_id=1, source_target_pairs={{0,16},{8,24},{16,0},{24,8},{1,17},{9,25},{17,1},{25,9},{2,18},{10... | collective-permute-start | bytes 307208 | tf_op jit(solution)/shard_map/ppermute | solution.py:639
  16.9 4.7 %collective-permute-start.6 = (bf16[2,88,256]{2,1,0:T(8,128)(2,1)S(1)}, bf16[2,88,256]{2,1,0:T(8,128)(2,1)S(1)}, u32[]{:S(2)}, u32[]{:S(2)}) collective-permute-start(bf16[2,88,256]{2,1,0:T(8,128)(2,1)S(1)} %get-tuple-element.71), channel_id=1, source_target_pairs={{0,4},{4,0},{1,5},{5,1},{2,6},{6,2},{3,7},{7,3},{8,12},{12,8},{9,1... | collective-permute-start | bytes 270344 | tf_op jit(solution)/shard_map/ppermute | solution.py:639
  19.6 5.5 %collective-permute-start.9 = (bf16[5,40,256]{2,1,0:T(8,128)(2,1)S(1)}, bf16[5,40,256]{2,1,0:T(8,128)(2,1)S(1)}, u32[]{:S(2)}, u32[]{:S(2)}) collective-permute-start(bf16[5,40,256]{2,1,0:T(8,128)(2,1)S(1)} %chip_sum.2.total_ref), channel_id=1, source_target_pairs={{0,4},{4,0},{1,5},{5,1},{2,6},{6,2},{3,7},{7,3},{8,12},{12,8},{9,1... | collective-permute-start | bytes 307208 | tf_op jit(solution)/shard_map/ppermute | solution.py:639
  21.6 5.0 %collective-permute-start.10 = (bf16[5,40,256]{2,1,0:T(8,128)(2,1)S(1)}, bf16[5,40,256]{2,1,0:T(8,128)(2,1)S(1)}, u32[]{:S(2)}, u32[]{:S(2)}) collective-permute-start(bf16[5,40,256]{2,1,0:T(8,128)(2,1)S(1)} %chip_sum.3.total_ref), channel_id=1, source_target_pairs={{0,4},{4,0},{1,5},{5,1},{2,6},{6,2},{3,7},{7,3},{8,12},{12,8},{9,1... | collective-permute-start | bytes 307208 | tf_op jit(solution)/shard_map/ppermute | solution.py:639
  27.4 2.8 %collective-permute-start.12 = (bf16[1152,128]{1,0:T(8,128)(2,1)S(1)}, bf16[1152,128]{1,0:T(8,128)(2,1)S(1)}, u32[]{:S(2)}, u32[]{:S(2)}) collective-permute-start(bf16[1152,128]{1,0:T(8,128)(2,1)S(1)} %get-tuple-element.92), channel_id=1, source_target_pairs={{0,8},{8,0},{16,24},{24,16},{1,9},{9,1},{17,25},{25,17},{2,10},{10... | collective-permute-start | bytes 884744 | tf_op jit(solution)/shard_map/ppermute | solution.py:639
  28.7 18.7 %copy-start = (bf16[9,128,256]{2,1,0:T(8,128)(2,1)S(1)}, bf16[9,128,256]{2,1,0:T(8,128)(2,1)}, u32[]{:S(2)}) copy-start(bf16[9,128,256]{2,1,0:T(8,128)(2,1)} %w_first_ref.1) | copy-start | bytes 1769476
  28.7 1.6 %collective-permute-start.11 = (bf16[576,128]{1,0:T(8,128)(2,1)S(1)}, bf16[576,128]{1,0:T(8,128)(2,1)S(1)}, u32[]{:S(2)}, u32[]{:S(2)}) collective-permute-start(bf16[576,128]{1,0:T(8,128)(2,1)S(1)} %get-tuple-element.87), channel_id=1, source_target_pairs={{0,8},{8,0},{16,24},{24,16},{1,9},{9,1},{17,25},{25,17},{2,10},{10... | collective-permute-start | bytes 442376 | tf_op jit(solution)/shard_map/ppermute | solution.py:639
  30.3 9.6 %collective-permute-start.13 = (bf16[432,128]{1,0:T(8,128)(2,1)S(1)}, bf16[432,128]{1,0:T(8,128)(2,1)S(1)}, u32[]{:S(2)}, u32[]{:S(2)}) collective-permute-start(bf16[432,128]{1,0:T(8,128)(2,1)S(1)} %get-tuple-element.94), channel_id=1, source_target_pairs={{2,0},{3,1},{0,2},{1,3},{6,4},{7,5},{4,6},{5,7},{10,8},{11,9},{8,1... | collective-permute-start | bytes 331784 | tf_op jit(solution)/shard_map/ppermute | solution.py:941
  32.4 7.6 %collective-permute-start.14 = (bf16[432,128]{1,0:T(8,128)(2,1)S(1)}, bf16[432,128]{1,0:T(8,128)(2,1)S(1)}, u32[]{:S(2)}, u32[]{:S(2)}) collective-permute-start(bf16[432,128]{1,0:T(8,128)(2,1)S(1)} %get-tuple-element.95), channel_id=1, source_target_pairs={{1,0},{0,1},{3,2},{2,3},{5,4},{4,5},{7,6},{6,7},{9,8},{8,9},{11,10... | collective-permute-start | bytes 331784 | tf_op jit(solution)/shard_map/ppermute | solution.py:941
  34.1 7.9 %collective-permute-start.15 = (bf16[432,128]{1,0:T(8,128)(2,1)S(1)}, bf16[432,128]{1,0:T(8,128)(2,1)S(1)}, u32[]{:S(2)}, u32[]{:S(2)}) collective-permute-start(bf16[432,128]{1,0:T(8,128)(2,1)S(1)} %get-tuple-element.96), channel_id=1, source_target_pairs={{3,0},{2,1},{1,2},{0,3},{7,4},{6,5},{5,6},{4,7},{11,8},{10,9},{9,1... | collective-permute-start | bytes 331784 | tf_op jit(solution)/shard_map/ppermute | solution.py:941
  40.0 5.3 %collective-permute-start.16 = (bf16[432,128]{1,0:T(8,128)(2,1)S(1)}, bf16[432,128]{1,0:T(8,128)(2,1)S(1)}, u32[]{:S(2)}, u32[]{:S(2)}) collective-permute-start(bf16[432,128]{1,0:T(8,128)(2,1)S(1)} %share.1.refs_0_), channel_id=1, source_target_pairs={{0,16},{8,24},{16,0},{24,8},{1,17},{9,25},{17,1},{25,9},{2,18},{10... | collective-permute-start | bytes 331784 | tf_op jit(solution)/shard_map/ppermute | solution.py:639
  42.0 5.2 %collective-permute-start.17 = (bf16[432,128]{1,0:T(8,128)(2,1)S(1)}, bf16[432,128]{1,0:T(8,128)(2,1)S(1)}, u32[]{:S(2)}, u32[]{:S(2)}) collective-permute-start(bf16[432,128]{1,0:T(8,128)(2,1)S(1)} %collective-permute-done.15.refs_1_), channel_id=1, source_target_pairs={{0,16},{8,24},{16,0},{24,8},{1,17},{9,25},{17,1},{25,9},{2,18},{10... | collective-permute-start | bytes 331784 | tf_op jit(solution)/shard_map/ppermute | solution.py:639
  47.3 1.4 %collective-permute-start.18 = (bf16[432,128]{1,0:T(8,128)(2,1)S(1)}, bf16[432,128]{1,0:T(8,128)(2,1)S(1)}, u32[]{:S(2)}, u32[]{:S(2)}) collective-permute-start(bf16[432,128]{1,0:T(8,128)(2,1)S(1)} %chips.1.mine_ref), channel_id=1, source_target_pairs={{0,8},{8,0},{16,24},{24,16},{1,9},{9,1},{17,25},{25,17},{2,10},{10... | collective-permute-start | bytes 331784 | tf_op jit(solution)/shard_map/ppermute | solution.py:639

commit v11 on v10

--- a/solution.py
+++ b/solution.py
@@ -997,7 +997,7 @@
     rows = blocks[0].shape[1]
     share_shape = jax.ShapeDtypeStruct((3 * rows, LANES), BF)
     shares = run("blocks", blocks_kernel, [share_shape] * columns, blocks)
-    parts = [to_partner(shares[step], step) for step in ((2, 1, 3) if columns == 4 else range(1, columns))]
+    parts = [to_partner(shares[step], step) for step in ((3, 1, 2) if columns == 4 else range(1, columns))]
     early = run("share", sum_kernel, [share_shape], [shares[0], *parts[:-1]])[0]
     early_got, late_got = swap(early, "lead", 2), swap(parts[-1], "lead", 2)
     both = run("chips", sum_kernel, [share_shape], [early, parts[-1], early_got, late_got])[0]

time: 49.6 us -> 51.7 us (1.042)
  waiting for transfers between devices: 11.7 us -> 14.2 us
    ppermute x3, waiting for transfers between devices: 5.19 us -> 6.76 us  [to_partner(): lax.ppermute(array, 'lon', [(partner(i, step, count), i) for i in range(c...]
    ppermute x14, waiting for transfers between devices: 6.53 us -> 7.39 us  [swap(): return lax.ppermute(array, axis, [(i, i ^ flip) for i in range(count)])]
  transfers between devices with their start and end apart: 19 -> 19, of which waited for: 9 -> 10; matrix products, arithmetic and copies ran while one was open for 0% -> 0% of each run, Pallas kernels for 20% -> 20%
where the time goes in v11:
time: 51.7 us; the launch traced here: 51.5 us
  starting transfers between devices  24 us (46%)
  waiting for transfers between devices  14.2 us (27%)
  Pallas kernels  12.5 us (24%)
  between operations  0.84 us (2%)
    ppermute x14, starting transfers between devices, swap(): return lax.ppermute(array, axis, [(i, i ^ flip) for i in range(count)])  15.4 us
    pallas_call x23, Pallas kernels, run(): pl.pallas_call(kernel, name=name, out_shape=out_shape, in_specs=specs, ou...  12.5 us
    ppermute x14, waiting for transfers between devices, swap(): return lax.ppermute(array, axis, [(i, i ^ flip) for i in range(count)])  7.39 us
    ppermute x3, waiting for transfers between devices, to_partner(): lax.ppermute(array, 'lon', [(partner(i, step, count), i) for i in range(c...  6.76 us
    ppermute x3, starting transfers between devices, to_partner(): lax.ppermute(array, 'lon', [(partner(i, step, count), i) for i in range(c...  4.47 us
    ppermute x2, starting transfers between devices, around(): return lax.ppermute(array, axis, pairs)  4.15 us
  transfers between devices with their start and end apart: 19, of which 10 were waited for; matrix products, arithmetic and copies ran while one was open for 0% of the time, Pallas kernels for 20%

profile of v11, /device:TPU:0, one launch (start us, length us, event | category | flops | bytes accessed | tf_op | source)
XLA Modules:
  0.0 51.5 jit_solution(7990534540651896488)
XLA Ops:
  0.6 3.0 %collective-permute-start.3 = (bf16[2,4,32,256]{3,2,1,0:T(8,128)(2,1)}, bf16[2,4,32,256]{3,2,1,0:T(8,128)(2,1)S(1)}, u32[]{:S(2)}, u32[]{:S(2)}) collective-permute-start(bf16[2,4,32,256]{3,2,1,0:T(8,128)(2,1)} %first_far.1), channel_id=1, source_target_pairs={{0,4},{4,0},{1,5},{5,1},{2,6},{6,2},{3,7},{7,3},{8,12},{12,8},{9,1... | collective-permute-start | bytes 393224 | tf_op jit(solution)/shard_map/ppermute | solution.py:639
  3.7 0.1 collective-permute-start.2
  3.7 1.3 %pack_columns.1 = (bf16[10,24,128]{2,1,0:T(8,128)(2,1)S(1)}, bf16[10,24,128]{2,1,0:T(8,128)(2,1)S(1)}) custom-call(bf16[2,8,4,32,128]{4,3,2,1,0:T(8,128)(2,1)} %grads_far.1, bf16[2,4,32,256]{3,2,1,0:T(8,128)(2,1)} %second_far.1, bf16[2,4,32,256]{3,2,1,0:T(8,128)(2,1)} %first_far.1), custom_call_target="tpu_custom_call" | custom-call | flops 1 | bytes 1 | tf_op jit(solution)/shard_map/pack_columns/pallas_call | solution.py:50
  5.0 2.1 %collective-permute-start = (bf16[10,24,128]{2,1,0:T(8,128)(2,1)S(1)}, bf16[10,24,128]{2,1,0:T(8,128)(2,1)S(1)}, u32[]{:S(2)}, u32[]{:S(2)}) collective-permute-start(bf16[10,24,128]{2,1,0:T(8,128)(2,1)S(1)} %get-tuple-element.54), channel_id=1, source_target_pairs={{0,1},{1,2},{2,3},{3,0},{4,5},{5,6},{6,7},{7,4},{8,9},{9,10},{10,1... | collective-permute-start | bytes 184328 | tf_op jit(solution)/shard_map/ppermute | solution.py:645
  7.1 2.1 %collective-permute-start.1 = (bf16[10,24,128]{2,1,0:T(8,128)(2,1)S(1)}, bf16[10,24,128]{2,1,0:T(8,128)(2,1)S(1)}, u32[]{:S(2)}, u32[]{:S(2)}) collective-permute-start(bf16[10,24,128]{2,1,0:T(8,128)(2,1)S(1)} %get-tuple-element.55), channel_id=1, source_target_pairs={{0,3},{1,0},{2,1},{3,2},{4,7},{5,4},{6,5},{7,6},{8,11},{9,8},{10,9... | collective-permute-start | bytes 184328 | tf_op jit(solution)/shard_map/ppermute | solution.py:645
  9.2 1.9 %stage.1 = (bf16[2,8,4,32,128]{4,3,2,1,0:T(8,128)(2,1)S(1)}, bf16[2,9,256,128]{3,2,1,0:T(8,128)(2,1)S(1)}, bf16[9,256,256]{2,1,0:T(8,128)(2,1)S(1)}, bf16[2,4,32...) custom-call(bf16[2,8,4,32,128]{4,3,2,1,0:T(8,128)(2,1)} %grads_far.1, ...), custom_call_target="tpu_custom_call" | custom-call | flops 1 | bytes 1 | tf_op jit(solution)/shard_map/stage/pallas_call | solution.py:50
  11.0 1.0 %head_conv_inside.1.inside_ref = f32[4,6,40,256]{3,2,1,0:T(8,128)S(1)} custom-call(bf16[2,8,4,32,128]{4,3,2,1,0:T(8,128)(2,1)S(1)} %get-tuple-element.56.grads_ref, bf16[2,9,256,128]{3,2,1,0:T(8,128)(2,1)S(1)} %get-tuple-element.57.weights_ref), custom_call_target="tpu_custom_call" | custom-call | flops 1 | bytes 1 | tf_op jit(solution)/shard_map/head_conv_inside/pallas_call | solution.py:50
  12.1 0.6 %head_conv_edges.1 = (bf16[2,5,40,256]{3,2,1,0:T(8,128)(2,1)S(1)}, bf16[2,5,40,256]{3,2,1,0:T(8,128)(2,1)S(1)}) custom-call(f32[4,6,40,256]{3,2,1,0:T(8,128)S(1)} %head_conv_inside.1.inside_ref, bf16[10,24,128]{2,1,0:T(8,128)(2,1)S(1)} %collective-permute-done.low_ref, bf16[10,24,128]{2,1,0:T(8,128)(2,1)S(1)} %collective-permute-done.1.high_ref, ...), custom_call_target="tpu_custom_call" | custom-call | flops 1 | bytes 1 | tf_op jit(solution)/shard_map/head_conv_edges/pallas_call | solution.py:50
  12.7 0.1 collective-permute-start.4
  12.8 0.5 collective-permute-start.7
  13.3 0.7 %head_conv.2.mine_ref = bf16[2,5,40,256]{3,2,1,0:T(8,128)(2,1)S(1)} custom-call(bf16[2,8,4,32,128]{4,3,2,1,0:T(8,128)(2,1)S(1)} %get-tuple-element.56.grads_ref, bf16[10,24,128]{2,1,0:T(8,128)(2,1)S(1)} %collective-permute-done.low_ref, bf16[10,24,128]{2,1,0:T(8,128)(2,1)S(1)} %collective-permute-done.1.high_ref, ...), custom_call_target="tpu_custom_call" | custom-call | flops 1 | bytes 1 | tf_op jit(solution)/shard_map/head_conv/pallas_call | solution.py:50
  14.0 0.3 collective-permute-done.4.got_ref
  14.3 1.7 %collective-permute-start.8 = (bf16[5,40,256]{2,1,0:T(8,128)(2,1)S(1)}, bf16[5,40,256]{2,1,0:T(8,128)(2,1)S(1)}, u32[]{:S(2)}, u32[]{:S(2)}) collective-permute-start(bf16[5,40,256]{2,1,0:T(8,128)(2,1)S(1)} %get-tuple-element.76), channel_id=1, source_target_pairs={{0,16},{8,24},{16,0},{24,8},{1,17},{9,25},{17,1},{25,9},{2,18},{10... | collective-permute-start | bytes 307208 | tf_op jit(solution)/shard_map/ppermute | solution.py:639
  16.0 0.4 near_parts.1
  16.5 0.4 collective-permute-start.5
  16.9 1.7 %collective-permute-start.6 = (bf16[2,88,256]{2,1,0:T(8,128)(2,1)S(1)}, bf16[2,88,256]{2,1,0:T(8,128)(2,1)S(1)}, u32[]{:S(2)}, u32[]{:S(2)}) collective-permute-start(bf16[2,88,256]{2,1,0:T(8,128)(2,1)S(1)} %get-tuple-element.71), channel_id=1, source_target_pairs={{0,4},{4,0},{1,5},{5,1},{2,6},{6,2},{3,7},{7,3},{8,12},{12,8},{9,1... | collective-permute-start | bytes 270344 | tf_op jit(solution)/shard_map/ppermute | solution.py:639
  18.6 0.7 %head_conv.3.mine_ref = bf16[2,5,40,256]{3,2,1,0:T(8,128)(2,1)S(1)} custom-call(bf16[2,8,4,32,128]{4,3,2,1,0:T(8,128)(2,1)S(1)} %get-tuple-element.56.grads_ref, bf16[10,24,128]{2,1,0:T(8,128)(2,1)S(1)} %collective-permute-done.low_ref, bf16[10,24,128]{2,1,0:T(8,128)(2,1)S(1)} %collective-permute-done.1.high_ref, ...), custom_call_target="tpu_custom_call" | custom-call | flops 1 | bytes 1 | tf_op jit(solution)/shard_map/head_conv/pallas_call | solution.py:50
  19.3 0.1 core_sum.3
  19.3 0.3 collective-permute-done.8.refs_1_
  19.6 1.9 %collective-permute-start.9 = (bf16[5,40,256]{2,1,0:T(8,128)(2,1)S(1)}, bf16[5,40,256]{2,1,0:T(8,128)(2,1)S(1)}, u32[]{:S(2)}, u32[]{:S(2)}) collective-permute-start(bf16[5,40,256]{2,1,0:T(8,128)(2,1)S(1)} %chip_sum.2.total_ref), channel_id=1, source_target_pairs={{0,4},{4,0},{1,5},{5,1},{2,6},{6,2},{3,7},{7,3},{8,12},{12,8},{9,1... | collective-permute-start | bytes 307208 | tf_op jit(solution)/shard_map/ppermute | solution.py:639
  21.6 0.0 collective-permute-done.6.halo_ref
  21.6 1.8 %collective-permute-start.10 = (bf16[5,40,256]{2,1,0:T(8,128)(2,1)S(1)}, bf16[5,40,256]{2,1,0:T(8,128)(2,1)S(1)}, u32[]{:S(2)}, u32[]{:S(2)}) collective-permute-start(bf16[5,40,256]{2,1,0:T(8,128)(2,1)S(1)} %chip_sum.3.total_ref), channel_id=1, source_target_pairs={{0,4},{4,0},{1,5},{5,1},{2,6},{6,2},{3,7},{7,3},{8,12},{12,8},{9,1... | collective-permute-start | bytes 307208 | tf_op jit(solution)/shard_map/ppermute | solution.py:639
  23.4 0.6 %far_parts.1 = (f32[2,4,40,256]{3,2,1,0:T(8,128)S(1)}, f32[2,4,40,256]{3,2,1,0:T(8,128)S(1)}, bf16[256,512]{1,0:T(8,128)(2,1)S(1)}) custom-call(bf16[2,4,32,256]{3,2,1,0:T(8,128)(2,1)S(1)} %get-tuple-element.52.first_ref, bf16[2,4,32,256]{3,2,1,0:T(8,128)(2,1)S(1)} %collective-permute-done.2.tile_second, ...), custom_call_target="tpu_custom_call" | custom-call | flops 1 | bytes 1 | tf_op jit(solution)/shard_map/far_parts/pallas_call | solution.py:50
  24.0 1.1 %collective-permute-done.9.line_ref = bf16[5,40,256]{2,1,0:T(8,128)(2,1)S(1)} collective-permute-done((bf16[5,40,256]{2,1,0:T(8,128)(2,1)S(1)}, bf16[5,40,256]{2,1,0:T(8,128)(2,1)S(1)}, u32[]{:S(2)}, u32[]{:S(2)}) %collective-permute-start.9) | collective-permute-done | bytes 102432 | tf_op jit(solution)/shard_map/ppermute | solution.py:639
  25.1 0.4 latent_grads.2
  25.5 0.7 %second_conv.2.refs_0_ = bf16[3,10,32,256]{3,2,1,0:T(8,128)(2,1)S(1)} custom-call(bf16[10,40,768]{2,1,0:T(8,128)(2,1)S(1)} %get-tuple-element.77.cat_ref, f32[2,4,40,256]{3,2,1,0:T(8,128)S(1)} %get-tuple-element.78.near_ref, f32[2,4,40,256]{3,2,1,0:T(8,128)S(1)} %get-tuple-element.79.far_ref, bf16[2,88,256]{2,1,0:T(8,128)(2,1)S(1)} %collective-permute-done.6.halo_ref, ...), custom_call_target="tpu_custom_call" | custom-call | flops 1 | bytes 1 | tf_op jit(solution)/shard_map/second_conv/pallas_call | solution.py:50
  26.2 0.3 collective-permute-done.10.line_ref
  26.6 0.4 latent_grads.3
  26.9 0.5 second_weight_grads.1
  27.4 0.1 collective-permute-start.12
  27.5 0.7 %second_conv.3.refs_1_ = bf16[3,10,32,256]{3,2,1,0:T(8,128)(2,1)S(1)} custom-call(bf16[10,40,768]{2,1,0:T(8,128)(2,1)S(1)} %get-tuple-element.85.cat_ref, f32[2,4,40,256]{3,2,1,0:T(8,128)S(1)} %get-tuple-element.78.near_ref, f32[2,4,40,256]{3,2,1,0:T(8,128)S(1)} %get-tuple-element.79.far_ref, bf16[2,88,256]{2,1,0:T(8,128)(2,1)S(1)} %collective-permute-done.6.halo_ref, ...), custom_call_target="tpu_custom_call" | custom-call | flops 1 | bytes 1 | tf_op jit(solution)/shard_map/second_conv/pallas_call | solution.py:50
  28.2 0.4 first_weight_grads.1
  28.7 0.6 %collective-permute-start.11 = (bf16[576,128]{1,0:T(8,128)(2,1)S(1)}, bf16[576,128]{1,0:T(8,128)(2,1)S(1)}, u32[]{:S(2)}, u32[]{:S(2)}) collective-permute-start(bf16[576,128]{1,0:T(8,128)(2,1)S(1)} %get-tuple-element.87), channel_id=1, source_target_pairs={{0,8},{8,0},{16,24},{24,16},{1,9},{9,1},{17,25},{25,17},{2,10},{10... | collective-permute-start | bytes 442376 | tf_op jit(solution)/shard_map/ppermute | solution.py:639
  29.2 1.0 %collective-permute-done.11 = bf16[576,128]{1,0:T(8,128)(2,1)S(1)} collective-permute-done((bf16[576,128]{1,0:T(8,128)(2,1)S(1)}, bf16[576,128]{1,0:T(8,128)(2,1)S(1)}, u32[]{:S(2)}, u32[]{:S(2)}) %collective-permute-start.11) | collective-permute-done | bytes 147488 | tf_op jit(solution)/shard_map/ppermute | solution.py:639
  30.2 0.1 blocks.1
  30.3 3.2 %collective-permute-start.13 = (bf16[432,128]{1,0:T(8,128)(2,1)S(1)}, bf16[432,128]{1,0:T(8,128)(2,1)S(1)}, u32[]{:S(2)}, u32[]{:S(2)}) collective-permute-start(bf16[432,128]{1,0:T(8,128)(2,1)S(1)} %get-tuple-element.94), channel_id=1, source_target_pairs={{3,0},{2,1},{1,2},{0,3},{7,4},{6,5},{5,6},{4,7},{11,8},{10,9},{9,1... | collective-permute-start | bytes 331784 | tf_op jit(solution)/shard_map/ppermute | solution.py:941
  33.5 1.3 %collective-permute-start.15 = (bf16[432,128]{1,0:T(8,128)(2,1)S(1)}, bf16[432,128]{1,0:T(8,128)(2,1)S(1)}, u32[]{:S(2)}, u32[]{:S(2)}) collective-permute-start(bf16[432,128]{1,0:T(8,128)(2,1)S(1)} %get-tuple-element.96), channel_id=1, source_target_pairs={{2,0},{3,1},{0,2},{1,3},{6,4},{7,5},{4,6},{5,7},{10,8},{11,9},{8,1... | collective-permute-start | bytes 331784 | tf_op jit(solution)/shard_map/ppermute | solution.py:941
  34.8 3.3 %collective-permute-done.13.refs_1_ = bf16[432,128]{1,0:T(8,128)(2,1)S(1)} collective-permute-done((bf16[432,128]{1,0:T(8,128)(2,1)S(1)}, bf16[432,128]{1,0:T(8,128)(2,1)S(1)}, u32[]{:S(2)}, u32[]{:S(2)}) %collective-permute-start.13) | collective-permute-done | bytes 110624 | tf_op jit(solution)/shard_map/ppermute | solution.py:941
  38.2 3.4 %collective-permute-done.14.refs_2_ = bf16[432,128]{1,0:T(8,128)(2,1)S(1)} collective-permute-done((bf16[432,128]{1,0:T(8,128)(2,1)S(1)}, bf16[432,128]{1,0:T(8,128)(2,1)S(1)}, u32[]{:S(2)}, u32[]{:S(2)}) %collective-permute-start.14) | collective-permute-done | bytes 110624 | tf_op jit(solution)/shard_map/ppermute | solution.py:941
  41.6 2.0 %collective-permute-start.16 = (bf16[432,128]{1,0:T(8,128)(2,1)S(1)}, bf16[432,128]{1,0:T(8,128)(2,1)S(1)}, u32[]{:S(2)}, u32[]{:S(2)}) collective-permute-start(bf16[432,128]{1,0:T(8,128)(2,1)S(1)} %share.1.refs_0_), channel_id=1, source_target_pairs={{0,16},{8,24},{16,0},{24,8},{1,17},{9,25},{17,1},{25,9},{2,18},{10... | collective-permute-start | bytes 331784 | tf_op jit(solution)/shard_map/ppermute | solution.py:639
  43.6 1.4 %collective-permute-start.17 = (bf16[432,128]{1,0:T(8,128)(2,1)S(1)}, bf16[432,128]{1,0:T(8,128)(2,1)S(1)}, u32[]{:S(2)}, u32[]{:S(2)}) collective-permute-start(bf16[432,128]{1,0:T(8,128)(2,1)S(1)} %collective-permute-done.15.refs_1_), channel_id=1, source_target_pairs={{0,16},{8,24},{16,0},{24,8},{1,17},{9,25},{17,1},{25,9},{2,18},{10... | collective-permute-start | bytes 331784 | tf_op jit(solution)/shard_map/ppermute | solution.py:639
  45.1 2.5 %collective-permute-done.16.refs_2_ = bf16[432,128]{1,0:T(8,128)(2,1)S(1)} collective-permute-done((bf16[432,128]{1,0:T(8,128)(2,1)S(1)}, bf16[432,128]{1,0:T(8,128)(2,1)S(1)}, u32[]{:S(2)}, u32[]{:S(2)}) %collective-permute-start.16) | collective-permute-done | bytes 110624 | tf_op jit(solution)/shard_map/ppermute | solution.py:639
  47.6 1.7 %collective-permute-done.17.refs_3_ = bf16[432,128]{1,0:T(8,128)(2,1)S(1)} collective-permute-done((bf16[432,128]{1,0:T(8,128)(2,1)S(1)}, bf16[432,128]{1,0:T(8,128)(2,1)S(1)}, u32[]{:S(2)}, u32[]{:S(2)}) %collective-permute-start.17) | collective-permute-done | bytes 110624 | tf_op jit(solution)/shard_map/ppermute | solution.py:639
  49.3 0.1 chips.1.mine_ref
  49.3 0.1 collective-permute-start.18
  49.4 1.1 %input_conv.1 = bf16[2,4,32,128]{3,2,1,0:T(8,128)(2,1)} custom-call(bf16[9,128,256]{2,1,0:T(8,128)(2,1)S(1)} %copy-done, bf16[3,10,32,256]{3,2,1,0:T(8,128)(2,1)S(1)} %second_conv.2.refs_0_, bf16[3,10,32,256]{3,2,1,0:T(8,128)(2,1)S(1)} %second_conv.3.refs_1_), custom_call_target="tpu_custom_call" | custom-call | flops 1 | bytes 1 | tf_op jit(solution)/shard_map/input_conv/pallas_call | solution.py:50
  50.5 0.2 collective-permute-done.18.other_ref
  50.7 0.8 %cores.1 = (f32[288,128]{1,0:T(8,128)}, f32[576,128]{1,0:T(8,128)}) custom-call(bf16[432,128]{1,0:T(8,128)(2,1)S(1)} %chips.1.mine_ref, bf16[432,128]{1,0:T(8,128)(2,1)S(1)} %collective-permute-done.18.other_ref), custom_call_target="tpu_custom_call" | custom-call | flops 1 | bytes 1 | tf_op jit(solution)/shard_map/cores/pallas_call | solution.py:50
  (15 shorter events, 0.2 us)
Async XLA Ops:
  0.6 11.4 %collective-permute-start.3 = (bf16[2,4,32,256]{3,2,1,0:T(8,128)(2,1)}, bf16[2,4,32,256]{3,2,1,0:T(8,128)(2,1)S(1)}, u32[]{:S(2)}, u32[]{:S(2)}) collective-permute-start(bf16[2,4,32,256]{3,2,1,0:T(8,128)(2,1)} %first_far.1), channel_id=1, source_target_pairs={{0,4},{4,0},{1,5},{5,1},{2,6},{6,2},{3,7},{7,3},{8,12},{12,8},{9,1... | collective-permute-start | bytes 393224 | tf_op jit(solution)/shard_map/ppermute | solution.py:639
  3.7 8.4 %collective-permute-start.2 = (bf16[2,4,32,256]{3,2,1,0:T(8,128)(2,1)}, bf16[2,4,32,256]{3,2,1,0:T(8,128)(2,1)S(1)}, u32[]{:S(2)}, u32[]{:S(2)}) collective-permute-start(bf16[2,4,32,256]{3,2,1,0:T(8,128)(2,1)} %second_far.1), channel_id=1, source_target_pairs={{0,4},{4,0},{1,5},{5,1},{2,6},{6,2},{3,7},{7,3},{8,12},{12,8},{9,1... | collective-permute-start | bytes 393224 | tf_op jit(solution)/shard_map/ppermute | solution.py:639
  5.0 7.0 %collective-permute-start = (bf16[10,24,128]{2,1,0:T(8,128)(2,1)S(1)}, bf16[10,24,128]{2,1,0:T(8,128)(2,1)S(1)}, u32[]{:S(2)}, u32[]{:S(2)}) collective-permute-start(bf16[10,24,128]{2,1,0:T(8,128)(2,1)S(1)} %get-tuple-element.54), channel_id=1, source_target_pairs={{0,1},{1,2},{2,3},{3,0},{4,5},{5,6},{6,7},{7,4},{8,9},{9,10},{10,1... | collective-permute-start | bytes 184328 | tf_op jit(solution)/shard_map/ppermute | solution.py:645
  7.1 5.0 %collective-permute-start.1 = (bf16[10,24,128]{2,1,0:T(8,128)(2,1)S(1)}, bf16[10,24,128]{2,1,0:T(8,128)(2,1)S(1)}, u32[]{:S(2)}, u32[]{:S(2)}) collective-permute-start(bf16[10,24,128]{2,1,0:T(8,128)(2,1)S(1)} %get-tuple-element.55), channel_id=1, source_target_pairs={{0,3},{1,0},{2,1},{3,2},{4,7},{5,4},{6,5},{7,6},{8,11},{9,8},{10,9... | collective-permute-start | bytes 184328 | tf_op jit(solution)/shard_map/ppermute | solution.py:645
  12.7 1.5 %collective-permute-start.4 = (bf16[2,5,40,256]{3,2,1,0:T(8,128)(2,1)S(1)}, bf16[2,5,40,256]{3,2,1,0:T(8,128)(2,1)S(1)}, u32[]{:S(2)}, u32[]{:S(2)}) collective-permute-start(bf16[2,5,40,256]{3,2,1,0:T(8,128)(2,1)S(1)} %get-tuple-element.65), channel_id=1, source_target_pairs={{0,8},{8,0},{16,24},{24,16},{1,9},{9,1},{17,25},{25,17},{2,10},{10... | collective-permute-start | bytes 614408 | tf_op jit(solution)/shard_map/ppermute | solution.py:639
  12.8 6.4 %collective-permute-start.7 = (bf16[2,5,40,256]{3,2,1,0:T(8,128)(2,1)S(1)}, bf16[2,5,40,256]{3,2,1,0:T(8,128)(2,1)S(1)}, u32[]{:S(2)}, u32[]{:S(2)}) collective-permute-start(bf16[2,5,40,256]{3,2,1,0:T(8,128)(2,1)S(1)} %get-tuple-element.74), channel_id=1, source_target_pairs={{0,8},{8,0},{16,24},{24,16},{1,9},{9,1},{17,25},{25,17},{2,10},{10... | collective-permute-start | bytes 614408 | tf_op jit(solution)/shard_map/ppermute | solution.py:639
  14.3 5.3 %collective-permute-start.8 = (bf16[5,40,256]{2,1,0:T(8,128)(2,1)S(1)}, bf16[5,40,256]{2,1,0:T(8,128)(2,1)S(1)}, u32[]{:S(2)}, u32[]{:S(2)}) collective-permute-start(bf16[5,40,256]{2,1,0:T(8,128)(2,1)S(1)} %get-tuple-element.76), channel_id=1, source_target_pairs={{0,16},{8,24},{16,0},{24,8},{1,17},{9,25},{17,1},{25,9},{2,18},{10... | collective-permute-start | bytes 307208 | tf_op jit(solution)/shard_map/ppermute | solution.py:639
  16.5 5.1 %collective-permute-start.5 = (bf16[5,40,256]{2,1,0:T(8,128)(2,1)S(1)}, bf16[5,40,256]{2,1,0:T(8,128)(2,1)S(1)}, u32[]{:S(2)}, u32[]{:S(2)}) collective-permute-start(bf16[5,40,256]{2,1,0:T(8,128)(2,1)S(1)} %get-tuple-element.70), channel_id=1, source_target_pairs={{0,16},{8,24},{16,0},{24,8},{1,17},{9,25},{17,1},{25,9},{2,18},{10... | collective-permute-start | bytes 307208 | tf_op jit(solution)/shard_map/ppermute | solution.py:639
  16.9 4.7 %collective-permute-start.6 = (bf16[2,88,256]{2,1,0:T(8,128)(2,1)S(1)}, bf16[2,88,256]{2,1,0:T(8,128)(2,1)S(1)}, u32[]{:S(2)}, u32[]{:S(2)}) collective-permute-start(bf16[2,88,256]{2,1,0:T(8,128)(2,1)S(1)} %get-tuple-element.71), channel_id=1, source_target_pairs={{0,4},{4,0},{1,5},{5,1},{2,6},{6,2},{3,7},{7,3},{8,12},{12,8},{9,1... | collective-permute-start | bytes 270344 | tf_op jit(solution)/shard_map/ppermute | solution.py:639
  19.6 5.5 %collective-permute-start.9 = (bf16[5,40,256]{2,1,0:T(8,128)(2,1)S(1)}, bf16[5,40,256]{2,1,0:T(8,128)(2,1)S(1)}, u32[]{:S(2)}, u32[]{:S(2)}) collective-permute-start(bf16[5,40,256]{2,1,0:T(8,128)(2,1)S(1)} %chip_sum.2.total_ref), channel_id=1, source_target_pairs={{0,4},{4,0},{1,5},{5,1},{2,6},{6,2},{3,7},{7,3},{8,12},{12,8},{9,1... | collective-permute-start | bytes 307208 | tf_op jit(solution)/shard_map/ppermute | solution.py:639
  21.6 5.0 %collective-permute-start.10 = (bf16[5,40,256]{2,1,0:T(8,128)(2,1)S(1)}, bf16[5,40,256]{2,1,0:T(8,128)(2,1)S(1)}, u32[]{:S(2)}, u32[]{:S(2)}) collective-permute-start(bf16[5,40,256]{2,1,0:T(8,128)(2,1)S(1)} %chip_sum.3.total_ref), channel_id=1, source_target_pairs={{0,4},{4,0},{1,5},{5,1},{2,6},{6,2},{3,7},{7,3},{8,12},{12,8},{9,1... | collective-permute-start | bytes 307208 | tf_op jit(solution)/shard_map/ppermute | solution.py:639
  27.4 2.8 %collective-permute-start.12 = (bf16[1152,128]{1,0:T(8,128)(2,1)S(1)}, bf16[1152,128]{1,0:T(8,128)(2,1)S(1)}, u32[]{:S(2)}, u32[]{:S(2)}) collective-permute-start(bf16[1152,128]{1,0:T(8,128)(2,1)S(1)} %get-tuple-element.92), channel_id=1, source_target_pairs={{0,8},{8,0},{16,24},{24,16},{1,9},{9,1},{17,25},{25,17},{2,10},{10... | collective-permute-start | bytes 884744 | tf_op jit(solution)/shard_map/ppermute | solution.py:639
  28.7 20.7 %copy-start = (bf16[9,128,256]{2,1,0:T(8,128)(2,1)S(1)}, bf16[9,128,256]{2,1,0:T(8,128)(2,1)}, u32[]{:S(2)}) copy-start(bf16[9,128,256]{2,1,0:T(8,128)(2,1)} %w_first_ref.1) | copy-start | bytes 1769476
  28.7 1.6 %collective-permute-start.11 = (bf16[576,128]{1,0:T(8,128)(2,1)S(1)}, bf16[576,128]{1,0:T(8,128)(2,1)S(1)}, u32[]{:S(2)}, u32[]{:S(2)}) collective-permute-start(bf16[576,128]{1,0:T(8,128)(2,1)S(1)} %get-tuple-element.87), channel_id=1, source_target_pairs={{0,8},{8,0},{16,24},{24,16},{1,9},{9,1},{17,25},{25,17},{2,10},{10... | collective-permute-start | bytes 442376 | tf_op jit(solution)/shard_map/ppermute | solution.py:639
  30.3 7.8 %collective-permute-start.13 = (bf16[432,128]{1,0:T(8,128)(2,1)S(1)}, bf16[432,128]{1,0:T(8,128)(2,1)S(1)}, u32[]{:S(2)}, u32[]{:S(2)}) collective-permute-start(bf16[432,128]{1,0:T(8,128)(2,1)S(1)} %get-tuple-element.94), channel_id=1, source_target_pairs={{3,0},{2,1},{1,2},{0,3},{7,4},{6,5},{5,6},{4,7},{11,8},{10,9},{9,1... | collective-permute-start | bytes 331784 | tf_op jit(solution)/shard_map/ppermute | solution.py:941
  33.5 8.0 %collective-permute-start.14 = (bf16[432,128]{1,0:T(8,128)(2,1)S(1)}, bf16[432,128]{1,0:T(8,128)(2,1)S(1)}, u32[]{:S(2)}, u32[]{:S(2)}) collective-permute-start(bf16[432,128]{1,0:T(8,128)(2,1)S(1)} %get-tuple-element.95), channel_id=1, source_target_pairs={{1,0},{0,1},{3,2},{2,3},{5,4},{4,5},{7,6},{6,7},{9,8},{8,9},{11,10... | collective-permute-start | bytes 331784 | tf_op jit(solution)/shard_map/ppermute | solution.py:941
  33.5 10.1 %collective-permute-start.15 = (bf16[432,128]{1,0:T(8,128)(2,1)S(1)}, bf16[432,128]{1,0:T(8,128)(2,1)S(1)}, u32[]{:S(2)}, u32[]{:S(2)}) collective-permute-start(bf16[432,128]{1,0:T(8,128)(2,1)S(1)} %get-tuple-element.96), channel_id=1, source_target_pairs={{2,0},{3,1},{0,2},{1,3},{6,4},{7,5},{4,6},{5,7},{10,8},{11,9},{8,1... | collective-permute-start | bytes 331784 | tf_op jit(solution)/shard_map/ppermute | solution.py:941
  41.6 6.0 %collective-permute-start.16 = (bf16[432,128]{1,0:T(8,128)(2,1)S(1)}, bf16[432,128]{1,0:T(8,128)(2,1)S(1)}, u32[]{:S(2)}, u32[]{:S(2)}) collective-permute-start(bf16[432,128]{1,0:T(8,128)(2,1)S(1)} %share.1.refs_0_), channel_id=1, source_target_pairs={{0,16},{8,24},{16,0},{24,8},{1,17},{9,25},{17,1},{25,9},{2,18},{10... | collective-permute-start | bytes 331784 | tf_op jit(solution)/shard_map/ppermute | solution.py:639
  43.6 5.6 %collective-permute-start.17 = (bf16[432,128]{1,0:T(8,128)(2,1)S(1)}, bf16[432,128]{1,0:T(8,128)(2,1)S(1)}, u32[]{:S(2)}, u32[]{:S(2)}) collective-permute-start(bf16[432,128]{1,0:T(8,128)(2,1)S(1)} %collective-permute-done.15.refs_1_), channel_id=1, source_target_pairs={{0,16},{8,24},{16,0},{24,8},{1,17},{9,25},{17,1},{25,9},{2,18},{10... | collective-permute-start | bytes 331784 | tf_op jit(solution)/shard_map/ppermute | solution.py:639
  49.3 1.4 %collective-permute-start.18 = (bf16[432,128]{1,0:T(8,128)(2,1)S(1)}, bf16[432,128]{1,0:T(8,128)(2,1)S(1)}, u32[]{:S(2)}, u32[]{:S(2)}) collective-permute-start(bf16[432,128]{1,0:T(8,128)(2,1)S(1)} %chips.1.mine_ref), channel_id=1, source_target_pairs={{0,8},{8,0},{16,24},{24,16},{1,9},{9,1},{17,25},{25,17},{2,10},{10... | collective-permute-start | bytes 331784 | tf_op jit(solution)/shard_map/ppermute | solution.py:639
